TPU v7x, 32 devices: a whole 2x2x4 slice. The times are simulated.
32 devices in a mesh: var: 16 (over z, y, core), head: 2 (over x).
Axes of the slice: x: 2, y: 2, z: 4, core: 2. Of those that a mesh axis runs over, the one named last changes fastest.
Arguments:
- queries: bfloat16 [6144, 1024], P('var', 'head'), may hold values from -6 to 6
- keys: bfloat16 [6144, 1024], P('var', 'head'), may hold values from -6 to 6
- values: bfloat16 [6144, 1024], P('var', 'head'), may hold values from -6 to 6
- out_grad: bfloat16 [6144, 1024], P('var', 'head'), may hold values from -6 to 6
- log_sum_exp: float32 [16, 6144], P('head', 'var'), may hold values from 4.5 to 7.5
- key_blocks: int32 [48, 8], replicated, may hold values from 0 to 47, as said below
- w_qkv: bfloat16 [3, 1024, 1024], P(None, None, 'head'), may hold values from -0.1875 to 0.1875
Outputs:
- query_gradient: bfloat16 [6144, 1024], P('var', 'head')
- key_grad: bfloat16 [6144, 1024], P('var', 'head')
- value_grad: bfloat16 [6144, 1024], P('var', 'head')
- input_grad: bfloat16 [6144, 1024], P(('var', 'head'))
Inputs may be any that keep to these rules, and one draw needn't show every extreme that they name: `key_blocks`: row b lists 8 different key blocks: b itself first, and the others within 8 blocks of b.
All inputs are finite; a program needn't handle non-finite values.
Results may differ from a plain program's by a relative error of at most 0.0057.
Values may be sent and summed in bfloat16 or wider, within the bound.
No kernel may reach another device: no remote copies, remote signals or barrier semaphores. Data moves between devices by JAX's collectives and lax.ppermute only.
A program may use at most 128 MiB of HBM per device.

v0:
```python
import jax
import jax.numpy as jnp
from jax import lax
from jax.sharding import PartitionSpec as P

PATCHES = 16
VARS_BLK = 8
SPAN = 8


def shifted(value, axis, steps):
    count = lax.axis_size(axis)
    initial, last = (max(0, -steps), min(count, count - steps))
    return lax.ppermute(value, axis, [(source, source + steps) for source in range(initial, last)])


def join_window(
    lower_pieces, own_piece, upper_pieces, margin_dev, blocks_here, block_rows, axis_at
):
    joined = jnp.concatenate(lower_pieces + [own_piece] + upper_pieces, axis=axis_at)
    start_row = (margin_dev * blocks_here - SPAN) * block_rows
    window_rows = (blocks_here + 2 * SPAN) * block_rows
    return lax.slice_in_dim(joined, start_row, start_row + window_rows, axis=axis_at)


def body(queries, keys, values, out_grad, log_sum_exp, key_blocks, w_qkv):
    tok_rows, features = queries.shape
    head_count = log_sum_exp.shape[0]
    head_dim = features // head_count
    block_rows = VARS_BLK * PATCHES
    blocks_here = tok_rows // block_rows
    slot_count = key_blocks.shape[1]
    margin_dev = -(-SPAN // blocks_here)
    logit_scale = head_dim ** (-0.5)
    first_block = lax.axis_index("var") * blocks_here
    patch_index = jnp.arange(block_rows, dtype=jnp.int32) % PATCHES
    usable = jnp.tile(patch_index, slot_count)[None, :] <= patch_index[:, None]
    feature_head = jnp.arange(features, dtype=jnp.int32) // head_dim
    head_mask = (feature_head[None, :] == jnp.arange(head_count, dtype=jnp.int32)[:, None]).astype(
        jnp.bfloat16
    )
    stacked = jnp.stack([keys, values])
    lower_keys = []
    upper_keys = []
    for offset in list(range(margin_dev, 0, -1)) + list(range(-1, -margin_dev - 1, -1)):
        received = shifted(stacked, "var", offset)
        if offset > 0:
            lower_keys.append(received)
        else:
            upper_keys.append(received)
    nearby = join_window(lower_keys, stacked, upper_keys, margin_dev, blocks_here, block_rows, 1)
    nearby = nearby.reshape(2, blocks_here + 2 * SPAN, block_rows, features)
    own_lists = lax.dynamic_slice_in_dim(key_blocks, first_block, blocks_here, 0)
    near_index = own_lists - (first_block - SPAN)
    query_blocks = queries.reshape(blocks_here, block_rows, features)
    grad_blocks = out_grad.reshape(blocks_here, block_rows, features)
    lse_blocks = log_sum_exp.reshape(head_count, blocks_here, block_rows).transpose(1, 0, 2)

    def attend(index_row, query_row_block, gradient_row_block, lse_rows):
        picked_pair = nearby[:, index_row].reshape(2, slot_count * block_rows, features)
        key_row_block = picked_pair[0]
        value_row_block = picked_pair[1]
        masked_query = query_row_block[None] * head_mask[:, None, :]
        masked_grad = gradient_row_block[None] * head_mask[:, None, :]
        score_matrix = (
            jnp.einsum(
                "tlf,uf->tlu", masked_query, key_row_block, preferred_element_type=jnp.float32
            )
            * logit_scale
        )
        soft_probs = jnp.where(usable[None], jnp.exp(score_matrix - lse_rows[:, :, None]), 0.0)
        probability_gradient = jnp.einsum(
            "tlf,uf->tlu", masked_grad, value_row_block, preferred_element_type=jnp.float32
        )
        row_delta = jnp.sum(soft_probs * probability_gradient, axis=-1)
        score_gradient = (soft_probs * (probability_gradient - row_delta[:, :, None])).astype(
            jnp.bfloat16
        )
        masked_keys = key_row_block[None] * head_mask[:, None, :]
        query_gradient = jnp.einsum(
            "tlu,tuf->lf", score_gradient, masked_keys, preferred_element_type=jnp.float32
        )
        query_gradient = (query_gradient * logit_scale).astype(jnp.bfloat16)
        return (
            soft_probs.astype(jnp.bfloat16),
            score_gradient,
            query_gradient,
            row_delta,
            masked_query,
            masked_grad,
        )

    span_blocks = (2 * margin_dev + 1) * blocks_here
    shift_base = margin_dev * blocks_here - SPAN

    def query_step(partial_value, inputs):
        index_row, query_row_block, gradient_row_block, lse_rows = inputs
        (
            rounded_probability,
            score_gradient,
            query_gradient,
            row_delta,
            masked_query,
            masked_grad,
        ) = attend(index_row, query_row_block, gradient_row_block, lse_rows)
        key_portion = (
            jnp.einsum(
                "tlu,tlf->uf", score_gradient, masked_query, preferred_element_type=jnp.float32
            )
            * logit_scale
        )
        value_portion = jnp.einsum(
            "tlu,tlf->uf", rounded_probability, masked_grad, preferred_element_type=jnp.float32
        )
        both_parts = jnp.stack([key_portion, value_portion]).reshape(
            2, slot_count, block_rows, features
        )
        partial_value = partial_value.at[:, index_row + shift_base].add(both_parts)
        return (partial_value, query_gradient)

    partial_value = jnp.zeros((2, span_blocks, block_rows, features), jnp.float32)
    partial_value, query_grads = lax.scan(
        query_step, partial_value, (near_index, query_blocks, grad_blocks, lse_blocks)
    )
    centre = margin_dev * blocks_here
    reach_low = centre - SPAN
    reach_high = centre + blocks_here + SPAN
    summed = partial_value[:, centre : centre + blocks_here]
    for offset in list(range(-margin_dev, 0)) + list(range(1, margin_dev + 1)):
        slab_start = centre + offset * blocks_here
        piece_low = max(slab_start, reach_low)
        piece_high = min(slab_start + blocks_here, reach_high)
        received = shifted(partial_value[:, piece_low:piece_high], "var", offset)
        summed = summed.at[:, piece_low - slab_start : piece_high - slab_start].add(received)
    key_grad = summed[0].reshape(tok_rows, features).astype(jnp.bfloat16)
    value_grad = summed[1].reshape(tok_rows, features).astype(jnp.bfloat16)
    query_gradient = query_grads.reshape(tok_rows, features)
    all_grads = jnp.stack([query_gradient, key_grad, value_grad])
    gradient_row_block = all_grads
    input_grad = lax.psum_scatter(
        jnp.einsum("snf,sif->ni", gradient_row_block, w_qkv, preferred_element_type=jnp.float32),
        "head",
        scatter_dimension=0,
        tiled=True,
    )
    return (query_gradient, key_grad, value_grad, input_grad.astype(jnp.bfloat16))


def solution(mesh):
    in_specs = (
        P("var", "head"),
        P("var", "head"),
        P("var", "head"),
        P("var", "head"),
        P("head", "var"),
        P(),
        P(None, None, "head"),
    )
    out_specs = (P("var", "head"), P("var", "head"), P("var", "head"), P(("var", "head"), None))
    return jax.shard_map(body, mesh=mesh, in_specs=in_specs, out_specs=out_specs, check_vma=False)
```

profile of v0, /device:TPU:0, one launch (start us, length us, event | category | flops | bytes accessed | tf_op | source)
XLA Modules:
  0.0 363.6 jit_solution(13148540115013417728)
XLA Ops:
  7.2 2.3 pad_maximum_fusion
  9.5 5.2 %collective-permute-start = (bf16[2,384,512]{2,1,0:T(8,128)(2,1)}, bf16[2,384,512]{2,1,0:T(8,128)(2,1)}, u32[]{:S(2)}, u32[]{:S(2)}) collective-permute-start(bf16[2,384,512]{2,1,0:T(8,128)(2,1)} %pad_maximum_fusion), channel_id=1, source_target_pairs={{0,6},{2,8},{4,10},{6,12},{8,14},{10,16},{12,18},{14,20},{16,22},{... | collective-permute-start | bytes 2359304 | tf_op jit(solution)/shard_map/ppermute | solution.py:14
  14.7 1.3 collective-permute-start.4
  16.0 1.3 collective-permute-start.3
  17.3 4.2 %collective-permute-start.2 = (bf16[2,384,512]{2,1,0:T(8,128)(2,1)}, bf16[2,384,512]{2,1,0:T(8,128)(2,1)}, u32[]{:S(2)}, u32[]{:S(2)}) collective-permute-start(bf16[2,384,512]{2,1,0:T(8,128)(2,1)} %pad_maximum_fusion), channel_id=1, source_target_pairs={{0,2},{2,4},{4,6},{6,8},{8,10},{10,12},{12,14},{14,16},{16,18},{18... | collective-permute-start | bytes 2359304 | tf_op jit(solution)/shard_map/ppermute | solution.py:14
  21.5 4.3 %collective-permute-start.1 = (bf16[2,384,512]{2,1,0:T(8,128)(2,1)}, bf16[2,384,512]{2,1,0:T(8,128)(2,1)}, u32[]{:S(2)}, u32[]{:S(2)}) collective-permute-start(bf16[2,384,512]{2,1,0:T(8,128)(2,1)} %pad_maximum_fusion), channel_id=1, source_target_pairs={{0,4},{2,6},{4,8},{6,10},{8,12},{10,14},{12,16},{14,18},{16,20},{1... | collective-permute-start | bytes 2359304 | tf_op jit(solution)/shard_map/ppermute | solution.py:14
  27.2 34.2 %collective-permute-done = bf16[2,384,512]{2,1,0:T(8,128)(2,1)} collective-permute-done((bf16[2,384,512]{2,1,0:T(8,128)(2,1)}, bf16[2,384,512]{2,1,0:T(8,128)(2,1)}, u32[]{:S(2)}, u32[]{:S(2)}) %collective-permute-start) | collective-permute-done | bytes 786464 | tf_op jit(solution)/shard_map/ppermute | solution.py:14
  61.5 1.3 collective-permute-start.5
  62.8 1.2 constant_dynamic-update-slice_fusion.6
  63.9 14.4 %collective-permute-done.1 = bf16[2,384,512]{2,1,0:T(8,128)(2,1)} collective-permute-done((bf16[2,384,512]{2,1,0:T(8,128)(2,1)}, bf16[2,384,512]{2,1,0:T(8,128)(2,1)}, u32[]{:S(2)}, u32[]{:S(2)}) %collective-permute-start.1) | collective-permute-done | bytes 786464 | tf_op jit(solution)/shard_map/ppermute | solution.py:14
  78.3 1.2 constant_dynamic-update-slice_fusion.5
  79.5 1.2 constant_dynamic-update-slice_fusion.4
  80.8 1.2 constant_dynamic-update-slice_fusion.2
  82.0 1.2 constant_dynamic-update-slice_fusion.1
  83.3 2.5 slice.219
  85.8 5.6 %broadcast_in_dim.44 = f32[2,21,128,512]{3,2,1,0:T(8,128)} broadcast(f32[]{:T(128)} %constant.270.clone.1), dimensions={} | broadcast | bytes 11010052 | tf_op jit(solution)/shard_map/broadcast_in_dim | solution.py:121
  91.4 94.3 %while.26 = (s32[]{:T(128)}, f32[2,21,128,512]{3,2,1,0:T(8,128)}, bf16[3,128,512]{2,1,0:T(8,128)(2,1)}, s32[3,8]{1,0:T(4,128)S(1)}, bf16[3,128,512]{2,1,0:T(8,12...) while((s32[]{:T(128)}, f32[2,21,128,512]{3,2,1,0:T(8,128)}, ...), condition=%wide.region_3.4_spmd.clone.clone, body=%wide.region_0.3_spmd.clone.clone.sunk | while | flops 5393620992 | bytes 69963656 | solution.py:122
  94.9 4.5 %gather_fusion = bf16[8,2,128,512]{3,2,1,0:T(8,128)(2,1)} fusion(bf16[2,19,128,512]{3,2,1,0:T(8,128)(2,1)} %get-tuple-element.446, s32[1024]{0:T(1024)} %pad_clamp_fusion.2), kind=kCustom, calls=%fused_computation.clone.clone.1 | custom fusion | bytes 4194336 | tf_op jit(solution)/shard_map/while/body/eval_jaxpr/gather | solution.py:60
  99.5 1.7 fusion.94
  101.2 1.3 fusion.96
  102.5 1.6 fusion.97
  104.1 1.8 multiply_reduce_fusion.2
  105.9 1.3 multiply_convert_fusion.2
  107.2 2.0 fusion.98
  109.2 1.3 bitcast_multiply_fusion.2
  110.5 2.7 maximum_bitcast_fusion.2
  113.2 9.6 %scatter_fusion = f32[2,21,128,512]{3,2,1,0:T(8,128)} fusion(f32[2,21,128,512]{3,2,1,0:T(8,128)} %get-tuple-element.430, s32[8]{0:T(128)S(1)} %copy-done.7, f32[8,2,128,512]{3,2,1,0:T(8,128)} %maximum_bitcast_fusion.2), kind=kCustom, calls=%fused_computation.1.clone.clone.1 | custom fusion | flops 1048576 | bytes 12582944 | tf_op jit(solution)/shard_map/while/body/eval_jaxpr/scatter-add | solution.py:118
  125.4 1.0 dynamic-slice_bitcast_fusion.5
  126.4 4.5 %gather_fusion = bf16[8,2,128,512]{3,2,1,0:T(8,128)(2,1)} fusion(bf16[2,19,128,512]{3,2,1,0:T(8,128)(2,1)} %get-tuple-element.446, s32[1024]{0:T(1024)} %pad_clamp_fusion.2), kind=kCustom, calls=%fused_computation.clone.clone.1 | custom fusion | bytes 4194336 | tf_op jit(solution)/shard_map/while/body/eval_jaxpr/gather | solution.py:60
  130.9 1.7 fusion.94
  132.6 1.3 fusion.96
  133.9 1.6 fusion.97
  135.5 1.8 multiply_reduce_fusion.2
  137.3 1.3 multiply_convert_fusion.2
  138.7 2.0 fusion.98
  140.7 1.3 bitcast_multiply_fusion.2
  142.0 2.7 maximum_bitcast_fusion.2
  144.7 9.6 %scatter_fusion = f32[2,21,128,512]{3,2,1,0:T(8,128)} fusion(f32[2,21,128,512]{3,2,1,0:T(8,128)} %get-tuple-element.430, s32[8]{0:T(128)S(1)} %copy-done.7, f32[8,2,128,512]{3,2,1,0:T(8,128)} %maximum_bitcast_fusion.2), kind=kCustom, calls=%fused_computation.1.clone.clone.1 | custom fusion | flops 1048576 | bytes 12582944 | tf_op jit(solution)/shard_map/while/body/eval_jaxpr/scatter-add | solution.py:118
  157.8 4.5 %gather_fusion = bf16[8,2,128,512]{3,2,1,0:T(8,128)(2,1)} fusion(bf16[2,19,128,512]{3,2,1,0:T(8,128)(2,1)} %get-tuple-element.446, s32[1024]{0:T(1024)} %pad_clamp_fusion.2), kind=kCustom, calls=%fused_computation.clone.clone.1 | custom fusion | bytes 4194336 | tf_op jit(solution)/shard_map/while/body/eval_jaxpr/gather | solution.py:60
  162.4 1.7 fusion.94
  164.1 1.3 fusion.96
  165.4 1.6 fusion.97
  167.0 1.8 multiply_reduce_fusion.2
  168.8 1.3 multiply_convert_fusion.2
  170.2 2.0 fusion.98
  172.2 1.3 bitcast_multiply_fusion.2
  173.5 2.7 maximum_bitcast_fusion.2
  176.2 9.6 %scatter_fusion = f32[2,21,128,512]{3,2,1,0:T(8,128)} fusion(f32[2,21,128,512]{3,2,1,0:T(8,128)} %get-tuple-element.430, s32[8]{0:T(128)S(1)} %copy-done.7, f32[8,2,128,512]{3,2,1,0:T(8,128)} %maximum_bitcast_fusion.2), kind=kCustom, calls=%fused_computation.1.clone.clone.1 | custom fusion | flops 1048576 | bytes 12582944 | tf_op jit(solution)/shard_map/while/body/eval_jaxpr/scatter-add | solution.py:118
  185.7 1.8 fusion.61
  187.6 1.5 collective-permute-start.6
  189.0 4.5 %fusion.62 = (f32[2,3,128,512]{3,2,1,0:T(8,128)S(1)}, f32[2,3,128,512]{3,2,1,0:T(8,128)S(1)}, f32[2,3,128,512]{3,2,1,0:T(8,128)S(1)}, f32[2,3,128,512]{3,2,1,0:T(8,128)S(1)}, f32[2,3,128,512]{3,2,1,0:T(8,128)S(1)}) fusion(f32[2,21,128,512]{3,2,1,0:T(8,128)} %get-tuple-element.471), kind=kLoop, calls=%fused_computation.87 | loop fusion | bytes 15728640 | tf_op jit(solution)/shard_map/slice | solution.py:133
  193.6 1.3 collective-permute-start.7
  194.9 6.4 %collective-permute-start.9 = (f32[2,3,128,512]{3,2,1,0:T(8,128)S(1)}, f32[2,3,128,512]{3,2,1,0:T(8,128)S(1)}, u32[]{:S(2)}, u32[]{:S(2)}) collective-permute-start(f32[2,3,128,512]{3,2,1,0:T(8,128)S(1)} %get-tuple-element.328), channel_id=1, source_target_pairs={{0,2},{2,4},{4,6},{6,8},{8,10},{10,12},{12,14},{14,16},{16,18},{18... | collective-permute-start | bytes 4718600 | tf_op jit(solution)/shard_map/ppermute | solution.py:14
  201.3 1.3 collective-permute-start.8
  202.6 5.7 %collective-permute-start.10 = (f32[2,3,128,512]{3,2,1,0:T(8,128)S(1)}, f32[2,3,128,512]{3,2,1,0:T(8,128)S(1)}, u32[]{:S(2)}, u32[]{:S(2)}) collective-permute-start(f32[2,3,128,512]{3,2,1,0:T(8,128)S(1)} %get-tuple-element.331), channel_id=1, source_target_pairs={{0,4},{2,6},{4,8},{6,10},{8,12},{10,14},{12,16},{14,18},{16,20},{1... | collective-permute-start | bytes 4718600 | tf_op jit(solution)/shard_map/ppermute | solution.py:14
  208.3 8.2 %collective-permute-done.6 = f32[2,2,128,512]{3,2,1,0:T(8,128)S(1)} collective-permute-done((f32[2,2,128,512]{3,2,1,0:T(8,128)S(1)}, f32[2,2,128,512]{3,2,1,0:T(8,128)S(1)}, u32[]{:S(2)}, u32[]{:S(2)}) %collective-permute-start.6) | collective-permute-done | bytes 1048608 | tf_op jit(solution)/shard_map/ppermute | solution.py:14
  216.5 1.3 collective-permute-start.11
  217.8 1.4 add_dynamic-update-slice_fusion
  219.3 13.7 %collective-permute-done.7 = f32[2,3,128,512]{3,2,1,0:T(8,128)S(1)} collective-permute-done((f32[2,3,128,512]{3,2,1,0:T(8,128)S(1)}, f32[2,3,128,512]{3,2,1,0:T(8,128)S(1)}, u32[]{:S(2)}, u32[]{:S(2)}) %collective-permute-start.7) | collective-permute-done | bytes 1572896 | tf_op jit(solution)/shard_map/ppermute | solution.py:14
  233.0 64.6 %collective-permute-done.10 = f32[2,3,128,512]{3,2,1,0:T(8,128)S(1)} collective-permute-done((f32[2,3,128,512]{3,2,1,0:T(8,128)S(1)}, f32[2,3,128,512]{3,2,1,0:T(8,128)S(1)}, u32[]{:S(2)}, u32[]{:S(2)}) %collective-permute-start.10) | collective-permute-done | bytes 1572896 | tf_op jit(solution)/shard_map/ppermute | solution.py:14
  298.5 21.5 %collective-permute-done.11 = f32[2,2,128,512]{3,2,1,0:T(8,128)S(1)} collective-permute-done((f32[2,2,128,512]{3,2,1,0:T(8,128)S(1)}, f32[2,2,128,512]{3,2,1,0:T(8,128)S(1)}, u32[]{:S(2)}, u32[]{:S(2)}) %collective-permute-start.11) | collective-permute-done | bytes 1048608 | tf_op jit(solution)/shard_map/ppermute | solution.py:14
  321.2 2.6 convolution_bitcast_fusion
  323.8 31.0 %reduce-scatter.2.cloned.1.call-done = f32[192,1024]{1,0:T(8,128)} async-done(((f32[384,1024]{1,0:T(8,128)}), f32[192,1024]{1,0:T(8,128)}) %reduce-scatter.2.cloned.1.call-update) | async-done | bytes 786448 | tf_op jit(solution)/shard_map/reduce_scatter | solution.py:140
  354.8 1.9 convert_element_type.67
  (87 shorter events, 13.3 us)
Async XLA Ops:
  7.2 314.0 %copy-start = (bf16[3,1024,512]{2,1,0:T(8,128)(2,1)S(1)}, bf16[3,1024,512]{2,1,0:T(8,128)(2,1)}, u32[]{:S(2)}) copy-start(bf16[3,1024,512]{2,1,0:T(8,128)(2,1)} %param.35) | copy-start | bytes 9437188
  7.2 73.5 %copy-start.1 = (bf16[384,512]{1,0:T(8,128)(2,1)S(1)}, bf16[384,512]{1,0:T(8,128)(2,1)}, u32[]{:S(2)}) copy-start(bf16[384,512]{1,0:T(8,128)(2,1)} %param.31) | copy-start | bytes 1179652
  7.2 347.6 %reduce-scatter.2.cloned.1.call-start = ((), (), s32[]{:S(2)}) async-start(), calls=%async_computation.1 | async-start | bytes 2359296 | tf_op jit(solution)/shard_map/reduce_scatter | solution.py:140
  9.5 52.0 %collective-permute-start = (bf16[2,384,512]{2,1,0:T(8,128)(2,1)}, bf16[2,384,512]{2,1,0:T(8,128)(2,1)}, u32[]{:S(2)}, u32[]{:S(2)}) collective-permute-start(bf16[2,384,512]{2,1,0:T(8,128)(2,1)} %pad_maximum_fusion), channel_id=1, source_target_pairs={{0,6},{2,8},{4,10},{6,12},{8,14},{10,16},{12,18},{14,20},{16,22},{... | collective-permute-start | bytes 2359304 | tf_op jit(solution)/shard_map/ppermute | solution.py:14
  14.7 67.3 %collective-permute-start.4 = (bf16[2,384,512]{2,1,0:T(8,128)(2,1)}, bf16[2,384,512]{2,1,0:T(8,128)(2,1)}, u32[]{:S(2)}, u32[]{:S(2)}) collective-permute-start(bf16[2,384,512]{2,1,0:T(8,128)(2,1)} %pad_maximum_fusion), channel_id=1, source_target_pairs={{4,0},{6,2},{8,4},{10,6},{12,8},{14,10},{16,12},{18,14},{20,16},{2... | collective-permute-start | bytes 2359304 | tf_op jit(solution)/shard_map/ppermute | solution.py:14
  16.0 64.8 %collective-permute-start.3 = (bf16[2,384,512]{2,1,0:T(8,128)(2,1)}, bf16[2,384,512]{2,1,0:T(8,128)(2,1)}, u32[]{:S(2)}, u32[]{:S(2)}) collective-permute-start(bf16[2,384,512]{2,1,0:T(8,128)(2,1)} %pad_maximum_fusion), channel_id=1, source_target_pairs={{2,0},{4,2},{6,4},{8,6},{10,8},{12,10},{14,12},{16,14},{18,16},{20... | collective-permute-start | bytes 2359304 | tf_op jit(solution)/shard_map/ppermute | solution.py:14
  17.3 62.2 %collective-permute-start.2 = (bf16[2,384,512]{2,1,0:T(8,128)(2,1)}, bf16[2,384,512]{2,1,0:T(8,128)(2,1)}, u32[]{:S(2)}, u32[]{:S(2)}) collective-permute-start(bf16[2,384,512]{2,1,0:T(8,128)(2,1)} %pad_maximum_fusion), channel_id=1, source_target_pairs={{0,2},{2,4},{4,6},{6,8},{8,10},{10,12},{12,14},{14,16},{16,18},{18... | collective-permute-start | bytes 2359304 | tf_op jit(solution)/shard_map/ppermute | solution.py:14
  21.5 56.9 %collective-permute-start.1 = (bf16[2,384,512]{2,1,0:T(8,128)(2,1)}, bf16[2,384,512]{2,1,0:T(8,128)(2,1)}, u32[]{:S(2)}, u32[]{:S(2)}) collective-permute-start(bf16[2,384,512]{2,1,0:T(8,128)(2,1)} %pad_maximum_fusion), channel_id=1, source_target_pairs={{0,4},{2,6},{4,8},{6,10},{8,12},{10,14},{12,16},{14,18},{16,20},{1... | collective-permute-start | bytes 2359304 | tf_op jit(solution)/shard_map/ppermute | solution.py:14
  26.6 54.1 %copy-start.2 = (bf16[384,512]{1,0:T(8,128)(2,1)S(1)}, bf16[384,512]{1,0:T(8,128)(2,1)}, u32[]{:S(2)}) copy-start(bf16[384,512]{1,0:T(8,128)(2,1)} %param.30) | copy-start | bytes 1179652
  61.5 21.7 %collective-permute-start.5 = (bf16[2,384,512]{2,1,0:T(8,128)(2,1)}, bf16[2,384,512]{2,1,0:T(8,128)(2,1)S(1)}, u32[]{:S(2)}, u32[]{:S(2)}) collective-permute-start(bf16[2,384,512]{2,1,0:T(8,128)(2,1)} %pad_maximum_fusion), channel_id=1, source_target_pairs={{6,0},{8,2},{10,4},{12,6},{14,8},{16,10},{18,12},{20,14},{22,16},{... | collective-permute-start | bytes 2359304 | tf_op jit(solution)/shard_map/ppermute | solution.py:14
  85.8 5.6 %copy-start.5 = (s32[512]{0:T(512)S(1)}, s32[512]{0:T(512)}, u32[]{:S(2)}) copy-start(s32[512]{0:T(512)} %add_select_fusion) | copy-start | bytes 6148
  91.4 0.5 copy-start.8
  91.4 1.2 copy-start.10
  110.5 2.7 copy-start.7
  113.2 9.6 %copy-start.6 = (s32[512]{0:T(512)S(1)}, s32[512]{0:T(512)}, u32[]{:S(2)}) copy-start(s32[512]{0:T(512)} %get-tuple-element.482) | copy-start | bytes 6148 | tf_op jit(solution)/shard_map/while
  113.2 9.6 %copy-start.9 = (s32[128]{0:T(128)S(1)}, s32[128]{0:T(128)}, u32[]{:S(2)}) copy-start(s32[128]{0:T(128)} %copy-done.8) | copy-start | bytes 1540 | tf_op jit(solution)/shard_map/while
  113.2 9.6 %copy-start.11 = (s32[3,8]{1,0:T(4,128)S(1)}, s32[3,8]{1,0:T(4,128)}, u32[]{:S(2)}) copy-start(s32[3,8]{1,0:T(4,128)} %copy-done.10) | copy-start | bytes 292 | tf_op jit(solution)/shard_map/while
  122.8 0.5 copy-start.8
  122.8 1.2 copy-start.10
  142.0 2.7 copy-start.7
  144.7 9.6 %copy-start.6 = (s32[512]{0:T(512)S(1)}, s32[512]{0:T(512)}, u32[]{:S(2)}) copy-start(s32[512]{0:T(512)} %get-tuple-element.482) | copy-start | bytes 6148 | tf_op jit(solution)/shard_map/while
  144.7 9.6 %copy-start.9 = (s32[128]{0:T(128)S(1)}, s32[128]{0:T(128)}, u32[]{:S(2)}) copy-start(s32[128]{0:T(128)} %copy-done.8) | copy-start | bytes 1540 | tf_op jit(solution)/shard_map/while
  144.7 9.6 %copy-start.11 = (s32[3,8]{1,0:T(4,128)S(1)}, s32[3,8]{1,0:T(4,128)}, u32[]{:S(2)}) copy-start(s32[3,8]{1,0:T(4,128)} %copy-done.10) | copy-start | bytes 292 | tf_op jit(solution)/shard_map/while
  154.3 0.5 copy-start.8
  154.3 1.2 copy-start.10
  173.5 2.7 copy-start.7
  176.1 9.6 %copy-start.6 = (s32[512]{0:T(512)S(1)}, s32[512]{0:T(512)}, u32[]{:S(2)}) copy-start(s32[512]{0:T(512)} %get-tuple-element.482) | copy-start | bytes 6148 | tf_op jit(solution)/shard_map/while
  176.1 9.6 %copy-start.9 = (s32[128]{0:T(128)S(1)}, s32[128]{0:T(128)}, u32[]{:S(2)}) copy-start(s32[128]{0:T(128)} %copy-done.8) | copy-start | bytes 1540 | tf_op jit(solution)/shard_map/while
  176.1 9.6 %copy-start.11 = (s32[3,8]{1,0:T(4,128)S(1)}, s32[3,8]{1,0:T(4,128)}, u32[]{:S(2)}) copy-start(s32[3,8]{1,0:T(4,128)} %copy-done.10) | copy-start | bytes 292 | tf_op jit(solution)/shard_map/while
  187.6 28.9 %collective-permute-start.6 = (f32[2,2,128,512]{3,2,1,0:T(8,128)S(1)}, f32[2,2,128,512]{3,2,1,0:T(8,128)S(1)}, u32[]{:S(2)}, u32[]{:S(2)}) collective-permute-start(f32[2,2,128,512]{3,2,1,0:T(8,128)S(1)} %get-tuple-element.326), channel_id=1, source_target_pairs={{6,0},{8,2},{10,4},{12,6},{14,8},{16,10},{18,12},{20,14},{22,16},{... | collective-permute-start | bytes 3145736 | tf_op jit(solution)/shard_map/ppermute | solution.py:14
  193.6 39.4 %collective-permute-start.7 = (f32[2,3,128,512]{3,2,1,0:T(8,128)S(1)}, f32[2,3,128,512]{3,2,1,0:T(8,128)S(1)}, u32[]{:S(2)}, u32[]{:S(2)}) collective-permute-start(f32[2,3,128,512]{3,2,1,0:T(8,128)S(1)} %get-tuple-element.327), channel_id=1, source_target_pairs={{4,0},{6,2},{8,4},{10,6},{12,8},{14,10},{16,12},{18,14},{20,16},{2... | collective-permute-start | bytes 4718600 | tf_op jit(solution)/shard_map/ppermute | solution.py:14
  194.9 38.1 %collective-permute-start.9 = (f32[2,3,128,512]{3,2,1,0:T(8,128)S(1)}, f32[2,3,128,512]{3,2,1,0:T(8,128)S(1)}, u32[]{:S(2)}, u32[]{:S(2)}) collective-permute-start(f32[2,3,128,512]{3,2,1,0:T(8,128)S(1)} %get-tuple-element.328), channel_id=1, source_target_pairs={{0,2},{2,4},{4,6},{6,8},{8,10},{10,12},{12,14},{14,16},{16,18},{18... | collective-permute-start | bytes 4718600 | tf_op jit(solution)/shard_map/ppermute | solution.py:14
  201.3 31.7 %collective-permute-start.8 = (f32[2,3,128,512]{3,2,1,0:T(8,128)S(1)}, f32[2,3,128,512]{3,2,1,0:T(8,128)S(1)}, u32[]{:S(2)}, u32[]{:S(2)}) collective-permute-start(f32[2,3,128,512]{3,2,1,0:T(8,128)S(1)} %get-tuple-element.329), channel_id=1, source_target_pairs={{2,0},{4,2},{6,4},{8,6},{10,8},{12,10},{14,12},{16,14},{18,16},{20... | collective-permute-start | bytes 4718600 | tf_op jit(solution)/shard_map/ppermute | solution.py:14
  202.6 95.0 %collective-permute-start.10 = (f32[2,3,128,512]{3,2,1,0:T(8,128)S(1)}, f32[2,3,128,512]{3,2,1,0:T(8,128)S(1)}, u32[]{:S(2)}, u32[]{:S(2)}) collective-permute-start(f32[2,3,128,512]{3,2,1,0:T(8,128)S(1)} %get-tuple-element.331), channel_id=1, source_target_pairs={{0,4},{2,6},{4,8},{6,10},{8,12},{10,14},{12,16},{14,18},{16,20},{1... | collective-permute-start | bytes 4718600 | tf_op jit(solution)/shard_map/ppermute | solution.py:14
  216.5 103.6 %collective-permute-start.11 = (f32[2,2,128,512]{3,2,1,0:T(8,128)S(1)}, f32[2,2,128,512]{3,2,1,0:T(8,128)S(1)}, u32[]{:S(2)}, u32[]{:S(2)}) collective-permute-start(f32[2,2,128,512]{3,2,1,0:T(8,128)S(1)} %get-tuple-element.325), channel_id=1, source_target_pairs={{0,6},{2,8},{4,10},{6,12},{8,14},{10,16},{12,18},{14,20},{16,22},{... | collective-permute-start | bytes 3145736 | tf_op jit(solution)/shard_map/ppermute | solution.py:14
  298.5 22.7 %copy-start.12 = (bf16[3,128,512]{2,1,0:T(8,128)(2,1)S(1)}, bf16[3,128,512]{2,1,0:T(8,128)(2,1)}, u32[]{:S(2)}) copy-start(bf16[3,128,512]{2,1,0:T(8,128)(2,1)} %get-tuple-element.472) | copy-start | bytes 1179652
  320.4 0.7 copy-start.4
  320.4 3.3 copy-start.3
Sparse Core Ops, SparseCore 0:
  323.9 30.8 reduce-scatter.1
where the time goes:
time: 365 us; the launch traced here: 364 us
  waiting for transfers between devices  188 us (52%)
  other arithmetic  53.7 us (15%)
  local copies, waits for them, and re-layouts  46 us (13%)
  starting transfers between devices  35.1 us (10%)
  matrix products  26.6 us (7%)
  between operations  14.3 us (4%)
    ppermute x12, waiting for transfers between devices, shifted(): lax.ppermute(value, axis, [(source, source + steps) for source in range(i...  157 us
    ppermute x12, starting transfers between devices, shifted(): lax.ppermute(value, axis, [(source, source + steps) for source in range(i...  35.1 us
    reduce_scatter x1, waiting for transfers between devices, body(): lax.psum_scatter(jnp.einsum('snf,sif->ni', gradient_row_block, w_qkv, pre...  31 us
    scatter-add x3, other arithmetic, query_step(): partial_value = partial_value.at[:, index_row + shift_base].add(both_parts)  28.7 us
    gather x3, local copies, waits for them, and re-layouts, attend(): nearby[:, index_row].reshape(2, slot_count * block_rows, features)  13.6 us
    another operation x3, other arithmetic, query_step(): jnp.stack([key_portion, value_portion])  8.02 us
  transfers between devices with their start and end apart: 13, of which 7 were waited for; matrix products, arithmetic and copies ran while one was open for 4% of the time, Pallas kernels for 0%

commit v1 on v0

v1 whole, which is shorter than its diff:
```python
import functools

import jax
import jax.numpy as jnp
from jax import lax
from jax.experimental import pallas as pl
from jax.experimental.pallas import tpu as pltpu
from jax.sharding import PartitionSpec as P

PATCHES = 16
BLOCK = 128
SPAN = 8
GROUP = 4
LANES = 128
LSE_ROWS = 16
F32 = jnp.float32
BF16 = jnp.bfloat16
VMEM_LIMIT = 40 * 1024 * 1024


def vmem():
    return pl.BlockSpec(memory_space=pltpu.VMEM)


def split_three(x):
    high = x.astype(BF16).astype(F32)
    rest = x - high
    mid = rest.astype(BF16).astype(F32)
    return high, mid, rest - mid


def pack_kernel(slots, head_dim, q_ref, k_ref, v_ref, g_ref, lse_ref, kv_ref, qo_ref):
    rows = q_ref.shape[0]
    blocks = rows // BLOCK
    scale = head_dim ** (-0.5)
    for member in range(GROUP):
        for slot in range(slots):
            head = member * slots + slot
            at = slice(head * head_dim, (head + 1) * head_dim)
            kv_ref[member, slot] = jnp.concatenate([k_ref[:, at], v_ref[:, at]], axis=1)
            scaled = (q_ref[:, at].astype(F32) * scale).astype(BF16)
            qo_ref[member, slot, :rows] = jnp.concatenate([scaled, g_ref[:, at]], axis=1)
            lse = lse_ref[head : head + 1, :]
            parts = [
                part[:, b * BLOCK : (b + 1) * BLOCK] for part in split_three(lse) for b in range(blocks)
            ]
            parts.append(jnp.zeros((LSE_ROWS - len(parts), BLOCK), F32))
            qo_ref[member, slot, rows:] = jnp.concatenate(parts, axis=0).astype(BF16)


def attend_kernel(
    slots,
    blocks_here,
    head_dim,
    kb_ref,
    own_ref,
    low_ref,
    high_ref,
    qo_ref,
    own_out,
    low_out,
    high_out,
    dq_out,
    kv_win,
    k_turn,
    acc,
    kv_pick,
    kt_pick,
    both,
    prob,
    prod,
    scores,
    sems,
):
    group_blocks = GROUP * blocks_here
    window = group_blocks + 2 * SPAN
    rows = blocks_here * BLOCK
    slot_count = kb_ref.shape[1]
    keys = slot_count * BLOCK
    chunk = 2 * BLOCK
    scale = head_dim ** (-0.5)
    first = (lax.axis_index("var") // GROUP) * group_blocks
    key_patch = lax.broadcasted_iota(jnp.int32, (PATCHES, BLOCK), 0)
    query_patch = lax.broadcasted_iota(jnp.int32, (PATCHES, BLOCK), 1) % PATCHES
    usable = key_patch <= query_patch
    lane = lax.broadcasted_iota(jnp.int32, (BLOCK, LANES), 1)

    for slot in range(slots):
        copies = [
            pltpu.make_async_copy(low_ref.at[slot], kv_win.at[pl.ds(0, SPAN)], sems.at[0]),
            pltpu.make_async_copy(
                high_ref.at[slot], kv_win.at[pl.ds(SPAN + group_blocks, SPAN)], sems.at[1]
            ),
        ]
        for member in range(GROUP):
            copies.append(
                pltpu.make_async_copy(
                    own_ref.at[member, slot],
                    kv_win.at[pl.ds(SPAN + member * blocks_here, blocks_here)],
                    sems.at[2 + member],
                )
            )
        for copy in copies:
            copy.start()
        acc[...] = jnp.zeros_like(acc)
        for copy in copies:
            copy.wait()

        @pl.loop(0, window)
        def _(block):
            k_turn[block] = kv_win[block][:, :head_dim].T

        for member in range(GROUP):
            lse_parts = qo_ref[member, slot, rows:].astype(F32)

            for local in range(blocks_here):
                query_block = member * blocks_here + local
                lse = (
                    lse_parts[local : local + 1]
                    + lse_parts[blocks_here + local : blocks_here + local + 1]
                ) + lse_parts[2 * blocks_here + local : 2 * blocks_here + local + 1]
                shift = jnp.where(usable, -lse, -1e30)
                qo = qo_ref[member, slot, local * BLOCK : (local + 1) * BLOCK]
                zero = jnp.zeros_like(qo)
                both[:BLOCK] = jnp.where(lane < head_dim, qo, zero)
                both[BLOCK:] = jnp.where(lane < head_dim, zero, qo)
                index = [
                    kb_ref[first + query_block, s] - first + SPAN for s in range(slot_count)
                ]
                for s in range(slot_count):
                    kv_pick[s * BLOCK : (s + 1) * BLOCK] = kv_win[index[s]]
                    kt_pick[:, s * BLOCK : (s + 1) * BLOCK] = k_turn[index[s]]
                delta = jnp.zeros((8, BLOCK), F32)
                for at in range(0, keys, chunk):
                    x = lax.dot_general(
                        kv_pick[at : at + chunk],
                        both[...],
                        (((1,), (1,)), ((), ())),
                        preferred_element_type=F32,
                    )
                    s_part = x[:, :BLOCK].reshape(chunk // PATCHES, PATCHES, BLOCK)
                    p = jnp.exp(s_part + shift[None]).reshape(chunk, BLOCK)
                    t = p * x[:, BLOCK:]
                    prob[at : at + chunk] = p
                    prod[at : at + chunk] = t
                    delta = delta + jnp.sum(t.reshape(chunk // 8, 8, BLOCK), axis=0)
                delta = jnp.sum(delta, axis=0, keepdims=True)
                dq = jnp.zeros((head_dim, BLOCK), F32)
                for at in range(0, keys, chunk):
                    p = prob[at : at + chunk]
                    ds = (prod[at : at + chunk] - p * delta).astype(BF16)
                    scores[at : at + chunk, :BLOCK] = ds
                    scores[at : at + chunk, BLOCK:] = p.astype(BF16)
                    dq = dq + jnp.dot(
                        kt_pick[:, at : at + chunk], ds, preferred_element_type=F32
                    )
                    r = jnp.dot(scores[at : at + chunk], both[...], preferred_element_type=F32)
                    for s in range(chunk // BLOCK):
                        where = index[at // BLOCK + s]
                        acc[where] = acc[where] + r[s * BLOCK : (s + 1) * BLOCK]
                dq_out[
                    member,
                    local * BLOCK : (local + 1) * BLOCK,
                    slot * head_dim : (slot + 1) * head_dim,
                ] = (dq * scale).T.astype(BF16)

        low_out[slot] = acc[:SPAN].astype(BF16)
        high_out[slot] = acc[SPAN + group_blocks :].astype(BF16)
        own_out[slot] = acc[SPAN : SPAN + group_blocks]


def finish_kernel(
    slots, head_dim, dkv_ref, dq_ref, w_ref, dq_out, dk_out, dv_out, send_out, keep_out, grads
):
    half = keep_out.shape[0]
    for member in range(GROUP):
        for slot in range(slots):
            head = member * slots + slot
            at = slice(head * head_dim, (head + 1) * head_dim)
            both = dkv_ref[member, slot]
            grads[1, :, at] = both[:, :head_dim]
            grads[2, :, at] = both[:, head_dim:]
            grads[0, :, at] = dq_ref[member, :, slot * head_dim : (slot + 1) * head_dim]
    dq_out[...] = grads[0]
    dk_out[...] = grads[1]
    dv_out[...] = grads[2]
    me = lax.axis_index("head")
    heads = lax.axis_size("head")
    for piece in range(heads):
        owner = (me + 1 + piece) % heads
        begin = pl.multiple_of(owner * half, half)
        total = None
        for s in range(3):
            part = lax.dot_general(
                grads[s, pl.ds(begin, half), :],
                w_ref[s],
                (((1,), (1,)), ((), ())),
                preferred_element_type=F32,
            )
            total = part if total is None else total + part
        if piece == heads - 1:
            keep_out[...] = total
        else:
            send_out[piece] = total.astype(BF16)


def body(queries, keys, values, out_grad, log_sum_exp, key_blocks, w_qkv):
    rows, features = queries.shape
    head_count = log_sum_exp.shape[0]
    head_dim = features // head_count
    slots = head_count // GROUP
    blocks_here = rows // BLOCK
    group_blocks = GROUP * blocks_here
    window = group_blocks + 2 * SPAN
    slot_count = key_blocks.shape[1]
    devices = lax.axis_size("var")
    heads = lax.axis_size("head")
    width = w_qkv.shape[1]
    groups = [[base + i for i in range(GROUP)] for base in range(0, devices, GROUP)]
    params = pltpu.CompilerParams(vmem_limit_bytes=VMEM_LIMIT)

    def swap(x):
        return lax.all_to_all(x, "var", 0, 0, axis_index_groups=groups)

    def up(x):
        return lax.ppermute(x, "var", [(n, n + GROUP) for n in range(devices - GROUP)])

    def down(x):
        return lax.ppermute(x, "var", [(n + GROUP, n) for n in range(devices - GROUP)])

    kv, qo = pl.pallas_call(
        functools.partial(pack_kernel, slots, head_dim),
        out_shape=(
            jax.ShapeDtypeStruct((GROUP, slots, rows, LANES), BF16),
            jax.ShapeDtypeStruct((GROUP, slots, rows + LSE_ROWS, LANES), BF16),
        ),
        in_specs=[vmem()] * 5,
        out_specs=(vmem(), vmem()),
        compiler_params=params,
    )(queries, keys, values, out_grad, log_sum_exp)

    own = swap(kv)
    lined = own.transpose(1, 0, 2, 3).reshape(slots, group_blocks, BLOCK, LANES)
    low = up(lined[:, group_blocks - SPAN :])
    high = down(lined[:, :SPAN])
    qo = swap(qo)
    own = own.reshape(GROUP, slots, blocks_here, BLOCK, LANES)

    anyspec = pl.BlockSpec(memory_space=pl.ANY)
    pairs = slots * group_blocks * slot_count * BLOCK * BLOCK
    own_sum, low_part, high_part, dq = pl.pallas_call(
        functools.partial(attend_kernel, slots, blocks_here, head_dim),
        out_shape=(
            jax.ShapeDtypeStruct((slots, group_blocks, BLOCK, LANES), F32),
            jax.ShapeDtypeStruct((slots, SPAN, BLOCK, LANES), BF16),
            jax.ShapeDtypeStruct((slots, SPAN, BLOCK, LANES), BF16),
            jax.ShapeDtypeStruct((GROUP, rows, slots * head_dim), BF16),
        ),
        in_specs=[pl.BlockSpec(memory_space=pltpu.SMEM), anyspec, anyspec, anyspec, vmem()],
        out_specs=(vmem(),) * 4,
        scratch_shapes=[
            pltpu.VMEM((window, BLOCK, LANES), BF16),
            pltpu.VMEM((window, head_dim, BLOCK), BF16),
            pltpu.VMEM((window, BLOCK, LANES), F32),
            pltpu.VMEM((slot_count * BLOCK, LANES), BF16),
            pltpu.VMEM((head_dim, slot_count * BLOCK), BF16),
            pltpu.VMEM((2 * BLOCK, LANES), BF16),
            pltpu.VMEM((slot_count * BLOCK, BLOCK), F32),
            pltpu.VMEM((slot_count * BLOCK, BLOCK), F32),
            pltpu.VMEM((slot_count * BLOCK, 2 * BLOCK), BF16),
            pltpu.SemaphoreType.DMA((2 + GROUP,)),
        ],
        compiler_params=params,
        cost_estimate=pl.CostEstimate(
            flops=10 * pairs * head_dim, bytes_accessed=4_000_000, transcendentals=pairs
        ),
    )(key_blocks, own, low, high, qo)

    from_above = down(low_part).astype(F32)
    from_below = up(high_part).astype(F32)
    rest = ((0, 0), (0, 0))
    left = group_blocks - SPAN
    dkv = (
        own_sum
        + jnp.pad(from_above, ((0, 0), (left, 0)) + rest)
        + jnp.pad(from_below, ((0, 0), (0, left)) + rest)
    ).astype(BF16)
    dkv = dkv.reshape(slots, GROUP, rows, LANES).transpose(1, 0, 2, 3)
    dq = swap(dq)
    dkv = swap(dkv)

    half = rows // heads
    dq_out, dk_out, dv_out, send, keep = pl.pallas_call(
        functools.partial(finish_kernel, slots, head_dim),
        out_shape=(
            jax.ShapeDtypeStruct((rows, features), BF16),
            jax.ShapeDtypeStruct((rows, features), BF16),
            jax.ShapeDtypeStruct((rows, features), BF16),
            jax.ShapeDtypeStruct((heads - 1, half, width), BF16),
            jax.ShapeDtypeStruct((half, width), F32),
        ),
        in_specs=[vmem()] * 3,
        out_specs=(vmem(),) * 5,
        scratch_shapes=[pltpu.VMEM((3, rows, features), BF16)],
        compiler_params=params,
    )(dkv, dq, w_qkv)
    total = keep
    for piece in range(heads - 1):
        turn = piece + 1
        got = lax.ppermute(send[piece], "head", [(n, (n + turn) % heads) for n in range(heads)])
        total = total + got.astype(F32)
    return dq_out, dk_out, dv_out, total.astype(BF16)


def solution(mesh):
    in_specs = (
        P("var", "head"),
        P("var", "head"),
        P("var", "head"),
        P("var", "head"),
        P("head", "var"),
        P(),
        P(None, None, "head"),
    )
    out_specs = (P("var", "head"), P("var", "head"), P("var", "head"), P(("var", "head"), None))
    return jax.shard_map(body, mesh=mesh, in_specs=in_specs, out_specs=out_specs, check_vma=False)
```

time: 365 us -> 118 us (0.32)
  waiting for transfers between devices: 188 us -> 27.1 us
  other arithmetic: 53.7 us -> 1.07 us
  local copies, waits for them, and re-layouts: 46 us -> 11.2 us
  blocking collectives: 0 us -> 30.9 us
  matrix products: 26.6 us -> 0 us
  Pallas kernels: 0 us -> 25.3 us
  starting transfers between devices: 35.1 us -> 20.6 us
  between operations: 14.3 us -> 0.76 us
    ppermute x12 -> x5, waiting for transfers between devices: 157 us -> 22.1 us  [the longest x2 11.7 us: down(): lax.ppermute(x, 'var', [(n + GROUP, n) for n in range(devices - GROUP)])]
    reduce_scatter x1 -> x0, waiting for transfers between devices: 31 us -> none  [body(): lax.psum_scatter(jnp.einsum('snf,sif->ni', gradient_row_block, w_qkv, pre...]
    all_to_all x0 -> x2, blocking collectives: none -> 30.9 us  [swap(): return lax.all_to_all(x, 'var', 0, 0, axis_index_groups=groups)]
    scatter-add x5 -> x0, other arithmetic: 30.4 us -> none  [the longest x3 28.7 us: query_step(): partial_value = partial_value.at[:, index_row + shift_base].add(both_parts)]
    dot_general x16 -> x0, matrix products: 26.6 us -> none  [the longest x3 6.02 us: attend(): jnp.einsum('tlu,tuf->lf', score_gradient, masked_keys, preferred_element_...]
    pallas_call x0 -> x3, Pallas kernels: none -> 25.3 us  [the longest x1 20.8 us: body(): pl.pallas_call(functools.partial(attend_kernel, slots, blocks_here, head_...]
    ppermute x12 -> x5, starting transfers between devices: 35.1 us -> 13.7 us  [the longest x2 9.62 us: up(): lax.ppermute(x, 'var', [(n, n + GROUP) for n in range(devices - GROUP)])]
    gather x3 -> x0, local copies, waits for them, and re-layouts: 13.6 us -> none  [attend(): nearby[:, index_row].reshape(2, slot_count * block_rows, features)]
  transfers between devices with their start and end apart: 13 -> 7, of which waited for: 7 -> 6; matrix products, arithmetic and copies ran while one was open for 4% -> 2% of each run, Pallas kernels for 0% -> 0%
where the time goes in v1:
time: 118 us; the launch traced here: 117 us
  blocking collectives  30.9 us (26%)
  waiting for transfers between devices  27.1 us (23%)
  Pallas kernels  25.3 us (21%)
  starting transfers between devices  20.6 us (17%)
  local copies, waits for them, and re-layouts  11.2 us (9%)
    all_to_all x2, blocking collectives, swap(): return lax.all_to_all(x, 'var', 0, 0, axis_index_groups=groups)  30.9 us
    pallas_call x1, Pallas kernels, body(): pl.pallas_call(functools.partial(attend_kernel, slots, blocks_here, head_...  20.8 us
    ppermute x2, waiting for transfers between devices, down(): lax.ppermute(x, 'var', [(n + GROUP, n) for n in range(devices - GROUP)])  11.7 us
    ppermute x2, starting transfers between devices, up(): lax.ppermute(x, 'var', [(n, n + GROUP) for n in range(devices - GROUP)])  9.62 us
    unnamed x25, local copies, waits for them, and re-layouts  9.21 us
    ppermute x1, waiting for transfers between devices, body(): lax.ppermute(send[piece], 'head', [(n, (n + turn) % heads) for n in range...  9 us
    all_to_all x2, starting transfers between devices, swap(): return lax.all_to_all(x, 'var', 0, 0, axis_index_groups=groups)  6.97 us
    all_to_all x2, waiting for transfers between devices, swap(): return lax.all_to_all(x, 'var', 0, 0, axis_index_groups=groups)  4.91 us
  transfers between devices with their start and end apart: 7, of which 6 were waited for; matrix products, arithmetic and copies ran while one was open for 2% of the time, Pallas kernels for 0%

profile of v1, /device:TPU:0, one launch (start us, length us, event | category | flops | bytes accessed | tf_op | source)
XLA Modules:
  0.0 117.0 jit_solution(14372622392422379301)
XLA Ops:
  0.6 0.0 copy-start.2
  0.6 1.0 copy-done.2
  1.6 0.0 copy-start.3
  1.6 1.0 copy-done.3
  2.6 0.0 copy-start.4
  2.6 1.0 copy-done.4
  3.6 0.0 copy-start.5
  3.6 1.0 copy-done.5
  4.6 0.0 copy-start.6
  4.6 0.7 copy-done.6
  5.3 1.4 %shard_map.102 = (bf16[4,2,384,128]{3,2,1,0:T(8,128)(2,1)S(1)}, bf16[4,2,400,128]{3,2,1,0:T(8,128)(2,1)}) custom-call(bf16[384,512]{1,0:T(8,128)(2,1)S(1)} %copy-done.2, bf16[384,512]{1,0:T(8,128)(2,1)S(1)} %copy-done.3, bf16[384,512]{1,0:T(8,128)(2,1)S(1)} %copy-done.4, bf16[384,512]{1,0:T(8,128)(2,1)S(1)} %copy-done.5, f32[8,384]{1,0:T(8,128)S(1)} %copy-done.6), custom_call_target="tpu_custom_call" | custom-call | tf_op jit(solution)/shard_map/pallas_call | solution.py:231
  6.7 15.7 %all_to_all.20 = bf16[4,2,384,128]{3,2,1,0:T(8,128)(2,1)S(1)} all-to-all(bf16[4,2,384,128]{3,2,1,0:T(8,128)(2,1)S(1)} %get-tuple-element.15), channel_id=1, replica_groups={{0,2,4,6},{8,10,12,14},{16,18,20,22},{24,26,28,30},{1,3,5,7},{9,11,13,1..., dimensions={0} | all-to-all | bytes 1572864 | tf_op jit(solution)/shard_map/all_to_all | solution.py:223
  22.4 3.5 %all-to-all-start.1 = ((bf16[4,2,400,128]{3,2,1,0:T(8,128)(2,1)}), bf16[4,2,400,128]{3,2,1,0:T(8,128)(2,1)S(1)}, u32[]{:S(2)}, u32[]{:S(2)}) async-start(bf16[4,2,400,128]{3,2,1,0:T(8,128)(2,1)} %get-tuple-element.16), calls=%async_computation.1 | async-start | bytes 1638400 | tf_op jit(solution)/shard_map/all_to_all | solution.py:223
  25.9 0.0 copy-start.11
  25.9 0.1 copy.13
  26.0 1.0 fusion
  27.0 1.3 %collective-permute-start.1 = (bf16[2,8,128,128]{3,2,1,0:T(8,128)(2,1)}, bf16[2,8,128,128]{3,2,1,0:T(8,128)(2,1)S(1)}, u32[]{:S(2)}, u32[]{:S(2)}) collective-permute-start(bf16[2,8,128,128]{3,2,1,0:T(8,128)(2,1)} %get-tuple-element.26), channel_id=1, source_target_pairs={{8,0},{10,2},{12,4},{14,6},{16,8},{18,10},{20,12},{22,14},{24,16},... | collective-permute-start | bytes 1572872 | tf_op jit(solution)/shard_map/ppermute | solution.py:229
  28.3 4.6 %collective-permute-start = (bf16[2,8,128,128]{3,2,1,0:T(8,128)(2,1)S(1)}, bf16[2,8,128,128]{3,2,1,0:T(8,128)(2,1)S(1)}, u32[]{:S(2)}, u32[]{:S(2)}) collective-permute-start(bf16[2,8,128,128]{3,2,1,0:T(8,128)(2,1)S(1)} %get-tuple-element.27), channel_id=1, source_target_pairs={{0,8},{2,10},{4,12},{6,14},{8,16},{10,18},{12,20},{14,22},{16,24},... | collective-permute-start | bytes 1572872 | tf_op jit(solution)/shard_map/ppermute | solution.py:226
  32.9 0.0 copy-done.11
  32.9 0.1 copy.14.kb_ref
  32.9 4.9 %all-to-all-done.1.qo_ref = bf16[4,2,400,128]{3,2,1,0:T(8,128)(2,1)S(1)} async-done(((bf16[4,2,400,128]{3,2,1,0:T(8,128)(2,1)}), bf16[4,2,400,128]{3,2,1,0:T(8,128)(2,1)S(1)}, u32[]{:S(2)}, u32[]{:S(2)}) %all-to-all-start.1) | async-done | bytes 819232 | tf_op jit(solution)/shard_map/all_to_all | solution.py:223
  37.9 5.5 %collective-permute-done.1.high_ref = bf16[2,8,128,128]{3,2,1,0:T(8,128)(2,1)S(1)} collective-permute-done((bf16[2,8,128,128]{3,2,1,0:T(8,128)(2,1)}, bf16[2,8,128,128]{3,2,1,0:T(8,128)(2,1)S(1)}, u32[]{:S(2)}, u32[]{:S(2)}) %collective-permute-start.1) | collective-permute-done | bytes 524320 | tf_op jit(solution)/shard_map/ppermute | solution.py:229
  43.4 0.0 copy-start.7
  43.4 0.8 copy-done.7
  44.2 0.2 collective-permute-done.low_ref
  44.3 0.0 copy-start.9
  44.3 0.8 copy-done.9
  45.1 0.0 copy-start.8
  45.1 1.0 copy-done.8
  46.2 0.0 copy-start.10
  46.2 1.0 copy-done.10
  47.2 20.8 %shard_map.103 = (f32[2,12,128,128]{3,2,1,0:T(8,128)S(1)}, bf16[2,8,128,128]{3,2,1,0:T(8,128)(2,1)}, bf16[2,8,128,128]{3,2,1,0:T(8,128)(2,1)}, bf16[4,384,128]{2,1,0:T(8,128)(2,1)S(1)}) custom-call(s32[48,8]{1,0:T(8,128)S(1)} %copy.14.kb_ref, bf16[4,2,3,128,128]{4,3,2,1,0:T(8,128)(2,1)S(1)} %bitcast.12, bf16[2,8,128,128]{3,2,1,0:T(8,128)(2,1)S(1)} %copy-done.10, ...), custom_call_target="tpu_custom_call" | custom-call | flops 2013265920 | bytes 4000000 | tf_op jit(solution)/shard_map/pallas_call | solution.py:251
  68.0 0.0 copy-start.1
  68.0 0.7 copy-done.1
  68.7 1.3 %collective-permute-start.2 = (bf16[2,8,128,128]{3,2,1,0:T(8,128)(2,1)}, bf16[2,8,128,128]{3,2,1,0:T(8,128)(2,1)S(1)}, u32[]{:S(2)}, u32[]{:S(2)}) collective-permute-start(bf16[2,8,128,128]{3,2,1,0:T(8,128)(2,1)} %get-tuple-element.18), channel_id=1, source_target_pairs={{8,0},{10,2},{12,4},{14,6},{16,8},{18,10},{20,12},{22,14},{24,16},... | collective-permute-start | bytes 1572872 | tf_op jit(solution)/shard_map/ppermute | solution.py:229
  70.0 5.0 %collective-permute-start.3 = (bf16[2,8,128,128]{3,2,1,0:T(8,128)(2,1)}, bf16[2,8,128,128]{3,2,1,0:T(8,128)(2,1)S(1)}, u32[]{:S(2)}, u32[]{:S(2)}) collective-permute-start(bf16[2,8,128,128]{3,2,1,0:T(8,128)(2,1)} %get-tuple-element.19), channel_id=1, source_target_pairs={{0,8},{2,10},{4,12},{6,14},{8,16},{10,18},{12,20},{14,22},{16,24},... | collective-permute-start | bytes 1572872 | tf_op jit(solution)/shard_map/ppermute | solution.py:226
  75.1 3.5 %all-to-all-start.3 = ((bf16[4,384,128]{2,1,0:T(8,128)(2,1)}), bf16[4,384,128]{2,1,0:T(8,128)(2,1)S(1)}, u32[]{:S(2)}, u32[]{:S(2)}) async-start(bf16[4,384,128]{2,1,0:T(8,128)(2,1)} %copy-done.1), calls=%async_computation.3 | async-start | bytes 786432 | tf_op jit(solution)/shard_map/all_to_all | solution.py:223
  78.6 6.2 %collective-permute-done.2 = bf16[2,8,128,128]{3,2,1,0:T(8,128)(2,1)S(1)} collective-permute-done((bf16[2,8,128,128]{3,2,1,0:T(8,128)(2,1)}, bf16[2,8,128,128]{3,2,1,0:T(8,128)(2,1)S(1)}, u32[]{:S(2)}, u32[]{:S(2)}) %collective-permute-start.2) | collective-permute-done | bytes 524320 | tf_op jit(solution)/shard_map/ppermute | solution.py:229
  84.8 1.3 %collective-permute-done.3 = bf16[2,8,128,128]{3,2,1,0:T(8,128)(2,1)S(1)} collective-permute-done((bf16[2,8,128,128]{3,2,1,0:T(8,128)(2,1)}, bf16[2,8,128,128]{3,2,1,0:T(8,128)(2,1)S(1)}, u32[]{:S(2)}, u32[]{:S(2)}) %collective-permute-start.3) | collective-permute-done | bytes 524320 | tf_op jit(solution)/shard_map/ppermute | solution.py:226
  86.0 0.2 add_convert_fusion
  86.3 0.0 copy-start
  86.3 0.9 copy_bitcast_fusion
  87.2 0.0 all-to-all-done.3.dq_ref
  87.2 15.2 %all_to_all.21.dkv_ref = bf16[4,2,384,128]{3,2,1,0:T(8,128)(2,1)S(1)} all-to-all(bf16[4,2,384,128]{3,2,1,0:T(8,128)(2,1)} %copy_bitcast_fusion), channel_id=1, replica_groups={{0,2,4,6},{8,10,12,14},{16,18,20,22},{24,26,28,30},{1,3,5,7},{9,11,13,1..., dimensions={0} | all-to-all | bytes 1572864 | tf_op jit(solution)/shard_map/all_to_all | solution.py:223
  102.5 0.0 copy-done
  102.5 3.2 %shard_map.104 = (bf16[384,512]{1,0:T(8,128)(2,1)}, bf16[384,512]{1,0:T(8,128)(2,1)}, bf16[384,512]{1,0:T(8,128)(2,1)}, bf16[1,192,1024]{2,1,0:T(8,128)(2,1)S(1)}, f32[192,1024]{1,0:T(8,128)S(1)}) custom-call(bf16[4,2,384,128]{3,2,1,0:T(8,128)(2,1)S(1)} %all_to_all.21.dkv_ref, bf16[4,384,128]{2,1,0:T(8,128)(2,1)S(1)} %all-to-all-done.3.dq_ref, ...), custom_call_target="tpu_custom_call" | custom-call | tf_op jit(solution)/shard_map/pallas_call | solution.py:293
  105.7 1.5 %collective-permute-start.4 = (bf16[192,1024]{1,0:T(8,128)(2,1)S(1)}, bf16[192,1024]{1,0:T(8,128)(2,1)S(1)}, u32[]{:S(2)}, u32[]{:S(2)}) collective-permute-start(bf16[192,1024]{1,0:T(8,128)(2,1)S(1)} %bitcast.13), channel_id=1, source_target_pairs={{0,1},{1,0},{2,3},{3,2},{4,5},{5,4},{6,7},{7,6},{8,9},{9,8},{10,11... | collective-permute-start | bytes 1179656 | tf_op jit(solution)/shard_map/ppermute | solution.py:310
  107.2 9.0 %collective-permute-done.4 = bf16[192,1024]{1,0:T(8,128)(2,1)S(1)} collective-permute-done((bf16[192,1024]{1,0:T(8,128)(2,1)S(1)}, bf16[192,1024]{1,0:T(8,128)(2,1)S(1)}, u32[]{:S(2)}, u32[]{:S(2)}) %collective-permute-start.4) | collective-permute-done | bytes 393248 | tf_op jit(solution)/shard_map/ppermute | solution.py:310
  116.2 0.8 add_convert_fusion.1
Async XLA Ops:
  0.6 1.0 copy-start.2
  1.6 1.0 copy-start.3
  2.6 1.0 copy-start.4
  3.6 1.0 copy-start.5
  4.6 0.7 copy-start.6
  22.4 15.5 %all-to-all-start.1 = ((bf16[4,2,400,128]{3,2,1,0:T(8,128)(2,1)}), bf16[4,2,400,128]{3,2,1,0:T(8,128)(2,1)S(1)}, u32[]{:S(2)}, u32[]{:S(2)}) async-start(bf16[4,2,400,128]{3,2,1,0:T(8,128)(2,1)} %get-tuple-element.16), calls=%async_computation.1 | async-start | bytes 1638400 | tf_op jit(solution)/shard_map/all_to_all | solution.py:223
  25.9 7.0 %copy-start.11 = (s32[48,8]{0,1:T(8,128)S(1)}, s32[48,8]{0,1:T(8,128)}, u32[]{:S(2)}) copy-start(s32[48,8]{0,1:T(8,128)} %param.12) | copy-start | bytes 4612
  27.0 16.4 %collective-permute-start.1 = (bf16[2,8,128,128]{3,2,1,0:T(8,128)(2,1)}, bf16[2,8,128,128]{3,2,1,0:T(8,128)(2,1)S(1)}, u32[]{:S(2)}, u32[]{:S(2)}) collective-permute-start(bf16[2,8,128,128]{3,2,1,0:T(8,128)(2,1)} %get-tuple-element.26), channel_id=1, source_target_pairs={{8,0},{10,2},{12,4},{14,6},{16,8},{18,10},{20,12},{22,14},{24,16},... | collective-permute-start | bytes 1572872 | tf_op jit(solution)/shard_map/ppermute | solution.py:229
  28.3 16.1 %collective-permute-start = (bf16[2,8,128,128]{3,2,1,0:T(8,128)(2,1)S(1)}, bf16[2,8,128,128]{3,2,1,0:T(8,128)(2,1)S(1)}, u32[]{:S(2)}, u32[]{:S(2)}) collective-permute-start(bf16[2,8,128,128]{3,2,1,0:T(8,128)(2,1)S(1)} %get-tuple-element.27), channel_id=1, source_target_pairs={{0,8},{2,10},{4,12},{6,14},{8,16},{10,18},{12,20},{14,22},{16,24},... | collective-permute-start | bytes 1572872 | tf_op jit(solution)/shard_map/ppermute | solution.py:226
  43.4 0.8 copy-start.7
  44.3 0.8 copy-start.9
  45.1 1.0 copy-start.8
  46.2 1.0 copy-start.10
  68.0 0.7 copy-start.1
  68.7 16.0 %collective-permute-start.2 = (bf16[2,8,128,128]{3,2,1,0:T(8,128)(2,1)}, bf16[2,8,128,128]{3,2,1,0:T(8,128)(2,1)S(1)}, u32[]{:S(2)}, u32[]{:S(2)}) collective-permute-start(bf16[2,8,128,128]{3,2,1,0:T(8,128)(2,1)} %get-tuple-element.18), channel_id=1, source_target_pairs={{8,0},{10,2},{12,4},{14,6},{16,8},{18,10},{20,12},{22,14},{24,16},... | collective-permute-start | bytes 1572872 | tf_op jit(solution)/shard_map/ppermute | solution.py:229
  70.0 16.0 %collective-permute-start.3 = (bf16[2,8,128,128]{3,2,1,0:T(8,128)(2,1)}, bf16[2,8,128,128]{3,2,1,0:T(8,128)(2,1)S(1)}, u32[]{:S(2)}, u32[]{:S(2)}) collective-permute-start(bf16[2,8,128,128]{3,2,1,0:T(8,128)(2,1)} %get-tuple-element.19), channel_id=1, source_target_pairs={{0,8},{2,10},{4,12},{6,14},{8,16},{10,18},{12,20},{14,22},{16,24},... | collective-permute-start | bytes 1572872 | tf_op jit(solution)/shard_map/ppermute | solution.py:226
  75.1 12.2 %all-to-all-start.3 = ((bf16[4,384,128]{2,1,0:T(8,128)(2,1)}), bf16[4,384,128]{2,1,0:T(8,128)(2,1)S(1)}, u32[]{:S(2)}, u32[]{:S(2)}) async-start(bf16[4,384,128]{2,1,0:T(8,128)(2,1)} %copy-done.1), calls=%async_computation.3 | async-start | bytes 786432 | tf_op jit(solution)/shard_map/all_to_all | solution.py:223
  86.3 16.2 %copy-start = (bf16[3,1024,512]{2,1,0:T(8,128)(2,1)S(1)}, bf16[3,1024,512]{2,1,0:T(8,128)(2,1)}, u32[]{:S(2)}) copy-start(bf16[3,1024,512]{2,1,0:T(8,128)(2,1)} %w_ref.1) | copy-start | bytes 9437188
  105.7 10.5 %collective-permute-start.4 = (bf16[192,1024]{1,0:T(8,128)(2,1)S(1)}, bf16[192,1024]{1,0:T(8,128)(2,1)S(1)}, u32[]{:S(2)}, u32[]{:S(2)}) collective-permute-start(bf16[192,1024]{1,0:T(8,128)(2,1)S(1)} %bitcast.13), channel_id=1, source_target_pairs={{0,1},{1,0},{2,3},{3,2},{4,5},{5,4},{6,7},{7,6},{8,9},{9,8},{10,11... | collective-permute-start | bytes 1179656 | tf_op jit(solution)/shard_map/ppermute | solution.py:310

commit v2 on v0

v2 whole, which is shorter than its diff:
```python
import functools

import jax
import jax.numpy as jnp
from jax import lax
from jax.experimental import pallas as pl
from jax.experimental.pallas import tpu as pltpu
from jax.sharding import PartitionSpec as P

PATCHES = 16
BLOCK = 128
HALF = BLOCK // 2
SPAN = 8
GROUP = 4
LANES = 128
LSE_ROWS = 16
LOADS = 3
F32 = jnp.float32
BF16 = jnp.bfloat16
MIB = 1024 * 1024


def vmem():
    return pl.BlockSpec(memory_space=pltpu.VMEM)


def params(mib):
    return pltpu.CompilerParams(vmem_limit_bytes=mib * MIB)


def shaped(shape, dtype=BF16):
    return jax.ShapeDtypeStruct(shape, dtype)


def dot(a, b):
    return jnp.dot(a, b, preferred_element_type=F32)


def dot_nt(a, b):
    return lax.dot_general(a, b, (((1,), (1,)), ((), ())), preferred_element_type=F32)


def token_at(place):
    return (((place & (HALF - 1)) >> 3) << 4) + ((place >> 6) << 3) + (place & 7)


def one_where(mask):
    return jnp.where(mask, 1.0, 0.0).astype(BF16)


def reorder_matrix(inverse):
    row = lax.broadcasted_iota(jnp.int32, (BLOCK, BLOCK), 0)
    col = lax.broadcasted_iota(jnp.int32, (BLOCK, BLOCK), 1)
    return one_where(row == token_at(col)) if inverse else one_where(col == token_at(row))


def split_three(x):
    high = x.astype(BF16).astype(F32)
    rest = x - high
    mid = rest.astype(BF16).astype(F32)
    return high, mid, rest - mid


def widen(x):
    if x.shape[1] == LANES:
        return x
    return jnp.concatenate([x, jnp.zeros((x.shape[0], LANES - x.shape[1]), x.dtype)], axis=1)


def load_all(pairs, sems):
    copies = []
    for i, (source, target) in enumerate(pairs):
        rows = source.shape[0] // LOADS
        for part in range(LOADS):
            at = pl.ds(part * rows, rows)
            copies.append(pltpu.make_async_copy(source.at[at], target.at[at], sems.at[i, part]))
    for copy in copies:
        copy.start()
    for copy in copies:
        copy.wait()


def pack_kv_kernel(k_hbm, v_hbm, *rest):
    outs, (k_ref, v_ref, turned, sems) = rest[:GROUP], rest[GROUP:]
    load_all([(k_hbm, k_ref), (v_hbm, v_ref)], sems)
    rows, features = k_ref.shape
    width = features // GROUP
    order = reorder_matrix(False)
    for b in range(rows // BLOCK):
        at = slice(b * BLOCK, (b + 1) * BLOCK)
        for half, ref in enumerate((k_ref, v_ref)):
            moved = dot(order, ref[at]).astype(BF16)
            for member in range(GROUP):
                turned[member, at, half * LANES : (half + 1) * LANES] = widen(
                    moved[:, member * width : (member + 1) * width]
                )
    me = lax.axis_index("var") % GROUP
    for distance, out in enumerate(outs):
        out[...] = turned[me ^ distance]


def pack_qo_kernel(slots, head_dim, q_hbm, g_hbm, lse_ref, qo_ref, q_ref, g_ref, sems):
    load_all([(q_hbm, q_ref), (g_hbm, g_ref)], sems)
    rows, features = q_ref.shape
    width = features // GROUP
    blocks = rows // BLOCK
    order = reorder_matrix(False)
    scale = head_dim ** (-0.5)
    for b in range(blocks):
        at = slice(b * BLOCK, (b + 1) * BLOCK)
        for half, ref in enumerate((q_ref, g_ref)):
            moved = dot(order, ref[at])
            if half == 0:
                moved = moved * scale
            moved = moved.astype(BF16)
            for member in range(GROUP):
                qo_ref[member, at, half * LANES : (half + 1) * LANES] = widen(
                    moved[:, member * width : (member + 1) * width]
                )
    token = lax.broadcasted_iota(jnp.int32, (BLOCK, 2 * LANES), 0)
    lane = lax.broadcasted_iota(jnp.int32, (BLOCK, 2 * LANES), 1)
    place = ((lane >> 7) << 6) + (lane & (HALF - 1))
    hit = token == token_at(place)
    upper = (lane & HALF) != 0
    spread = [one_where(hit & ~upper), one_where(hit & upper)]
    for member in range(GROUP):
        total = None
        for slot in range(slots):
            lse = lse_ref[member * slots + slot : member * slots + slot + 1, :]
            parts = [
                part[:, b * BLOCK : (b + 1) * BLOCK]
                for part in split_three(lse)
                for b in range(blocks)
            ]
            parts.append(jnp.zeros((LSE_ROWS - len(parts), BLOCK), F32))
            moved = dot(jnp.concatenate(parts, axis=0).astype(BF16), spread[slot])
            total = moved if total is None else total + moved
        qo_ref[member, rows:] = total.astype(BF16)


def exchange_start(group_blocks):
    odd = (lax.axis_index("var") // GROUP) % 2
    reach = group_blocks - SPAN
    return (1 - odd) * reach, odd * reach


def line_kernel(*refs):
    pieces, (own, first_out, second_out) = refs[:GROUP], refs[GROUP:]
    blocks = pieces[0].shape[0] // BLOCK
    me = lax.axis_index("var") % GROUP
    for distance, piece in enumerate(pieces):
        own[pl.ds((me ^ distance) * blocks, blocks)] = piece[...].reshape(blocks, BLOCK, 2 * LANES)
    first, second = exchange_start(GROUP * blocks)
    first_out[...] = own[pl.ds(first, SPAN)]
    second_out[...] = own[pl.ds(second, SPAN)]


def attend_kernel(
    blocks_here,
    head_dim,
    kb_ref,
    own_ref,
    first_ref,
    second_ref,
    qo_ref,
    own_out,
    first_out,
    second_out,
    dq_out,
    kv_win,
    k_turn,
    acc,
    shifts,
    queries,
    grads,
    crossed,
    prob,
    slope,
):
    group_blocks = GROUP * blocks_here
    window = group_blocks + 2 * SPAN
    rows = blocks_here * BLOCK
    slot_count = kb_ref.shape[1]
    scale = head_dim ** (-0.5)
    base = (lax.axis_index("var") // GROUP) * group_blocks
    odd = (lax.axis_index("var") // GROUP) % 2
    top = window - SPAN
    first_at, second_at = (1 - odd) * top, odd * top
    low = slice(0, LANES)
    high = slice(LANES, 2 * LANES)

    kv_win[SPAN : SPAN + group_blocks] = own_ref[...]
    kv_win[pl.ds(first_at, SPAN)] = first_ref[...]
    kv_win[pl.ds(second_at, SPAN)] = second_ref[...]
    key_patch = lax.broadcasted_iota(jnp.int32, (8, LANES), 0)
    query_patch = lax.broadcasted_iota(jnp.int32, (8, LANES), 1) & 7
    usable = key_patch <= query_patch
    for member in range(GROUP):
        parts = qo_ref[member, rows:].astype(F32)
        for local in range(blocks_here):
            lse = (
                parts[local : local + 1] + parts[blocks_here + local : blocks_here + local + 1]
            ) + parts[2 * blocks_here + local : 2 * blocks_here + local + 1]
            at = member * blocks_here + local
            shifts[at, 0, :, low] = jnp.where(usable, -lse[:, low], -1e30)
            shifts[at, 0, :, high] = jnp.broadcast_to(-lse[:, high], (8, LANES))
            shifts[at, 1, :, low] = jnp.where(usable, -lse[:, high], -1e30)
    acc[...] = jnp.zeros_like(acc)
    crossed[...] = jnp.zeros_like(crossed)

    @pl.loop(0, window)
    def _(block):
        k_turn[block] = kv_win[block, :, low].T

    unorder = reorder_matrix(True)
    lane = lax.broadcasted_iota(jnp.int32, (HALF, LANES), 1)
    head_a = lane < HALF

    def picks(query_block):
        return [kb_ref[base + query_block, s] - base + SPAN for s in range(slot_count)]

    def lay_out(member, local, buf):
        at = pl.multiple_of(local * BLOCK, BLOCK)
        for part in range(2):
            rows_at = pl.ds(at + part * HALF, HALF)
            for cols, target in ((low, queries), (high, grads)):
                tile = qo_ref[member, rows_at, cols]
                zero = jnp.zeros_like(tile)
                both = jnp.concatenate(
                    [jnp.where(head_a, tile, zero), jnp.where(head_a, zero, tile)], axis=0
                )
                target[buf, part * BLOCK : (part + 1) * BLOCK] = both
                if part == 1:
                    side = 0 if target is queries else 1
                    crossed[
                        buf, side * BLOCK : (side + 1) * BLOCK, side * LANES : (side + 1) * LANES
                    ] = both

    def gather(index, rows_of, cols):
        return jnp.concatenate([kv_win[i, rows_of, cols] for i in index], axis=0)

    early = slice(0, HALF)
    late = slice(HALF, BLOCK)
    both_cols = slice(0, 2 * LANES)
    early_rows = slot_count * HALF

    def forward(query_block, buf):
        lay_out(query_block // blocks_here, query_block % blocks_here, buf)
        index = picks(query_block)
        s = dot_nt(gather(index, early, low), queries[buf])
        g = dot_nt(gather(index, early, high), grads[buf])
        x = dot_nt(gather(index, late, both_cols), crossed[buf])
        shift = shifts[query_block, 0][None]
        p = jnp.exp(s.reshape(early_rows // 8, 8, 2 * LANES) + shift).reshape(early_rows, 2 * LANES)
        prob[buf, :early_rows] = p
        slope[buf, :early_rows] = g
        delta = jnp.sum((p * g).reshape(early_rows // 8, 8, 2 * LANES), axis=0)
        late_shift = shifts[query_block, 1, :, low][None]
        q = jnp.exp(x[:, low].reshape(early_rows // 8, 8, LANES) + late_shift).reshape(
            early_rows, LANES
        )
        prob[buf, early_rows:, low] = q
        slope[buf, early_rows:, low] = x[:, high]
        more = jnp.sum((q * x[:, high]).reshape(early_rows // 8, 8, LANES), axis=0)
        delta_low = jnp.sum(delta[:, low], axis=0, keepdims=True)
        delta_high = jnp.sum(delta[:, high] + more, axis=0, keepdims=True)
        return jnp.concatenate([delta_low, delta_high], axis=1)

    def backward(query_block, buf, delta):
        index = picks(query_block)
        p = prob[buf, :early_rows]
        ds = (p * (slope[buf, :early_rows] - delta)).astype(BF16)
        q = prob[buf, early_rows:, low]
        ds_late = (q * (slope[buf, early_rows:, low] - delta[:, high])).astype(BF16)
        dk = dot(ds, queries[buf])
        dv = dot(p.astype(BF16), grads[buf])
        r = dot(jnp.concatenate([ds_late, q.astype(BF16)], axis=1), crossed[buf])
        nothing = jnp.zeros((HALF, LANES), BF16)
        pieces = []
        for s in range(slot_count):
            at = slice(s * HALF, (s + 1) * HALF)
            where = index[s]
            acc[where, early, low] = acc[where, early, low] + dk[at]
            acc[where, early, high] = acc[where, early, high] + dv[at]
            acc[where, late] = acc[where, late] + r[at]
            pieces.append(ds[at])
            pieces.append(jnp.concatenate([nothing, ds_late[at]], axis=1))
        keys_turned = jnp.concatenate([k_turn[i] for i in index], axis=1)
        dq = dot(keys_turned, jnp.concatenate(pieces, axis=0)) * scale
        halves = []
        for cols in (low, high):
            turned = dq[:, cols].T
            halves.append(jnp.where(head_a, turned[:HALF], turned[HALF:]))
        moved = dot(unorder, jnp.concatenate(halves, axis=0).astype(BF16)).astype(BF16)
        dq_out[pl.ds(pl.multiple_of(query_block * BLOCK, BLOCK), BLOCK)] = moved

    delta = forward(0, 0)

    def step(j, delta):
        block = 2 * j
        later = forward(block + 1, 1)
        backward(block, 0, delta)
        last = forward(block + 2, 0)
        backward(block + 1, 1, later)
        return last

    delta = lax.fori_loop(0, (group_blocks - 1) // 2, step, delta)
    if group_blocks % 2 == 0:
        later = forward(group_blocks - 1, 1)
        backward(group_blocks - 2, 0, delta)
        backward(group_blocks - 1, 1, later)
    else:
        backward(group_blocks - 1, 0, delta)

    first_out[...] = acc[pl.ds(first_at, SPAN)].astype(BF16)
    second_out[...] = acc[pl.ds(second_at, SPAN)].astype(BF16)
    own_out[...] = acc[SPAN : SPAN + group_blocks]


def owner_start(piece, half):
    heads = lax.axis_size("head")
    return pl.multiple_of(((lax.axis_index("head") + 1 + piece) % heads) * half, half)


def combine_kernel(own_ref, first_ref, second_ref, away_out, home_out, total, moved):
    group_blocks = own_ref.shape[0]
    blocks_here = group_blocks // GROUP
    half = home_out.shape[1]
    first, second = exchange_start(group_blocks)
    total[...] = own_ref[...]
    for start, ref in ((first, first_ref), (second, second_ref)):
        at = pl.ds(start, SPAN)
        total[at] = total[at] + ref[...].astype(F32)
    unorder = reorder_matrix(True)
    for block in range(group_blocks):
        at = (block % blocks_here) * BLOCK
        moved[block // blocks_here, at : at + BLOCK] = dot(
            unorder, total[block].astype(BF16)
        ).astype(BF16)
    away = away_out.shape[1] // half
    for member in range(GROUP):
        for piece in range(away):
            away_out[member, piece * half : (piece + 1) * half] = moved[
                member, pl.ds(owner_start(piece, half), half)
            ]
        home_out[member] = moved[member, pl.ds(owner_start(away, half), half)]


def gather_rows(grads, dq_ref, start, dkv_ref, dkv_at):
    half = grads.shape[1]
    width = grads.shape[2] // GROUP
    for member in range(GROUP):
        at = slice(member * width, (member + 1) * width)
        both = dkv_ref[member, dkv_at * half : (dkv_at + 1) * half]
        grads[0, :, at] = dq_ref[member, pl.ds(start, half)][:, :width]
        grads[1, :, at] = both[:, :width]
        grads[2, :, at] = both[:, LANES : LANES + width]


def product(grads, w_ref):
    total = dot_nt(grads[0], w_ref[0])
    for s in (1, 2):
        total = total + dot_nt(grads[s], w_ref[s])
    return total


def away_kernel(dq_ref, dkv_ref, w_ref, *rest):
    outs, grads = rest[:-1], rest[-1]
    half = grads.shape[1]
    for piece, out in enumerate(outs):
        gather_rows(grads, dq_ref, owner_start(piece, half), dkv_ref, piece)
        out[...] = product(grads, w_ref).astype(BF16)


def home_kernel(dq_ref, away_ref, home_ref, w_ref, dq_out, dk_out, dv_out, keep_out, grads):
    half = grads.shape[1]
    away = away_ref.shape[1] // half
    for piece in range(away + 1):
        start = owner_start(piece, half)
        if piece < away:
            gather_rows(grads, dq_ref, start, away_ref, piece)
        else:
            gather_rows(grads, dq_ref, start, home_ref, 0)
        at = pl.ds(start, half)
        dq_out[at] = grads[0]
        dk_out[at] = grads[1]
        dv_out[at] = grads[2]
    keep_out[...] = product(grads, w_ref)


def body(queries, keys, values, out_grad, log_sum_exp, key_blocks, w_qkv):
    rows, features = queries.shape
    head_count = log_sum_exp.shape[0]
    head_dim = features // head_count
    slots = head_count // GROUP
    blocks_here = rows // BLOCK
    group_blocks = GROUP * blocks_here
    window = group_blocks + 2 * SPAN
    slot_count = key_blocks.shape[1]
    devices = lax.axis_size("var")
    heads = lax.axis_size("head")
    half = rows // heads
    model = w_qkv.shape[1]
    wide = 2 * LANES
    groups = [[start + i for i in range(GROUP)] for start in range(0, devices, GROUP)]
    hbm = pl.BlockSpec(memory_space=pltpu.HBM)

    def swap(x):
        return lax.all_to_all(x, "var", 0, 0, axis_index_groups=groups)

    def trade(x, distance):
        return lax.ppermute(x, "var", [(n, n ^ distance) for n in range(devices)])

    def trade_first(x):
        pairs = [(n, n ^ GROUP) for n in range(devices) if (n ^ GROUP) < devices]
        return lax.ppermute(x, "var", pairs)

    def trade_second(x):
        pairs = []
        for n in range(devices):
            other = n + GROUP if (n // GROUP) % 2 else n - GROUP
            if 0 <= other < devices:
                pairs.append((n, other))
        return lax.ppermute(x, "var", pairs)

    loaded = [pltpu.VMEM((rows, features), BF16), pltpu.VMEM((rows, features), BF16)]
    sems = [pltpu.SemaphoreType.DMA((2, LOADS))]
    kvs = pl.pallas_call(
        pack_kv_kernel,
        out_shape=(shaped((rows, wide)),) * GROUP,
        in_specs=[hbm] * 2,
        out_specs=(vmem(),) * GROUP,
        scratch_shapes=loaded + [pltpu.VMEM((GROUP, rows, wide), BF16)] + sems,
        compiler_params=params(48),
    )(keys, values)
    qo = pl.pallas_call(
        functools.partial(pack_qo_kernel, slots, head_dim),
        out_shape=shaped((GROUP, rows + LSE_ROWS, wide)),
        in_specs=[hbm, hbm, vmem()],
        out_specs=vmem(),
        scratch_shapes=loaded + sems,
        compiler_params=params(12),
    )(queries, out_grad, log_sum_exp)

    pieces = [kvs[0]] + [None] * (GROUP - 1)
    for distance in (2, 3, 1):
        pieces[distance] = trade(kvs[distance], distance)
    own, first_send, second_send = pl.pallas_call(
        line_kernel,
        out_shape=(
            shaped((group_blocks, BLOCK, wide)),
            shaped((SPAN, BLOCK, wide)),
            shaped((SPAN, BLOCK, wide)),
        ),
        in_specs=[vmem()] * GROUP,
        out_specs=(vmem(),) * 3,
        compiler_params=params(12),
    )(*pieces)
    first = trade_first(first_send)
    second = trade_second(second_send)
    qo = swap(qo)

    pairs = group_blocks * slot_count * BLOCK * BLOCK * slots
    own_sum, first_part, second_part, dq = pl.pallas_call(
        functools.partial(attend_kernel, blocks_here, head_dim),
        out_shape=(
            shaped((group_blocks, BLOCK, wide), F32),
            shaped((SPAN, BLOCK, wide)),
            shaped((SPAN, BLOCK, wide)),
            shaped((group_blocks * BLOCK, LANES)),
        ),
        in_specs=[pl.BlockSpec(memory_space=pltpu.SMEM)] + [vmem()] * 4,
        out_specs=(vmem(),) * 4,
        scratch_shapes=[
            pltpu.VMEM((window, BLOCK, wide), BF16),
            pltpu.VMEM((window, LANES, BLOCK), BF16),
            pltpu.VMEM((window, BLOCK, wide), F32),
            pltpu.VMEM((group_blocks, 2, 8, wide), F32),
            pltpu.VMEM((2, wide, LANES), BF16),
            pltpu.VMEM((2, wide, LANES), BF16),
            pltpu.VMEM((2, wide, wide), BF16),
            pltpu.VMEM((2, slot_count * BLOCK, wide), F32),
            pltpu.VMEM((2, slot_count * BLOCK, wide), F32),
        ],
        compiler_params=params(24),
        cost_estimate=pl.CostEstimate(
            flops=40 * pairs * head_dim, bytes_accessed=2_000_000, transcendentals=pairs
        ),
    )(key_blocks, own, first, second, qo)

    first_back = trade_first(first_part)
    second_back = trade_second(second_part)
    dq = swap(dq.reshape(GROUP, rows, LANES))
    away, home = pl.pallas_call(
        combine_kernel,
        out_shape=(shaped((GROUP, rows - half, wide)), shaped((GROUP, half, wide))),
        in_specs=[vmem()] * 3,
        out_specs=(vmem(),) * 2,
        scratch_shapes=[
            pltpu.VMEM((group_blocks, BLOCK, wide), F32),
            pltpu.VMEM((GROUP, rows, wide), BF16),
        ],
        compiler_params=params(16),
    )(own_sum, first_back, second_back)
    away = swap(away)
    home = swap(home)

    grads = [pltpu.VMEM((3, half, features), BF16)]
    sends = pl.pallas_call(
        away_kernel,
        out_shape=(shaped((half, model)),) * (heads - 1),
        in_specs=[vmem()] * 3,
        out_specs=(vmem(),) * (heads - 1),
        scratch_shapes=grads,
        compiler_params=params(16),
        cost_estimate=pl.CostEstimate(
            flops=6 * (rows - half) * features * model, bytes_accessed=4_000_000, transcendentals=0
        ),
    )(dq, away, w_qkv)
    dq_out, dk_out, dv_out, total = pl.pallas_call(
        home_kernel,
        out_shape=(shaped((rows, features)),) * 3 + (shaped((half, model), F32),),
        in_specs=[vmem()] * 4,
        out_specs=(vmem(),) * 4,
        scratch_shapes=grads,
        compiler_params=params(16),
        cost_estimate=pl.CostEstimate(
            flops=6 * half * features * model, bytes_accessed=6_000_000, transcendentals=0
        ),
    )(dq, away, home, w_qkv)
    for piece, send in enumerate(sends):
        got = lax.ppermute(send, "head", [(n, (n + piece + 1) % heads) for n in range(heads)])
        total = total + got.astype(F32)
    return dq_out, dk_out, dv_out, total.astype(BF16)


def solution(mesh):
    in_specs = (
        P("var", "head"),
        P("var", "head"),
        P("var", "head"),
        P("var", "head"),
        P("head", "var"),
        P(),
        P(None, None, "head"),
    )
    out_specs = (P("var", "head"), P("var", "head"), P("var", "head"), P(("var", "head"), None))
    return jax.shard_map(body, mesh=mesh, in_specs=in_specs, out_specs=out_specs, check_vma=False)
```

time: 365 us -> 97.9 us (0.27)
  waiting for transfers between devices: 188 us -> 19.5 us
  other arithmetic: 53.7 us -> 0.84 us
  local copies, waits for them, and re-layouts: 46 us -> 9.6 us
  matrix products: 26.6 us -> 0 us
  Pallas kernels: 0 us -> 24.9 us
  blocking collectives: 0 us -> 20.8 us
  starting transfers between devices: 35.1 us -> 20 us
  between operations: 14.3 us -> 0.75 us
    ppermute x12 -> x8, waiting for transfers between devices: 157 us -> 11.7 us  [the longest x2 10.9 us: trade_first(): return lax.ppermute(x, 'var', pairs)]
    reduce_scatter x1 -> x0, waiting for transfers between devices: 31 us -> none  [body(): lax.psum_scatter(jnp.einsum('snf,sif->ni', gradient_row_block, w_qkv, pre...]
    scatter-add x5 -> x0, other arithmetic: 30.4 us -> none  [the longest x3 28.7 us: query_step(): partial_value = partial_value.at[:, index_row + shift_base].add(both_parts)]
    dot_general x16 -> x0, matrix products: 26.6 us -> none  [the longest x3 6.02 us: attend(): jnp.einsum('tlu,tuf->lf', score_gradient, masked_keys, preferred_element_...]
    pallas_call x0 -> x7, Pallas kernels: none -> 24.9 us  [the longest x1 14.8 us: body(): pl.pallas_call(functools.partial(attend_kernel, blocks_here, head_dim), o...]
    ppermute x12 -> x8, starting transfers between devices: 35.1 us -> 13 us  [the longest x2 6.18 us: trade_first(): return lax.ppermute(x, 'var', pairs)]
    all_to_all x0 -> x2, blocking collectives: none -> 20.8 us  [swap(): return lax.all_to_all(x, 'var', 0, 0, axis_index_groups=groups)]
    slice x7 -> x0, local copies, waits for them, and re-layouts: 14.1 us -> none  [the longest x2 6.33 us: body(): received = shifted(partial_value[:, piece_low:piece_high], 'var', offset)]
  transfers between devices with their start and end apart: 13 -> 10, of which waited for: 7 -> 4; matrix products, arithmetic and copies ran while one was open for 4% -> 0% of each run, Pallas kernels for 0% -> 8%
where the time goes in v2:
time: 97.9 us; the launch traced here: 96.4 us
  Pallas kernels  24.9 us (25%)
  blocking collectives  20.8 us (21%)
  starting transfers between devices  20 us (20%)
  waiting for transfers between devices  19.5 us (20%)
  local copies, waits for them, and re-layouts  9.6 us (10%)
    all_to_all x2, blocking collectives, swap(): return lax.all_to_all(x, 'var', 0, 0, axis_index_groups=groups)  20.8 us
    pallas_call x1, Pallas kernels, body(): pl.pallas_call(functools.partial(attend_kernel, blocks_here, head_dim), o...  14.8 us
    ppermute x2, waiting for transfers between devices, trade_first(): return lax.ppermute(x, 'var', pairs)  10.9 us
    unnamed x27, local copies, waits for them, and re-layouts  9.6 us
    all_to_all x2, waiting for transfers between devices, swap(): return lax.all_to_all(x, 'var', 0, 0, axis_index_groups=groups)  7.82 us
    all_to_all x2, starting transfers between devices, swap(): return lax.all_to_all(x, 'var', 0, 0, axis_index_groups=groups)  6.97 us
    ppermute x2, starting transfers between devices, trade_first(): return lax.ppermute(x, 'var', pairs)  6.18 us
    ppermute x3, starting transfers between devices, trade(): return lax.ppermute(x, 'var', [(n, n ^ distance) for n in range(devices)])  3.18 us
  transfers between devices with their start and end apart: 10, of which 4 were waited for; matrix products, arithmetic and copies ran while one was open for 0% of the time, Pallas kernels for 8%

profile of v2, /device:TPU:0, one launch (start us, length us, event | category | flops | bytes accessed | tf_op | source)
XLA Modules:
  0.0 96.4 jit_solution(16748882563690614008)
XLA Ops:
  0.6 0.0 copy-start.3
  0.6 1.0 %copy-done.3 = bf16[384,512]{1,0:T(8,128)(2,1)S(1)} copy-done((bf16[384,512]{1,0:T(8,128)(2,1)S(1)}, bf16[384,512]{1,0:T(8,128)(2,1)}, u32[]{:S(2)}) %copy-start.3) | copy-done | bytes 393240
  1.6 0.0 copy-start.4
  1.6 1.0 %copy-done.4 = bf16[384,512]{1,0:T(8,128)(2,1)S(1)} copy-done((bf16[384,512]{1,0:T(8,128)(2,1)S(1)}, bf16[384,512]{1,0:T(8,128)(2,1)}, u32[]{:S(2)}) %copy-start.4) | copy-done | bytes 393240
  2.6 0.0 copy-start.12
  2.6 1.5 %shard_map.102 = (bf16[384,256]{1,0:T(8,128)(2,1)S(1)}, bf16[384,256]{1,0:T(8,128)(2,1)S(1)}, bf16[384,256]{1,0:T(8,128)(2,1)S(1)}, bf16[384,256]{1,0:T(8,128)(2,1)S(1)}) custom-call(bf16[384,512]{1,0:T(8,128)(2,1)S(1)} %copy-done.3, bf16[384,512]{1,0:T(8,128)(2,1)S(1)} %copy-done.4), custom_call_target="tpu_custom_call" | custom-call | tf_op jit(solution)/shard_map/pallas_call | solution.py:428
  4.1 0.5 collective-permute-start
  4.6 2.6 %collective-permute-start.1 = (bf16[384,256]{1,0:T(8,128)(2,1)S(1)}, bf16[384,256]{1,0:T(8,128)(2,1)S(1)}, u32[]{:S(2)}, u32[]{:S(2)}) collective-permute-start(bf16[384,256]{1,0:T(8,128)(2,1)S(1)} %get-tuple-element.23), channel_id=1, source_target_pairs={{0,4},{2,6},{4,0},{6,2},{8,12},{10,14},{12,8},{14,10},{16,20},{18,... | collective-permute-start | bytes 589832 | tf_op jit(solution)/shard_map/ppermute | solution.py:412
  7.2 0.1 collective-permute-start.2
  7.3 0.0 copy-start.9
  7.3 1.0 %copy-done.9 = bf16[384,512]{1,0:T(8,128)(2,1)S(1)} copy-done((bf16[384,512]{1,0:T(8,128)(2,1)S(1)}, bf16[384,512]{1,0:T(8,128)(2,1)}, u32[]{:S(2)}) %copy-start.9) | copy-done | bytes 393240
  8.3 0.0 copy-start.10
  8.3 1.0 %copy-done.10 = bf16[384,512]{1,0:T(8,128)(2,1)S(1)} copy-done((bf16[384,512]{1,0:T(8,128)(2,1)S(1)}, bf16[384,512]{1,0:T(8,128)(2,1)}, u32[]{:S(2)}) %copy-start.10) | copy-done | bytes 393240
  9.3 0.0 copy-start.11
  9.3 0.7 copy-done.11
  10.0 2.4 %shard_map.104 = bf16[4,400,256]{2,1,0:T(8,128)(2,1)} custom-call(bf16[384,512]{1,0:T(8,128)(2,1)S(1)} %copy-done.9, bf16[384,512]{1,0:T(8,128)(2,1)S(1)} %copy-done.10, f32[8,384]{1,0:T(8,128)S(1)} %copy-done.11), custom_call_target="tpu_custom_call" | custom-call | tf_op jit(solution)/shard_map/pallas_call | solution.py:436
  12.4 3.5 %all-to-all-start = ((bf16[4,400,256]{2,1,0:T(8,128)(2,1)}), bf16[4,400,256]{2,1,0:T(8,128)(2,1)S(1)}, u32[]{:S(2)}, u32[]{:S(2)}) async-start(bf16[4,400,256]{2,1,0:T(8,128)(2,1)} %shard_map.104), calls=%async_computation | async-start | bytes 1638400 | tf_op jit(solution)/shard_map/all_to_all | solution.py:409
  15.9 0.0 collective-permute-done.refs_1_
  15.9 0.0 collective-permute-done.1.refs_2_
  15.9 0.8 collective-permute-done.2.refs_3_
  16.6 1.0 %shard_map.103 = (bf16[12,128,256]{2,1,0:T(8,128)(2,1)S(1)}, bf16[8,128,256]{2,1,0:T(8,128)(2,1)}, bf16[8,128,256]{2,1,0:T(8,128)(2,1)S(1)}) custom-call(bf16[384,256]{1,0:T(8,128)(2,1)S(1)} %get-tuple-element.21.refs_0_, bf16[384,256]{1,0:T(8,128)(2,1)S(1)} %collective-permute-done.refs_1_, bf16[384,256]{1,0:T(8,128)(2,1)S(1)} %collective-permute-done.1.refs_2_, ...), custom_call_target="tpu_custom_call" | custom-call | tf_op jit(solution)/shard_map/pallas_call | solution.py:448
  17.6 1.6 %collective-permute-start.3 = (bf16[8,128,256]{2,1,0:T(8,128)(2,1)}, bf16[8,128,256]{2,1,0:T(8,128)(2,1)S(1)}, u32[]{:S(2)}, u32[]{:S(2)}) collective-permute-start(bf16[8,128,256]{2,1,0:T(8,128)(2,1)} %get-tuple-element.26), channel_id=1, source_target_pairs={{0,8},{2,10},{4,12},{6,14},{8,0},{10,2},{12,4},{14,6},{16,24},{18,... | collective-permute-start | bytes 1572872 | tf_op jit(solution)/shard_map/ppermute | solution.py:416
  19.2 0.7 collective-permute-start.4
  19.9 0.0 copy-done.12
  19.9 0.1 copy.11.kb_ref
  20.0 7.8 %all-to-all-done.qo_ref = bf16[4,400,256]{2,1,0:T(8,128)(2,1)S(1)} async-done(((bf16[4,400,256]{2,1,0:T(8,128)(2,1)}), bf16[4,400,256]{2,1,0:T(8,128)(2,1)S(1)}, u32[]{:S(2)}, u32[]{:S(2)}) %all-to-all-start) | async-done | bytes 819232 | tf_op jit(solution)/shard_map/all_to_all | solution.py:409
  27.8 4.0 %collective-permute-done.3.first_ref = bf16[8,128,256]{2,1,0:T(8,128)(2,1)S(1)} collective-permute-done((bf16[8,128,256]{2,1,0:T(8,128)(2,1)}, bf16[8,128,256]{2,1,0:T(8,128)(2,1)S(1)}, u32[]{:S(2)}, u32[]{:S(2)}) %collective-permute-start.3) | collective-permute-done | bytes 524320 | tf_op jit(solution)/shard_map/ppermute | solution.py:416
  31.8 0.0 collective-permute-done.4.second_ref
  31.8 14.8 %shard_map.105 = (f32[12,128,256]{2,1,0:T(8,128)S(1)}, bf16[8,128,256]{2,1,0:T(8,128)(2,1)}, bf16[8,128,256]{2,1,0:T(8,128)(2,1)}, bf16[1536,128]{1,0:T(8,128)(2,1)S(1)}) custom-call(s32[48,8]{1,0:T(8,128)S(1)} %copy.11.kb_ref, bf16[12,128,256]{2,1,0:T(8,128)(2,1)S(1)} %get-tuple-element.25.own_ref, ...), custom_call_target="tpu_custom_call" | custom-call | flops 8053063680 | bytes 2000000 | tf_op jit(solution)/shard_map/pallas_call | solution.py:464
  46.6 0.0 copy-start.1
  46.6 1.2 %copy-done.1 = f32[12,128,256]{2,1,0:T(8,128)} copy-done((f32[12,128,256]{2,1,0:T(8,128)}, f32[12,128,256]{2,1,0:T(8,128)S(1)}, u32[]{:S(2)}) %copy-start.1) | copy-done | bytes 1572888
  47.8 0.0 copy-start.5
  47.8 0.7 copy-done.5
  48.5 0.0 copy-start
  48.5 4.5 %collective-permute-start.5 = (bf16[8,128,256]{2,1,0:T(8,128)(2,1)}, bf16[8,128,256]{2,1,0:T(8,128)(2,1)}, u32[]{:S(2)}, u32[]{:S(2)}) collective-permute-start(bf16[8,128,256]{2,1,0:T(8,128)(2,1)} %get-tuple-element.30), channel_id=1, source_target_pairs={{0,8},{2,10},{4,12},{6,14},{8,0},{10,2},{12,4},{14,6},{16,24},{18,... | collective-permute-start | bytes 1572872 | tf_op jit(solution)/shard_map/ppermute | solution.py:416
  53.1 1.5 %collective-permute-start.6 = (bf16[8,128,256]{2,1,0:T(8,128)(2,1)}, bf16[8,128,256]{2,1,0:T(8,128)(2,1)}, u32[]{:S(2)}, u32[]{:S(2)}) collective-permute-start(bf16[8,128,256]{2,1,0:T(8,128)(2,1)} %get-tuple-element.31), channel_id=1, source_target_pairs={{8,16},{10,18},{12,20},{14,22},{16,8},{18,10},{20,12},{22,14},{9,1... | collective-permute-start | bytes 1572872 | tf_op jit(solution)/shard_map/ppermute | solution.py:424
  54.5 3.5 %all-to-all-start.1 = ((bf16[4,384,128]{2,1,0:T(8,128)(2,1)}), bf16[4,384,128]{2,1,0:T(8,128)(2,1)S(1)}, u32[]{:S(2)}, u32[]{:S(2)}) async-start(bf16[4,384,128]{2,1,0:T(8,128)(2,1)} %bitcast.1), calls=%async_computation.1 | async-start | bytes 786432 | tf_op jit(solution)/shard_map/all_to_all | solution.py:409
  58.0 6.9 %collective-permute-done.5.first_ref = bf16[8,128,256]{2,1,0:T(8,128)(2,1)} collective-permute-done((bf16[8,128,256]{2,1,0:T(8,128)(2,1)}, bf16[8,128,256]{2,1,0:T(8,128)(2,1)}, u32[]{:S(2)}, u32[]{:S(2)}) %collective-permute-start.5) | collective-permute-done | bytes 524320 | tf_op jit(solution)/shard_map/ppermute | solution.py:416
  64.9 0.0 collective-permute-done.6.second_ref
  64.9 0.0 copy-start.2
  64.9 1.4 %copy-done.2 = f32[12,128,256]{2,1,0:T(8,128)S(1)} copy-done((f32[12,128,256]{2,1,0:T(8,128)S(1)}, f32[12,128,256]{2,1,0:T(8,128)}, u32[]{:S(2)}) %copy-start.2) | copy-done | bytes 1572888
  66.3 2.2 %shard_map.106 = (bf16[4,192,256]{2,1,0:T(8,128)(2,1)S(1)}, bf16[4,192,256]{2,1,0:T(8,128)(2,1)S(1)}) custom-call(f32[12,128,256]{2,1,0:T(8,128)S(1)} %copy-done.2, bf16[8,128,256]{2,1,0:T(8,128)(2,1)} %collective-permute-done.5.first_ref, bf16[8,128,256]{2,1,0:T(8,128)(2,1)} %collective-permute-done.6.second_ref), custom_call_target="tpu_custom_call" | custom-call | tf_op jit(solution)/shard_map/pallas_call | solution.py:494
  68.5 0.0 copy-start.6
  68.5 0.7 copy-done.6
  69.2 0.0 copy-start.8
  69.2 0.7 copy-done.8
  70.0 0.0 all-to-all-done.1.dq_ref
  70.0 0.0 copy-start.7
  70.0 11.0 %all_to_all.20.away_ref.dkv_ref = bf16[4,192,256]{2,1,0:T(8,128)(2,1)S(1)} all-to-all(bf16[4,192,256]{2,1,0:T(8,128)(2,1)} %copy-done.8), channel_id=1, replica_groups={{0,2,4,6},{8,10,12,14},{16,18,20,22},{24,26,28,30},{1,3,5,7},{9,11,13,1..., dimensions={0} | all-to-all | bytes 786432 | tf_op jit(solution)/shard_map/all_to_all | solution.py:409
  81.0 0.0 copy-done
  81.0 1.2 %shard_map.108 = bf16[192,1024]{1,0:T(8,128)(2,1)S(1)} custom-call(bf16[4,384,128]{2,1,0:T(8,128)(2,1)S(1)} %all-to-all-done.1.dq_ref, bf16[4,192,256]{2,1,0:T(8,128)(2,1)S(1)} %all_to_all.20.away_ref.dkv_ref, bf16[3,1024,512]{2,1,0:T(8,128)(2,1)S(1)} %copy-done), custom_call_target="tpu_custom_call" | custom-call | flops 603979776 | bytes 4000000 | tf_op jit(solution)/shard_map/pallas_call | solution.py:509
  82.2 1.6 %collective-permute-start.7 = (bf16[192,1024]{1,0:T(8,128)(2,1)S(1)}, bf16[192,1024]{1,0:T(8,128)(2,1)S(1)}, u32[]{:S(2)}, u32[]{:S(2)}) collective-permute-start(bf16[192,1024]{1,0:T(8,128)(2,1)S(1)} %shard_map.108), channel_id=1, source_target_pairs={{0,1},{1,0},{2,3},{3,2},{4,5},{5,4},{6,7},{7,6},{8,9},{9,8},{10,11... | collective-permute-start | bytes 1179656 | tf_op jit(solution)/shard_map/ppermute | solution.py:532
  83.7 0.0 copy-done.7
  83.7 9.8 %all_to_all.21.home_ref = bf16[4,192,256]{2,1,0:T(8,128)(2,1)S(1)} all-to-all(bf16[4,192,256]{2,1,0:T(8,128)(2,1)S(1)} %copy-done.7), channel_id=1, replica_groups={{0,2,4,6},{8,10,12,14},{16,18,20,22},{24,26,28,30},{1,3,5,7},{9,11,13,1..., dimensions={0} | all-to-all | bytes 786432 | tf_op jit(solution)/shard_map/all_to_all | solution.py:409
  93.6 2.0 %shard_map.107 = (bf16[384,512]{1,0:T(8,128)(2,1)}, bf16[384,512]{1,0:T(8,128)(2,1)}, bf16[384,512]{1,0:T(8,128)(2,1)}, f32[192,1024]{1,0:T(8,128)S(1)}) custom-call(bf16[4,384,128]{2,1,0:T(8,128)(2,1)S(1)} %all-to-all-done.1.dq_ref, bf16[4,192,256]{2,1,0:T(8,128)(2,1)S(1)} %all_to_all.20.away_ref.dkv_ref, bf16[4,192,256]{2,1,0:T(8,128)(2,1)S(1)} %all_to_all.21.home_ref, ...), custom_call_target="tpu_custom_call" | custom-call | flops 603979776 | bytes 6000000 | tf_op jit(solution)/shard_map/pallas_call | solution.py:520
  95.6 0.0 collective-permute-done.7
  95.6 0.8 add_convert_fusion
Async XLA Ops:
  0.6 1.0 %copy-start.3 = (bf16[384,512]{1,0:T(8,128)(2,1)S(1)}, bf16[384,512]{1,0:T(8,128)(2,1)}, u32[]{:S(2)}) copy-start(bf16[384,512]{1,0:T(8,128)(2,1)} %k_hbm.1) | copy-start | bytes 1179652
  1.6 1.0 %copy-start.4 = (bf16[384,512]{1,0:T(8,128)(2,1)S(1)}, bf16[384,512]{1,0:T(8,128)(2,1)}, u32[]{:S(2)}) copy-start(bf16[384,512]{1,0:T(8,128)(2,1)} %v_hbm.1) | copy-start | bytes 1179652
  2.6 17.3 %copy-start.12 = (s32[48,8]{0,1:T(8,128)S(1)}, s32[48,8]{0,1:T(8,128)}, u32[]{:S(2)}) copy-start(s32[48,8]{0,1:T(8,128)} %param.12) | copy-start | bytes 4612
  4.1 11.8 %collective-permute-start = (bf16[384,256]{1,0:T(8,128)(2,1)S(1)}, bf16[384,256]{1,0:T(8,128)(2,1)S(1)}, u32[]{:S(2)}, u32[]{:S(2)}) collective-permute-start(bf16[384,256]{1,0:T(8,128)(2,1)S(1)} %get-tuple-element.22), channel_id=1, source_target_pairs={{0,2},{2,0},{4,6},{6,4},{8,10},{10,8},{12,14},{14,12},{16,18},{18,... | collective-permute-start | bytes 589832 | tf_op jit(solution)/shard_map/ppermute | solution.py:412
  4.6 11.3 %collective-permute-start.1 = (bf16[384,256]{1,0:T(8,128)(2,1)S(1)}, bf16[384,256]{1,0:T(8,128)(2,1)S(1)}, u32[]{:S(2)}, u32[]{:S(2)}) collective-permute-start(bf16[384,256]{1,0:T(8,128)(2,1)S(1)} %get-tuple-element.23), channel_id=1, source_target_pairs={{0,4},{2,6},{4,0},{6,2},{8,12},{10,14},{12,8},{14,10},{16,20},{18,... | collective-permute-start | bytes 589832 | tf_op jit(solution)/shard_map/ppermute | solution.py:412
  7.2 9.4 %collective-permute-start.2 = (bf16[384,256]{1,0:T(8,128)(2,1)S(1)}, bf16[384,256]{1,0:T(8,128)(2,1)S(1)}, u32[]{:S(2)}, u32[]{:S(2)}) collective-permute-start(bf16[384,256]{1,0:T(8,128)(2,1)S(1)} %get-tuple-element.24), channel_id=1, source_target_pairs={{0,6},{2,4},{4,2},{6,0},{8,14},{10,12},{12,10},{14,8},{16,22},{18,... | collective-permute-start | bytes 589832 | tf_op jit(solution)/shard_map/ppermute | solution.py:412
  7.3 1.0 %copy-start.9 = (bf16[384,512]{1,0:T(8,128)(2,1)S(1)}, bf16[384,512]{1,0:T(8,128)(2,1)}, u32[]{:S(2)}) copy-start(bf16[384,512]{1,0:T(8,128)(2,1)} %q_hbm.1) | copy-start | bytes 1179652
  8.3 1.0 %copy-start.10 = (bf16[384,512]{1,0:T(8,128)(2,1)S(1)}, bf16[384,512]{1,0:T(8,128)(2,1)}, u32[]{:S(2)}) copy-start(bf16[384,512]{1,0:T(8,128)(2,1)} %g_hbm.1) | copy-start | bytes 1179652
  9.3 0.7 copy-start.11
  12.4 15.5 %all-to-all-start = ((bf16[4,400,256]{2,1,0:T(8,128)(2,1)}), bf16[4,400,256]{2,1,0:T(8,128)(2,1)S(1)}, u32[]{:S(2)}, u32[]{:S(2)}) async-start(bf16[4,400,256]{2,1,0:T(8,128)(2,1)} %shard_map.104), calls=%async_computation | async-start | bytes 1638400 | tf_op jit(solution)/shard_map/all_to_all | solution.py:409
  17.6 14.2 %collective-permute-start.3 = (bf16[8,128,256]{2,1,0:T(8,128)(2,1)}, bf16[8,128,256]{2,1,0:T(8,128)(2,1)S(1)}, u32[]{:S(2)}, u32[]{:S(2)}) collective-permute-start(bf16[8,128,256]{2,1,0:T(8,128)(2,1)} %get-tuple-element.26), channel_id=1, source_target_pairs={{0,8},{2,10},{4,12},{6,14},{8,0},{10,2},{12,4},{14,6},{16,24},{18,... | collective-permute-start | bytes 1572872 | tf_op jit(solution)/shard_map/ppermute | solution.py:416
  19.2 12.6 %collective-permute-start.4 = (bf16[8,128,256]{2,1,0:T(8,128)(2,1)S(1)}, bf16[8,128,256]{2,1,0:T(8,128)(2,1)S(1)}, u32[]{:S(2)}, u32[]{:S(2)}) collective-permute-start(bf16[8,128,256]{2,1,0:T(8,128)(2,1)S(1)} %get-tuple-element.27), channel_id=1, source_target_pairs={{8,16},{10,18},{12,20},{14,22},{16,8},{18,10},{20,12},{22,14},{9,1... | collective-permute-start | bytes 1572872 | tf_op jit(solution)/shard_map/ppermute | solution.py:424
  46.6 1.2 %copy-start.1 = (f32[12,128,256]{2,1,0:T(8,128)}, f32[12,128,256]{2,1,0:T(8,128)S(1)}, u32[]{:S(2)}) copy-start(f32[12,128,256]{2,1,0:T(8,128)S(1)} %get-tuple-element.29.own_ref) | copy-start | bytes 4718596
  47.8 0.7 copy-start.5
  48.5 32.5 %copy-start = (bf16[3,1024,512]{2,1,0:T(8,128)(2,1)S(1)}, bf16[3,1024,512]{2,1,0:T(8,128)(2,1)}, u32[]{:S(2)}) copy-start(bf16[3,1024,512]{2,1,0:T(8,128)(2,1)} %w_ref.3) | copy-start | bytes 9437188
  48.5 16.4 %collective-permute-start.5 = (bf16[8,128,256]{2,1,0:T(8,128)(2,1)}, bf16[8,128,256]{2,1,0:T(8,128)(2,1)}, u32[]{:S(2)}, u32[]{:S(2)}) collective-permute-start(bf16[8,128,256]{2,1,0:T(8,128)(2,1)} %get-tuple-element.30), channel_id=1, source_target_pairs={{0,8},{2,10},{4,12},{6,14},{8,0},{10,2},{12,4},{14,6},{16,24},{18,... | collective-permute-start | bytes 1572872 | tf_op jit(solution)/shard_map/ppermute | solution.py:416
  53.1 11.9 %collective-permute-start.6 = (bf16[8,128,256]{2,1,0:T(8,128)(2,1)}, bf16[8,128,256]{2,1,0:T(8,128)(2,1)}, u32[]{:S(2)}, u32[]{:S(2)}) collective-permute-start(bf16[8,128,256]{2,1,0:T(8,128)(2,1)} %get-tuple-element.31), channel_id=1, source_target_pairs={{8,16},{10,18},{12,20},{14,22},{16,8},{18,10},{20,12},{22,14},{9,1... | collective-permute-start | bytes 1572872 | tf_op jit(solution)/shard_map/ppermute | solution.py:424
  54.5 15.5 %all-to-all-start.1 = ((bf16[4,384,128]{2,1,0:T(8,128)(2,1)}), bf16[4,384,128]{2,1,0:T(8,128)(2,1)S(1)}, u32[]{:S(2)}, u32[]{:S(2)}) async-start(bf16[4,384,128]{2,1,0:T(8,128)(2,1)} %bitcast.1), calls=%async_computation.1 | async-start | bytes 786432 | tf_op jit(solution)/shard_map/all_to_all | solution.py:409
  64.9 1.4 %copy-start.2 = (f32[12,128,256]{2,1,0:T(8,128)S(1)}, f32[12,128,256]{2,1,0:T(8,128)}, u32[]{:S(2)}) copy-start(f32[12,128,256]{2,1,0:T(8,128)} %copy-done.1) | copy-start | bytes 4718596
  68.5 0.7 copy-start.6
  69.2 0.7 copy-start.8
  70.0 13.7 %copy-start.7 = (bf16[4,192,256]{2,1,0:T(8,128)(2,1)S(1)}, bf16[4,192,256]{2,1,0:T(8,128)(2,1)}, u32[]{:S(2)}) copy-start(bf16[4,192,256]{2,1,0:T(8,128)(2,1)} %copy-done.6) | copy-start | bytes 1179652
  82.2 13.4 %collective-permute-start.7 = (bf16[192,1024]{1,0:T(8,128)(2,1)S(1)}, bf16[192,1024]{1,0:T(8,128)(2,1)S(1)}, u32[]{:S(2)}, u32[]{:S(2)}) collective-permute-start(bf16[192,1024]{1,0:T(8,128)(2,1)S(1)} %shard_map.108), channel_id=1, source_target_pairs={{0,1},{1,0},{2,3},{3,2},{4,5},{5,4},{6,7},{7,6},{8,9},{9,8},{10,11... | collective-permute-start | bytes 1179656 | tf_op jit(solution)/shard_map/ppermute | solution.py:532

commit v3 on v2

--- a/solution.py
+++ b/solution.py
@@ -80,26 +80,34 @@
         copy.wait()
 
 
-def pack_kv_kernel(k_hbm, v_hbm, *rest):
-    outs, (k_ref, v_ref, turned, sems) = rest[:GROUP], rest[GROUP:]
-    load_all([(k_hbm, k_ref), (v_hbm, v_ref)], sems)
-    rows, features = k_ref.shape
+def send_pieces(outs, stage):
+    me = lax.axis_index("var") % GROUP
+    for distance, out in enumerate(outs):
+        out[...] = stage[me ^ distance]
+
+
+def stage_pieces(stage, pieces):
+    me = lax.axis_index("var") % GROUP
+    for distance, piece in enumerate(pieces):
+        stage[me ^ distance] = piece[...]
+
+
+def pack_kernel(x_hbm, *rest):
+    outs, (x_ref, turned, sems) = rest[:GROUP], rest[GROUP:]
+    load_all([(x_hbm, x_ref)], sems)
+    rows, features = x_ref.shape
     width = features // GROUP
     order = reorder_matrix(False)
     for b in range(rows // BLOCK):
         at = slice(b * BLOCK, (b + 1) * BLOCK)
-        for half, ref in enumerate((k_ref, v_ref)):
-            moved = dot(order, ref[at]).astype(BF16)
-            for member in range(GROUP):
-                turned[member, at, half * LANES : (half + 1) * LANES] = widen(
-                    moved[:, member * width : (member + 1) * width]
-                )
-    me = lax.axis_index("var") % GROUP
-    for distance, out in enumerate(outs):
-        out[...] = turned[me ^ distance]
-
-
-def pack_qo_kernel(slots, head_dim, q_hbm, g_hbm, lse_ref, qo_ref, q_ref, g_ref, sems):
+        moved = dot(order, x_ref[at]).astype(BF16)
+        for member in range(GROUP):
+            turned[member, at] = widen(moved[:, member * width : (member + 1) * width])
+    send_pieces(outs, turned)
+
+
+def pack_qo_kernel(slots, head_dim, q_hbm, g_hbm, lse_ref, *rest):
+    outs, (q_ref, g_ref, qo_ref, sems) = rest[:GROUP], rest[GROUP:]
     load_all([(q_hbm, q_ref), (g_hbm, g_ref)], sems)
     rows, features = q_ref.shape
     width = features // GROUP
@@ -136,6 +144,7 @@
             moved = dot(jnp.concatenate(parts, axis=0).astype(BF16), spread[slot])
             total = moved if total is None else total + moved
         qo_ref[member, rows:] = total.astype(BF16)
+    send_pieces(outs, qo_ref)
 
 
 def exchange_start(group_blocks):
@@ -149,7 +158,7 @@
     blocks = pieces[0].shape[0] // BLOCK
     me = lax.axis_index("var") % GROUP
     for distance, piece in enumerate(pieces):
-        own[pl.ds((me ^ distance) * blocks, blocks)] = piece[...].reshape(blocks, BLOCK, 2 * LANES)
+        own[pl.ds((me ^ distance) * blocks, blocks)] = piece[...].reshape(blocks, BLOCK, LANES)
     first, second = exchange_start(GROUP * blocks)
     first_out[...] = own[pl.ds(first, SPAN)]
     second_out[...] = own[pl.ds(second, SPAN)]
@@ -159,24 +168,13 @@
     blocks_here,
     head_dim,
     kb_ref,
-    own_ref,
-    first_ref,
-    second_ref,
-    qo_ref,
-    own_out,
-    first_out,
-    second_out,
-    dq_out,
-    kv_win,
-    k_turn,
-    acc,
-    shifts,
-    queries,
-    grads,
-    crossed,
-    prob,
-    slope,
+    *refs,
 ):
+    key_refs, value_refs, refs = refs[:3], refs[3:6], refs[6:]
+    qo_pieces, refs = refs[:GROUP], refs[GROUP:]
+    key_outs, value_outs, refs = refs[:3], refs[3:6], refs[6:]
+    dq_outs, refs = refs[:GROUP], refs[GROUP:]
+    kv_win, k_turn, acc, shifts, queries, grads, crossed, prob, slope, qo_ref, dq_all = refs
     group_blocks = GROUP * blocks_here
     window = group_blocks + 2 * SPAN
     rows = blocks_here * BLOCK
@@ -189,9 +187,11 @@
     low = slice(0, LANES)
     high = slice(LANES, 2 * LANES)
 
-    kv_win[SPAN : SPAN + group_blocks] = own_ref[...]
-    kv_win[pl.ds(first_at, SPAN)] = first_ref[...]
-    kv_win[pl.ds(second_at, SPAN)] = second_ref[...]
+    for cols, (own_ref, first_ref, second_ref) in ((low, key_refs), (high, value_refs)):
+        kv_win[SPAN : SPAN + group_blocks, :, cols] = own_ref[...]
+        kv_win[pl.ds(first_at, SPAN), :, cols] = first_ref[...]
+        kv_win[pl.ds(second_at, SPAN), :, cols] = second_ref[...]
+    stage_pieces(qo_ref, qo_pieces)
     key_patch = lax.broadcasted_iota(jnp.int32, (8, LANES), 0)
     query_patch = lax.broadcasted_iota(jnp.int32, (8, LANES), 1) & 7
     usable = key_patch <= query_patch
@@ -292,7 +292,8 @@
             turned = dq[:, cols].T
             halves.append(jnp.where(head_a, turned[:HALF], turned[HALF:]))
         moved = dot(unorder, jnp.concatenate(halves, axis=0).astype(BF16)).astype(BF16)
-        dq_out[pl.ds(pl.multiple_of(query_block * BLOCK, BLOCK), BLOCK)] = moved
+        local = pl.multiple_of((query_block % blocks_here) * BLOCK, BLOCK)
+        dq_all[query_block // blocks_here, pl.ds(local, BLOCK)] = moved
 
     delta = forward(0, 0)
 
@@ -312,9 +313,16 @@
     else:
         backward(group_blocks - 1, 0, delta)
 
-    first_out[...] = acc[pl.ds(first_at, SPAN)].astype(BF16)
-    second_out[...] = acc[pl.ds(second_at, SPAN)].astype(BF16)
-    own_out[...] = acc[SPAN : SPAN + group_blocks]
+    groups = BLOCK // 16
+    for cols, (own_out, first_out, second_out) in ((low, key_outs), (high, value_outs)):
+        for out, start, count in (
+            (first_out, first_at, SPAN),
+            (second_out, second_at, SPAN),
+            (own_out, SPAN, group_blocks),
+        ):
+            part = acc[pl.ds(start, count), :, cols].reshape(count, 2, groups, 8, LANES)
+            out[...] = jnp.swapaxes(part, 1, 2).reshape(count, BLOCK, LANES).astype(out.dtype)
+    send_pieces(dq_outs, dq_all)
 
 
 def owner_start(piece, half):
@@ -322,39 +330,45 @@
     return pl.multiple_of(((lax.axis_index("head") + 1 + piece) % heads) * half, half)
 
 
-def combine_kernel(own_ref, first_ref, second_ref, away_out, home_out, total, moved):
+def add_parts(own_ref, first_ref, second_ref, total, moved):
     group_blocks = own_ref.shape[0]
-    blocks_here = group_blocks // GROUP
-    half = home_out.shape[1]
     first, second = exchange_start(group_blocks)
     total[...] = own_ref[...]
     for start, ref in ((first, first_ref), (second, second_ref)):
         at = pl.ds(start, SPAN)
         total[at] = total[at] + ref[...].astype(F32)
-    unorder = reorder_matrix(True)
-    for block in range(group_blocks):
-        at = (block % blocks_here) * BLOCK
-        moved[block // blocks_here, at : at + BLOCK] = dot(
-            unorder, total[block].astype(BF16)
-        ).astype(BF16)
-    away = away_out.shape[1] // half
-    for member in range(GROUP):
+    moved[...] = total[...].astype(BF16).reshape(moved.shape)
+
+
+def combine_kernel(own_ref, first_ref, second_ref, *rest):
+    outs, (total, moved) = rest[:GROUP], rest[GROUP:]
+    add_parts(own_ref, first_ref, second_ref, total, moved)
+    send_pieces(outs, moved)
+
+
+def combine_split_kernel(own_ref, first_ref, second_ref, *rest):
+    aways, homes, (total, moved) = rest[:GROUP], rest[GROUP : 2 * GROUP], rest[2 * GROUP :]
+    add_parts(own_ref, first_ref, second_ref, total, moved)
+    half = homes[0].shape[0]
+    away = aways[0].shape[0] // half
+    me = lax.axis_index("var") % GROUP
+    for distance in range(GROUP):
+        member = me ^ distance
         for piece in range(away):
-            away_out[member, piece * half : (piece + 1) * half] = moved[
+            aways[distance][piece * half : (piece + 1) * half] = moved[
                 member, pl.ds(owner_start(piece, half), half)
             ]
-        home_out[member] = moved[member, pl.ds(owner_start(away, half), half)]
-
-
-def gather_rows(grads, dq_ref, start, dkv_ref, dkv_at):
+        homes[distance][...] = moved[member, pl.ds(owner_start(away, half), half)]
+
+
+def gather_rows(grads, stages, start, dv_stage, dv_at):
     half = grads.shape[1]
     width = grads.shape[2] // GROUP
     for member in range(GROUP):
         at = slice(member * width, (member + 1) * width)
-        both = dkv_ref[member, dkv_at * half : (dkv_at + 1) * half]
-        grads[0, :, at] = dq_ref[member, pl.ds(start, half)][:, :width]
-        grads[1, :, at] = both[:, :width]
-        grads[2, :, at] = both[:, LANES : LANES + width]
+        for s, stage in enumerate(stages):
+            grads[s, :, at] = stage[member, pl.ds(start, half)][:, :width]
+        grads[2, :, at] = dv_stage[member, dv_at * half : (dv_at + 1) * half][:, :width]
 
 
 def product(grads, w_ref):
@@ -364,23 +378,33 @@
     return total
 
 
-def away_kernel(dq_ref, dkv_ref, w_ref, *rest):
-    outs, grads = rest[:-1], rest[-1]
+def away_kernel(*refs):
+    dqs, dks, dvs, (w_ref, *rest) = refs[:4], refs[4:8], refs[8:12], refs[12:]
+    outs, (grads, dq, dk, dv) = rest[:-4], rest[-4:]
     half = grads.shape[1]
+    stage_pieces(dq, dqs)
+    stage_pieces(dk, dks)
+    stage_pieces(dv, dvs)
     for piece, out in enumerate(outs):
-        gather_rows(grads, dq_ref, owner_start(piece, half), dkv_ref, piece)
+        gather_rows(grads, (dq, dk), owner_start(piece, half), dv, piece)
         out[...] = product(grads, w_ref).astype(BF16)
 
 
-def home_kernel(dq_ref, away_ref, home_ref, w_ref, dq_out, dk_out, dv_out, keep_out, grads):
+def home_kernel(*refs):
+    dqs, dks, aways, homes, rest = refs[:4], refs[4:8], refs[8:12], refs[12:16], refs[16:]
+    w_ref, dq_out, dk_out, dv_out, keep_out, grads, dq, dk, away_dv, home_dv = rest
     half = grads.shape[1]
-    away = away_ref.shape[1] // half
+    away = away_dv.shape[1] // half
+    stage_pieces(dq, dqs)
+    stage_pieces(dk, dks)
+    stage_pieces(away_dv, aways)
+    stage_pieces(home_dv, homes)
     for piece in range(away + 1):
         start = owner_start(piece, half)
         if piece < away:
-            gather_rows(grads, dq_ref, start, away_ref, piece)
+            gather_rows(grads, (dq, dk), start, away_dv, piece)
         else:
-            gather_rows(grads, dq_ref, start, home_ref, 0)
+            gather_rows(grads, (dq, dk), start, home_dv, 0)
         at = pl.ds(start, half)
         dq_out[at] = grads[0]
         dk_out[at] = grads[1]
@@ -402,11 +426,7 @@
     half = rows // heads
     model = w_qkv.shape[1]
     wide = 2 * LANES
-    groups = [[start + i for i in range(GROUP)] for start in range(0, devices, GROUP)]
     hbm = pl.BlockSpec(memory_space=pltpu.HBM)
-
-    def swap(x):
-        return lax.all_to_all(x, "var", 0, 0, axis_index_groups=groups)
 
     def trade(x, distance):
         return lax.ppermute(x, "var", [(n, n ^ distance) for n in range(devices)])
@@ -423,54 +443,68 @@
                 pairs.append((n, other))
         return lax.ppermute(x, "var", pairs)
 
-    loaded = [pltpu.VMEM((rows, features), BF16), pltpu.VMEM((rows, features), BF16)]
-    sems = [pltpu.SemaphoreType.DMA((2, LOADS))]
-    kvs = pl.pallas_call(
-        pack_kv_kernel,
-        out_shape=(shaped((rows, wide)),) * GROUP,
-        in_specs=[hbm] * 2,
-        out_specs=(vmem(),) * GROUP,
-        scratch_shapes=loaded + [pltpu.VMEM((GROUP, rows, wide), BF16)] + sems,
-        compiler_params=params(48),
-    )(keys, values)
-    qo = pl.pallas_call(
-        functools.partial(pack_qo_kernel, slots, head_dim),
-        out_shape=shaped((GROUP, rows + LSE_ROWS, wide)),
-        in_specs=[hbm, hbm, vmem()],
-        out_specs=vmem(),
-        scratch_shapes=loaded + sems,
-        compiler_params=params(12),
-    )(queries, out_grad, log_sum_exp)
-
-    pieces = [kvs[0]] + [None] * (GROUP - 1)
-    for distance in (2, 3, 1):
-        pieces[distance] = trade(kvs[distance], distance)
-    own, first_send, second_send = pl.pallas_call(
-        line_kernel,
-        out_shape=(
-            shaped((group_blocks, BLOCK, wide)),
-            shaped((SPAN, BLOCK, wide)),
-            shaped((SPAN, BLOCK, wide)),
-        ),
-        in_specs=[vmem()] * GROUP,
-        out_specs=(vmem(),) * 3,
-        compiler_params=params(12),
-    )(*pieces)
-    first = trade_first(first_send)
-    second = trade_second(second_send)
-    qo = swap(qo)
+    def swap(pieces):
+        got = [pieces[0]] + [None] * (GROUP - 1)
+        for distance in (2, 3, 1):
+            got[distance] = trade(pieces[distance], distance)
+        return got
+
+    def staged(count, width=LANES):
+        return pltpu.VMEM((GROUP, count, width), BF16)
+
+    loaded = pltpu.VMEM((rows, features), BF16)
+    block = (BLOCK, LANES)
+
+    def pack(x):
+        return pl.pallas_call(
+            pack_kernel,
+            out_shape=(shaped((rows, LANES)),) * GROUP,
+            in_specs=[hbm],
+            out_specs=(vmem(),) * GROUP,
+            scratch_shapes=[loaded, staged(rows), pltpu.SemaphoreType.DMA((1, LOADS))],
+            compiler_params=params(8),
+        )(x)
+
+    def line_up(pieces):
+        return pl.pallas_call(
+            line_kernel,
+            out_shape=(shaped((group_blocks,) + block),) + (shaped((SPAN,) + block),) * 2,
+            in_specs=[vmem()] * GROUP,
+            out_specs=(vmem(),) * 3,
+            compiler_params=params(8),
+        )(*pieces)
+
+    key_pieces = swap(pack(keys))
+    value_pieces = swap(pack(values))
+    own_keys, first_keys, second_keys = line_up(key_pieces)
+    first_keys = trade_first(first_keys)
+    second_keys = trade_second(second_keys)
+    own_values, first_values, second_values = line_up(value_pieces)
+    first_values = trade_first(first_values)
+    second_values = trade_second(second_values)
+    qos = swap(
+        pl.pallas_call(
+            functools.partial(pack_qo_kernel, slots, head_dim),
+            out_shape=(shaped((rows + LSE_ROWS, wide)),) * GROUP,
+            in_specs=[hbm, hbm, vmem()],
+            out_specs=(vmem(),) * GROUP,
+            scratch_shapes=[
+                loaded,
+                loaded,
+                staged(rows + LSE_ROWS, wide),
+                pltpu.SemaphoreType.DMA((2, LOADS)),
+            ],
+            compiler_params=params(8),
+        )(queries, out_grad, log_sum_exp)
+    )
 
     pairs = group_blocks * slot_count * BLOCK * BLOCK * slots
-    own_sum, first_part, second_part, dq = pl.pallas_call(
+    sums = (shaped((group_blocks,) + block, F32),) + (shaped((SPAN,) + block),) * 2
+    results = pl.pallas_call(
         functools.partial(attend_kernel, blocks_here, head_dim),
-        out_shape=(
-            shaped((group_blocks, BLOCK, wide), F32),
-            shaped((SPAN, BLOCK, wide)),
-            shaped((SPAN, BLOCK, wide)),
-            shaped((group_blocks * BLOCK, LANES)),
-        ),
-        in_specs=[pl.BlockSpec(memory_space=pltpu.SMEM)] + [vmem()] * 4,
-        out_specs=(vmem(),) * 4,
+        out_shape=sums + sums + (shaped((rows, LANES)),) * GROUP,
+        in_specs=[pl.BlockSpec(memory_space=pltpu.SMEM)] + [vmem()] * (6 + GROUP),
+        out_specs=(vmem(),) * (6 + GROUP),
         scratch_shapes=[
             pltpu.VMEM((window, BLOCK, wide), BF16),
             pltpu.VMEM((window, LANES, BLOCK), BF16),
@@ -481,53 +515,75 @@
             pltpu.VMEM((2, wide, wide), BF16),
             pltpu.VMEM((2, slot_count * BLOCK, wide), F32),
             pltpu.VMEM((2, slot_count * BLOCK, wide), F32),
+            staged(rows + LSE_ROWS, wide),
+            staged(rows),
         ],
         compiler_params=params(24),
         cost_estimate=pl.CostEstimate(
             flops=40 * pairs * head_dim, bytes_accessed=2_000_000, transcendentals=pairs
         ),
-    )(key_blocks, own, first, second, qo)
-
+    )(
+        key_blocks,
+        own_keys,
+        first_keys,
+        second_keys,
+        own_values,
+        first_values,
+        second_values,
+        *qos,
+    )
+    key_sum, first_part, second_part = results[:3]
     first_back = trade_first(first_part)
     second_back = trade_second(second_part)
-    dq = swap(dq.reshape(GROUP, rows, LANES))
-    away, home = pl.pallas_call(
-        combine_kernel,
-        out_shape=(shaped((GROUP, rows - half, wide)), shaped((GROUP, half, wide))),
+    value_sum, first_part, second_part = results[3:6]
+    first_value_back = trade_first(first_part)
+    second_value_back = trade_second(second_part)
+    dqs = swap(results[6:])
+    summing = [pltpu.VMEM((group_blocks,) + block, F32), staged(rows)]
+    dks = swap(
+        pl.pallas_call(
+            combine_kernel,
+            out_shape=(shaped((rows, LANES)),) * GROUP,
+            in_specs=[vmem()] * 3,
+            out_specs=(vmem(),) * GROUP,
+            scratch_shapes=summing,
+            compiler_params=params(8),
+        )(key_sum, first_back, second_back)
+    )
+    split = pl.pallas_call(
+        combine_split_kernel,
+        out_shape=(shaped((rows - half, LANES)),) * GROUP + (shaped((half, LANES)),) * GROUP,
         in_specs=[vmem()] * 3,
-        out_specs=(vmem(),) * 2,
-        scratch_shapes=[
-            pltpu.VMEM((group_blocks, BLOCK, wide), F32),
-            pltpu.VMEM((GROUP, rows, wide), BF16),
-        ],
-        compiler_params=params(16),
-    )(own_sum, first_back, second_back)
-    away = swap(away)
-    home = swap(home)
-
-    grads = [pltpu.VMEM((3, half, features), BF16)]
+        out_specs=(vmem(),) * (2 * GROUP),
+        scratch_shapes=summing,
+        compiler_params=params(8),
+    )(value_sum, first_value_back, second_value_back)
+    aways = swap(split[:GROUP])
+    homes = swap(split[GROUP:])
+
+    grads = pltpu.VMEM((3, half, features), BF16)
     sends = pl.pallas_call(
         away_kernel,
         out_shape=(shaped((half, model)),) * (heads - 1),
-        in_specs=[vmem()] * 3,
+        in_specs=[vmem()] * (3 * GROUP + 1),
         out_specs=(vmem(),) * (heads - 1),
-        scratch_shapes=grads,
-        compiler_params=params(16),
+        scratch_shapes=[grads, staged(rows), staged(rows), staged(rows - half)],
+        compiler_params=params(12),
         cost_estimate=pl.CostEstimate(
             flops=6 * (rows - half) * features * model, bytes_accessed=4_000_000, transcendentals=0
         ),
-    )(dq, away, w_qkv)
+    )(*dqs, *dks, *aways, w_qkv)
     dq_out, dk_out, dv_out, total = pl.pallas_call(
         home_kernel,
         out_shape=(shaped((rows, features)),) * 3 + (shaped((half, model), F32),),
-        in_specs=[vmem()] * 4,
+        in_specs=[vmem()] * (4 * GROUP + 1),
         out_specs=(vmem(),) * 4,
-        scratch_shapes=grads,
-        compiler_params=params(16),
+        scratch_shapes=[grads, staged(rows), staged(rows), staged(rows - half), staged(half)],
+        compiler_params=params(12),
         cost_estimate=pl.CostEstimate(
             flops=6 * half * features * model, bytes_accessed=6_000_000, transcendentals=0
         ),
-    )(dq, away, home, w_qkv)
+    )(*dqs, *dks, *aways, *homes, w_qkv)
     for piece, send in enumerate(sends):
         got = lax.ppermute(send, "head", [(n, (n + piece + 1) % heads) for n in range(heads)])
         total = total + got.astype(F32)

time: 97.9 us -> 89.6 us (0.915)
  blocking collectives: 20.8 us -> 0 us
  starting transfers between devices: 20 us -> 32 us
  waiting for transfers between devices: 19.5 us -> 27.6 us
  local copies, waits for them, and re-layouts: 9.6 us -> 5.46 us
  Pallas kernels: 24.9 us -> 21.9 us
    all_to_all x2 -> x0, blocking collectives: 20.8 us -> none  [swap(): return lax.all_to_all(x, 'var', 0, 0, axis_index_groups=groups)]
    ppermute x3 -> x21, waiting for transfers between devices: 0.76 us -> 18.8 us  [trade(): return lax.ppermute(x, 'var', [(n, n ^ distance) for n in range(devices)])]
    ppermute x3 -> x21, starting transfers between devices: 3.18 us -> 15.9 us  [trade(): return lax.ppermute(x, 'var', [(n, n ^ distance) for n in range(devices)])]
    all_to_all x2 -> x0, waiting for transfers between devices: 7.82 us -> none  [swap(): return lax.all_to_all(x, 'var', 0, 0, axis_index_groups=groups)]
    all_to_all x2 -> x0, starting transfers between devices: 6.97 us -> none  [swap(): return lax.all_to_all(x, 'var', 0, 0, axis_index_groups=groups)]
    ppermute x2 -> x4, starting transfers between devices: 6.18 us -> 11.9 us  [trade_first(): return lax.ppermute(x, 'var', pairs)]
    ppermute x2 -> x4, waiting for transfers between devices: 10.9 us -> 6.02 us  [trade_first(): return lax.ppermute(x, 'var', pairs)]
    unnamed x27 -> x13, local copies, waits for them, and re-layouts: 9.6 us -> 5.46 us
  transfers between devices with their start and end apart: 10 -> 30, of which waited for: 4 -> 10; matrix products, arithmetic and copies ran while one was open for 0% -> 1% of each run, Pallas kernels for 8% -> 5%
where the time goes in v3:
time: 89.6 us; the launch traced here: 88.6 us
  starting transfers between devices  32 us (36%)
  waiting for transfers between devices  27.6 us (31%)
  Pallas kernels  21.9 us (24%)
  local copies, waits for them, and re-layouts  5.46 us (6%)
    ppermute x21, waiting for transfers between devices, trade(): return lax.ppermute(x, 'var', [(n, n ^ distance) for n in range(devices)])  18.8 us
    ppermute x21, starting transfers between devices, trade(): return lax.ppermute(x, 'var', [(n, n ^ distance) for n in range(devices)])  15.9 us
    pallas_call x1, Pallas kernels, body(): pl.pallas_call(functools.partial(attend_kernel, blocks_here, head_dim), o...  14.4 us
    ppermute x4, starting transfers between devices, trade_first(): return lax.ppermute(x, 'var', pairs)  11.9 us
    ppermute x4, waiting for transfers between devices, trade_first(): return lax.ppermute(x, 'var', pairs)  6.02 us
    unnamed x13, local copies, waits for them, and re-layouts  5.46 us
    ppermute x1, waiting for transfers between devices, body(): lax.ppermute(send, 'head', [(n, (n + piece + 1) % heads) for n in range(h...  2.83 us
    ppermute x4, starting transfers between devices, trade_second(): return lax.ppermute(x, 'var', pairs)  2.66 us
  transfers between devices with their start and end apart: 30, of which 10 were waited for; matrix products, arithmetic and copies ran while one was open for 1% of the time, Pallas kernels for 5%

profile of v3, /device:TPU:0, one launch (start us, length us, event | category | flops | bytes accessed | tf_op | source)
XLA Modules:
  0.0 88.6 jit_solution(10126107387419042716)
XLA Ops:
  0.6 1.0 %copy-done.1 = bf16[384,512]{1,0:T(8,128)(2,1)S(1)} copy-done((bf16[384,512]{1,0:T(8,128)(2,1)S(1)}, bf16[384,512]{1,0:T(8,128)(2,1)}, u32[]{:S(2)}) %copy-start.1) | copy-done | bytes 393240
  1.6 1.0 %copy-done.2 = bf16[384,512]{1,0:T(8,128)(2,1)S(1)} copy-done((bf16[384,512]{1,0:T(8,128)(2,1)S(1)}, bf16[384,512]{1,0:T(8,128)(2,1)}, u32[]{:S(2)}) %copy-start.2) | copy-done | bytes 393240
  2.6 0.7 copy-done.5
  3.3 2.2 %shard_map.106 = (bf16[400,256]{1,0:T(8,128)(2,1)S(1)}, bf16[400,256]{1,0:T(8,128)(2,1)S(1)}, bf16[400,256]{1,0:T(8,128)(2,1)S(1)}, bf16[400,256]{1,0:T(8,128)(2,1)}) custom-call(bf16[384,512]{1,0:T(8,128)(2,1)S(1)} %copy-done.1, bf16[384,512]{1,0:T(8,128)(2,1)S(1)} %copy-done.2, f32[8,384]{1,0:T(8,128)S(1)} %copy-done.5), custom_call_target="tpu_custom_call" | custom-call | tf_op jit(solution)/shard_map/pallas_call | solution.py:486
  5.5 0.5 collective-permute-start.10
  6.1 1.0 %copy-done.3 = bf16[384,512]{1,0:T(8,128)(2,1)S(1)} copy-done((bf16[384,512]{1,0:T(8,128)(2,1)S(1)}, bf16[384,512]{1,0:T(8,128)(2,1)}, u32[]{:S(2)}) %copy-start.3) | copy-done | bytes 393240
  7.1 0.8 shard_map.104
  7.8 0.1 collective-permute-start.5
  8.0 3.0 %collective-permute-start.6 = (bf16[384,128]{1,0:T(8,128)(2,1)S(1)}, bf16[384,128]{1,0:T(8,128)(2,1)S(1)}, u32[]{:S(2)}, u32[]{:S(2)}) collective-permute-start(bf16[384,128]{1,0:T(8,128)(2,1)S(1)} %get-tuple-element.57), channel_id=1, source_target_pairs={{0,4},{2,6},{4,0},{6,2},{8,12},{10,14},{12,8},{14,10},{16,20},{18,... | collective-permute-start | bytes 294920 | tf_op jit(solution)/shard_map/ppermute | solution.py:432
  10.9 0.0 collective-permute-start.7
  10.9 1.4 %collective-permute-start.11 = (bf16[400,256]{1,0:T(8,128)(2,1)S(1)}, bf16[400,256]{1,0:T(8,128)(2,1)S(1)}, u32[]{:S(2)}, u32[]{:S(2)}) collective-permute-start(bf16[400,256]{1,0:T(8,128)(2,1)S(1)} %get-tuple-element.64), channel_id=1, source_target_pairs={{0,4},{2,6},{4,0},{6,2},{8,12},{10,14},{12,8},{14,10},{16,20},{18,... | collective-permute-start | bytes 614408 | tf_op jit(solution)/shard_map/ppermute | solution.py:432
  12.4 1.0 %copy-done.4 = bf16[384,512]{1,0:T(8,128)(2,1)S(1)} copy-done((bf16[384,512]{1,0:T(8,128)(2,1)S(1)}, bf16[384,512]{1,0:T(8,128)(2,1)}, u32[]{:S(2)}) %copy-start.4) | copy-done | bytes 393240
  13.4 0.8 shard_map.102
  14.2 0.5 collective-permute-start
  14.7 1.9 %collective-permute-start.1 = (bf16[384,128]{1,0:T(8,128)(2,1)S(1)}, bf16[384,128]{1,0:T(8,128)(2,1)S(1)}, u32[]{:S(2)}, u32[]{:S(2)}) collective-permute-start(bf16[384,128]{1,0:T(8,128)(2,1)S(1)} %get-tuple-element.50), channel_id=1, source_target_pairs={{0,4},{2,6},{4,0},{6,2},{8,12},{10,14},{12,8},{14,10},{16,20},{18,... | collective-permute-start | bytes 294920 | tf_op jit(solution)/shard_map/ppermute | solution.py:432
  16.6 0.0 collective-permute-done.7.refs_3_
  16.6 1.5 %collective-permute-start.2 = (bf16[384,128]{1,0:T(8,128)(2,1)S(1)}, bf16[384,128]{1,0:T(8,128)(2,1)S(1)}, u32[]{:S(2)}, u32[]{:S(2)}) collective-permute-start(bf16[384,128]{1,0:T(8,128)(2,1)S(1)} %get-tuple-element.51), channel_id=1, source_target_pairs={{0,6},{2,4},{4,2},{6,0},{8,14},{10,12},{12,10},{14,8},{16,22},{18,... | collective-permute-start | bytes 294920 | tf_op jit(solution)/shard_map/ppermute | solution.py:432
  18.1 0.1 shard_map.105
  18.2 0.0 collective-permute-done.refs_1_
  18.2 1.6 %collective-permute-start.8 = (bf16[8,128,128]{2,1,0:T(8,128)(2,1)S(1)}, bf16[8,128,128]{2,1,0:T(8,128)(2,1)S(1)}, u32[]{:S(2)}, u32[]{:S(2)}) collective-permute-start(bf16[8,128,128]{2,1,0:T(8,128)(2,1)S(1)} %get-tuple-element.60), channel_id=1, source_target_pairs={{0,8},{2,10},{4,12},{6,14},{8,0},{10,2},{12,4},{14,6},{16,24},{18,... | collective-permute-start | bytes 786440 | tf_op jit(solution)/shard_map/ppermute | solution.py:436
  19.8 2.9 %collective-permute-done.1.refs_2_ = bf16[384,128]{1,0:T(8,128)(2,1)S(1)} collective-permute-done((bf16[384,128]{1,0:T(8,128)(2,1)S(1)}, bf16[384,128]{1,0:T(8,128)(2,1)S(1)}, u32[]{:S(2)}, u32[]{:S(2)}) %collective-permute-start.1) | collective-permute-done | bytes 98336 | tf_op jit(solution)/shard_map/ppermute | solution.py:432
  22.7 0.7 collective-permute-start.9
  23.4 1.3 %collective-permute-done.2.refs_3_ = bf16[384,128]{1,0:T(8,128)(2,1)S(1)} collective-permute-done((bf16[384,128]{1,0:T(8,128)(2,1)S(1)}, bf16[384,128]{1,0:T(8,128)(2,1)S(1)}, u32[]{:S(2)}, u32[]{:S(2)}) %collective-permute-start.2) | collective-permute-done | bytes 98336 | tf_op jit(solution)/shard_map/ppermute | solution.py:432
  24.7 0.1 shard_map.103
  24.8 3.5 %collective-permute-start.3 = (bf16[8,128,128]{2,1,0:T(8,128)(2,1)S(1)}, bf16[8,128,128]{2,1,0:T(8,128)(2,1)S(1)}, u32[]{:S(2)}, u32[]{:S(2)}) collective-permute-start(bf16[8,128,128]{2,1,0:T(8,128)(2,1)S(1)} %get-tuple-element.53), channel_id=1, source_target_pairs={{0,8},{2,10},{4,12},{6,14},{8,0},{10,2},{12,4},{14,6},{16,24},{18,... | collective-permute-start | bytes 786440 | tf_op jit(solution)/shard_map/ppermute | solution.py:436
  28.3 0.0 collective-permute-done.10.refs_7_
  28.3 0.7 collective-permute-start.4
  29.0 0.0 collective-permute-done.11.refs_8_
  29.0 0.1 collective-permute-start.12
  29.1 0.8 copy.11.kb_ref
  29.8 6.3 %collective-permute-done.12.refs_9_ = bf16[400,256]{1,0:T(8,128)(2,1)} collective-permute-done((bf16[400,256]{1,0:T(8,128)(2,1)}, bf16[400,256]{1,0:T(8,128)(2,1)}, u32[]{:S(2)}, u32[]{:S(2)}) %collective-permute-start.12) | collective-permute-done | bytes 204832 | tf_op jit(solution)/shard_map/ppermute | solution.py:432
  36.1 0.0 collective-permute-done.8.refs_4_
  36.1 0.0 collective-permute-done.9.refs_5_
  36.1 0.0 collective-permute-done.3.refs_1_
  36.1 0.0 copy-start
  36.2 14.4 %shard_map.107 = (f32[12,128,128]{2,1,0:T(8,128)S(1)}, bf16[8,128,128]{2,1,0:T(8,128)(2,1)S(1)}, bf16[8,128,128]{2,1,0:T(8,128)(2,1)S(1)}, f32[12,128,128]{2,1,0...) custom-call(s32[48,8]{1,0:T(8,128)S(1)} %copy.11.kb_ref, ...), custom_call_target="tpu_custom_call" | custom-call | flops 8053063680 | bytes 2000000 | tf_op jit(solution)/shard_map/pallas_call | solution.py:503
  50.6 3.8 %collective-permute-start.16 = (bf16[8,128,128]{2,1,0:T(8,128)(2,1)S(1)}, bf16[8,128,128]{2,1,0:T(8,128)(2,1)S(1)}, u32[]{:S(2)}, u32[]{:S(2)}) collective-permute-start(bf16[8,128,128]{2,1,0:T(8,128)(2,1)S(1)} %get-tuple-element.71), channel_id=1, source_target_pairs={{0,8},{2,10},{4,12},{6,14},{8,0},{10,2},{12,4},{14,6},{16,24},{18,... | collective-permute-start | bytes 786440 | tf_op jit(solution)/shard_map/ppermute | solution.py:436
  54.4 0.7 collective-permute-start.17
  55.0 2.9 %collective-permute-start.21 = (bf16[8,128,128]{2,1,0:T(8,128)(2,1)S(1)}, bf16[8,128,128]{2,1,0:T(8,128)(2,1)S(1)}, u32[]{:S(2)}, u32[]{:S(2)}) collective-permute-start(bf16[8,128,128]{2,1,0:T(8,128)(2,1)S(1)} %get-tuple-element.78), channel_id=1, source_target_pairs={{0,8},{2,10},{4,12},{6,14},{8,0},{10,2},{12,4},{14,6},{16,24},{18,... | collective-permute-start | bytes 786440 | tf_op jit(solution)/shard_map/ppermute | solution.py:436
  57.9 0.7 collective-permute-start.22
  58.6 0.1 collective-permute-start.13
  58.7 2.9 %collective-permute-done.16.first_ref = bf16[8,128,128]{2,1,0:T(8,128)(2,1)S(1)} collective-permute-done((bf16[8,128,128]{2,1,0:T(8,128)(2,1)S(1)}, bf16[8,128,128]{2,1,0:T(8,128)(2,1)S(1)}, u32[]{:S(2)}, u32[]{:S(2)}) %collective-permute-start.16) | collective-permute-done | bytes 262176 | tf_op jit(solution)/shard_map/ppermute | solution.py:436
  61.6 0.9 collective-permute-start.14
  62.4 0.3 shard_map.108
  62.7 3.1 %collective-permute-done.21.first_ref = bf16[8,128,128]{2,1,0:T(8,128)(2,1)S(1)} collective-permute-done((bf16[8,128,128]{2,1,0:T(8,128)(2,1)S(1)}, bf16[8,128,128]{2,1,0:T(8,128)(2,1)S(1)}, u32[]{:S(2)}, u32[]{:S(2)}) %collective-permute-start.21) | collective-permute-done | bytes 262176 | tf_op jit(solution)/shard_map/ppermute | solution.py:436
  65.8 0.0 collective-permute-start.18
  65.8 0.3 shard_map.109
  66.1 0.6 collective-permute-start.23
  66.7 1.3 %collective-permute-start.19 = (bf16[384,128]{1,0:T(8,128)(2,1)S(1)}, bf16[384,128]{1,0:T(8,128)(2,1)S(1)}, u32[]{:S(2)}, u32[]{:S(2)}) collective-permute-start(bf16[384,128]{1,0:T(8,128)(2,1)S(1)} %get-tuple-element.75), channel_id=1, source_target_pairs={{0,4},{2,6},{4,0},{6,2},{8,12},{10,14},{12,8},{14,10},{16,20},{18,... | collective-permute-start | bytes 294920 | tf_op jit(solution)/shard_map/ppermute | solution.py:432
  68.0 0.1 collective-permute-start.20
  68.1 1.3 %collective-permute-start.24 = (bf16[192,128]{1,0:T(8,128)(2,1)S(1)}, bf16[192,128]{1,0:T(8,128)(2,1)S(1)}, u32[]{:S(2)}, u32[]{:S(2)}) collective-permute-start(bf16[192,128]{1,0:T(8,128)(2,1)S(1)} %get-tuple-element.82), channel_id=1, source_target_pairs={{0,4},{2,6},{4,0},{6,2},{8,12},{10,14},{12,8},{14,10},{16,20},{18,... | collective-permute-start | bytes 147464 | tf_op jit(solution)/shard_map/ppermute | solution.py:432
  69.5 0.7 collective-permute-start.25
  70.2 4.9 %collective-permute-done.24.refs_10_ = bf16[192,128]{1,0:T(8,128)(2,1)S(1)} collective-permute-done((bf16[192,128]{1,0:T(8,128)(2,1)S(1)}, bf16[192,128]{1,0:T(8,128)(2,1)S(1)}, u32[]{:S(2)}, u32[]{:S(2)}) %collective-permute-start.24) | collective-permute-done | bytes 49184 | tf_op jit(solution)/shard_map/ppermute | solution.py:432
  75.1 0.1 collective-permute-done.25.refs_11_
  75.2 1.2 %shard_map.111 = bf16[192,1024]{1,0:T(8,128)(2,1)S(1)} custom-call(bf16[384,128]{1,0:T(8,128)(2,1)S(1)} %get-tuple-element.66.refs_0_, bf16[384,128]{1,0:T(8,128)(2,1)S(1)} %collective-permute-done.13.refs_1_, bf16[384,128]{1,0:T(8,128)(2,1)S(1)} %collective-permute-done.14.refs_2_, bf16[384,128]{1,0:T(8,128)(2,1)S(1)} %collective-permute-done.15.refs_3_, ...), custom_call_target="tpu_custom_call" | custom-call | flops 603979776 | bytes 4000000 | tf_op jit(solution)/shard_map/pallas_call | solution.py:565
  76.4 1.6 %collective-permute-start.29 = (bf16[192,1024]{1,0:T(8,128)(2,1)S(1)}, bf16[192,1024]{1,0:T(8,128)(2,1)S(1)}, u32[]{:S(2)}, u32[]{:S(2)}) collective-permute-start(bf16[192,1024]{1,0:T(8,128)(2,1)S(1)} %shard_map.111), channel_id=1, source_target_pairs={{0,1},{1,0},{2,3},{3,2},{4,5},{5,4},{6,7},{7,6},{8,9},{9,8},{10,11... | collective-permute-start | bytes 1179656 | tf_op jit(solution)/shard_map/ppermute | solution.py:588
  78.0 0.0 collective-permute-start.26
  78.0 1.4 %collective-permute-start.27 = (bf16[192,128]{1,0:T(8,128)(2,1)S(1)}, bf16[192,128]{1,0:T(8,128)(2,1)S(1)}, u32[]{:S(2)}, u32[]{:S(2)}) collective-permute-start(bf16[192,128]{1,0:T(8,128)(2,1)S(1)} %get-tuple-element.86), channel_id=1, source_target_pairs={{0,4},{2,6},{4,0},{6,2},{8,12},{10,14},{12,8},{14,10},{16,20},{18,... | collective-permute-start | bytes 147464 | tf_op jit(solution)/shard_map/ppermute | solution.py:432
  79.3 0.5 collective-permute-start.28
  79.8 2.3 %collective-permute-done.27.refs_14_ = bf16[192,128]{1,0:T(8,128)(2,1)S(1)} collective-permute-done((bf16[192,128]{1,0:T(8,128)(2,1)S(1)}, bf16[192,128]{1,0:T(8,128)(2,1)S(1)}, u32[]{:S(2)}, u32[]{:S(2)}) %collective-permute-start.27) | collective-permute-done | bytes 49184 | tf_op jit(solution)/shard_map/ppermute | solution.py:432
  82.1 1.0 %collective-permute-done.28.refs_15_ = bf16[192,128]{1,0:T(8,128)(2,1)S(1)} collective-permute-done((bf16[192,128]{1,0:T(8,128)(2,1)S(1)}, bf16[192,128]{1,0:T(8,128)(2,1)S(1)}, u32[]{:S(2)}, u32[]{:S(2)}) %collective-permute-start.28) | collective-permute-done | bytes 49184 | tf_op jit(solution)/shard_map/ppermute | solution.py:432
  83.1 1.9 %shard_map.110 = (bf16[384,512]{1,0:T(8,128)(2,1)}, bf16[384,512]{1,0:T(8,128)(2,1)}, bf16[384,512]{1,0:T(8,128)(2,1)}, f32[192,1024]{1,0:T(8,128)S(1)}) custom-call(bf16[384,128]{1,0:T(8,128)(2,1)S(1)} %get-tuple-element.66.refs_0_, bf16[384,128]{1,0:T(8,128)(2,1)S(1)} %collective-permute-done.13.refs_1_, ...), custom_call_target="tpu_custom_call" | custom-call | flops 603979776 | bytes 6000000 | tf_op jit(solution)/shard_map/pallas_call | solution.py:576
  85.0 2.8 %collective-permute-done.29 = bf16[192,1024]{1,0:T(8,128)(2,1)S(1)} collective-permute-done((bf16[192,1024]{1,0:T(8,128)(2,1)S(1)}, bf16[192,1024]{1,0:T(8,128)(2,1)S(1)}, u32[]{:S(2)}, u32[]{:S(2)}) %collective-permute-start.29) | collective-permute-done | bytes 393248 | tf_op jit(solution)/shard_map/ppermute | solution.py:588
  87.8 0.8 add_convert_fusion
  (20 shorter events, 0.0 us)
Async XLA Ops:
  0.6 1.0 %copy-start.1 = (bf16[384,512]{1,0:T(8,128)(2,1)S(1)}, bf16[384,512]{1,0:T(8,128)(2,1)}, u32[]{:S(2)}) copy-start(bf16[384,512]{1,0:T(8,128)(2,1)} %q_hbm.1) | copy-start | bytes 1179652
  1.6 1.0 %copy-start.2 = (bf16[384,512]{1,0:T(8,128)(2,1)S(1)}, bf16[384,512]{1,0:T(8,128)(2,1)}, u32[]{:S(2)}) copy-start(bf16[384,512]{1,0:T(8,128)(2,1)} %g_hbm.1) | copy-start | bytes 1179652
  2.6 0.7 copy-start.5
  5.5 22.8 %collective-permute-start.10 = (bf16[400,256]{1,0:T(8,128)(2,1)S(1)}, bf16[400,256]{1,0:T(8,128)(2,1)S(1)}, u32[]{:S(2)}, u32[]{:S(2)}) collective-permute-start(bf16[400,256]{1,0:T(8,128)(2,1)S(1)} %get-tuple-element.63), channel_id=1, source_target_pairs={{0,2},{2,0},{4,6},{6,4},{8,10},{10,8},{12,14},{14,12},{16,18},{18,... | collective-permute-start | bytes 614408 | tf_op jit(solution)/shard_map/ppermute | solution.py:432
  6.1 1.0 %copy-start.3 = (bf16[384,512]{1,0:T(8,128)(2,1)S(1)}, bf16[384,512]{1,0:T(8,128)(2,1)}, u32[]{:S(2)}) copy-start(bf16[384,512]{1,0:T(8,128)(2,1)} %x_hbm.3) | copy-start | bytes 1179652
  7.8 6.3 %collective-permute-start.5 = (bf16[384,128]{1,0:T(8,128)(2,1)S(1)}, bf16[384,128]{1,0:T(8,128)(2,1)S(1)}, u32[]{:S(2)}, u32[]{:S(2)}) collective-permute-start(bf16[384,128]{1,0:T(8,128)(2,1)S(1)} %get-tuple-element.56), channel_id=1, source_target_pairs={{0,2},{2,0},{4,6},{6,4},{8,10},{10,8},{12,14},{14,12},{16,18},{18,... | collective-permute-start | bytes 294920 | tf_op jit(solution)/shard_map/ppermute | solution.py:432
  8.0 6.7 %collective-permute-start.6 = (bf16[384,128]{1,0:T(8,128)(2,1)S(1)}, bf16[384,128]{1,0:T(8,128)(2,1)S(1)}, u32[]{:S(2)}, u32[]{:S(2)}) collective-permute-start(bf16[384,128]{1,0:T(8,128)(2,1)S(1)} %get-tuple-element.57), channel_id=1, source_target_pairs={{0,4},{2,6},{4,0},{6,2},{8,12},{10,14},{12,8},{14,10},{16,20},{18,... | collective-permute-start | bytes 294920 | tf_op jit(solution)/shard_map/ppermute | solution.py:432
  10.9 5.7 %collective-permute-start.7 = (bf16[384,128]{1,0:T(8,128)(2,1)S(1)}, bf16[384,128]{1,0:T(8,128)(2,1)S(1)}, u32[]{:S(2)}, u32[]{:S(2)}) collective-permute-start(bf16[384,128]{1,0:T(8,128)(2,1)S(1)} %get-tuple-element.58), channel_id=1, source_target_pairs={{0,6},{2,4},{4,2},{6,0},{8,14},{10,12},{12,10},{14,8},{16,22},{18,... | collective-permute-start | bytes 294920 | tf_op jit(solution)/shard_map/ppermute | solution.py:432
  10.9 18.0 %collective-permute-start.11 = (bf16[400,256]{1,0:T(8,128)(2,1)S(1)}, bf16[400,256]{1,0:T(8,128)(2,1)S(1)}, u32[]{:S(2)}, u32[]{:S(2)}) collective-permute-start(bf16[400,256]{1,0:T(8,128)(2,1)S(1)} %get-tuple-element.64), channel_id=1, source_target_pairs={{0,4},{2,6},{4,0},{6,2},{8,12},{10,14},{12,8},{14,10},{16,20},{18,... | collective-permute-start | bytes 614408 | tf_op jit(solution)/shard_map/ppermute | solution.py:432
  12.4 1.0 %copy-start.4 = (bf16[384,512]{1,0:T(8,128)(2,1)S(1)}, bf16[384,512]{1,0:T(8,128)(2,1)}, u32[]{:S(2)}) copy-start(bf16[384,512]{1,0:T(8,128)(2,1)} %x_hbm.2) | copy-start | bytes 1179652
  14.2 4.0 %collective-permute-start = (bf16[384,128]{1,0:T(8,128)(2,1)S(1)}, bf16[384,128]{1,0:T(8,128)(2,1)S(1)}, u32[]{:S(2)}, u32[]{:S(2)}) collective-permute-start(bf16[384,128]{1,0:T(8,128)(2,1)S(1)} %get-tuple-element.49), channel_id=1, source_target_pairs={{0,2},{2,0},{4,6},{6,4},{8,10},{10,8},{12,14},{14,12},{16,18},{18,... | collective-permute-start | bytes 294920 | tf_op jit(solution)/shard_map/ppermute | solution.py:432
  14.7 8.0 %collective-permute-start.1 = (bf16[384,128]{1,0:T(8,128)(2,1)S(1)}, bf16[384,128]{1,0:T(8,128)(2,1)S(1)}, u32[]{:S(2)}, u32[]{:S(2)}) collective-permute-start(bf16[384,128]{1,0:T(8,128)(2,1)S(1)} %get-tuple-element.50), channel_id=1, source_target_pairs={{0,4},{2,6},{4,0},{6,2},{8,12},{10,14},{12,8},{14,10},{16,20},{18,... | collective-permute-start | bytes 294920 | tf_op jit(solution)/shard_map/ppermute | solution.py:432
  16.6 8.1 %collective-permute-start.2 = (bf16[384,128]{1,0:T(8,128)(2,1)S(1)}, bf16[384,128]{1,0:T(8,128)(2,1)S(1)}, u32[]{:S(2)}, u32[]{:S(2)}) collective-permute-start(bf16[384,128]{1,0:T(8,128)(2,1)S(1)} %get-tuple-element.51), channel_id=1, source_target_pairs={{0,6},{2,4},{4,2},{6,0},{8,14},{10,12},{12,10},{14,8},{16,22},{18,... | collective-permute-start | bytes 294920 | tf_op jit(solution)/shard_map/ppermute | solution.py:432
  18.2 17.9 %collective-permute-start.8 = (bf16[8,128,128]{2,1,0:T(8,128)(2,1)S(1)}, bf16[8,128,128]{2,1,0:T(8,128)(2,1)S(1)}, u32[]{:S(2)}, u32[]{:S(2)}) collective-permute-start(bf16[8,128,128]{2,1,0:T(8,128)(2,1)S(1)} %get-tuple-element.60), channel_id=1, source_target_pairs={{0,8},{2,10},{4,12},{6,14},{8,0},{10,2},{12,4},{14,6},{16,24},{18,... | collective-permute-start | bytes 786440 | tf_op jit(solution)/shard_map/ppermute | solution.py:436
  22.7 13.4 %collective-permute-start.9 = (bf16[8,128,128]{2,1,0:T(8,128)(2,1)S(1)}, bf16[8,128,128]{2,1,0:T(8,128)(2,1)S(1)}, u32[]{:S(2)}, u32[]{:S(2)}) collective-permute-start(bf16[8,128,128]{2,1,0:T(8,128)(2,1)S(1)} %get-tuple-element.61), channel_id=1, source_target_pairs={{8,16},{10,18},{12,20},{14,22},{16,8},{18,10},{20,12},{22,14},{9,1... | collective-permute-start | bytes 786440 | tf_op jit(solution)/shard_map/ppermute | solution.py:444
  24.8 11.4 %collective-permute-start.3 = (bf16[8,128,128]{2,1,0:T(8,128)(2,1)S(1)}, bf16[8,128,128]{2,1,0:T(8,128)(2,1)S(1)}, u32[]{:S(2)}, u32[]{:S(2)}) collective-permute-start(bf16[8,128,128]{2,1,0:T(8,128)(2,1)S(1)} %get-tuple-element.53), channel_id=1, source_target_pairs={{0,8},{2,10},{4,12},{6,14},{8,0},{10,2},{12,4},{14,6},{16,24},{18,... | collective-permute-start | bytes 786440 | tf_op jit(solution)/shard_map/ppermute | solution.py:436
  28.3 7.8 %collective-permute-start.4 = (bf16[8,128,128]{2,1,0:T(8,128)(2,1)S(1)}, bf16[8,128,128]{2,1,0:T(8,128)(2,1)S(1)}, u32[]{:S(2)}, u32[]{:S(2)}) collective-permute-start(bf16[8,128,128]{2,1,0:T(8,128)(2,1)S(1)} %get-tuple-element.54), channel_id=1, source_target_pairs={{8,16},{10,18},{12,20},{14,22},{16,8},{18,10},{20,12},{22,14},{9,1... | collective-permute-start | bytes 786440 | tf_op jit(solution)/shard_map/ppermute | solution.py:444
  29.0 7.1 %collective-permute-start.12 = (bf16[400,256]{1,0:T(8,128)(2,1)}, bf16[400,256]{1,0:T(8,128)(2,1)}, u32[]{:S(2)}, u32[]{:S(2)}) collective-permute-start(bf16[400,256]{1,0:T(8,128)(2,1)} %get-tuple-element.65), channel_id=1, source_target_pairs={{0,6},{2,4},{4,2},{6,0},{8,14},{10,12},{12,10},{14,8},{16,22},{18,... | collective-permute-start | bytes 614408 | tf_op jit(solution)/shard_map/ppermute | solution.py:432
  36.1 39.1 %copy-start = (bf16[3,1024,512]{2,1,0:T(8,128)(2,1)S(1)}, bf16[3,1024,512]{2,1,0:T(8,128)(2,1)}, u32[]{:S(2)}) copy-start(bf16[3,1024,512]{2,1,0:T(8,128)(2,1)} %refs_12_.1) | copy-start | bytes 9437188
  50.6 11.0 %collective-permute-start.16 = (bf16[8,128,128]{2,1,0:T(8,128)(2,1)S(1)}, bf16[8,128,128]{2,1,0:T(8,128)(2,1)S(1)}, u32[]{:S(2)}, u32[]{:S(2)}) collective-permute-start(bf16[8,128,128]{2,1,0:T(8,128)(2,1)S(1)} %get-tuple-element.71), channel_id=1, source_target_pairs={{0,8},{2,10},{4,12},{6,14},{8,0},{10,2},{12,4},{14,6},{16,24},{18,... | collective-permute-start | bytes 786440 | tf_op jit(solution)/shard_map/ppermute | solution.py:436
  54.4 8.1 %collective-permute-start.17 = (bf16[8,128,128]{2,1,0:T(8,128)(2,1)S(1)}, bf16[8,128,128]{2,1,0:T(8,128)(2,1)S(1)}, u32[]{:S(2)}, u32[]{:S(2)}) collective-permute-start(bf16[8,128,128]{2,1,0:T(8,128)(2,1)S(1)} %get-tuple-element.72), channel_id=1, source_target_pairs={{8,16},{10,18},{12,20},{14,22},{16,8},{18,10},{20,12},{22,14},{9,1... | collective-permute-start | bytes 786440 | tf_op jit(solution)/shard_map/ppermute | solution.py:444
  55.0 10.8 %collective-permute-start.21 = (bf16[8,128,128]{2,1,0:T(8,128)(2,1)S(1)}, bf16[8,128,128]{2,1,0:T(8,128)(2,1)S(1)}, u32[]{:S(2)}, u32[]{:S(2)}) collective-permute-start(bf16[8,128,128]{2,1,0:T(8,128)(2,1)S(1)} %get-tuple-element.78), channel_id=1, source_target_pairs={{0,8},{2,10},{4,12},{6,14},{8,0},{10,2},{12,4},{14,6},{16,24},{18,... | collective-permute-start | bytes 786440 | tf_op jit(solution)/shard_map/ppermute | solution.py:436
  57.9 7.9 %collective-permute-start.22 = (bf16[8,128,128]{2,1,0:T(8,128)(2,1)S(1)}, bf16[8,128,128]{2,1,0:T(8,128)(2,1)S(1)}, u32[]{:S(2)}, u32[]{:S(2)}) collective-permute-start(bf16[8,128,128]{2,1,0:T(8,128)(2,1)S(1)} %get-tuple-element.79), channel_id=1, source_target_pairs={{8,16},{10,18},{12,20},{14,22},{16,8},{18,10},{20,12},{22,14},{9,1... | collective-permute-start | bytes 786440 | tf_op jit(solution)/shard_map/ppermute | solution.py:444
  58.6 8.1 %collective-permute-start.13 = (bf16[384,128]{1,0:T(8,128)(2,1)S(1)}, bf16[384,128]{1,0:T(8,128)(2,1)S(1)}, u32[]{:S(2)}, u32[]{:S(2)}) collective-permute-start(bf16[384,128]{1,0:T(8,128)(2,1)S(1)} %get-tuple-element.67), channel_id=1, source_target_pairs={{0,2},{2,0},{4,6},{6,4},{8,10},{10,8},{12,14},{14,12},{16,18},{18,... | collective-permute-start | bytes 294920 | tf_op jit(solution)/shard_map/ppermute | solution.py:432
  61.6 6.4 %collective-permute-start.14 = (bf16[384,128]{1,0:T(8,128)(2,1)S(1)}, bf16[384,128]{1,0:T(8,128)(2,1)S(1)}, u32[]{:S(2)}, u32[]{:S(2)}) collective-permute-start(bf16[384,128]{1,0:T(8,128)(2,1)S(1)} %get-tuple-element.68), channel_id=1, source_target_pairs={{0,4},{2,6},{4,0},{6,2},{8,12},{10,14},{12,8},{14,10},{16,20},{18,... | collective-permute-start | bytes 294920 | tf_op jit(solution)/shard_map/ppermute | solution.py:432
  62.4 5.7 %collective-permute-start.15 = (bf16[384,128]{1,0:T(8,128)(2,1)S(1)}, bf16[384,128]{1,0:T(8,128)(2,1)S(1)}, u32[]{:S(2)}, u32[]{:S(2)}) collective-permute-start(bf16[384,128]{1,0:T(8,128)(2,1)S(1)} %get-tuple-element.69), channel_id=1, source_target_pairs={{0,6},{2,4},{4,2},{6,0},{8,14},{10,12},{12,10},{14,8},{16,22},{18,... | collective-permute-start | bytes 294920 | tf_op jit(solution)/shard_map/ppermute | solution.py:432
  65.8 9.4 %collective-permute-start.18 = (bf16[384,128]{1,0:T(8,128)(2,1)S(1)}, bf16[384,128]{1,0:T(8,128)(2,1)S(1)}, u32[]{:S(2)}, u32[]{:S(2)}) collective-permute-start(bf16[384,128]{1,0:T(8,128)(2,1)S(1)} %get-tuple-element.74), channel_id=1, source_target_pairs={{0,2},{2,0},{4,6},{6,4},{8,10},{10,8},{12,14},{14,12},{16,18},{18,... | collective-permute-start | bytes 294920 | tf_op jit(solution)/shard_map/ppermute | solution.py:432
  66.1 3.4 %collective-permute-start.23 = (bf16[192,128]{1,0:T(8,128)(2,1)S(1)}, bf16[192,128]{1,0:T(8,128)(2,1)S(1)}, u32[]{:S(2)}, u32[]{:S(2)}) collective-permute-start(bf16[192,128]{1,0:T(8,128)(2,1)S(1)} %get-tuple-element.81), channel_id=1, source_target_pairs={{0,2},{2,0},{4,6},{6,4},{8,10},{10,8},{12,14},{14,12},{16,18},{18,... | collective-permute-start | bytes 147464 | tf_op jit(solution)/shard_map/ppermute | solution.py:432
  66.7 8.5 %collective-permute-start.19 = (bf16[384,128]{1,0:T(8,128)(2,1)S(1)}, bf16[384,128]{1,0:T(8,128)(2,1)S(1)}, u32[]{:S(2)}, u32[]{:S(2)}) collective-permute-start(bf16[384,128]{1,0:T(8,128)(2,1)S(1)} %get-tuple-element.75), channel_id=1, source_target_pairs={{0,4},{2,6},{4,0},{6,2},{8,12},{10,14},{12,8},{14,10},{16,20},{18,... | collective-permute-start | bytes 294920 | tf_op jit(solution)/shard_map/ppermute | solution.py:432
  68.0 7.2 %collective-permute-start.20 = (bf16[384,128]{1,0:T(8,128)(2,1)S(1)}, bf16[384,128]{1,0:T(8,128)(2,1)S(1)}, u32[]{:S(2)}, u32[]{:S(2)}) collective-permute-start(bf16[384,128]{1,0:T(8,128)(2,1)S(1)} %get-tuple-element.76), channel_id=1, source_target_pairs={{0,6},{2,4},{4,2},{6,0},{8,14},{10,12},{12,10},{14,8},{16,22},{18,... | collective-permute-start | bytes 294920 | tf_op jit(solution)/shard_map/ppermute | solution.py:432
  68.1 7.0 %collective-permute-start.24 = (bf16[192,128]{1,0:T(8,128)(2,1)S(1)}, bf16[192,128]{1,0:T(8,128)(2,1)S(1)}, u32[]{:S(2)}, u32[]{:S(2)}) collective-permute-start(bf16[192,128]{1,0:T(8,128)(2,1)S(1)} %get-tuple-element.82), channel_id=1, source_target_pairs={{0,4},{2,6},{4,0},{6,2},{8,12},{10,14},{12,8},{14,10},{16,20},{18,... | collective-permute-start | bytes 147464 | tf_op jit(solution)/shard_map/ppermute | solution.py:432
  69.5 5.7 %collective-permute-start.25 = (bf16[192,128]{1,0:T(8,128)(2,1)S(1)}, bf16[192,128]{1,0:T(8,128)(2,1)S(1)}, u32[]{:S(2)}, u32[]{:S(2)}) collective-permute-start(bf16[192,128]{1,0:T(8,128)(2,1)S(1)} %get-tuple-element.83), channel_id=1, source_target_pairs={{0,6},{2,4},{4,2},{6,0},{8,14},{10,12},{12,10},{14,8},{16,22},{18,... | collective-permute-start | bytes 147464 | tf_op jit(solution)/shard_map/ppermute | solution.py:432
  76.4 11.4 %collective-permute-start.29 = (bf16[192,1024]{1,0:T(8,128)(2,1)S(1)}, bf16[192,1024]{1,0:T(8,128)(2,1)S(1)}, u32[]{:S(2)}, u32[]{:S(2)}) collective-permute-start(bf16[192,1024]{1,0:T(8,128)(2,1)S(1)} %shard_map.111), channel_id=1, source_target_pairs={{0,1},{1,0},{2,3},{3,2},{4,5},{5,4},{6,7},{7,6},{8,9},{9,8},{10,11... | collective-permute-start | bytes 1179656 | tf_op jit(solution)/shard_map/ppermute | solution.py:588
  78.0 1.9 %collective-permute-start.26 = (bf16[192,128]{1,0:T(8,128)(2,1)S(1)}, bf16[192,128]{1,0:T(8,128)(2,1)S(1)}, u32[]{:S(2)}, u32[]{:S(2)}) collective-permute-start(bf16[192,128]{1,0:T(8,128)(2,1)S(1)} %get-tuple-element.85), channel_id=1, source_target_pairs={{0,2},{2,0},{4,6},{6,4},{8,10},{10,8},{12,14},{14,12},{16,18},{18,... | collective-permute-start | bytes 147464 | tf_op jit(solution)/shard_map/ppermute | solution.py:432
  78.0 4.1 %collective-permute-start.27 = (bf16[192,128]{1,0:T(8,128)(2,1)S(1)}, bf16[192,128]{1,0:T(8,128)(2,1)S(1)}, u32[]{:S(2)}, u32[]{:S(2)}) collective-permute-start(bf16[192,128]{1,0:T(8,128)(2,1)S(1)} %get-tuple-element.86), channel_id=1, source_target_pairs={{0,4},{2,6},{4,0},{6,2},{8,12},{10,14},{12,8},{14,10},{16,20},{18,... | collective-permute-start | bytes 147464 | tf_op jit(solution)/shard_map/ppermute | solution.py:432
  79.3 3.8 %collective-permute-start.28 = (bf16[192,128]{1,0:T(8,128)(2,1)S(1)}, bf16[192,128]{1,0:T(8,128)(2,1)S(1)}, u32[]{:S(2)}, u32[]{:S(2)}) collective-permute-start(bf16[192,128]{1,0:T(8,128)(2,1)S(1)} %get-tuple-element.87), channel_id=1, source_target_pairs={{0,6},{2,4},{4,2},{6,0},{8,14},{10,12},{12,10},{14,8},{16,22},{18,... | collective-permute-start | bytes 147464 | tf_op jit(solution)/shard_map/ppermute | solution.py:432

commit v4 on v3

--- a/solution.py
+++ b/solution.py
@@ -18,6 +18,7 @@
 F32 = jnp.float32
 BF16 = jnp.bfloat16
 MIB = 1024 * 1024
+PACK_MIB = 62
 
 
 def vmem():
@@ -65,6 +66,18 @@
     if x.shape[1] == LANES:
         return x
     return jnp.concatenate([x, jnp.zeros((x.shape[0], LANES - x.shape[1]), x.dtype)], axis=1)
+
+
+def send_pieces(outs, stage):
+    me = lax.axis_index("var") % GROUP
+    for distance, out in enumerate(outs):
+        out[...] = stage[me ^ distance]
+
+
+def stage_pieces(stage, pieces):
+    me = lax.axis_index("var") % GROUP
+    for distance, piece in enumerate(pieces):
+        stage[me ^ distance] = piece[...]
 
 
 def load_all(pairs, sems):
@@ -76,55 +89,41 @@
             copies.append(pltpu.make_async_copy(source.at[at], target.at[at], sems.at[i, part]))
     for copy in copies:
         copy.start()
-    for copy in copies:
-        copy.wait()
-
-
-def send_pieces(outs, stage):
-    me = lax.axis_index("var") % GROUP
-    for distance, out in enumerate(outs):
-        out[...] = stage[me ^ distance]
-
-
-def stage_pieces(stage, pieces):
-    me = lax.axis_index("var") % GROUP
-    for distance, piece in enumerate(pieces):
-        stage[me ^ distance] = piece[...]
-
-
-def pack_kernel(x_hbm, *rest):
-    outs, (x_ref, turned, sems) = rest[:GROUP], rest[GROUP:]
-    load_all([(x_hbm, x_ref)], sems)
-    rows, features = x_ref.shape
+    return [copies[i * LOADS : (i + 1) * LOADS] for i in range(len(pairs))]
+
+
+def reorder_into(staged, half, ref, scale=None):
+    rows, features = ref.shape
     width = features // GROUP
     order = reorder_matrix(False)
     for b in range(rows // BLOCK):
         at = slice(b * BLOCK, (b + 1) * BLOCK)
-        moved = dot(order, x_ref[at]).astype(BF16)
+        moved = dot(order, ref[at])
+        if scale is not None:
+            moved = moved * scale
+        moved = moved.astype(BF16)
         for member in range(GROUP):
-            turned[member, at] = widen(moved[:, member * width : (member + 1) * width])
+            staged[member, at, half * LANES : (half + 1) * LANES] = widen(
+                moved[:, member * width : (member + 1) * width]
+            )
+
+
+def pack_kv_kernel(k_hbm, v_hbm, *rest):
+    outs, (k_ref, v_ref, turned, sems) = rest[:GROUP], rest[GROUP:]
+    arrivals = load_all([(k_hbm, k_ref), (v_hbm, v_ref)], sems)
+    for half, ref in enumerate((k_ref, v_ref)):
+        for copy in arrivals[half]:
+            copy.wait()
+        reorder_into(turned, half, ref)
     send_pieces(outs, turned)
 
 
-def pack_qo_kernel(slots, head_dim, q_hbm, g_hbm, lse_ref, *rest):
-    outs, (q_ref, g_ref, qo_ref, sems) = rest[:GROUP], rest[GROUP:]
-    load_all([(q_hbm, q_ref), (g_hbm, g_ref)], sems)
-    rows, features = q_ref.shape
-    width = features // GROUP
+def pack_qo_kernel(slots, head_dim, q_ref, g_ref, lse_ref, after_ref, *rest):
+    outs, qo_ref = rest[:GROUP], rest[GROUP]
+    rows = q_ref.shape[0]
     blocks = rows // BLOCK
-    order = reorder_matrix(False)
-    scale = head_dim ** (-0.5)
-    for b in range(blocks):
-        at = slice(b * BLOCK, (b + 1) * BLOCK)
-        for half, ref in enumerate((q_ref, g_ref)):
-            moved = dot(order, ref[at])
-            if half == 0:
-                moved = moved * scale
-            moved = moved.astype(BF16)
-            for member in range(GROUP):
-                qo_ref[member, at, half * LANES : (half + 1) * LANES] = widen(
-                    moved[:, member * width : (member + 1) * width]
-                )
+    reorder_into(qo_ref, 0, q_ref, head_dim ** (-0.5))
+    reorder_into(qo_ref, 1, g_ref)
     token = lax.broadcasted_iota(jnp.int32, (BLOCK, 2 * LANES), 0)
     lane = lax.broadcasted_iota(jnp.int32, (BLOCK, 2 * LANES), 1)
     place = ((lane >> 7) << 6) + (lane & (HALF - 1))
@@ -147,21 +146,29 @@
     send_pieces(outs, qo_ref)
 
 
+def below_first():
+    me = lax.axis_index("var")
+    return (me // GROUP + me) % 2
+
+
 def exchange_start(group_blocks):
-    odd = (lax.axis_index("var") // GROUP) % 2
+    odd = below_first()
     reach = group_blocks - SPAN
     return (1 - odd) * reach, odd * reach
 
 
-def line_kernel(*refs):
-    pieces, (own, first_out, second_out) = refs[:GROUP], refs[GROUP:]
-    blocks = pieces[0].shape[0] // BLOCK
+def line_kernel(carried, *refs):
+    pieces, refs = refs[:GROUP], refs[GROUP + carried :]
+    own, first_out, second_out = refs[:3]
+    rows = pieces[0].shape[0]
+    blocks = rows // BLOCK
     me = lax.axis_index("var") % GROUP
-    for distance, piece in enumerate(pieces):
-        own[pl.ds((me ^ distance) * blocks, blocks)] = piece[...].reshape(blocks, BLOCK, LANES)
+    for distance in range(GROUP):
+        at = pl.ds(pl.multiple_of((me ^ distance) * rows, rows), rows)
+        own[at] = pieces[distance][...]
     first, second = exchange_start(GROUP * blocks)
-    first_out[...] = own[pl.ds(first, SPAN)]
-    second_out[...] = own[pl.ds(second, SPAN)]
+    for start, out in ((first, first_out), (second, second_out)):
+        out[...] = own[pl.ds(pl.multiple_of(start * BLOCK, BLOCK), SPAN * BLOCK)]
 
 
 def attend_kernel(
@@ -170,7 +177,7 @@
     kb_ref,
     *refs,
 ):
-    key_refs, value_refs, refs = refs[:3], refs[3:6], refs[6:]
+    kv_refs, refs = refs[:3], refs[3:]
     qo_pieces, refs = refs[:GROUP], refs[GROUP:]
     key_outs, value_outs, refs = refs[:3], refs[3:6], refs[6:]
     dq_outs, refs = refs[:GROUP], refs[GROUP:]
@@ -181,16 +188,16 @@
     slot_count = kb_ref.shape[1]
     scale = head_dim ** (-0.5)
     base = (lax.axis_index("var") // GROUP) * group_blocks
-    odd = (lax.axis_index("var") // GROUP) % 2
+    odd = below_first()
     top = window - SPAN
     first_at, second_at = (1 - odd) * top, odd * top
     low = slice(0, LANES)
     high = slice(LANES, 2 * LANES)
 
-    for cols, (own_ref, first_ref, second_ref) in ((low, key_refs), (high, value_refs)):
-        kv_win[SPAN : SPAN + group_blocks, :, cols] = own_ref[...]
-        kv_win[pl.ds(first_at, SPAN), :, cols] = first_ref[...]
-        kv_win[pl.ds(second_at, SPAN), :, cols] = second_ref[...]
+    for ref, start, count in zip(
+        kv_refs, (SPAN, first_at, second_at), (group_blocks, SPAN, SPAN)
+    ):
+        kv_win[pl.ds(start, count)] = ref[...].reshape(count, BLOCK, 2 * LANES)
     stage_pieces(qo_ref, qo_pieces)
     key_patch = lax.broadcasted_iota(jnp.int32, (8, LANES), 0)
     query_patch = lax.broadcasted_iota(jnp.int32, (8, LANES), 1) & 7
@@ -431,17 +438,19 @@
     def trade(x, distance):
         return lax.ppermute(x, "var", [(n, n ^ distance) for n in range(devices)])
 
-    def trade_first(x):
-        pairs = [(n, n ^ GROUP) for n in range(devices) if (n ^ GROUP) < devices]
-        return lax.ppermute(x, "var", pairs)
-
-    def trade_second(x):
+    def trade_level(x, turn):
         pairs = []
         for n in range(devices):
-            other = n + GROUP if (n // GROUP) % 2 else n - GROUP
+            other = n - GROUP if (n // GROUP + n + turn) % 2 else n + GROUP
             if 0 <= other < devices:
                 pairs.append((n, other))
         return lax.ppermute(x, "var", pairs)
+
+    def trade_first(x):
+        return trade_level(x, 0)
+
+    def trade_second(x):
+        return trade_level(x, 1)
 
     def swap(pieces):
         got = [pieces[0]] + [None] * (GROUP - 1)
@@ -452,58 +461,56 @@
     def staged(count, width=LANES):
         return pltpu.VMEM((GROUP, count, width), BF16)
 
-    loaded = pltpu.VMEM((rows, features), BF16)
     block = (BLOCK, LANES)
-
-    def pack(x):
-        return pl.pallas_call(
-            pack_kernel,
-            out_shape=(shaped((rows, LANES)),) * GROUP,
-            in_specs=[hbm],
-            out_specs=(vmem(),) * GROUP,
-            scratch_shapes=[loaded, staged(rows), pltpu.SemaphoreType.DMA((1, LOADS))],
-            compiler_params=params(8),
-        )(x)
-
-    def line_up(pieces):
-        return pl.pallas_call(
-            line_kernel,
-            out_shape=(shaped((group_blocks,) + block),) + (shaped((SPAN,) + block),) * 2,
-            in_specs=[vmem()] * GROUP,
-            out_specs=(vmem(),) * 3,
-            compiler_params=params(8),
-        )(*pieces)
-
-    key_pieces = swap(pack(keys))
-    value_pieces = swap(pack(values))
-    own_keys, first_keys, second_keys = line_up(key_pieces)
-    first_keys = trade_first(first_keys)
-    second_keys = trade_second(second_keys)
-    own_values, first_values, second_values = line_up(value_pieces)
-    first_values = trade_first(first_values)
-    second_values = trade_second(second_values)
-    qos = swap(
-        pl.pallas_call(
-            functools.partial(pack_qo_kernel, slots, head_dim),
-            out_shape=(shaped((rows + LSE_ROWS, wide)),) * GROUP,
-            in_specs=[hbm, hbm, vmem()],
-            out_specs=(vmem(),) * GROUP,
-            scratch_shapes=[
-                loaded,
-                loaded,
-                staged(rows + LSE_ROWS, wide),
-                pltpu.SemaphoreType.DMA((2, LOADS)),
-            ],
-            compiler_params=params(8),
-        )(queries, out_grad, log_sum_exp)
-    )
+    anywhere = pl.BlockSpec(memory_space=pl.ANY)
+
+    def cost(flops, moved):
+        return pl.CostEstimate(flops=flops, bytes_accessed=moved, transcendentals=0)
+
+    size = rows * features * 2
+
+    kvs = pl.pallas_call(
+        pack_kv_kernel,
+        out_shape=(shaped((rows, wide)),) * GROUP,
+        in_specs=[hbm] * 2,
+        out_specs=(vmem(),) * GROUP,
+        scratch_shapes=[pltpu.VMEM((rows, features), BF16)] * 2
+        + [staged(rows, wide), pltpu.SemaphoreType.DMA((2, LOADS))],
+        compiler_params=params(PACK_MIB),
+        cost_estimate=cost(4 * rows * features * BLOCK, 5 * size),
+    )(keys, values)
+    kvs = swap(kvs)
+    qos = pl.pallas_call(
+        functools.partial(pack_qo_kernel, slots, head_dim),
+        out_shape=(shaped((rows + LSE_ROWS, wide)),) * GROUP,
+        in_specs=[vmem()] * 3 + [anywhere],
+        out_specs=(vmem(),) * GROUP,
+        scratch_shapes=[staged(rows + LSE_ROWS, wide)],
+        compiler_params=params(8),
+        cost_estimate=cost(4 * rows * features * BLOCK, 10 * size),
+    )(queries, out_grad, log_sum_exp, kvs[1])
+    carried = tuple(qos[1:])
+    own, first, second, *carried = pl.pallas_call(
+        functools.partial(line_kernel, len(carried)),
+        out_shape=(shaped((GROUP * rows, wide)),)
+        + (shaped((SPAN * BLOCK, wide)),) * 2
+        + tuple(shaped(x.shape) for x in carried),
+        in_specs=[vmem()] * GROUP + [anywhere] * len(carried),
+        out_specs=(vmem(),) * 3 + (anywhere,) * len(carried),
+        input_output_aliases={GROUP + i: 3 + i for i in range(len(carried))},
+        compiler_params=params(8),
+        cost_estimate=cost(0, 5 * size),
+    )(*kvs, *carried)
+    first = trade_first(first)
+    second = trade_second(second)
+    qos = swap([qos[0], *carried])
 
     pairs = group_blocks * slot_count * BLOCK * BLOCK * slots
     sums = (shaped((group_blocks,) + block, F32),) + (shaped((SPAN,) + block),) * 2
     results = pl.pallas_call(
         functools.partial(attend_kernel, blocks_here, head_dim),
         out_shape=sums + sums + (shaped((rows, LANES)),) * GROUP,
-        in_specs=[pl.BlockSpec(memory_space=pltpu.SMEM)] + [vmem()] * (6 + GROUP),
+        in_specs=[pl.BlockSpec(memory_space=pltpu.SMEM)] + [vmem()] * (3 + GROUP),
         out_specs=(vmem(),) * (6 + GROUP),
         scratch_shapes=[
             pltpu.VMEM((window, BLOCK, wide), BF16),
@@ -524,12 +531,9 @@
         ),
     )(
         key_blocks,
-        own_keys,
-        first_keys,
-        second_keys,
-        own_values,
-        first_values,
-        second_values,
+        own,
+        first,
+        second,
         *qos,
     )
     key_sum, first_part, second_part = results[:3]
@@ -548,6 +552,7 @@
             out_specs=(vmem(),) * GROUP,
             scratch_shapes=summing,
             compiler_params=params(8),
+            cost_estimate=cost(0, 4 * size),
         )(key_sum, first_back, second_back)
     )
     split = pl.pallas_call(
@@ -557,6 +562,7 @@
         out_specs=(vmem(),) * (2 * GROUP),
         scratch_shapes=summing,
         compiler_params=params(8),
+        cost_estimate=cost(0, 4 * size),
     )(value_sum, first_value_back, second_value_back)
     aways = swap(split[:GROUP])
     homes = swap(split[GROUP:])

time: 89.6 us -> 90 us (level)
  starting transfers between devices: 32 us -> 33.4 us
  waiting for transfers between devices: 27.6 us -> 28.9 us
    ppermute x21 -> x18, waiting for transfers between devices: 18.8 us -> 23.9 us  [trade(): return lax.ppermute(x, 'var', [(n, n ^ distance) for n in range(devices)])]
    ppermute x8 -> x6, waiting for transfers between devices: 6.03 us -> 2.3 us  [trade_level(): return lax.ppermute(x, 'var', pairs)]
    pallas_call x1, Pallas kernels: 2.2 us -> 0.48 us  [body(): pl.pallas_call(functools.partial(pack_qo_kernel, slots, head_dim), out_sh...]
    ppermute x21 -> x18, starting transfers between devices: 15.9 us -> 17.4 us  [trade(): return lax.ppermute(x, 'var', [(n, n ^ distance) for n in range(devices)])]
    pallas_call x4 -> x2, Pallas kernels: 1.71 us -> 2.61 us  [the longest x1 2.47 us: body(): pl.pallas_call(pack_kv_kernel, out_shape=(shaped((rows, wide)),) * GROUP,...]
    unnamed x13 -> x17, local copies, waits for them, and re-layouts: 5.46 us -> 4.65 us
    ppermute x8 -> x6, starting transfers between devices: 14.5 us -> 14.5 us  [trade_level(): return lax.ppermute(x, 'var', pairs)]
  transfers between devices with their start and end apart: 30 -> 25, of which waited for: 10 -> 10; matrix products, arithmetic and copies ran while one was open for 1% -> 0% of each run, Pallas kernels for 5% -> 3%
where the time goes in v4:
time: 90 us; the launch traced here: 89.6 us
  starting transfers between devices  33.4 us (37%)
  waiting for transfers between devices  28.9 us (32%)
  Pallas kernels  21 us (23%)
  local copies, waits for them, and re-layouts  4.65 us (5%)
    ppermute x18, waiting for transfers between devices, trade(): return lax.ppermute(x, 'var', [(n, n ^ distance) for n in range(devices)])  23.9 us
    ppermute x18, starting transfers between devices, trade(): return lax.ppermute(x, 'var', [(n, n ^ distance) for n in range(devices)])  17.4 us
    ppermute x6, starting transfers between devices, trade_level(): return lax.ppermute(x, 'var', pairs)  14.5 us
    pallas_call x1, Pallas kernels, body(): pl.pallas_call(functools.partial(attend_kernel, blocks_here, head_dim), o...  14.4 us
    unnamed x17, local copies, waits for them, and re-layouts  4.65 us
    ppermute x1, waiting for transfers between devices, body(): lax.ppermute(send, 'head', [(n, (n + piece + 1) % heads) for n in range(h...  2.66 us
    pallas_call x1, Pallas kernels, body(): pl.pallas_call(pack_kv_kernel, out_shape=(shaped((rows, wide)),) * GROUP,...  2.47 us
    ppermute x6, waiting for transfers between devices, trade_level(): return lax.ppermute(x, 'var', pairs)  2.3 us
  transfers between devices with their start and end apart: 25, of which 10 were waited for; matrix products, arithmetic and copies ran while one was open for 0% of the time, Pallas kernels for 3%

profile of v4, /device:TPU:0, one launch (start us, length us, event | category | flops | bytes accessed | tf_op | source)
XLA Modules:
  0.0 89.6 jit_solution(14440989290666317454)
XLA Ops:
  0.6 2.5 %shard_map.102 = (bf16[384,256]{1,0:T(8,128)(2,1)}, bf16[384,256]{1,0:T(8,128)(2,1)}, bf16[384,256]{1,0:T(8,128)(2,1)}, bf16[384,256]{1,0:T(8,128)(2,1)}) custom-call(bf16[384,512]{1,0:T(8,128)(2,1)} %k_hbm.1, bf16[384,512]{1,0:T(8,128)(2,1)} %v_hbm.1), custom_call_target="tpu_custom_call" | custom-call | flops 100663296 | bytes 1966080 | tf_op jit(solution)/shard_map/pallas_call | solution.py:472
  3.1 0.5 collective-permute-start
  3.6 2.6 %collective-permute-start.1 = (bf16[384,256]{1,0:T(8,128)(2,1)}, bf16[384,256]{1,0:T(8,128)(2,1)S(1)}, u32[]{:S(2)}, u32[]{:S(2)}) collective-permute-start(bf16[384,256]{1,0:T(8,128)(2,1)} %get-tuple-element.46), channel_id=1, source_target_pairs={{0,4},{2,6},{4,0},{6,2},{8,12},{10,14},{12,8},{14,10},{16,20},{18,... | collective-permute-start | bytes 589832 | tf_op jit(solution)/shard_map/ppermute | solution.py:439
  6.2 0.1 collective-permute-start.2
  6.3 0.0 collective-permute-done.after_ref.refs_1_
  6.3 1.0 %copy-done.1 = bf16[384,512]{1,0:T(8,128)(2,1)S(1)} copy-done((bf16[384,512]{1,0:T(8,128)(2,1)S(1)}, bf16[384,512]{1,0:T(8,128)(2,1)}, u32[]{:S(2)}) %copy-start.1) | copy-done | bytes 393240
  7.3 1.0 %copy-done.2 = bf16[384,512]{1,0:T(8,128)(2,1)S(1)} copy-done((bf16[384,512]{1,0:T(8,128)(2,1)S(1)}, bf16[384,512]{1,0:T(8,128)(2,1)}, u32[]{:S(2)}) %copy-start.2) | copy-done | bytes 393240
  8.3 0.7 copy-done.4
  9.0 0.5 shard_map.103
  9.5 0.0 copy-start.5
  9.5 2.7 %collective-permute-done.1.refs_2_ = bf16[384,256]{1,0:T(8,128)(2,1)S(1)} collective-permute-done((bf16[384,256]{1,0:T(8,128)(2,1)}, bf16[384,256]{1,0:T(8,128)(2,1)S(1)}, u32[]{:S(2)}, u32[]{:S(2)}) %collective-permute-start.1) | collective-permute-done | bytes 196640 | tf_op jit(solution)/shard_map/ppermute | solution.py:439
  12.2 3.7 %collective-permute-done.2.refs_3_ = bf16[384,256]{1,0:T(8,128)(2,1)S(1)} collective-permute-done((bf16[384,256]{1,0:T(8,128)(2,1)}, bf16[384,256]{1,0:T(8,128)(2,1)S(1)}, u32[]{:S(2)}, u32[]{:S(2)}) %collective-permute-start.2) | collective-permute-done | bytes 196640 | tf_op jit(solution)/shard_map/ppermute | solution.py:439
  15.9 0.9 %copy-done.3 = bf16[384,256]{1,0:T(8,128)(2,1)S(1)} copy-done((bf16[384,256]{1,0:T(8,128)(2,1)S(1)}, bf16[384,256]{1,0:T(8,128)(2,1)}, u32[]{:S(2)}) %copy-start.3) | copy-done | bytes 196632
  16.8 0.1 shard_map.104
  17.0 3.5 %collective-permute-start.3 = (bf16[1024,256]{1,0:T(8,128)(2,1)S(1)}, bf16[1024,256]{1,0:T(8,128)(2,1)S(1)}, u32[]{:S(2)}, u32[]{:S(2)}) collective-permute-start(bf16[1024,256]{1,0:T(8,128)(2,1)S(1)} %get-tuple-element.52), channel_id=1, source_target_pairs={{0,8},{4,12},{8,0},{10,18},{12,4},{14,22},{16,24},{18,10},{20,28},... | collective-permute-start | bytes 1572872 | tf_op jit(solution)/shard_map/ppermute | solution.py:447
  20.5 0.7 collective-permute-start.4
  21.2 2.6 %collective-permute-start.5 = (bf16[400,256]{1,0:T(8,128)(2,1)S(1)}, bf16[400,256]{1,0:T(8,128)(2,1)}, u32[]{:S(2)}, u32[]{:S(2)}) collective-permute-start(bf16[400,256]{1,0:T(8,128)(2,1)S(1)} %get-tuple-element.55), channel_id=1, source_target_pairs={{0,2},{2,0},{4,6},{6,4},{8,10},{10,8},{12,14},{14,12},{16,18},{18,... | collective-permute-start | bytes 614408 | tf_op jit(solution)/shard_map/ppermute | solution.py:439
  23.8 1.5 %collective-permute-start.6 = (bf16[400,256]{1,0:T(8,128)(2,1)S(1)}, bf16[400,256]{1,0:T(8,128)(2,1)}, u32[]{:S(2)}, u32[]{:S(2)}) collective-permute-start(bf16[400,256]{1,0:T(8,128)(2,1)S(1)} %get-tuple-element.56), channel_id=1, source_target_pairs={{0,4},{2,6},{4,0},{6,2},{8,12},{10,14},{12,8},{14,10},{16,20},{18,... | collective-permute-start | bytes 614408 | tf_op jit(solution)/shard_map/ppermute | solution.py:439
  25.3 0.0 collective-permute-start.7
  25.3 0.1 copy.14.kb_ref
  25.4 0.0 collective-permute-done.5.refs_4_
  25.4 6.4 %collective-permute-done.6.refs_5_ = bf16[400,256]{1,0:T(8,128)(2,1)} collective-permute-done((bf16[400,256]{1,0:T(8,128)(2,1)S(1)}, bf16[400,256]{1,0:T(8,128)(2,1)}, u32[]{:S(2)}, u32[]{:S(2)}) %collective-permute-start.6) | collective-permute-done | bytes 204832 | tf_op jit(solution)/shard_map/ppermute | solution.py:439
  31.8 2.6 %collective-permute-done.7.refs_6_ = bf16[400,256]{1,0:T(8,128)(2,1)} collective-permute-done((bf16[400,256]{1,0:T(8,128)(2,1)S(1)}, bf16[400,256]{1,0:T(8,128)(2,1)}, u32[]{:S(2)}, u32[]{:S(2)}) %collective-permute-start.7) | collective-permute-done | bytes 204832 | tf_op jit(solution)/shard_map/ppermute | solution.py:439
  34.5 0.0 collective-permute-done.3.refs_1_
  34.5 0.0 collective-permute-done.4.refs_2_
  34.5 0.9 %copy-done.6 = bf16[400,256]{1,0:T(8,128)(2,1)S(1)} copy-done((bf16[400,256]{1,0:T(8,128)(2,1)S(1)}, bf16[400,256]{1,0:T(8,128)(2,1)}, u32[]{:S(2)}) %copy-start.6) | copy-done | bytes 204824
  35.4 14.4 %shard_map.105 = (f32[12,128,128]{2,1,0:T(8,128)S(1)}, bf16[8,128,128]{2,1,0:T(8,128)(2,1)S(1)}, bf16[8,128,128]{2,1,0:T(8,128)(2,1)S(1)}, f32[12,128,128]{2,1,0...) custom-call(s32[48,8]{1,0:T(8,128)S(1)} %copy.14.kb_ref, ...), custom_call_target="tpu_custom_call" | custom-call | flops 8053063680 | bytes 2000000 | tf_op jit(solution)/shard_map/pallas_call | solution.py:510
  49.8 4.6 %collective-permute-start.11 = (bf16[8,128,128]{2,1,0:T(8,128)(2,1)S(1)}, bf16[8,128,128]{2,1,0:T(8,128)(2,1)S(1)}, u32[]{:S(2)}, u32[]{:S(2)}) collective-permute-start(bf16[8,128,128]{2,1,0:T(8,128)(2,1)S(1)} %get-tuple-element.63), channel_id=1, source_target_pairs={{0,8},{4,12},{8,0},{10,18},{12,4},{14,22},{16,24},{18,10},{20,28},... | collective-permute-start | bytes 786440 | tf_op jit(solution)/shard_map/ppermute | solution.py:447
  54.4 0.7 collective-permute-start.12
  55.1 4.3 %collective-permute-start.16 = (bf16[8,128,128]{2,1,0:T(8,128)(2,1)S(1)}, bf16[8,128,128]{2,1,0:T(8,128)(2,1)S(1)}, u32[]{:S(2)}, u32[]{:S(2)}) collective-permute-start(bf16[8,128,128]{2,1,0:T(8,128)(2,1)S(1)} %get-tuple-element.70), channel_id=1, source_target_pairs={{0,8},{4,12},{8,0},{10,18},{12,4},{14,22},{16,24},{18,10},{20,28},... | collective-permute-start | bytes 786440 | tf_op jit(solution)/shard_map/ppermute | solution.py:447
  59.4 0.7 collective-permute-start.17
  60.1 1.6 %collective-permute-start.8 = (bf16[384,128]{1,0:T(8,128)(2,1)S(1)}, bf16[384,128]{1,0:T(8,128)(2,1)S(1)}, u32[]{:S(2)}, u32[]{:S(2)}) collective-permute-start(bf16[384,128]{1,0:T(8,128)(2,1)S(1)} %get-tuple-element.59), channel_id=1, source_target_pairs={{0,2},{2,0},{4,6},{6,4},{8,10},{10,8},{12,14},{14,12},{16,18},{18,... | collective-permute-start | bytes 294920 | tf_op jit(solution)/shard_map/ppermute | solution.py:439
  61.7 0.0 collective-permute-done.11.first_ref
  61.7 1.5 %collective-permute-start.9 = (bf16[384,128]{1,0:T(8,128)(2,1)S(1)}, bf16[384,128]{1,0:T(8,128)(2,1)S(1)}, u32[]{:S(2)}, u32[]{:S(2)}) collective-permute-start(bf16[384,128]{1,0:T(8,128)(2,1)S(1)} %get-tuple-element.60), channel_id=1, source_target_pairs={{0,4},{2,6},{4,0},{6,2},{8,12},{10,14},{12,8},{14,10},{16,20},{18,... | collective-permute-start | bytes 294920 | tf_op jit(solution)/shard_map/ppermute | solution.py:439
  63.2 0.0 collective-permute-done.12.second_ref
  63.2 0.1 collective-permute-start.10
  63.4 0.3 shard_map.106
  63.6 2.3 %collective-permute-done.16.first_ref = bf16[8,128,128]{2,1,0:T(8,128)(2,1)S(1)} collective-permute-done((bf16[8,128,128]{2,1,0:T(8,128)(2,1)S(1)}, bf16[8,128,128]{2,1,0:T(8,128)(2,1)S(1)}, u32[]{:S(2)}, u32[]{:S(2)}) %collective-permute-start.16) | collective-permute-done | bytes 262176 | tf_op jit(solution)/shard_map/ppermute | solution.py:447
  65.9 0.0 collective-permute-start.13
  65.9 0.0 collective-permute-done.17.second_ref
  65.9 0.3 shard_map.107
  66.2 1.4 %collective-permute-start.18 = (bf16[192,128]{1,0:T(8,128)(2,1)S(1)}, bf16[192,128]{1,0:T(8,128)(2,1)S(1)}, u32[]{:S(2)}, u32[]{:S(2)}) collective-permute-start(bf16[192,128]{1,0:T(8,128)(2,1)S(1)} %get-tuple-element.73), channel_id=1, source_target_pairs={{0,2},{2,0},{4,6},{6,4},{8,10},{10,8},{12,14},{14,12},{16,18},{18,... | collective-permute-start | bytes 147464 | tf_op jit(solution)/shard_map/ppermute | solution.py:439
  67.6 0.0 collective-permute-done.8.refs_1_
  67.6 1.5 %collective-permute-start.14 = (bf16[384,128]{1,0:T(8,128)(2,1)S(1)}, bf16[384,128]{1,0:T(8,128)(2,1)S(1)}, u32[]{:S(2)}, u32[]{:S(2)}) collective-permute-start(bf16[384,128]{1,0:T(8,128)(2,1)S(1)} %get-tuple-element.67), channel_id=1, source_target_pairs={{0,4},{2,6},{4,0},{6,2},{8,12},{10,14},{12,8},{14,10},{16,20},{18,... | collective-permute-start | bytes 294920 | tf_op jit(solution)/shard_map/ppermute | solution.py:439
  69.1 0.0 collective-permute-done.9.refs_2_
  69.1 0.0 collective-permute-start.15
  69.1 0.0 collective-permute-done.10.refs_3_
  69.1 1.4 %collective-permute-start.19 = (bf16[192,128]{1,0:T(8,128)(2,1)S(1)}, bf16[192,128]{1,0:T(8,128)(2,1)S(1)}, u32[]{:S(2)}, u32[]{:S(2)}) collective-permute-start(bf16[192,128]{1,0:T(8,128)(2,1)S(1)} %get-tuple-element.74), channel_id=1, source_target_pairs={{0,4},{2,6},{4,0},{6,2},{8,12},{10,14},{12,8},{14,10},{16,20},{18,... | collective-permute-start | bytes 147464 | tf_op jit(solution)/shard_map/ppermute | solution.py:439
  70.6 0.0 collective-permute-done.18.refs_9_
  70.6 0.5 collective-permute-start.20
  71.1 4.7 %collective-permute-done.19.refs_10_ = bf16[192,128]{1,0:T(8,128)(2,1)S(1)} collective-permute-done((bf16[192,128]{1,0:T(8,128)(2,1)S(1)}, bf16[192,128]{1,0:T(8,128)(2,1)S(1)}, u32[]{:S(2)}, u32[]{:S(2)}) %collective-permute-start.19) | collective-permute-done | bytes 49184 | tf_op jit(solution)/shard_map/ppermute | solution.py:439
  75.8 0.5 collective-permute-done.20.refs_11_
  76.3 0.0 collective-permute-done.13.refs_5_
  76.3 0.0 collective-permute-done.14.refs_6_
  76.3 1.2 %shard_map.109 = bf16[192,1024]{1,0:T(8,128)(2,1)S(1)} custom-call(bf16[384,128]{1,0:T(8,128)(2,1)S(1)} %get-tuple-element.58.refs_0_, bf16[384,128]{1,0:T(8,128)(2,1)S(1)} %collective-permute-done.8.refs_1_, bf16[384,128]{1,0:T(8,128)(2,1)S(1)} %collective-permute-done.9.refs_2_, bf16[384,128]{1,0:T(8,128)(2,1)S(1)} %collective-permute-done.10.refs_3_, ...), custom_call_target="tpu_custom_call" | custom-call | flops 603979776 | bytes 4000000 | tf_op jit(solution)/shard_map/pallas_call | solution.py:571
  77.5 1.6 %collective-permute-start.24 = (bf16[192,1024]{1,0:T(8,128)(2,1)S(1)}, bf16[192,1024]{1,0:T(8,128)(2,1)S(1)}, u32[]{:S(2)}, u32[]{:S(2)}) collective-permute-start(bf16[192,1024]{1,0:T(8,128)(2,1)S(1)} %shard_map.109), channel_id=1, source_target_pairs={{0,1},{1,0},{2,3},{3,2},{4,5},{5,4},{6,7},{7,6},{8,9},{9,8},{10,11... | collective-permute-start | bytes 1179656 | tf_op jit(solution)/shard_map/ppermute | solution.py:594
  79.1 0.0 collective-permute-start.21
  79.1 1.3 %collective-permute-start.22 = (bf16[192,128]{1,0:T(8,128)(2,1)S(1)}, bf16[192,128]{1,0:T(8,128)(2,1)S(1)}, u32[]{:S(2)}, u32[]{:S(2)}) collective-permute-start(bf16[192,128]{1,0:T(8,128)(2,1)S(1)} %get-tuple-element.78), channel_id=1, source_target_pairs={{0,4},{2,6},{4,0},{6,2},{8,12},{10,14},{12,8},{14,10},{16,20},{18,... | collective-permute-start | bytes 147464 | tf_op jit(solution)/shard_map/ppermute | solution.py:439
  80.4 0.5 collective-permute-start.23
  81.0 2.3 %collective-permute-done.22.refs_14_ = bf16[192,128]{1,0:T(8,128)(2,1)S(1)} collective-permute-done((bf16[192,128]{1,0:T(8,128)(2,1)S(1)}, bf16[192,128]{1,0:T(8,128)(2,1)S(1)}, u32[]{:S(2)}, u32[]{:S(2)}) %collective-permute-start.22) | collective-permute-done | bytes 49184 | tf_op jit(solution)/shard_map/ppermute | solution.py:439
  83.3 1.0 %collective-permute-done.23.refs_15_ = bf16[192,128]{1,0:T(8,128)(2,1)S(1)} collective-permute-done((bf16[192,128]{1,0:T(8,128)(2,1)S(1)}, bf16[192,128]{1,0:T(8,128)(2,1)S(1)}, u32[]{:S(2)}, u32[]{:S(2)}) %collective-permute-start.23) | collective-permute-done | bytes 49184 | tf_op jit(solution)/shard_map/ppermute | solution.py:439
  84.2 1.9 %shard_map.108 = (bf16[384,512]{1,0:T(8,128)(2,1)}, bf16[384,512]{1,0:T(8,128)(2,1)}, bf16[384,512]{1,0:T(8,128)(2,1)}, f32[192,1024]{1,0:T(8,128)S(1)}) custom-call(bf16[384,128]{1,0:T(8,128)(2,1)S(1)} %get-tuple-element.58.refs_0_, bf16[384,128]{1,0:T(8,128)(2,1)S(1)} %collective-permute-done.8.refs_1_, ...), custom_call_target="tpu_custom_call" | custom-call | flops 603979776 | bytes 6000000 | tf_op jit(solution)/shard_map/pallas_call | solution.py:582
  86.1 2.7 %collective-permute-done.24 = bf16[192,1024]{1,0:T(8,128)(2,1)S(1)} collective-permute-done((bf16[192,1024]{1,0:T(8,128)(2,1)S(1)}, bf16[192,1024]{1,0:T(8,128)(2,1)S(1)}, u32[]{:S(2)}, u32[]{:S(2)}) %collective-permute-start.24) | collective-permute-done | bytes 393248 | tf_op jit(solution)/shard_map/ppermute | solution.py:594
  88.7 0.8 add_convert_fusion
  (12 shorter events, 0.0 us)
Async XLA Ops:
  0.6 24.7 %copy-start.7 = (s32[48,8]{0,1:T(8,128)S(1)}, s32[48,8]{0,1:T(8,128)}, u32[]{:S(2)}) copy-start(s32[48,8]{0,1:T(8,128)} %param.12) | copy-start | bytes 4612
  3.1 3.2 %collective-permute-start = (bf16[384,256]{1,0:T(8,128)(2,1)}, bf16[384,256]{1,0:T(8,128)(2,1)S(1)}, u32[]{:S(2)}, u32[]{:S(2)}) collective-permute-start(bf16[384,256]{1,0:T(8,128)(2,1)} %get-tuple-element.45), channel_id=1, source_target_pairs={{0,2},{2,0},{4,6},{6,4},{8,10},{10,8},{12,14},{14,12},{16,18},{18,... | collective-permute-start | bytes 589832 | tf_op jit(solution)/shard_map/ppermute | solution.py:439
  3.6 8.6 %collective-permute-start.1 = (bf16[384,256]{1,0:T(8,128)(2,1)}, bf16[384,256]{1,0:T(8,128)(2,1)S(1)}, u32[]{:S(2)}, u32[]{:S(2)}) collective-permute-start(bf16[384,256]{1,0:T(8,128)(2,1)} %get-tuple-element.46), channel_id=1, source_target_pairs={{0,4},{2,6},{4,0},{6,2},{8,12},{10,14},{12,8},{14,10},{16,20},{18,... | collective-permute-start | bytes 589832 | tf_op jit(solution)/shard_map/ppermute | solution.py:439
  6.2 9.7 %collective-permute-start.2 = (bf16[384,256]{1,0:T(8,128)(2,1)}, bf16[384,256]{1,0:T(8,128)(2,1)S(1)}, u32[]{:S(2)}, u32[]{:S(2)}) collective-permute-start(bf16[384,256]{1,0:T(8,128)(2,1)} %get-tuple-element.47), channel_id=1, source_target_pairs={{0,6},{2,4},{4,2},{6,0},{8,14},{10,12},{12,10},{14,8},{16,22},{18,... | collective-permute-start | bytes 589832 | tf_op jit(solution)/shard_map/ppermute | solution.py:439
  6.3 1.0 %copy-start.1 = (bf16[384,512]{1,0:T(8,128)(2,1)S(1)}, bf16[384,512]{1,0:T(8,128)(2,1)}, u32[]{:S(2)}) copy-start(bf16[384,512]{1,0:T(8,128)(2,1)} %q_ref.1) | copy-start | bytes 1179652
  7.3 1.0 %copy-start.2 = (bf16[384,512]{1,0:T(8,128)(2,1)S(1)}, bf16[384,512]{1,0:T(8,128)(2,1)}, u32[]{:S(2)}) copy-start(bf16[384,512]{1,0:T(8,128)(2,1)} %g_ref.1) | copy-start | bytes 1179652
  8.3 0.7 copy-start.4
  9.5 15.8 %copy-start.5 = (bf16[400,256]{1,0:T(8,128)(2,1)}, bf16[400,256]{1,0:T(8,128)(2,1)S(1)}, u32[]{:S(2)}) copy-start(bf16[400,256]{1,0:T(8,128)(2,1)S(1)} %get-tuple-element.54.refs_3_) | copy-start | bytes 614404
  15.9 0.9 %copy-start.3 = (bf16[384,256]{1,0:T(8,128)(2,1)S(1)}, bf16[384,256]{1,0:T(8,128)(2,1)}, u32[]{:S(2)}) copy-start(bf16[384,256]{1,0:T(8,128)(2,1)} %get-tuple-element.44.refs_0_) | copy-start | bytes 589828
  17.0 17.5 %collective-permute-start.3 = (bf16[1024,256]{1,0:T(8,128)(2,1)S(1)}, bf16[1024,256]{1,0:T(8,128)(2,1)S(1)}, u32[]{:S(2)}, u32[]{:S(2)}) collective-permute-start(bf16[1024,256]{1,0:T(8,128)(2,1)S(1)} %get-tuple-element.52), channel_id=1, source_target_pairs={{0,8},{4,12},{8,0},{10,18},{12,4},{14,22},{16,24},{18,10},{20,28},... | collective-permute-start | bytes 1572872 | tf_op jit(solution)/shard_map/ppermute | solution.py:447
  20.5 14.0 %collective-permute-start.4 = (bf16[1024,256]{1,0:T(8,128)(2,1)S(1)}, bf16[1024,256]{1,0:T(8,128)(2,1)S(1)}, u32[]{:S(2)}, u32[]{:S(2)}) collective-permute-start(bf16[1024,256]{1,0:T(8,128)(2,1)S(1)} %get-tuple-element.53), channel_id=1, source_target_pairs={{2,10},{6,14},{8,16},{10,2},{12,20},{14,6},{16,8},{18,26},{20,12},... | collective-permute-start | bytes 1572872 | tf_op jit(solution)/shard_map/ppermute | solution.py:447
  21.2 4.2 %collective-permute-start.5 = (bf16[400,256]{1,0:T(8,128)(2,1)S(1)}, bf16[400,256]{1,0:T(8,128)(2,1)}, u32[]{:S(2)}, u32[]{:S(2)}) collective-permute-start(bf16[400,256]{1,0:T(8,128)(2,1)S(1)} %get-tuple-element.55), channel_id=1, source_target_pairs={{0,2},{2,0},{4,6},{6,4},{8,10},{10,8},{12,14},{14,12},{16,18},{18,... | collective-permute-start | bytes 614408 | tf_op jit(solution)/shard_map/ppermute | solution.py:439
  23.8 8.0 %collective-permute-start.6 = (bf16[400,256]{1,0:T(8,128)(2,1)S(1)}, bf16[400,256]{1,0:T(8,128)(2,1)}, u32[]{:S(2)}, u32[]{:S(2)}) collective-permute-start(bf16[400,256]{1,0:T(8,128)(2,1)S(1)} %get-tuple-element.56), channel_id=1, source_target_pairs={{0,4},{2,6},{4,0},{6,2},{8,12},{10,14},{12,8},{14,10},{16,20},{18,... | collective-permute-start | bytes 614408 | tf_op jit(solution)/shard_map/ppermute | solution.py:439
  25.3 9.1 %collective-permute-start.7 = (bf16[400,256]{1,0:T(8,128)(2,1)S(1)}, bf16[400,256]{1,0:T(8,128)(2,1)}, u32[]{:S(2)}, u32[]{:S(2)}) collective-permute-start(bf16[400,256]{1,0:T(8,128)(2,1)S(1)} %get-tuple-element.57), channel_id=1, source_target_pairs={{0,6},{2,4},{4,2},{6,0},{8,14},{10,12},{12,10},{14,8},{16,22},{18,... | collective-permute-start | bytes 614408 | tf_op jit(solution)/shard_map/ppermute | solution.py:439
  34.5 0.9 %copy-start.6 = (bf16[400,256]{1,0:T(8,128)(2,1)S(1)}, bf16[400,256]{1,0:T(8,128)(2,1)}, u32[]{:S(2)}) copy-start(bf16[400,256]{1,0:T(8,128)(2,1)} %copy-done.5) | copy-start | bytes 614404
  35.4 40.9 %copy-start = (bf16[3,1024,512]{2,1,0:T(8,128)(2,1)S(1)}, bf16[3,1024,512]{2,1,0:T(8,128)(2,1)}, u32[]{:S(2)}) copy-start(bf16[3,1024,512]{2,1,0:T(8,128)(2,1)} %refs_12_.1) | copy-start | bytes 9437188
  49.8 11.9 %collective-permute-start.11 = (bf16[8,128,128]{2,1,0:T(8,128)(2,1)S(1)}, bf16[8,128,128]{2,1,0:T(8,128)(2,1)S(1)}, u32[]{:S(2)}, u32[]{:S(2)}) collective-permute-start(bf16[8,128,128]{2,1,0:T(8,128)(2,1)S(1)} %get-tuple-element.63), channel_id=1, source_target_pairs={{0,8},{4,12},{8,0},{10,18},{12,4},{14,22},{16,24},{18,10},{20,28},... | collective-permute-start | bytes 786440 | tf_op jit(solution)/shard_map/ppermute | solution.py:447
  54.4 8.8 %collective-permute-start.12 = (bf16[8,128,128]{2,1,0:T(8,128)(2,1)S(1)}, bf16[8,128,128]{2,1,0:T(8,128)(2,1)S(1)}, u32[]{:S(2)}, u32[]{:S(2)}) collective-permute-start(bf16[8,128,128]{2,1,0:T(8,128)(2,1)S(1)} %get-tuple-element.64), channel_id=1, source_target_pairs={{2,10},{6,14},{8,16},{10,2},{12,20},{14,6},{16,8},{18,26},{20,12},... | collective-permute-start | bytes 786440 | tf_op jit(solution)/shard_map/ppermute | solution.py:447
  55.1 10.8 %collective-permute-start.16 = (bf16[8,128,128]{2,1,0:T(8,128)(2,1)S(1)}, bf16[8,128,128]{2,1,0:T(8,128)(2,1)S(1)}, u32[]{:S(2)}, u32[]{:S(2)}) collective-permute-start(bf16[8,128,128]{2,1,0:T(8,128)(2,1)S(1)} %get-tuple-element.70), channel_id=1, source_target_pairs={{0,8},{4,12},{8,0},{10,18},{12,4},{14,22},{16,24},{18,10},{20,28},... | collective-permute-start | bytes 786440 | tf_op jit(solution)/shard_map/ppermute | solution.py:447
  59.4 6.5 %collective-permute-start.17 = (bf16[8,128,128]{2,1,0:T(8,128)(2,1)S(1)}, bf16[8,128,128]{2,1,0:T(8,128)(2,1)S(1)}, u32[]{:S(2)}, u32[]{:S(2)}) collective-permute-start(bf16[8,128,128]{2,1,0:T(8,128)(2,1)S(1)} %get-tuple-element.71), channel_id=1, source_target_pairs={{2,10},{6,14},{8,16},{10,2},{12,20},{14,6},{16,8},{18,26},{20,12},... | collective-permute-start | bytes 786440 | tf_op jit(solution)/shard_map/ppermute | solution.py:447
  60.1 7.6 %collective-permute-start.8 = (bf16[384,128]{1,0:T(8,128)(2,1)S(1)}, bf16[384,128]{1,0:T(8,128)(2,1)S(1)}, u32[]{:S(2)}, u32[]{:S(2)}) collective-permute-start(bf16[384,128]{1,0:T(8,128)(2,1)S(1)} %get-tuple-element.59), channel_id=1, source_target_pairs={{0,2},{2,0},{4,6},{6,4},{8,10},{10,8},{12,14},{14,12},{16,18},{18,... | collective-permute-start | bytes 294920 | tf_op jit(solution)/shard_map/ppermute | solution.py:439
  61.7 7.4 %collective-permute-start.9 = (bf16[384,128]{1,0:T(8,128)(2,1)S(1)}, bf16[384,128]{1,0:T(8,128)(2,1)S(1)}, u32[]{:S(2)}, u32[]{:S(2)}) collective-permute-start(bf16[384,128]{1,0:T(8,128)(2,1)S(1)} %get-tuple-element.60), channel_id=1, source_target_pairs={{0,4},{2,6},{4,0},{6,2},{8,12},{10,14},{12,8},{14,10},{16,20},{18,... | collective-permute-start | bytes 294920 | tf_op jit(solution)/shard_map/ppermute | solution.py:439
  63.2 5.9 %collective-permute-start.10 = (bf16[384,128]{1,0:T(8,128)(2,1)S(1)}, bf16[384,128]{1,0:T(8,128)(2,1)S(1)}, u32[]{:S(2)}, u32[]{:S(2)}) collective-permute-start(bf16[384,128]{1,0:T(8,128)(2,1)S(1)} %get-tuple-element.61), channel_id=1, source_target_pairs={{0,6},{2,4},{4,2},{6,0},{8,14},{10,12},{12,10},{14,8},{16,22},{18,... | collective-permute-start | bytes 294920 | tf_op jit(solution)/shard_map/ppermute | solution.py:439
  65.9 10.4 %collective-permute-start.13 = (bf16[384,128]{1,0:T(8,128)(2,1)S(1)}, bf16[384,128]{1,0:T(8,128)(2,1)S(1)}, u32[]{:S(2)}, u32[]{:S(2)}) collective-permute-start(bf16[384,128]{1,0:T(8,128)(2,1)S(1)} %get-tuple-element.66), channel_id=1, source_target_pairs={{0,2},{2,0},{4,6},{6,4},{8,10},{10,8},{12,14},{14,12},{16,18},{18,... | collective-permute-start | bytes 294920 | tf_op jit(solution)/shard_map/ppermute | solution.py:439
  66.2 4.4 %collective-permute-start.18 = (bf16[192,128]{1,0:T(8,128)(2,1)S(1)}, bf16[192,128]{1,0:T(8,128)(2,1)S(1)}, u32[]{:S(2)}, u32[]{:S(2)}) collective-permute-start(bf16[192,128]{1,0:T(8,128)(2,1)S(1)} %get-tuple-element.73), channel_id=1, source_target_pairs={{0,2},{2,0},{4,6},{6,4},{8,10},{10,8},{12,14},{14,12},{16,18},{18,... | collective-permute-start | bytes 147464 | tf_op jit(solution)/shard_map/ppermute | solution.py:439
  67.6 8.7 %collective-permute-start.14 = (bf16[384,128]{1,0:T(8,128)(2,1)S(1)}, bf16[384,128]{1,0:T(8,128)(2,1)S(1)}, u32[]{:S(2)}, u32[]{:S(2)}) collective-permute-start(bf16[384,128]{1,0:T(8,128)(2,1)S(1)} %get-tuple-element.67), channel_id=1, source_target_pairs={{0,4},{2,6},{4,0},{6,2},{8,12},{10,14},{12,8},{14,10},{16,20},{18,... | collective-permute-start | bytes 294920 | tf_op jit(solution)/shard_map/ppermute | solution.py:439
  69.1 7.2 %collective-permute-start.15 = (bf16[384,128]{1,0:T(8,128)(2,1)S(1)}, bf16[384,128]{1,0:T(8,128)(2,1)S(1)}, u32[]{:S(2)}, u32[]{:S(2)}) collective-permute-start(bf16[384,128]{1,0:T(8,128)(2,1)S(1)} %get-tuple-element.68), channel_id=1, source_target_pairs={{0,6},{2,4},{4,2},{6,0},{8,14},{10,12},{12,10},{14,8},{16,22},{18,... | collective-permute-start | bytes 294920 | tf_op jit(solution)/shard_map/ppermute | solution.py:439
  69.1 6.7 %collective-permute-start.19 = (bf16[192,128]{1,0:T(8,128)(2,1)S(1)}, bf16[192,128]{1,0:T(8,128)(2,1)S(1)}, u32[]{:S(2)}, u32[]{:S(2)}) collective-permute-start(bf16[192,128]{1,0:T(8,128)(2,1)S(1)} %get-tuple-element.74), channel_id=1, source_target_pairs={{0,4},{2,6},{4,0},{6,2},{8,12},{10,14},{12,8},{14,10},{16,20},{18,... | collective-permute-start | bytes 147464 | tf_op jit(solution)/shard_map/ppermute | solution.py:439
  70.6 5.7 %collective-permute-start.20 = (bf16[192,128]{1,0:T(8,128)(2,1)S(1)}, bf16[192,128]{1,0:T(8,128)(2,1)S(1)}, u32[]{:S(2)}, u32[]{:S(2)}) collective-permute-start(bf16[192,128]{1,0:T(8,128)(2,1)S(1)} %get-tuple-element.75), channel_id=1, source_target_pairs={{0,6},{2,4},{4,2},{6,0},{8,14},{10,12},{12,10},{14,8},{16,22},{18,... | collective-permute-start | bytes 147464 | tf_op jit(solution)/shard_map/ppermute | solution.py:439
  77.5 11.2 %collective-permute-start.24 = (bf16[192,1024]{1,0:T(8,128)(2,1)S(1)}, bf16[192,1024]{1,0:T(8,128)(2,1)S(1)}, u32[]{:S(2)}, u32[]{:S(2)}) collective-permute-start(bf16[192,1024]{1,0:T(8,128)(2,1)S(1)} %shard_map.109), channel_id=1, source_target_pairs={{0,1},{1,0},{2,3},{3,2},{4,5},{5,4},{6,7},{7,6},{8,9},{9,8},{10,11... | collective-permute-start | bytes 1179656 | tf_op jit(solution)/shard_map/ppermute | solution.py:594
  79.1 1.9 %collective-permute-start.21 = (bf16[192,128]{1,0:T(8,128)(2,1)S(1)}, bf16[192,128]{1,0:T(8,128)(2,1)S(1)}, u32[]{:S(2)}, u32[]{:S(2)}) collective-permute-start(bf16[192,128]{1,0:T(8,128)(2,1)S(1)} %get-tuple-element.77), channel_id=1, source_target_pairs={{0,2},{2,0},{4,6},{6,4},{8,10},{10,8},{12,14},{14,12},{16,18},{18,... | collective-permute-start | bytes 147464 | tf_op jit(solution)/shard_map/ppermute | solution.py:439
  79.1 4.2 %collective-permute-start.22 = (bf16[192,128]{1,0:T(8,128)(2,1)S(1)}, bf16[192,128]{1,0:T(8,128)(2,1)S(1)}, u32[]{:S(2)}, u32[]{:S(2)}) collective-permute-start(bf16[192,128]{1,0:T(8,128)(2,1)S(1)} %get-tuple-element.78), channel_id=1, source_target_pairs={{0,4},{2,6},{4,0},{6,2},{8,12},{10,14},{12,8},{14,10},{16,20},{18,... | collective-permute-start | bytes 147464 | tf_op jit(solution)/shard_map/ppermute | solution.py:439
  80.4 3.8 %collective-permute-start.23 = (bf16[192,128]{1,0:T(8,128)(2,1)S(1)}, bf16[192,128]{1,0:T(8,128)(2,1)S(1)}, u32[]{:S(2)}, u32[]{:S(2)}) collective-permute-start(bf16[192,128]{1,0:T(8,128)(2,1)S(1)} %get-tuple-element.79), channel_id=1, source_target_pairs={{0,6},{2,4},{4,2},{6,0},{8,14},{10,12},{12,10},{14,8},{16,22},{18,... | collective-permute-start | bytes 147464 | tf_op jit(solution)/shard_map/ppermute | solution.py:439

commit v5 on v4

--- a/solution.py
+++ b/solution.py
@@ -118,8 +118,9 @@
     send_pieces(outs, turned)
 
 
-def pack_qo_kernel(slots, head_dim, q_ref, g_ref, lse_ref, after_ref, *rest):
-    outs, qo_ref = rest[:GROUP], rest[GROUP]
+def pack_qo_kernel(slots, head_dim, q_ref, g_ref, lse_ref, mine_ref, after_ref, *rest):
+    outs, (hold, qo_ref) = rest[:GROUP], rest[GROUP:]
+    hold[...] = mine_ref[...]
     rows = q_ref.shape[0]
     blocks = rows // BLOCK
     reorder_into(qo_ref, 0, q_ref, head_dim ** (-0.5))
@@ -158,9 +159,10 @@
 
 
 def line_kernel(carried, *refs):
-    pieces, refs = refs[:GROUP], refs[GROUP + carried :]
+    pieces, query_piece, refs = refs[:GROUP], refs[GROUP], refs[GROUP + 1 + carried :]
     own, first_out, second_out = refs[:3]
     rows = pieces[0].shape[0]
+    own[GROUP * rows :] = query_piece[...]
     blocks = rows // BLOCK
     me = lax.axis_index("var") % GROUP
     for distance in range(GROUP):
@@ -178,7 +180,7 @@
     *refs,
 ):
     kv_refs, refs = refs[:3], refs[3:]
-    qo_pieces, refs = refs[:GROUP], refs[GROUP:]
+    qo_pieces, refs = refs[: GROUP - 1], refs[GROUP - 1 :]
     key_outs, value_outs, refs = refs[:3], refs[3:6], refs[6:]
     dq_outs, refs = refs[:GROUP], refs[GROUP:]
     kv_win, k_turn, acc, shifts, queries, grads, crossed, prob, slope, qo_ref, dq_all = refs
@@ -197,8 +199,9 @@
     for ref, start, count in zip(
         kv_refs, (SPAN, first_at, second_at), (group_blocks, SPAN, SPAN)
     ):
-        kv_win[pl.ds(start, count)] = ref[...].reshape(count, BLOCK, 2 * LANES)
-    stage_pieces(qo_ref, qo_pieces)
+        kv_win[pl.ds(start, count)] = ref[: count * BLOCK].reshape(count, BLOCK, 2 * LANES)
+    own_queries = kv_refs[0].at[pl.ds(group_blocks * BLOCK, rows + LSE_ROWS)]
+    stage_pieces(qo_ref, (own_queries, *qo_pieces))
     key_patch = lax.broadcasted_iota(jnp.int32, (8, LANES), 0)
     query_patch = lax.broadcasted_iota(jnp.int32, (8, LANES), 1) & 7
     usable = key_patch <= query_patch
@@ -341,9 +344,19 @@
     group_blocks = own_ref.shape[0]
     first, second = exchange_start(group_blocks)
     total[...] = own_ref[...]
-    for start, ref in ((first, first_ref), (second, second_ref)):
-        at = pl.ds(start, SPAN)
-        total[at] = total[at] + ref[...].astype(F32)
+    level = lax.axis_index("var") // GROUP
+    levels = lax.axis_size("var") // GROUP
+    odd = below_first()
+    for other, start, ref in (
+        (level + 1 - 2 * odd, first, first_ref),
+        (level - 1 + 2 * odd, second, second_ref),
+    ):
+
+        @pl.when((other >= 0) & (other < levels))
+        def _(start=start, ref=ref):
+            at = pl.ds(start, SPAN)
+            total[at] = total[at] + ref[...].astype(F32)
+
     moved[...] = total[...].astype(BF16).reshape(moved.shape)
 
 
@@ -442,8 +455,7 @@
         pairs = []
         for n in range(devices):
             other = n - GROUP if (n // GROUP + n + turn) % 2 else n + GROUP
-            if 0 <= other < devices:
-                pairs.append((n, other))
+            pairs.append((n, other if 0 <= other < devices else n))
         return lax.ppermute(x, "var", pairs)
 
     def trade_first(x):
@@ -480,37 +492,37 @@
         cost_estimate=cost(4 * rows * features * BLOCK, 5 * size),
     )(keys, values)
     kvs = swap(kvs)
-    qos = pl.pallas_call(
+    *qos, kvs[0] = pl.pallas_call(
         functools.partial(pack_qo_kernel, slots, head_dim),
-        out_shape=(shaped((rows + LSE_ROWS, wide)),) * GROUP,
-        in_specs=[vmem()] * 3 + [anywhere],
-        out_specs=(vmem(),) * GROUP,
+        out_shape=(shaped((rows + LSE_ROWS, wide)),) * GROUP + (shaped((rows, wide)),),
+        in_specs=[vmem()] * 4 + [anywhere],
+        out_specs=(vmem(),) * (GROUP + 1),
         scratch_shapes=[staged(rows + LSE_ROWS, wide)],
         compiler_params=params(8),
         cost_estimate=cost(4 * rows * features * BLOCK, 10 * size),
-    )(queries, out_grad, log_sum_exp, kvs[1])
+    )(queries, out_grad, log_sum_exp, kvs[0], kvs[1])
     carried = tuple(qos[1:])
     own, first, second, *carried = pl.pallas_call(
         functools.partial(line_kernel, len(carried)),
-        out_shape=(shaped((GROUP * rows, wide)),)
+        out_shape=(shaped((GROUP * rows + rows + LSE_ROWS, wide)),)
         + (shaped((SPAN * BLOCK, wide)),) * 2
         + tuple(shaped(x.shape) for x in carried),
-        in_specs=[vmem()] * GROUP + [anywhere] * len(carried),
+        in_specs=[vmem()] * (GROUP + 1) + [anywhere] * len(carried),
         out_specs=(vmem(),) * 3 + (anywhere,) * len(carried),
-        input_output_aliases={GROUP + i: 3 + i for i in range(len(carried))},
+        input_output_aliases={GROUP + 1 + i: 3 + i for i in range(len(carried))},
         compiler_params=params(8),
         cost_estimate=cost(0, 5 * size),
-    )(*kvs, *carried)
+    )(*kvs, qos[0], *carried)
     first = trade_first(first)
     second = trade_second(second)
-    qos = swap([qos[0], *carried])
+    qos = swap([None, *carried])[1:]
 
     pairs = group_blocks * slot_count * BLOCK * BLOCK * slots
     sums = (shaped((group_blocks,) + block, F32),) + (shaped((SPAN,) + block),) * 2
     results = pl.pallas_call(
         functools.partial(attend_kernel, blocks_here, head_dim),
         out_shape=sums + sums + (shaped((rows, LANES)),) * GROUP,
-        in_specs=[pl.BlockSpec(memory_space=pltpu.SMEM)] + [vmem()] * (3 + GROUP),
+        in_specs=[pl.BlockSpec(memory_space=pltpu.SMEM)] + [vmem()] * (2 + GROUP),
         out_specs=(vmem(),) * (6 + GROUP),
         scratch_shapes=[
             pltpu.VMEM((window, BLOCK, wide), BF16),

time: 90 us -> 88.8 us (0.987)
  waiting for transfers between devices: 28.9 us -> 27.7 us
  local copies, waits for them, and re-layouts: 4.65 us -> 3.71 us
    unnamed x17 -> x13, local copies, waits for them, and re-layouts: 4.65 us -> 3.71 us
    ppermute x18, waiting for transfers between devices: 23.9 us -> 23 us  [trade(): return lax.ppermute(x, 'var', [(n, n ^ distance) for n in range(devices)])]
where the time goes in v5:
time: 88.8 us; the launch traced here: 88.4 us
  starting transfers between devices  33.8 us (38%)
  waiting for transfers between devices  27.7 us (31%)
  Pallas kernels  21.6 us (24%)
  local copies, waits for them, and re-layouts  3.71 us (4%)
    ppermute x18, waiting for transfers between devices, trade(): return lax.ppermute(x, 'var', [(n, n ^ distance) for n in range(devices)])  23 us
    ppermute x18, starting transfers between devices, trade(): return lax.ppermute(x, 'var', [(n, n ^ distance) for n in range(devices)])  18.2 us
    pallas_call x1, Pallas kernels, body(): pl.pallas_call(functools.partial(attend_kernel, blocks_here, head_dim), o...  14.3 us
    ppermute x6, starting transfers between devices, trade_level(): return lax.ppermute(x, 'var', pairs)  14.1 us
    unnamed x13, local copies, waits for them, and re-layouts  3.71 us
    ppermute x1, waiting for transfers between devices, body(): lax.ppermute(send, 'head', [(n, (n + piece + 1) % heads) for n in range(h...  2.66 us
    pallas_call x1, Pallas kernels, body(): pl.pallas_call(pack_kv_kernel, out_shape=(shaped((rows, wide)),) * GROUP,...  2.47 us
    ppermute x6, waiting for transfers between devices, trade_level(): return lax.ppermute(x, 'var', pairs)  2 us
  transfers between devices with their start and end apart: 25, of which 10 were waited for; matrix products, arithmetic and copies ran while one was open for 0% of the time, Pallas kernels for 3%

profile of v5, /device:TPU:0, one launch (start us, length us, event | category | flops | bytes accessed | tf_op | source)
XLA Modules:
  0.0 88.4 jit_solution(7742389962503860884)
XLA Ops:
  0.6 2.5 %shard_map.102 = (bf16[384,256]{1,0:T(8,128)(2,1)}, bf16[384,256]{1,0:T(8,128)(2,1)}, bf16[384,256]{1,0:T(8,128)(2,1)}, bf16[384,256]{1,0:T(8,128)(2,1)}) custom-call(bf16[384,512]{1,0:T(8,128)(2,1)} %k_hbm.1, bf16[384,512]{1,0:T(8,128)(2,1)} %v_hbm.1), custom_call_target="tpu_custom_call" | custom-call | flops 100663296 | bytes 1966080 | tf_op jit(solution)/shard_map/pallas_call | solution.py:484
  3.1 0.5 collective-permute-start
  3.6 2.6 %collective-permute-start.1 = (bf16[384,256]{1,0:T(8,128)(2,1)}, bf16[384,256]{1,0:T(8,128)(2,1)S(1)}, u32[]{:S(2)}, u32[]{:S(2)}) collective-permute-start(bf16[384,256]{1,0:T(8,128)(2,1)} %get-tuple-element.48), channel_id=1, source_target_pairs={{0,4},{2,6},{4,0},{6,2},{8,12},{10,14},{12,8},{14,10},{16,20},{18,... | collective-permute-start | bytes 589832 | tf_op jit(solution)/shard_map/ppermute | solution.py:452
  6.2 0.1 collective-permute-start.2
  6.3 0.0 collective-permute-done.after_ref.refs_1_
  6.3 1.0 %copy-done.1 = bf16[384,512]{1,0:T(8,128)(2,1)S(1)} copy-done((bf16[384,512]{1,0:T(8,128)(2,1)S(1)}, bf16[384,512]{1,0:T(8,128)(2,1)}, u32[]{:S(2)}) %copy-start.1) | copy-done | bytes 393240
  7.3 1.0 %copy-done.2 = bf16[384,512]{1,0:T(8,128)(2,1)S(1)} copy-done((bf16[384,512]{1,0:T(8,128)(2,1)S(1)}, bf16[384,512]{1,0:T(8,128)(2,1)}, u32[]{:S(2)}) %copy-start.2) | copy-done | bytes 393240
  8.3 0.9 %copy-done.3 = bf16[384,256]{1,0:T(8,128)(2,1)S(1)} copy-done((bf16[384,256]{1,0:T(8,128)(2,1)S(1)}, bf16[384,256]{1,0:T(8,128)(2,1)}, u32[]{:S(2)}) %copy-start.3) | copy-done | bytes 196632
  9.2 0.7 copy-done.4
  9.9 0.5 shard_map.103
  10.4 1.8 %collective-permute-done.1.refs_2_ = bf16[384,256]{1,0:T(8,128)(2,1)S(1)} collective-permute-done((bf16[384,256]{1,0:T(8,128)(2,1)}, bf16[384,256]{1,0:T(8,128)(2,1)S(1)}, u32[]{:S(2)}, u32[]{:S(2)}) %collective-permute-start.1) | collective-permute-done | bytes 196640 | tf_op jit(solution)/shard_map/ppermute | solution.py:452
  12.2 3.7 %collective-permute-done.2.refs_3_ = bf16[384,256]{1,0:T(8,128)(2,1)S(1)} collective-permute-done((bf16[384,256]{1,0:T(8,128)(2,1)}, bf16[384,256]{1,0:T(8,128)(2,1)S(1)}, u32[]{:S(2)}, u32[]{:S(2)}) %collective-permute-start.2) | collective-permute-done | bytes 196640 | tf_op jit(solution)/shard_map/ppermute | solution.py:452
  15.9 0.9 %shard_map.104 = (bf16[1936,256]{1,0:T(8,128)(2,1)S(1)}, bf16[1024,256]{1,0:T(8,128)(2,1)}, bf16[1024,256]{1,0:T(8,128)(2,1)S(1)}, bf16[400,256]{1,0:T(8,128)(2,...) custom-call(bf16[384,256]{1,0:T(8,128)(2,1)S(1)} %get-tuple-element., ...), custom_call_target="tpu_custom_call", output_to_operand_aliasing={{3}: (5, {}), {4}: (6, {}), {5}: (7, {})} | custom-call | bytes 1966080 | tf_op jit(solution)/shard_map/pallas_call | solution.py:505
  16.8 3.5 %collective-permute-start.3 = (bf16[1024,256]{1,0:T(8,128)(2,1)}, bf16[1024,256]{1,0:T(8,128)(2,1)S(1)}, u32[]{:S(2)}, u32[]{:S(2)}) collective-permute-start(bf16[1024,256]{1,0:T(8,128)(2,1)} %get-tuple-element.55), channel_id=1, source_target_pairs={{0,8},{2,2},{4,12},{6,6},{8,0},{10,18},{12,4},{14,22},{16,24},{18,... | collective-permute-start | bytes 1572872 | tf_op jit(solution)/shard_map/ppermute | solution.py:459
  20.4 0.7 collective-permute-start.4
  21.1 2.6 %collective-permute-start.5 = (bf16[400,256]{1,0:T(8,128)(2,1)S(1)}, bf16[400,256]{1,0:T(8,128)(2,1)S(1)}, u32[]{:S(2)}, u32[]{:S(2)}) collective-permute-start(bf16[400,256]{1,0:T(8,128)(2,1)S(1)} %get-tuple-element.57), channel_id=1, source_target_pairs={{0,2},{2,0},{4,6},{6,4},{8,10},{10,8},{12,14},{14,12},{16,18},{18,... | collective-permute-start | bytes 614408 | tf_op jit(solution)/shard_map/ppermute | solution.py:452
  23.6 1.5 %collective-permute-start.6 = (bf16[400,256]{1,0:T(8,128)(2,1)S(1)}, bf16[400,256]{1,0:T(8,128)(2,1)}, u32[]{:S(2)}, u32[]{:S(2)}) collective-permute-start(bf16[400,256]{1,0:T(8,128)(2,1)S(1)} %get-tuple-element.58), channel_id=1, source_target_pairs={{0,4},{2,6},{4,0},{6,2},{8,12},{10,14},{12,8},{14,10},{16,20},{18,... | collective-permute-start | bytes 614408 | tf_op jit(solution)/shard_map/ppermute | solution.py:452
  25.2 0.0 collective-permute-start.7
  25.2 0.1 copy.14.kb_ref
  25.2 0.0 collective-permute-done.5.refs_3_
  25.2 6.4 %collective-permute-done.6.refs_4_ = bf16[400,256]{1,0:T(8,128)(2,1)} collective-permute-done((bf16[400,256]{1,0:T(8,128)(2,1)S(1)}, bf16[400,256]{1,0:T(8,128)(2,1)}, u32[]{:S(2)}, u32[]{:S(2)}) %collective-permute-start.6) | collective-permute-done | bytes 204832 | tf_op jit(solution)/shard_map/ppermute | solution.py:452
  31.7 2.6 %collective-permute-done.7.refs_5_ = bf16[400,256]{1,0:T(8,128)(2,1)} collective-permute-done((bf16[400,256]{1,0:T(8,128)(2,1)S(1)}, bf16[400,256]{1,0:T(8,128)(2,1)}, u32[]{:S(2)}, u32[]{:S(2)}) %collective-permute-start.7) | collective-permute-done | bytes 204832 | tf_op jit(solution)/shard_map/ppermute | solution.py:452
  34.3 0.0 collective-permute-done.3.refs_1_
  34.3 0.0 collective-permute-done.4.refs_2_
  34.3 14.3 %shard_map.105 = (f32[12,128,128]{2,1,0:T(8,128)S(1)}, bf16[8,128,128]{2,1,0:T(8,128)(2,1)S(1)}, bf16[8,128,128]{2,1,0:T(8,128)(2,1)S(1)}, f32[12,128,128]{2,1,0...) custom-call(s32[48,8]{1,0:T(8,128)S(1)} %copy.14.kb_ref, ...), custom_call_target="tpu_custom_call" | custom-call | flops 8053063680 | bytes 2000000 | tf_op jit(solution)/shard_map/pallas_call | solution.py:522
  48.6 4.6 %collective-permute-start.11 = (bf16[8,128,128]{2,1,0:T(8,128)(2,1)S(1)}, bf16[8,128,128]{2,1,0:T(8,128)(2,1)S(1)}, u32[]{:S(2)}, u32[]{:S(2)}) collective-permute-start(bf16[8,128,128]{2,1,0:T(8,128)(2,1)S(1)} %get-tuple-element.65), channel_id=1, source_target_pairs={{0,8},{2,2},{4,12},{6,6},{8,0},{10,18},{12,4},{14,22},{16,24},{18,... | collective-permute-start | bytes 786440 | tf_op jit(solution)/shard_map/ppermute | solution.py:459
  53.2 0.7 collective-permute-start.12
  53.9 3.8 %collective-permute-start.16 = (bf16[8,128,128]{2,1,0:T(8,128)(2,1)S(1)}, bf16[8,128,128]{2,1,0:T(8,128)(2,1)S(1)}, u32[]{:S(2)}, u32[]{:S(2)}) collective-permute-start(bf16[8,128,128]{2,1,0:T(8,128)(2,1)S(1)} %get-tuple-element.72), channel_id=1, source_target_pairs={{0,8},{2,2},{4,12},{6,6},{8,0},{10,18},{12,4},{14,22},{16,24},{18,... | collective-permute-start | bytes 786440 | tf_op jit(solution)/shard_map/ppermute | solution.py:459
  57.8 0.7 collective-permute-start.17
  58.5 2.1 %collective-permute-start.8 = (bf16[384,128]{1,0:T(8,128)(2,1)S(1)}, bf16[384,128]{1,0:T(8,128)(2,1)S(1)}, u32[]{:S(2)}, u32[]{:S(2)}) collective-permute-start(bf16[384,128]{1,0:T(8,128)(2,1)S(1)} %get-tuple-element.61), channel_id=1, source_target_pairs={{0,2},{2,0},{4,6},{6,4},{8,10},{10,8},{12,14},{14,12},{16,18},{18,... | collective-permute-start | bytes 294920 | tf_op jit(solution)/shard_map/ppermute | solution.py:452
  60.5 0.0 collective-permute-done.11.first_ref
  60.5 1.5 %collective-permute-start.9 = (bf16[384,128]{1,0:T(8,128)(2,1)S(1)}, bf16[384,128]{1,0:T(8,128)(2,1)S(1)}, u32[]{:S(2)}, u32[]{:S(2)}) collective-permute-start(bf16[384,128]{1,0:T(8,128)(2,1)S(1)} %get-tuple-element.62), channel_id=1, source_target_pairs={{0,4},{2,6},{4,0},{6,2},{8,12},{10,14},{12,8},{14,10},{16,20},{18,... | collective-permute-start | bytes 294920 | tf_op jit(solution)/shard_map/ppermute | solution.py:452
  62.1 0.0 collective-permute-done.12.second_ref
  62.1 0.5 collective-permute-start.10
  62.6 0.2 shard_map.106
  62.7 2.0 %collective-permute-done.16.first_ref = bf16[8,128,128]{2,1,0:T(8,128)(2,1)S(1)} collective-permute-done((bf16[8,128,128]{2,1,0:T(8,128)(2,1)S(1)}, bf16[8,128,128]{2,1,0:T(8,128)(2,1)S(1)}, u32[]{:S(2)}, u32[]{:S(2)}) %collective-permute-start.16) | collective-permute-done | bytes 262176 | tf_op jit(solution)/shard_map/ppermute | solution.py:459
  64.7 0.0 collective-permute-start.13
  64.7 0.0 collective-permute-done.17.second_ref
  64.7 0.2 shard_map.107
  64.9 1.4 %collective-permute-start.18 = (bf16[192,128]{1,0:T(8,128)(2,1)S(1)}, bf16[192,128]{1,0:T(8,128)(2,1)S(1)}, u32[]{:S(2)}, u32[]{:S(2)}) collective-permute-start(bf16[192,128]{1,0:T(8,128)(2,1)S(1)} %get-tuple-element.75), channel_id=1, source_target_pairs={{0,2},{2,0},{4,6},{6,4},{8,10},{10,8},{12,14},{14,12},{16,18},{18,... | collective-permute-start | bytes 147464 | tf_op jit(solution)/shard_map/ppermute | solution.py:452
  66.4 0.0 collective-permute-done.8.refs_1_
  66.4 1.5 %collective-permute-start.14 = (bf16[384,128]{1,0:T(8,128)(2,1)S(1)}, bf16[384,128]{1,0:T(8,128)(2,1)S(1)}, u32[]{:S(2)}, u32[]{:S(2)}) collective-permute-start(bf16[384,128]{1,0:T(8,128)(2,1)S(1)} %get-tuple-element.69), channel_id=1, source_target_pairs={{0,4},{2,6},{4,0},{6,2},{8,12},{10,14},{12,8},{14,10},{16,20},{18,... | collective-permute-start | bytes 294920 | tf_op jit(solution)/shard_map/ppermute | solution.py:452
  67.9 0.0 collective-permute-done.9.refs_2_
  67.9 0.0 collective-permute-start.15
  67.9 0.0 collective-permute-done.10.refs_3_
  67.9 1.4 %collective-permute-start.19 = (bf16[192,128]{1,0:T(8,128)(2,1)S(1)}, bf16[192,128]{1,0:T(8,128)(2,1)S(1)}, u32[]{:S(2)}, u32[]{:S(2)}) collective-permute-start(bf16[192,128]{1,0:T(8,128)(2,1)S(1)} %get-tuple-element.76), channel_id=1, source_target_pairs={{0,4},{2,6},{4,0},{6,2},{8,12},{10,14},{12,8},{14,10},{16,20},{18,... | collective-permute-start | bytes 147464 | tf_op jit(solution)/shard_map/ppermute | solution.py:452
  69.3 0.0 collective-permute-done.18.refs_9_
  69.3 0.5 collective-permute-start.20
  69.9 4.7 %collective-permute-done.19.refs_10_ = bf16[192,128]{1,0:T(8,128)(2,1)S(1)} collective-permute-done((bf16[192,128]{1,0:T(8,128)(2,1)S(1)}, bf16[192,128]{1,0:T(8,128)(2,1)S(1)}, u32[]{:S(2)}, u32[]{:S(2)}) %collective-permute-start.19) | collective-permute-done | bytes 49184 | tf_op jit(solution)/shard_map/ppermute | solution.py:452
  74.6 0.5 collective-permute-done.20.refs_11_
  75.1 0.0 collective-permute-done.13.refs_5_
  75.1 0.0 collective-permute-done.14.refs_6_
  75.1 0.0 collective-permute-done.15.refs_7_
  75.1 1.2 %shard_map.109 = bf16[192,1024]{1,0:T(8,128)(2,1)S(1)} custom-call(bf16[384,128]{1,0:T(8,128)(2,1)S(1)} %get-tuple-element.60.refs_0_, bf16[384,128]{1,0:T(8,128)(2,1)S(1)} %collective-permute-done.8.refs_1_, bf16[384,128]{1,0:T(8,128)(2,1)S(1)} %collective-permute-done.9.refs_2_, bf16[384,128]{1,0:T(8,128)(2,1)S(1)} %collective-permute-done.10.refs_3_, ...), custom_call_target="tpu_custom_call" | custom-call | flops 603979776 | bytes 4000000 | tf_op jit(solution)/shard_map/pallas_call | solution.py:583
  76.3 1.5 %collective-permute-start.24 = (bf16[192,1024]{1,0:T(8,128)(2,1)S(1)}, bf16[192,1024]{1,0:T(8,128)(2,1)S(1)}, u32[]{:S(2)}, u32[]{:S(2)}) collective-permute-start(bf16[192,1024]{1,0:T(8,128)(2,1)S(1)} %shard_map.109), channel_id=1, source_target_pairs={{0,1},{1,0},{2,3},{3,2},{4,5},{5,4},{6,7},{7,6},{8,9},{9,8},{10,11... | collective-permute-start | bytes 1179656 | tf_op jit(solution)/shard_map/ppermute | solution.py:606
  77.8 0.0 collective-permute-start.21
  77.9 1.3 %collective-permute-start.22 = (bf16[192,128]{1,0:T(8,128)(2,1)S(1)}, bf16[192,128]{1,0:T(8,128)(2,1)S(1)}, u32[]{:S(2)}, u32[]{:S(2)}) collective-permute-start(bf16[192,128]{1,0:T(8,128)(2,1)S(1)} %get-tuple-element.80), channel_id=1, source_target_pairs={{0,4},{2,6},{4,0},{6,2},{8,12},{10,14},{12,8},{14,10},{16,20},{18,... | collective-permute-start | bytes 147464 | tf_op jit(solution)/shard_map/ppermute | solution.py:452
  79.2 0.5 collective-permute-start.23
  79.7 0.0 collective-permute-done.21.refs_13_
  79.7 2.3 %collective-permute-done.22.refs_14_ = bf16[192,128]{1,0:T(8,128)(2,1)S(1)} collective-permute-done((bf16[192,128]{1,0:T(8,128)(2,1)S(1)}, bf16[192,128]{1,0:T(8,128)(2,1)S(1)}, u32[]{:S(2)}, u32[]{:S(2)}) %collective-permute-start.22) | collective-permute-done | bytes 49184 | tf_op jit(solution)/shard_map/ppermute | solution.py:452
  82.0 1.0 %collective-permute-done.23.refs_15_ = bf16[192,128]{1,0:T(8,128)(2,1)S(1)} collective-permute-done((bf16[192,128]{1,0:T(8,128)(2,1)S(1)}, bf16[192,128]{1,0:T(8,128)(2,1)S(1)}, u32[]{:S(2)}, u32[]{:S(2)}) %collective-permute-start.23) | collective-permute-done | bytes 49184 | tf_op jit(solution)/shard_map/ppermute | solution.py:452
  83.0 1.9 %shard_map.108 = (bf16[384,512]{1,0:T(8,128)(2,1)}, bf16[384,512]{1,0:T(8,128)(2,1)}, bf16[384,512]{1,0:T(8,128)(2,1)}, f32[192,1024]{1,0:T(8,128)S(1)}) custom-call(bf16[384,128]{1,0:T(8,128)(2,1)S(1)} %get-tuple-element.60.refs_0_, bf16[384,128]{1,0:T(8,128)(2,1)S(1)} %collective-permute-done.8.refs_1_, ...), custom_call_target="tpu_custom_call" | custom-call | flops 603979776 | bytes 6000000 | tf_op jit(solution)/shard_map/pallas_call | solution.py:594
  84.8 2.7 %collective-permute-done.24 = bf16[192,1024]{1,0:T(8,128)(2,1)S(1)} collective-permute-done((bf16[192,1024]{1,0:T(8,128)(2,1)S(1)}, bf16[192,1024]{1,0:T(8,128)(2,1)S(1)}, u32[]{:S(2)}, u32[]{:S(2)}) %collective-permute-start.24) | collective-permute-done | bytes 393248 | tf_op jit(solution)/shard_map/ppermute | solution.py:606
  87.5 0.9 add_convert_fusion
  (8 shorter events, 0.0 us)
Async XLA Ops:
  0.6 24.5 %copy-start.5 = (s32[48,8]{0,1:T(8,128)S(1)}, s32[48,8]{0,1:T(8,128)}, u32[]{:S(2)}) copy-start(s32[48,8]{0,1:T(8,128)} %param.12) | copy-start | bytes 4612
  3.1 3.2 %collective-permute-start = (bf16[384,256]{1,0:T(8,128)(2,1)}, bf16[384,256]{1,0:T(8,128)(2,1)S(1)}, u32[]{:S(2)}, u32[]{:S(2)}) collective-permute-start(bf16[384,256]{1,0:T(8,128)(2,1)} %get-tuple-element.46), channel_id=1, source_target_pairs={{0,2},{2,0},{4,6},{6,4},{8,10},{10,8},{12,14},{14,12},{16,18},{18,... | collective-permute-start | bytes 589832 | tf_op jit(solution)/shard_map/ppermute | solution.py:452
  3.6 8.6 %collective-permute-start.1 = (bf16[384,256]{1,0:T(8,128)(2,1)}, bf16[384,256]{1,0:T(8,128)(2,1)S(1)}, u32[]{:S(2)}, u32[]{:S(2)}) collective-permute-start(bf16[384,256]{1,0:T(8,128)(2,1)} %get-tuple-element.48), channel_id=1, source_target_pairs={{0,4},{2,6},{4,0},{6,2},{8,12},{10,14},{12,8},{14,10},{16,20},{18,... | collective-permute-start | bytes 589832 | tf_op jit(solution)/shard_map/ppermute | solution.py:452
  6.2 9.7 %collective-permute-start.2 = (bf16[384,256]{1,0:T(8,128)(2,1)}, bf16[384,256]{1,0:T(8,128)(2,1)S(1)}, u32[]{:S(2)}, u32[]{:S(2)}) collective-permute-start(bf16[384,256]{1,0:T(8,128)(2,1)} %get-tuple-element.49), channel_id=1, source_target_pairs={{0,6},{2,4},{4,2},{6,0},{8,14},{10,12},{12,10},{14,8},{16,22},{18,... | collective-permute-start | bytes 589832 | tf_op jit(solution)/shard_map/ppermute | solution.py:452
  6.3 1.0 %copy-start.1 = (bf16[384,512]{1,0:T(8,128)(2,1)S(1)}, bf16[384,512]{1,0:T(8,128)(2,1)}, u32[]{:S(2)}) copy-start(bf16[384,512]{1,0:T(8,128)(2,1)} %q_ref.1) | copy-start | bytes 1179652
  7.3 1.0 %copy-start.2 = (bf16[384,512]{1,0:T(8,128)(2,1)S(1)}, bf16[384,512]{1,0:T(8,128)(2,1)}, u32[]{:S(2)}) copy-start(bf16[384,512]{1,0:T(8,128)(2,1)} %g_ref.1) | copy-start | bytes 1179652
  8.3 0.9 %copy-start.3 = (bf16[384,256]{1,0:T(8,128)(2,1)S(1)}, bf16[384,256]{1,0:T(8,128)(2,1)}, u32[]{:S(2)}) copy-start(bf16[384,256]{1,0:T(8,128)(2,1)} %get-tuple-element.45.mine_ref) | copy-start | bytes 589828
  9.2 0.7 copy-start.4
  16.8 17.5 %collective-permute-start.3 = (bf16[1024,256]{1,0:T(8,128)(2,1)}, bf16[1024,256]{1,0:T(8,128)(2,1)S(1)}, u32[]{:S(2)}, u32[]{:S(2)}) collective-permute-start(bf16[1024,256]{1,0:T(8,128)(2,1)} %get-tuple-element.55), channel_id=1, source_target_pairs={{0,8},{2,2},{4,12},{6,6},{8,0},{10,18},{12,4},{14,22},{16,24},{18,... | collective-permute-start | bytes 1572872 | tf_op jit(solution)/shard_map/ppermute | solution.py:459
  20.4 13.9 %collective-permute-start.4 = (bf16[1024,256]{1,0:T(8,128)(2,1)S(1)}, bf16[1024,256]{1,0:T(8,128)(2,1)S(1)}, u32[]{:S(2)}, u32[]{:S(2)}) collective-permute-start(bf16[1024,256]{1,0:T(8,128)(2,1)S(1)} %get-tuple-element.56), channel_id=1, source_target_pairs={{0,0},{2,10},{4,4},{6,14},{8,16},{10,2},{12,20},{14,6},{16,8},{18,... | collective-permute-start | bytes 1572872 | tf_op jit(solution)/shard_map/ppermute | solution.py:459
  21.1 4.2 %collective-permute-start.5 = (bf16[400,256]{1,0:T(8,128)(2,1)S(1)}, bf16[400,256]{1,0:T(8,128)(2,1)S(1)}, u32[]{:S(2)}, u32[]{:S(2)}) collective-permute-start(bf16[400,256]{1,0:T(8,128)(2,1)S(1)} %get-tuple-element.57), channel_id=1, source_target_pairs={{0,2},{2,0},{4,6},{6,4},{8,10},{10,8},{12,14},{14,12},{16,18},{18,... | collective-permute-start | bytes 614408 | tf_op jit(solution)/shard_map/ppermute | solution.py:452
  23.6 8.0 %collective-permute-start.6 = (bf16[400,256]{1,0:T(8,128)(2,1)S(1)}, bf16[400,256]{1,0:T(8,128)(2,1)}, u32[]{:S(2)}, u32[]{:S(2)}) collective-permute-start(bf16[400,256]{1,0:T(8,128)(2,1)S(1)} %get-tuple-element.58), channel_id=1, source_target_pairs={{0,4},{2,6},{4,0},{6,2},{8,12},{10,14},{12,8},{14,10},{16,20},{18,... | collective-permute-start | bytes 614408 | tf_op jit(solution)/shard_map/ppermute | solution.py:452
  25.2 9.1 %collective-permute-start.7 = (bf16[400,256]{1,0:T(8,128)(2,1)S(1)}, bf16[400,256]{1,0:T(8,128)(2,1)}, u32[]{:S(2)}, u32[]{:S(2)}) collective-permute-start(bf16[400,256]{1,0:T(8,128)(2,1)S(1)} %get-tuple-element.59), channel_id=1, source_target_pairs={{0,6},{2,4},{4,2},{6,0},{8,14},{10,12},{12,10},{14,8},{16,22},{18,... | collective-permute-start | bytes 614408 | tf_op jit(solution)/shard_map/ppermute | solution.py:452
  34.3 40.8 %copy-start = (bf16[3,1024,512]{2,1,0:T(8,128)(2,1)S(1)}, bf16[3,1024,512]{2,1,0:T(8,128)(2,1)}, u32[]{:S(2)}) copy-start(bf16[3,1024,512]{2,1,0:T(8,128)(2,1)} %refs_12_.1) | copy-start | bytes 9437188
  48.6 11.9 %collective-permute-start.11 = (bf16[8,128,128]{2,1,0:T(8,128)(2,1)S(1)}, bf16[8,128,128]{2,1,0:T(8,128)(2,1)S(1)}, u32[]{:S(2)}, u32[]{:S(2)}) collective-permute-start(bf16[8,128,128]{2,1,0:T(8,128)(2,1)S(1)} %get-tuple-element.65), channel_id=1, source_target_pairs={{0,8},{2,2},{4,12},{6,6},{8,0},{10,18},{12,4},{14,22},{16,24},{18,... | collective-permute-start | bytes 786440 | tf_op jit(solution)/shard_map/ppermute | solution.py:459
  53.2 8.8 %collective-permute-start.12 = (bf16[8,128,128]{2,1,0:T(8,128)(2,1)S(1)}, bf16[8,128,128]{2,1,0:T(8,128)(2,1)S(1)}, u32[]{:S(2)}, u32[]{:S(2)}) collective-permute-start(bf16[8,128,128]{2,1,0:T(8,128)(2,1)S(1)} %get-tuple-element.66), channel_id=1, source_target_pairs={{0,0},{2,10},{4,4},{6,14},{8,16},{10,2},{12,20},{14,6},{16,8},{18,... | collective-permute-start | bytes 786440 | tf_op jit(solution)/shard_map/ppermute | solution.py:459
  53.9 10.8 %collective-permute-start.16 = (bf16[8,128,128]{2,1,0:T(8,128)(2,1)S(1)}, bf16[8,128,128]{2,1,0:T(8,128)(2,1)S(1)}, u32[]{:S(2)}, u32[]{:S(2)}) collective-permute-start(bf16[8,128,128]{2,1,0:T(8,128)(2,1)S(1)} %get-tuple-element.72), channel_id=1, source_target_pairs={{0,8},{2,2},{4,12},{6,6},{8,0},{10,18},{12,4},{14,22},{16,24},{18,... | collective-permute-start | bytes 786440 | tf_op jit(solution)/shard_map/ppermute | solution.py:459
  57.8 7.0 %collective-permute-start.17 = (bf16[8,128,128]{2,1,0:T(8,128)(2,1)S(1)}, bf16[8,128,128]{2,1,0:T(8,128)(2,1)S(1)}, u32[]{:S(2)}, u32[]{:S(2)}) collective-permute-start(bf16[8,128,128]{2,1,0:T(8,128)(2,1)S(1)} %get-tuple-element.73), channel_id=1, source_target_pairs={{0,0},{2,10},{4,4},{6,14},{8,16},{10,2},{12,20},{14,6},{16,8},{18,... | collective-permute-start | bytes 786440 | tf_op jit(solution)/shard_map/ppermute | solution.py:459
  58.5 7.9 %collective-permute-start.8 = (bf16[384,128]{1,0:T(8,128)(2,1)S(1)}, bf16[384,128]{1,0:T(8,128)(2,1)S(1)}, u32[]{:S(2)}, u32[]{:S(2)}) collective-permute-start(bf16[384,128]{1,0:T(8,128)(2,1)S(1)} %get-tuple-element.61), channel_id=1, source_target_pairs={{0,2},{2,0},{4,6},{6,4},{8,10},{10,8},{12,14},{14,12},{16,18},{18,... | collective-permute-start | bytes 294920 | tf_op jit(solution)/shard_map/ppermute | solution.py:452
  60.5 7.4 %collective-permute-start.9 = (bf16[384,128]{1,0:T(8,128)(2,1)S(1)}, bf16[384,128]{1,0:T(8,128)(2,1)S(1)}, u32[]{:S(2)}, u32[]{:S(2)}) collective-permute-start(bf16[384,128]{1,0:T(8,128)(2,1)S(1)} %get-tuple-element.62), channel_id=1, source_target_pairs={{0,4},{2,6},{4,0},{6,2},{8,12},{10,14},{12,8},{14,10},{16,20},{18,... | collective-permute-start | bytes 294920 | tf_op jit(solution)/shard_map/ppermute | solution.py:452
  62.1 5.8 %collective-permute-start.10 = (bf16[384,128]{1,0:T(8,128)(2,1)S(1)}, bf16[384,128]{1,0:T(8,128)(2,1)S(1)}, u32[]{:S(2)}, u32[]{:S(2)}) collective-permute-start(bf16[384,128]{1,0:T(8,128)(2,1)S(1)} %get-tuple-element.63), channel_id=1, source_target_pairs={{0,6},{2,4},{4,2},{6,0},{8,14},{10,12},{12,10},{14,8},{16,22},{18,... | collective-permute-start | bytes 294920 | tf_op jit(solution)/shard_map/ppermute | solution.py:452
  64.7 10.4 %collective-permute-start.13 = (bf16[384,128]{1,0:T(8,128)(2,1)S(1)}, bf16[384,128]{1,0:T(8,128)(2,1)S(1)}, u32[]{:S(2)}, u32[]{:S(2)}) collective-permute-start(bf16[384,128]{1,0:T(8,128)(2,1)S(1)} %get-tuple-element.68), channel_id=1, source_target_pairs={{0,2},{2,0},{4,6},{6,4},{8,10},{10,8},{12,14},{14,12},{16,18},{18,... | collective-permute-start | bytes 294920 | tf_op jit(solution)/shard_map/ppermute | solution.py:452
  64.9 4.4 %collective-permute-start.18 = (bf16[192,128]{1,0:T(8,128)(2,1)S(1)}, bf16[192,128]{1,0:T(8,128)(2,1)S(1)}, u32[]{:S(2)}, u32[]{:S(2)}) collective-permute-start(bf16[192,128]{1,0:T(8,128)(2,1)S(1)} %get-tuple-element.75), channel_id=1, source_target_pairs={{0,2},{2,0},{4,6},{6,4},{8,10},{10,8},{12,14},{14,12},{16,18},{18,... | collective-permute-start | bytes 147464 | tf_op jit(solution)/shard_map/ppermute | solution.py:452
  66.4 8.7 %collective-permute-start.14 = (bf16[384,128]{1,0:T(8,128)(2,1)S(1)}, bf16[384,128]{1,0:T(8,128)(2,1)S(1)}, u32[]{:S(2)}, u32[]{:S(2)}) collective-permute-start(bf16[384,128]{1,0:T(8,128)(2,1)S(1)} %get-tuple-element.69), channel_id=1, source_target_pairs={{0,4},{2,6},{4,0},{6,2},{8,12},{10,14},{12,8},{14,10},{16,20},{18,... | collective-permute-start | bytes 294920 | tf_op jit(solution)/shard_map/ppermute | solution.py:452
  67.9 7.2 %collective-permute-start.15 = (bf16[384,128]{1,0:T(8,128)(2,1)S(1)}, bf16[384,128]{1,0:T(8,128)(2,1)S(1)}, u32[]{:S(2)}, u32[]{:S(2)}) collective-permute-start(bf16[384,128]{1,0:T(8,128)(2,1)S(1)} %get-tuple-element.70), channel_id=1, source_target_pairs={{0,6},{2,4},{4,2},{6,0},{8,14},{10,12},{12,10},{14,8},{16,22},{18,... | collective-permute-start | bytes 294920 | tf_op jit(solution)/shard_map/ppermute | solution.py:452
  67.9 6.7 %collective-permute-start.19 = (bf16[192,128]{1,0:T(8,128)(2,1)S(1)}, bf16[192,128]{1,0:T(8,128)(2,1)S(1)}, u32[]{:S(2)}, u32[]{:S(2)}) collective-permute-start(bf16[192,128]{1,0:T(8,128)(2,1)S(1)} %get-tuple-element.76), channel_id=1, source_target_pairs={{0,4},{2,6},{4,0},{6,2},{8,12},{10,14},{12,8},{14,10},{16,20},{18,... | collective-permute-start | bytes 147464 | tf_op jit(solution)/shard_map/ppermute | solution.py:452
  69.3 5.7 %collective-permute-start.20 = (bf16[192,128]{1,0:T(8,128)(2,1)S(1)}, bf16[192,128]{1,0:T(8,128)(2,1)S(1)}, u32[]{:S(2)}, u32[]{:S(2)}) collective-permute-start(bf16[192,128]{1,0:T(8,128)(2,1)S(1)} %get-tuple-element.77), channel_id=1, source_target_pairs={{0,6},{2,4},{4,2},{6,0},{8,14},{10,12},{12,10},{14,8},{16,22},{18,... | collective-permute-start | bytes 147464 | tf_op jit(solution)/shard_map/ppermute | solution.py:452
  76.3 11.2 %collective-permute-start.24 = (bf16[192,1024]{1,0:T(8,128)(2,1)S(1)}, bf16[192,1024]{1,0:T(8,128)(2,1)S(1)}, u32[]{:S(2)}, u32[]{:S(2)}) collective-permute-start(bf16[192,1024]{1,0:T(8,128)(2,1)S(1)} %shard_map.109), channel_id=1, source_target_pairs={{0,1},{1,0},{2,3},{3,2},{4,5},{5,4},{6,7},{7,6},{8,9},{9,8},{10,11... | collective-permute-start | bytes 1179656 | tf_op jit(solution)/shard_map/ppermute | solution.py:606
  77.8 1.9 %collective-permute-start.21 = (bf16[192,128]{1,0:T(8,128)(2,1)S(1)}, bf16[192,128]{1,0:T(8,128)(2,1)S(1)}, u32[]{:S(2)}, u32[]{:S(2)}) collective-permute-start(bf16[192,128]{1,0:T(8,128)(2,1)S(1)} %get-tuple-element.79), channel_id=1, source_target_pairs={{0,2},{2,0},{4,6},{6,4},{8,10},{10,8},{12,14},{14,12},{16,18},{18,... | collective-permute-start | bytes 147464 | tf_op jit(solution)/shard_map/ppermute | solution.py:452
  77.9 4.2 %collective-permute-start.22 = (bf16[192,128]{1,0:T(8,128)(2,1)S(1)}, bf16[192,128]{1,0:T(8,128)(2,1)S(1)}, u32[]{:S(2)}, u32[]{:S(2)}) collective-permute-start(bf16[192,128]{1,0:T(8,128)(2,1)S(1)} %get-tuple-element.80), channel_id=1, source_target_pairs={{0,4},{2,6},{4,0},{6,2},{8,12},{10,14},{12,8},{14,10},{16,20},{18,... | collective-permute-start | bytes 147464 | tf_op jit(solution)/shard_map/ppermute | solution.py:452
  79.2 3.8 %collective-permute-start.23 = (bf16[192,128]{1,0:T(8,128)(2,1)S(1)}, bf16[192,128]{1,0:T(8,128)(2,1)S(1)}, u32[]{:S(2)}, u32[]{:S(2)}) collective-permute-start(bf16[192,128]{1,0:T(8,128)(2,1)S(1)} %get-tuple-element.81), channel_id=1, source_target_pairs={{0,6},{2,4},{4,2},{6,0},{8,14},{10,12},{12,10},{14,8},{16,22},{18,... | collective-permute-start | bytes 147464 | tf_op jit(solution)/shard_map/ppermute | solution.py:452

commit v6 on v5

--- a/solution.py
+++ b/solution.py
@@ -455,8 +455,13 @@
         pairs = []
         for n in range(devices):
             other = n - GROUP if (n // GROUP + n + turn) % 2 else n + GROUP
-            pairs.append((n, other if 0 <= other < devices else n))
-        return lax.ppermute(x, "var", pairs)
+            for h in range(heads):
+                if 0 <= other < devices:
+                    target = other * heads + h
+                else:
+                    target = n * heads + (h ^ 1) % heads
+                pairs.append((n * heads + h, target))
+        return lax.ppermute(x, ("var", "head"), pairs)
 
     def trade_first(x):
         return trade_level(x, 0)

time: 88.8 us -> 83.4 us (0.939)
  starting transfers between devices: 33.8 us -> 23 us
  waiting for transfers between devices: 27.7 us -> 33.3 us
    ppermute x18, starting transfers between devices: 18.2 us -> 12.5 us  [trade(): return lax.ppermute(x, 'var', [(n, n ^ distance) for n in range(devices)])]
    ppermute x6, starting transfers between devices: 14.1 us -> 9.08 us  [trade_level(): return lax.ppermute(x, ('var', 'head'), pairs)]
    ppermute x6, waiting for transfers between devices: 2 us -> 6.9 us  [trade_level(): return lax.ppermute(x, ('var', 'head'), pairs)]
  transfers between devices with their start and end apart: 25 -> 25, of which waited for: 10 -> 12; matrix products, arithmetic and copies ran while one was open for 0% -> 0% of each run, Pallas kernels for 3% -> 3%
where the time goes in v6:
time: 83.4 us; the launch traced here: 83.1 us
  waiting for transfers between devices  33.3 us (40%)
  starting transfers between devices  23 us (28%)
  Pallas kernels  21.5 us (26%)
  local copies, waits for them, and re-layouts  3.71 us (4%)
  other arithmetic  0.86 us (1%)
    ppermute x18, waiting for transfers between devices, trade(): return lax.ppermute(x, 'var', [(n, n ^ distance) for n in range(devices)])  23.6 us
    pallas_call x1, Pallas kernels, body(): pl.pallas_call(functools.partial(attend_kernel, blocks_here, head_dim), o...  14.3 us
    ppermute x18, starting transfers between devices, trade(): return lax.ppermute(x, 'var', [(n, n ^ distance) for n in range(devices)])  12.5 us
    ppermute x6, starting transfers between devices, trade_level(): return lax.ppermute(x, ('var', 'head'), pairs)  9.08 us
    ppermute x6, waiting for transfers between devices, trade_level(): return lax.ppermute(x, ('var', 'head'), pairs)  6.9 us
    unnamed x13, local copies, waits for them, and re-layouts  3.71 us
    ppermute x1, waiting for transfers between devices, body(): lax.ppermute(send, 'head', [(n, (n + piece + 1) % heads) for n in range(h...  2.82 us
    pallas_call x1, Pallas kernels, body(): pl.pallas_call(pack_kv_kernel, out_shape=(shaped((rows, wide)),) * GROUP,...  2.47 us
  transfers between devices with their start and end apart: 25, of which 12 were waited for; matrix products, arithmetic and copies ran while one was open for 0% of the time, Pallas kernels for 3%

profile of v6, /device:TPU:0, one launch (start us, length us, event | category | flops | bytes accessed | tf_op | source)
XLA Modules:
  0.0 83.1 jit_solution(15453787766210489214)
XLA Ops:
  0.6 2.5 %shard_map.102 = (bf16[384,256]{1,0:T(8,128)(2,1)}, bf16[384,256]{1,0:T(8,128)(2,1)}, bf16[384,256]{1,0:T(8,128)(2,1)}, bf16[384,256]{1,0:T(8,128)(2,1)}) custom-call(bf16[384,512]{1,0:T(8,128)(2,1)} %k_hbm.1, bf16[384,512]{1,0:T(8,128)(2,1)} %v_hbm.1), custom_call_target="tpu_custom_call" | custom-call | flops 100663296 | bytes 1966080 | tf_op jit(solution)/shard_map/pallas_call | solution.py:489
  3.1 0.5 collective-permute-start
  3.6 2.6 %collective-permute-start.1 = (bf16[384,256]{1,0:T(8,128)(2,1)}, bf16[384,256]{1,0:T(8,128)(2,1)S(1)}, u32[]{:S(2)}, u32[]{:S(2)}) collective-permute-start(bf16[384,256]{1,0:T(8,128)(2,1)} %get-tuple-element.48), channel_id=1, source_target_pairs={{0,4},{2,6},{4,0},{6,2},{8,12},{10,14},{12,8},{14,10},{16,20},{18,... | collective-permute-start | bytes 589832 | tf_op jit(solution)/shard_map/ppermute | solution.py:452
  6.2 0.1 collective-permute-start.2
  6.3 0.0 collective-permute-done.after_ref.refs_1_
  6.3 1.0 %copy-done.1 = bf16[384,512]{1,0:T(8,128)(2,1)S(1)} copy-done((bf16[384,512]{1,0:T(8,128)(2,1)S(1)}, bf16[384,512]{1,0:T(8,128)(2,1)}, u32[]{:S(2)}) %copy-start.1) | copy-done | bytes 393240
  7.3 1.0 %copy-done.2 = bf16[384,512]{1,0:T(8,128)(2,1)S(1)} copy-done((bf16[384,512]{1,0:T(8,128)(2,1)S(1)}, bf16[384,512]{1,0:T(8,128)(2,1)}, u32[]{:S(2)}) %copy-start.2) | copy-done | bytes 393240
  8.3 0.9 %copy-done.3 = bf16[384,256]{1,0:T(8,128)(2,1)S(1)} copy-done((bf16[384,256]{1,0:T(8,128)(2,1)S(1)}, bf16[384,256]{1,0:T(8,128)(2,1)}, u32[]{:S(2)}) %copy-start.3) | copy-done | bytes 196632
  9.2 0.7 copy-done.4
  9.9 0.5 shard_map.103
  10.4 1.8 %collective-permute-done.1.refs_2_ = bf16[384,256]{1,0:T(8,128)(2,1)S(1)} collective-permute-done((bf16[384,256]{1,0:T(8,128)(2,1)}, bf16[384,256]{1,0:T(8,128)(2,1)S(1)}, u32[]{:S(2)}, u32[]{:S(2)}) %collective-permute-start.1) | collective-permute-done | bytes 196640 | tf_op jit(solution)/shard_map/ppermute | solution.py:452
  12.2 3.7 %collective-permute-done.2.refs_3_ = bf16[384,256]{1,0:T(8,128)(2,1)S(1)} collective-permute-done((bf16[384,256]{1,0:T(8,128)(2,1)}, bf16[384,256]{1,0:T(8,128)(2,1)S(1)}, u32[]{:S(2)}, u32[]{:S(2)}) %collective-permute-start.2) | collective-permute-done | bytes 196640 | tf_op jit(solution)/shard_map/ppermute | solution.py:452
  15.9 0.9 %shard_map.104 = (bf16[1936,256]{1,0:T(8,128)(2,1)S(1)}, bf16[1024,256]{1,0:T(8,128)(2,1)}, bf16[1024,256]{1,0:T(8,128)(2,1)S(1)}, bf16[400,256]{1,0:T(8,128)(2,...) custom-call(bf16[384,256]{1,0:T(8,128)(2,1)S(1)} %get-tuple-element., ...), custom_call_target="tpu_custom_call", output_to_operand_aliasing={{3}: (5, {}), {4}: (6, {}), {5}: (7, {})} | custom-call | bytes 1966080 | tf_op jit(solution)/shard_map/pallas_call | solution.py:510
  16.8 1.6 %collective-permute-start.3 = (bf16[1024,256]{1,0:T(8,128)(2,1)}, bf16[1024,256]{1,0:T(8,128)(2,1)S(1)}, u32[]{:S(2)}, u32[]{:S(2)}) collective-permute-start(bf16[1024,256]{1,0:T(8,128)(2,1)} %get-tuple-element.55), channel_id=1, source_target_pairs={{0,8},{1,9},{2,3},{3,2},{4,12},{5,13},{6,7},{7,6},{8,0},{9,1},{10,... | collective-permute-start | bytes 1572872 | tf_op jit(solution)/shard_map/ppermute | solution.py:464
  18.5 1.5 %collective-permute-start.4 = (bf16[1024,256]{1,0:T(8,128)(2,1)S(1)}, bf16[1024,256]{1,0:T(8,128)(2,1)S(1)}, u32[]{:S(2)}, u32[]{:S(2)}) collective-permute-start(bf16[1024,256]{1,0:T(8,128)(2,1)S(1)} %get-tuple-element.56), channel_id=1, source_target_pairs={{0,1},{1,0},{2,10},{3,11},{4,5},{5,4},{6,14},{7,15},{8,16},{9,17},... | collective-permute-start | bytes 1572872 | tf_op jit(solution)/shard_map/ppermute | solution.py:464
  19.9 0.0 collective-permute-start.5
  19.9 1.5 %collective-permute-start.6 = (bf16[400,256]{1,0:T(8,128)(2,1)S(1)}, bf16[400,256]{1,0:T(8,128)(2,1)}, u32[]{:S(2)}, u32[]{:S(2)}) collective-permute-start(bf16[400,256]{1,0:T(8,128)(2,1)S(1)} %get-tuple-element.58), channel_id=1, source_target_pairs={{0,4},{2,6},{4,0},{6,2},{8,12},{10,14},{12,8},{14,10},{16,20},{18,... | collective-permute-start | bytes 614408 | tf_op jit(solution)/shard_map/ppermute | solution.py:452
  21.5 0.3 collective-permute-start.7
  21.8 0.1 copy.14.kb_ref
  21.9 0.0 collective-permute-done.5.refs_3_
  21.9 6.0 %collective-permute-done.6.refs_4_ = bf16[400,256]{1,0:T(8,128)(2,1)} collective-permute-done((bf16[400,256]{1,0:T(8,128)(2,1)S(1)}, bf16[400,256]{1,0:T(8,128)(2,1)}, u32[]{:S(2)}, u32[]{:S(2)}) %collective-permute-start.6) | collective-permute-done | bytes 204832 | tf_op jit(solution)/shard_map/ppermute | solution.py:452
  27.9 3.6 %collective-permute-done.7.refs_5_ = bf16[400,256]{1,0:T(8,128)(2,1)} collective-permute-done((bf16[400,256]{1,0:T(8,128)(2,1)S(1)}, bf16[400,256]{1,0:T(8,128)(2,1)}, u32[]{:S(2)}, u32[]{:S(2)}) %collective-permute-start.7) | collective-permute-done | bytes 204832 | tf_op jit(solution)/shard_map/ppermute | solution.py:452
  31.5 0.0 collective-permute-done.3.refs_1_
  31.6 0.0 collective-permute-done.4.refs_2_
  31.6 14.3 %shard_map.105 = (f32[12,128,128]{2,1,0:T(8,128)S(1)}, bf16[8,128,128]{2,1,0:T(8,128)(2,1)S(1)}, bf16[8,128,128]{2,1,0:T(8,128)(2,1)S(1)}, f32[12,128,128]{2,1,0...) custom-call(s32[48,8]{1,0:T(8,128)S(1)} %copy.14.kb_ref, ...), custom_call_target="tpu_custom_call" | custom-call | flops 8053063680 | bytes 2000000 | tf_op jit(solution)/shard_map/pallas_call | solution.py:527
  45.8 1.7 %collective-permute-start.11 = (bf16[8,128,128]{2,1,0:T(8,128)(2,1)S(1)}, bf16[8,128,128]{2,1,0:T(8,128)(2,1)S(1)}, u32[]{:S(2)}, u32[]{:S(2)}) collective-permute-start(bf16[8,128,128]{2,1,0:T(8,128)(2,1)S(1)} %get-tuple-element.65), channel_id=1, source_target_pairs={{0,8},{1,9},{2,3},{3,2},{4,12},{5,13},{6,7},{7,6},{8,0},{9,1},{10,... | collective-permute-start | bytes 786440 | tf_op jit(solution)/shard_map/ppermute | solution.py:464
  47.6 1.5 %collective-permute-start.12 = (bf16[8,128,128]{2,1,0:T(8,128)(2,1)S(1)}, bf16[8,128,128]{2,1,0:T(8,128)(2,1)S(1)}, u32[]{:S(2)}, u32[]{:S(2)}) collective-permute-start(bf16[8,128,128]{2,1,0:T(8,128)(2,1)S(1)} %get-tuple-element.66), channel_id=1, source_target_pairs={{0,1},{1,0},{2,10},{3,11},{4,5},{5,4},{6,14},{7,15},{8,16},{9,17},... | collective-permute-start | bytes 786440 | tf_op jit(solution)/shard_map/ppermute | solution.py:464
  49.1 1.6 %collective-permute-start.16 = (bf16[8,128,128]{2,1,0:T(8,128)(2,1)S(1)}, bf16[8,128,128]{2,1,0:T(8,128)(2,1)S(1)}, u32[]{:S(2)}, u32[]{:S(2)}) collective-permute-start(bf16[8,128,128]{2,1,0:T(8,128)(2,1)S(1)} %get-tuple-element.72), channel_id=1, source_target_pairs={{0,8},{1,9},{2,3},{3,2},{4,12},{5,13},{6,7},{7,6},{8,0},{9,1},{10,... | collective-permute-start | bytes 786440 | tf_op jit(solution)/shard_map/ppermute | solution.py:464
  50.7 1.1 %collective-permute-start.17 = (bf16[8,128,128]{2,1,0:T(8,128)(2,1)S(1)}, bf16[8,128,128]{2,1,0:T(8,128)(2,1)S(1)}, u32[]{:S(2)}, u32[]{:S(2)}) collective-permute-start(bf16[8,128,128]{2,1,0:T(8,128)(2,1)S(1)} %get-tuple-element.73), channel_id=1, source_target_pairs={{0,1},{1,0},{2,10},{3,11},{4,5},{5,4},{6,14},{7,15},{8,16},{9,17},... | collective-permute-start | bytes 786440 | tf_op jit(solution)/shard_map/ppermute | solution.py:464
  51.8 0.0 collective-permute-start.8
  51.8 2.9 %collective-permute-done.11.first_ref = bf16[8,128,128]{2,1,0:T(8,128)(2,1)S(1)} collective-permute-done((bf16[8,128,128]{2,1,0:T(8,128)(2,1)S(1)}, bf16[8,128,128]{2,1,0:T(8,128)(2,1)S(1)}, u32[]{:S(2)}, u32[]{:S(2)}) %collective-permute-start.11) | collective-permute-done | bytes 262176 | tf_op jit(solution)/shard_map/ppermute | solution.py:464
  54.7 1.5 %collective-permute-start.9 = (bf16[384,128]{1,0:T(8,128)(2,1)S(1)}, bf16[384,128]{1,0:T(8,128)(2,1)S(1)}, u32[]{:S(2)}, u32[]{:S(2)}) collective-permute-start(bf16[384,128]{1,0:T(8,128)(2,1)S(1)} %get-tuple-element.62), channel_id=1, source_target_pairs={{0,4},{2,6},{4,0},{6,2},{8,12},{10,14},{12,8},{14,10},{16,20},{18,... | collective-permute-start | bytes 294920 | tf_op jit(solution)/shard_map/ppermute | solution.py:452
  56.2 0.6 collective-permute-done.12.second_ref
  56.8 0.0 collective-permute-start.10
  56.8 0.2 shard_map.106
  57.0 3.3 %collective-permute-done.16.first_ref = bf16[8,128,128]{2,1,0:T(8,128)(2,1)S(1)} collective-permute-done((bf16[8,128,128]{2,1,0:T(8,128)(2,1)S(1)}, bf16[8,128,128]{2,1,0:T(8,128)(2,1)S(1)}, u32[]{:S(2)}, u32[]{:S(2)}) %collective-permute-start.16) | collective-permute-done | bytes 262176 | tf_op jit(solution)/shard_map/ppermute | solution.py:464
  60.3 0.0 collective-permute-start.13
  60.3 0.0 collective-permute-done.17.second_ref
  60.4 0.2 shard_map.107
  60.5 0.6 collective-permute-start.18
  61.1 0.0 collective-permute-done.8.refs_1_
  61.1 1.5 %collective-permute-start.14 = (bf16[384,128]{1,0:T(8,128)(2,1)S(1)}, bf16[384,128]{1,0:T(8,128)(2,1)S(1)}, u32[]{:S(2)}, u32[]{:S(2)}) collective-permute-start(bf16[384,128]{1,0:T(8,128)(2,1)S(1)} %get-tuple-element.69), channel_id=1, source_target_pairs={{0,4},{2,6},{4,0},{6,2},{8,12},{10,14},{12,8},{14,10},{16,20},{18,... | collective-permute-start | bytes 294920 | tf_op jit(solution)/shard_map/ppermute | solution.py:452
  62.6 0.0 collective-permute-done.9.refs_2_
  62.6 0.0 collective-permute-start.15
  62.6 0.0 collective-permute-done.10.refs_3_
  62.6 1.4 %collective-permute-start.19 = (bf16[192,128]{1,0:T(8,128)(2,1)S(1)}, bf16[192,128]{1,0:T(8,128)(2,1)S(1)}, u32[]{:S(2)}, u32[]{:S(2)}) collective-permute-start(bf16[192,128]{1,0:T(8,128)(2,1)S(1)} %get-tuple-element.76), channel_id=1, source_target_pairs={{0,4},{2,6},{4,0},{6,2},{8,12},{10,14},{12,8},{14,10},{16,20},{18,... | collective-permute-start | bytes 147464 | tf_op jit(solution)/shard_map/ppermute | solution.py:452
  64.0 0.0 collective-permute-done.18.refs_9_
  64.0 0.6 collective-permute-start.20
  64.6 4.7 %collective-permute-done.19.refs_10_ = bf16[192,128]{1,0:T(8,128)(2,1)S(1)} collective-permute-done((bf16[192,128]{1,0:T(8,128)(2,1)S(1)}, bf16[192,128]{1,0:T(8,128)(2,1)S(1)}, u32[]{:S(2)}, u32[]{:S(2)}) %collective-permute-start.19) | collective-permute-done | bytes 49184 | tf_op jit(solution)/shard_map/ppermute | solution.py:452
  69.4 0.4 collective-permute-done.20.refs_11_
  69.8 0.0 collective-permute-done.13.refs_5_
  69.8 0.0 collective-permute-done.14.refs_6_
  69.8 0.0 collective-permute-done.15.refs_7_
  69.8 1.2 %shard_map.109 = bf16[192,1024]{1,0:T(8,128)(2,1)S(1)} custom-call(bf16[384,128]{1,0:T(8,128)(2,1)S(1)} %get-tuple-element.60.refs_0_, bf16[384,128]{1,0:T(8,128)(2,1)S(1)} %collective-permute-done.8.refs_1_, bf16[384,128]{1,0:T(8,128)(2,1)S(1)} %collective-permute-done.9.refs_2_, bf16[384,128]{1,0:T(8,128)(2,1)S(1)} %collective-permute-done.10.refs_3_, ...), custom_call_target="tpu_custom_call" | custom-call | flops 603979776 | bytes 4000000 | tf_op jit(solution)/shard_map/pallas_call | solution.py:588
  71.0 1.4 %collective-permute-start.24 = (bf16[192,1024]{1,0:T(8,128)(2,1)S(1)}, bf16[192,1024]{1,0:T(8,128)(2,1)S(1)}, u32[]{:S(2)}, u32[]{:S(2)}) collective-permute-start(bf16[192,1024]{1,0:T(8,128)(2,1)S(1)} %shard_map.109), channel_id=1, source_target_pairs={{0,1},{1,0},{2,3},{3,2},{4,5},{5,4},{6,7},{7,6},{8,9},{9,8},{10,11... | collective-permute-start | bytes 1179656 | tf_op jit(solution)/shard_map/ppermute | solution.py:611
  72.4 0.0 collective-permute-start.21
  72.4 1.3 %collective-permute-start.22 = (bf16[192,128]{1,0:T(8,128)(2,1)S(1)}, bf16[192,128]{1,0:T(8,128)(2,1)S(1)}, u32[]{:S(2)}, u32[]{:S(2)}) collective-permute-start(bf16[192,128]{1,0:T(8,128)(2,1)S(1)} %get-tuple-element.80), channel_id=1, source_target_pairs={{0,4},{2,6},{4,0},{6,2},{8,12},{10,14},{12,8},{14,10},{16,20},{18,... | collective-permute-start | bytes 147464 | tf_op jit(solution)/shard_map/ppermute | solution.py:452
  73.8 0.5 collective-permute-start.23
  74.3 0.0 collective-permute-done.21.refs_13_
  74.3 2.3 %collective-permute-done.22.refs_14_ = bf16[192,128]{1,0:T(8,128)(2,1)S(1)} collective-permute-done((bf16[192,128]{1,0:T(8,128)(2,1)S(1)}, bf16[192,128]{1,0:T(8,128)(2,1)S(1)}, u32[]{:S(2)}, u32[]{:S(2)}) %collective-permute-start.22) | collective-permute-done | bytes 49184 | tf_op jit(solution)/shard_map/ppermute | solution.py:452
  76.6 1.0 %collective-permute-done.23.refs_15_ = bf16[192,128]{1,0:T(8,128)(2,1)S(1)} collective-permute-done((bf16[192,128]{1,0:T(8,128)(2,1)S(1)}, bf16[192,128]{1,0:T(8,128)(2,1)S(1)}, u32[]{:S(2)}, u32[]{:S(2)}) %collective-permute-start.23) | collective-permute-done | bytes 49184 | tf_op jit(solution)/shard_map/ppermute | solution.py:452
  77.6 1.9 %shard_map.108 = (bf16[384,512]{1,0:T(8,128)(2,1)}, bf16[384,512]{1,0:T(8,128)(2,1)}, bf16[384,512]{1,0:T(8,128)(2,1)}, f32[192,1024]{1,0:T(8,128)S(1)}) custom-call(bf16[384,128]{1,0:T(8,128)(2,1)S(1)} %get-tuple-element.60.refs_0_, bf16[384,128]{1,0:T(8,128)(2,1)S(1)} %collective-permute-done.8.refs_1_, ...), custom_call_target="tpu_custom_call" | custom-call | flops 603979776 | bytes 6000000 | tf_op jit(solution)/shard_map/pallas_call | solution.py:599
  79.4 2.8 %collective-permute-done.24 = bf16[192,1024]{1,0:T(8,128)(2,1)S(1)} collective-permute-done((bf16[192,1024]{1,0:T(8,128)(2,1)S(1)}, bf16[192,1024]{1,0:T(8,128)(2,1)S(1)}, u32[]{:S(2)}, u32[]{:S(2)}) %collective-permute-start.24) | collective-permute-done | bytes 393248 | tf_op jit(solution)/shard_map/ppermute | solution.py:611
  82.2 0.9 %add_convert_fusion = bf16[192,1024]{1,0:T(8,128)(2,1)} fusion(f32[192,1024]{1,0:T(8,128)S(1)} %get-tuple-element.85, bf16[192,1024]{1,0:T(8,128)(2,1)S(1)} %collective-permute-done.24), kind=kLoop, calls=%fused_computation | loop fusion | flops 589824 | bytes 1572864 | tf_op jit(solution)/shard_map/convert_element_type | solution.py:613
  (8 shorter events, 0.0 us)
Async XLA Ops:
  0.6 21.2 %copy-start.5 = (s32[48,8]{0,1:T(8,128)S(1)}, s32[48,8]{0,1:T(8,128)}, u32[]{:S(2)}) copy-start(s32[48,8]{0,1:T(8,128)} %param.12) | copy-start | bytes 4612
  3.1 3.2 %collective-permute-start = (bf16[384,256]{1,0:T(8,128)(2,1)}, bf16[384,256]{1,0:T(8,128)(2,1)S(1)}, u32[]{:S(2)}, u32[]{:S(2)}) collective-permute-start(bf16[384,256]{1,0:T(8,128)(2,1)} %get-tuple-element.46), channel_id=1, source_target_pairs={{0,2},{2,0},{4,6},{6,4},{8,10},{10,8},{12,14},{14,12},{16,18},{18,... | collective-permute-start | bytes 589832 | tf_op jit(solution)/shard_map/ppermute | solution.py:452
  3.6 8.6 %collective-permute-start.1 = (bf16[384,256]{1,0:T(8,128)(2,1)}, bf16[384,256]{1,0:T(8,128)(2,1)S(1)}, u32[]{:S(2)}, u32[]{:S(2)}) collective-permute-start(bf16[384,256]{1,0:T(8,128)(2,1)} %get-tuple-element.48), channel_id=1, source_target_pairs={{0,4},{2,6},{4,0},{6,2},{8,12},{10,14},{12,8},{14,10},{16,20},{18,... | collective-permute-start | bytes 589832 | tf_op jit(solution)/shard_map/ppermute | solution.py:452
  6.2 9.7 %collective-permute-start.2 = (bf16[384,256]{1,0:T(8,128)(2,1)}, bf16[384,256]{1,0:T(8,128)(2,1)S(1)}, u32[]{:S(2)}, u32[]{:S(2)}) collective-permute-start(bf16[384,256]{1,0:T(8,128)(2,1)} %get-tuple-element.49), channel_id=1, source_target_pairs={{0,6},{2,4},{4,2},{6,0},{8,14},{10,12},{12,10},{14,8},{16,22},{18,... | collective-permute-start | bytes 589832 | tf_op jit(solution)/shard_map/ppermute | solution.py:452
  6.3 1.0 %copy-start.1 = (bf16[384,512]{1,0:T(8,128)(2,1)S(1)}, bf16[384,512]{1,0:T(8,128)(2,1)}, u32[]{:S(2)}) copy-start(bf16[384,512]{1,0:T(8,128)(2,1)} %q_ref.1) | copy-start | bytes 1179652
  7.3 1.0 %copy-start.2 = (bf16[384,512]{1,0:T(8,128)(2,1)S(1)}, bf16[384,512]{1,0:T(8,128)(2,1)}, u32[]{:S(2)}) copy-start(bf16[384,512]{1,0:T(8,128)(2,1)} %g_ref.1) | copy-start | bytes 1179652
  8.3 0.9 %copy-start.3 = (bf16[384,256]{1,0:T(8,128)(2,1)S(1)}, bf16[384,256]{1,0:T(8,128)(2,1)}, u32[]{:S(2)}) copy-start(bf16[384,256]{1,0:T(8,128)(2,1)} %get-tuple-element.45.mine_ref) | copy-start | bytes 589828
  9.2 0.7 copy-start.4
  16.8 14.7 %collective-permute-start.3 = (bf16[1024,256]{1,0:T(8,128)(2,1)}, bf16[1024,256]{1,0:T(8,128)(2,1)S(1)}, u32[]{:S(2)}, u32[]{:S(2)}) collective-permute-start(bf16[1024,256]{1,0:T(8,128)(2,1)} %get-tuple-element.55), channel_id=1, source_target_pairs={{0,8},{1,9},{2,3},{3,2},{4,12},{5,13},{6,7},{7,6},{8,0},{9,1},{10,... | collective-permute-start | bytes 1572872 | tf_op jit(solution)/shard_map/ppermute | solution.py:464
  18.5 13.1 %collective-permute-start.4 = (bf16[1024,256]{1,0:T(8,128)(2,1)S(1)}, bf16[1024,256]{1,0:T(8,128)(2,1)S(1)}, u32[]{:S(2)}, u32[]{:S(2)}) collective-permute-start(bf16[1024,256]{1,0:T(8,128)(2,1)S(1)} %get-tuple-element.56), channel_id=1, source_target_pairs={{0,1},{1,0},{2,10},{3,11},{4,5},{5,4},{6,14},{7,15},{8,16},{9,17},... | collective-permute-start | bytes 1572872 | tf_op jit(solution)/shard_map/ppermute | solution.py:464
  19.9 1.9 %collective-permute-start.5 = (bf16[400,256]{1,0:T(8,128)(2,1)S(1)}, bf16[400,256]{1,0:T(8,128)(2,1)S(1)}, u32[]{:S(2)}, u32[]{:S(2)}) collective-permute-start(bf16[400,256]{1,0:T(8,128)(2,1)S(1)} %get-tuple-element.57), channel_id=1, source_target_pairs={{0,2},{2,0},{4,6},{6,4},{8,10},{10,8},{12,14},{14,12},{16,18},{18,... | collective-permute-start | bytes 614408 | tf_op jit(solution)/shard_map/ppermute | solution.py:452
  19.9 8.0 %collective-permute-start.6 = (bf16[400,256]{1,0:T(8,128)(2,1)S(1)}, bf16[400,256]{1,0:T(8,128)(2,1)}, u32[]{:S(2)}, u32[]{:S(2)}) collective-permute-start(bf16[400,256]{1,0:T(8,128)(2,1)S(1)} %get-tuple-element.58), channel_id=1, source_target_pairs={{0,4},{2,6},{4,0},{6,2},{8,12},{10,14},{12,8},{14,10},{16,20},{18,... | collective-permute-start | bytes 614408 | tf_op jit(solution)/shard_map/ppermute | solution.py:452
  21.5 10.1 %collective-permute-start.7 = (bf16[400,256]{1,0:T(8,128)(2,1)S(1)}, bf16[400,256]{1,0:T(8,128)(2,1)}, u32[]{:S(2)}, u32[]{:S(2)}) collective-permute-start(bf16[400,256]{1,0:T(8,128)(2,1)S(1)} %get-tuple-element.59), channel_id=1, source_target_pairs={{0,6},{2,4},{4,2},{6,0},{8,14},{10,12},{12,10},{14,8},{16,22},{18,... | collective-permute-start | bytes 614408 | tf_op jit(solution)/shard_map/ppermute | solution.py:452
  31.6 38.2 %copy-start = (bf16[3,1024,512]{2,1,0:T(8,128)(2,1)S(1)}, bf16[3,1024,512]{2,1,0:T(8,128)(2,1)}, u32[]{:S(2)}) copy-start(bf16[3,1024,512]{2,1,0:T(8,128)(2,1)} %refs_12_.1) | copy-start | bytes 9437188
  45.8 8.9 %collective-permute-start.11 = (bf16[8,128,128]{2,1,0:T(8,128)(2,1)S(1)}, bf16[8,128,128]{2,1,0:T(8,128)(2,1)S(1)}, u32[]{:S(2)}, u32[]{:S(2)}) collective-permute-start(bf16[8,128,128]{2,1,0:T(8,128)(2,1)S(1)} %get-tuple-element.65), channel_id=1, source_target_pairs={{0,8},{1,9},{2,3},{3,2},{4,12},{5,13},{6,7},{7,6},{8,0},{9,1},{10,... | collective-permute-start | bytes 786440 | tf_op jit(solution)/shard_map/ppermute | solution.py:464
  47.6 9.2 %collective-permute-start.12 = (bf16[8,128,128]{2,1,0:T(8,128)(2,1)S(1)}, bf16[8,128,128]{2,1,0:T(8,128)(2,1)S(1)}, u32[]{:S(2)}, u32[]{:S(2)}) collective-permute-start(bf16[8,128,128]{2,1,0:T(8,128)(2,1)S(1)} %get-tuple-element.66), channel_id=1, source_target_pairs={{0,1},{1,0},{2,10},{3,11},{4,5},{5,4},{6,14},{7,15},{8,16},{9,17},... | collective-permute-start | bytes 786440 | tf_op jit(solution)/shard_map/ppermute | solution.py:464
  49.1 11.3 %collective-permute-start.16 = (bf16[8,128,128]{2,1,0:T(8,128)(2,1)S(1)}, bf16[8,128,128]{2,1,0:T(8,128)(2,1)S(1)}, u32[]{:S(2)}, u32[]{:S(2)}) collective-permute-start(bf16[8,128,128]{2,1,0:T(8,128)(2,1)S(1)} %get-tuple-element.72), channel_id=1, source_target_pairs={{0,8},{1,9},{2,3},{3,2},{4,12},{5,13},{6,7},{7,6},{8,0},{9,1},{10,... | collective-permute-start | bytes 786440 | tf_op jit(solution)/shard_map/ppermute | solution.py:464
  50.7 9.7 %collective-permute-start.17 = (bf16[8,128,128]{2,1,0:T(8,128)(2,1)S(1)}, bf16[8,128,128]{2,1,0:T(8,128)(2,1)S(1)}, u32[]{:S(2)}, u32[]{:S(2)}) collective-permute-start(bf16[8,128,128]{2,1,0:T(8,128)(2,1)S(1)} %get-tuple-element.73), channel_id=1, source_target_pairs={{0,1},{1,0},{2,10},{3,11},{4,5},{5,4},{6,14},{7,15},{8,16},{9,17},... | collective-permute-start | bytes 786440 | tf_op jit(solution)/shard_map/ppermute | solution.py:464
  51.8 9.3 %collective-permute-start.8 = (bf16[384,128]{1,0:T(8,128)(2,1)S(1)}, bf16[384,128]{1,0:T(8,128)(2,1)S(1)}, u32[]{:S(2)}, u32[]{:S(2)}) collective-permute-start(bf16[384,128]{1,0:T(8,128)(2,1)S(1)} %get-tuple-element.61), channel_id=1, source_target_pairs={{0,2},{2,0},{4,6},{6,4},{8,10},{10,8},{12,14},{14,12},{16,18},{18,... | collective-permute-start | bytes 294920 | tf_op jit(solution)/shard_map/ppermute | solution.py:452
  54.7 7.9 %collective-permute-start.9 = (bf16[384,128]{1,0:T(8,128)(2,1)S(1)}, bf16[384,128]{1,0:T(8,128)(2,1)S(1)}, u32[]{:S(2)}, u32[]{:S(2)}) collective-permute-start(bf16[384,128]{1,0:T(8,128)(2,1)S(1)} %get-tuple-element.62), channel_id=1, source_target_pairs={{0,4},{2,6},{4,0},{6,2},{8,12},{10,14},{12,8},{14,10},{16,20},{18,... | collective-permute-start | bytes 294920 | tf_op jit(solution)/shard_map/ppermute | solution.py:452
  56.8 5.8 %collective-permute-start.10 = (bf16[384,128]{1,0:T(8,128)(2,1)S(1)}, bf16[384,128]{1,0:T(8,128)(2,1)S(1)}, u32[]{:S(2)}, u32[]{:S(2)}) collective-permute-start(bf16[384,128]{1,0:T(8,128)(2,1)S(1)} %get-tuple-element.63), channel_id=1, source_target_pairs={{0,6},{2,4},{4,2},{6,0},{8,14},{10,12},{12,10},{14,8},{16,22},{18,... | collective-permute-start | bytes 294920 | tf_op jit(solution)/shard_map/ppermute | solution.py:452
  60.3 9.5 %collective-permute-start.13 = (bf16[384,128]{1,0:T(8,128)(2,1)S(1)}, bf16[384,128]{1,0:T(8,128)(2,1)S(1)}, u32[]{:S(2)}, u32[]{:S(2)}) collective-permute-start(bf16[384,128]{1,0:T(8,128)(2,1)S(1)} %get-tuple-element.68), channel_id=1, source_target_pairs={{0,2},{2,0},{4,6},{6,4},{8,10},{10,8},{12,14},{14,12},{16,18},{18,... | collective-permute-start | bytes 294920 | tf_op jit(solution)/shard_map/ppermute | solution.py:452
  60.5 3.5 %collective-permute-start.18 = (bf16[192,128]{1,0:T(8,128)(2,1)S(1)}, bf16[192,128]{1,0:T(8,128)(2,1)S(1)}, u32[]{:S(2)}, u32[]{:S(2)}) collective-permute-start(bf16[192,128]{1,0:T(8,128)(2,1)S(1)} %get-tuple-element.75), channel_id=1, source_target_pairs={{0,2},{2,0},{4,6},{6,4},{8,10},{10,8},{12,14},{14,12},{16,18},{18,... | collective-permute-start | bytes 147464 | tf_op jit(solution)/shard_map/ppermute | solution.py:452
  61.1 8.7 %collective-permute-start.14 = (bf16[384,128]{1,0:T(8,128)(2,1)S(1)}, bf16[384,128]{1,0:T(8,128)(2,1)S(1)}, u32[]{:S(2)}, u32[]{:S(2)}) collective-permute-start(bf16[384,128]{1,0:T(8,128)(2,1)S(1)} %get-tuple-element.69), channel_id=1, source_target_pairs={{0,4},{2,6},{4,0},{6,2},{8,12},{10,14},{12,8},{14,10},{16,20},{18,... | collective-permute-start | bytes 294920 | tf_op jit(solution)/shard_map/ppermute | solution.py:452
  62.6 7.2 %collective-permute-start.15 = (bf16[384,128]{1,0:T(8,128)(2,1)S(1)}, bf16[384,128]{1,0:T(8,128)(2,1)S(1)}, u32[]{:S(2)}, u32[]{:S(2)}) collective-permute-start(bf16[384,128]{1,0:T(8,128)(2,1)S(1)} %get-tuple-element.70), channel_id=1, source_target_pairs={{0,6},{2,4},{4,2},{6,0},{8,14},{10,12},{12,10},{14,8},{16,22},{18,... | collective-permute-start | bytes 294920 | tf_op jit(solution)/shard_map/ppermute | solution.py:452
  62.6 6.7 %collective-permute-start.19 = (bf16[192,128]{1,0:T(8,128)(2,1)S(1)}, bf16[192,128]{1,0:T(8,128)(2,1)S(1)}, u32[]{:S(2)}, u32[]{:S(2)}) collective-permute-start(bf16[192,128]{1,0:T(8,128)(2,1)S(1)} %get-tuple-element.76), channel_id=1, source_target_pairs={{0,4},{2,6},{4,0},{6,2},{8,12},{10,14},{12,8},{14,10},{16,20},{18,... | collective-permute-start | bytes 147464 | tf_op jit(solution)/shard_map/ppermute | solution.py:452
  64.0 5.7 %collective-permute-start.20 = (bf16[192,128]{1,0:T(8,128)(2,1)S(1)}, bf16[192,128]{1,0:T(8,128)(2,1)S(1)}, u32[]{:S(2)}, u32[]{:S(2)}) collective-permute-start(bf16[192,128]{1,0:T(8,128)(2,1)S(1)} %get-tuple-element.77), channel_id=1, source_target_pairs={{0,6},{2,4},{4,2},{6,0},{8,14},{10,12},{12,10},{14,8},{16,22},{18,... | collective-permute-start | bytes 147464 | tf_op jit(solution)/shard_map/ppermute | solution.py:452
  71.0 11.2 %collective-permute-start.24 = (bf16[192,1024]{1,0:T(8,128)(2,1)S(1)}, bf16[192,1024]{1,0:T(8,128)(2,1)S(1)}, u32[]{:S(2)}, u32[]{:S(2)}) collective-permute-start(bf16[192,1024]{1,0:T(8,128)(2,1)S(1)} %shard_map.109), channel_id=1, source_target_pairs={{0,1},{1,0},{2,3},{3,2},{4,5},{5,4},{6,7},{7,6},{8,9},{9,8},{10,11... | collective-permute-start | bytes 1179656 | tf_op jit(solution)/shard_map/ppermute | solution.py:611
  72.4 1.9 %collective-permute-start.21 = (bf16[192,128]{1,0:T(8,128)(2,1)S(1)}, bf16[192,128]{1,0:T(8,128)(2,1)S(1)}, u32[]{:S(2)}, u32[]{:S(2)}) collective-permute-start(bf16[192,128]{1,0:T(8,128)(2,1)S(1)} %get-tuple-element.79), channel_id=1, source_target_pairs={{0,2},{2,0},{4,6},{6,4},{8,10},{10,8},{12,14},{14,12},{16,18},{18,... | collective-permute-start | bytes 147464 | tf_op jit(solution)/shard_map/ppermute | solution.py:452
  72.4 4.2 %collective-permute-start.22 = (bf16[192,128]{1,0:T(8,128)(2,1)S(1)}, bf16[192,128]{1,0:T(8,128)(2,1)S(1)}, u32[]{:S(2)}, u32[]{:S(2)}) collective-permute-start(bf16[192,128]{1,0:T(8,128)(2,1)S(1)} %get-tuple-element.80), channel_id=1, source_target_pairs={{0,4},{2,6},{4,0},{6,2},{8,12},{10,14},{12,8},{14,10},{16,20},{18,... | collective-permute-start | bytes 147464 | tf_op jit(solution)/shard_map/ppermute | solution.py:452
  73.8 3.8 %collective-permute-start.23 = (bf16[192,128]{1,0:T(8,128)(2,1)S(1)}, bf16[192,128]{1,0:T(8,128)(2,1)S(1)}, u32[]{:S(2)}, u32[]{:S(2)}) collective-permute-start(bf16[192,128]{1,0:T(8,128)(2,1)S(1)} %get-tuple-element.81), channel_id=1, source_target_pairs={{0,6},{2,4},{4,2},{6,0},{8,14},{10,12},{12,10},{14,8},{16,22},{18,... | collective-permute-start | bytes 147464 | tf_op jit(solution)/shard_map/ppermute | solution.py:452

commit v7 on v6

--- a/solution.py
+++ b/solution.py
@@ -11,6 +11,7 @@
 BLOCK = 128
 HALF = BLOCK // 2
 SPAN = 8
+OUTER = SPAN // 2
 GROUP = 4
 LANES = 128
 LSE_ROWS = 16
@@ -173,17 +174,17 @@
         out[...] = own[pl.ds(pl.multiple_of(start * BLOCK, BLOCK), SPAN * BLOCK)]
 
 
-def attend_kernel(
-    blocks_here,
-    head_dim,
-    kb_ref,
-    *refs,
-):
-    kv_refs, refs = refs[:3], refs[3:]
-    qo_pieces, refs = refs[: GROUP - 1], refs[GROUP - 1 :]
-    key_outs, value_outs, refs = refs[:3], refs[3:6], refs[6:]
-    dq_outs, refs = refs[:GROUP], refs[GROUP:]
-    kv_win, k_turn, acc, shifts, queries, grads, crossed, prob, slope, qo_ref, dq_all = refs
+def attend_kernel(last, blocks_here, head_dim, kb_ref, *refs):
+    if last:
+        kv_win, k_turn, shifts, qo_ref, before, dq_before, *refs = refs
+        own_out, first_out, second_out, *refs = refs
+        dq_outs, refs = refs[:GROUP], refs[GROUP:]
+        acc, queries, grads, crossed, prob, slope, dq_all = refs
+    else:
+        kv_refs, refs = refs[:3], refs[3:]
+        qo_pieces, refs = refs[: GROUP - 1], refs[GROUP - 1 :]
+        first_out, second_out, kv_win, k_turn, shifts, qo_ref, kept_out, dq_all, *refs = refs
+        acc, queries, grads, crossed, prob, slope = refs
     group_blocks = GROUP * blocks_here
     window = group_blocks + 2 * SPAN
     rows = blocks_here * BLOCK
@@ -191,36 +192,38 @@
     scale = head_dim ** (-0.5)
     base = (lax.axis_index("var") // GROUP) * group_blocks
     odd = below_first()
-    top = window - SPAN
-    first_at, second_at = (1 - odd) * top, odd * top
     low = slice(0, LANES)
     high = slice(LANES, 2 * LANES)
 
-    for ref, start, count in zip(
-        kv_refs, (SPAN, first_at, second_at), (group_blocks, SPAN, SPAN)
-    ):
-        kv_win[pl.ds(start, count)] = ref[: count * BLOCK].reshape(count, BLOCK, 2 * LANES)
-    own_queries = kv_refs[0].at[pl.ds(group_blocks * BLOCK, rows + LSE_ROWS)]
-    stage_pieces(qo_ref, (own_queries, *qo_pieces))
-    key_patch = lax.broadcasted_iota(jnp.int32, (8, LANES), 0)
-    query_patch = lax.broadcasted_iota(jnp.int32, (8, LANES), 1) & 7
-    usable = key_patch <= query_patch
-    for member in range(GROUP):
-        parts = qo_ref[member, rows:].astype(F32)
-        for local in range(blocks_here):
-            lse = (
-                parts[local : local + 1] + parts[blocks_here + local : blocks_here + local + 1]
-            ) + parts[2 * blocks_here + local : 2 * blocks_here + local + 1]
-            at = member * blocks_here + local
-            shifts[at, 0, :, low] = jnp.where(usable, -lse[:, low], -1e30)
-            shifts[at, 0, :, high] = jnp.broadcast_to(-lse[:, high], (8, LANES))
-            shifts[at, 1, :, low] = jnp.where(usable, -lse[:, high], -1e30)
     acc[...] = jnp.zeros_like(acc)
     crossed[...] = jnp.zeros_like(crossed)
-
-    @pl.loop(0, window)
-    def _(block):
-        k_turn[block] = kv_win[block, :, low].T
+    if last:
+        dq_all[...] = dq_before[...]
+    else:
+        top = window - SPAN
+        for ref, start, count in zip(
+            kv_refs, (SPAN, (1 - odd) * top, odd * top), (group_blocks, SPAN, SPAN)
+        ):
+            kv_win[pl.ds(start, count)] = ref[: count * BLOCK].reshape(count, BLOCK, 2 * LANES)
+        own_queries = kv_refs[0].at[pl.ds(group_blocks * BLOCK, rows + LSE_ROWS)]
+        stage_pieces(qo_ref, (own_queries, *qo_pieces))
+        key_patch = lax.broadcasted_iota(jnp.int32, (8, LANES), 0)
+        query_patch = lax.broadcasted_iota(jnp.int32, (8, LANES), 1) & 7
+        usable = key_patch <= query_patch
+        for member in range(GROUP):
+            parts = qo_ref[member, rows:].astype(F32)
+            for local in range(blocks_here):
+                lse = (
+                    parts[local : local + 1] + parts[blocks_here + local : blocks_here + local + 1]
+                ) + parts[2 * blocks_here + local : 2 * blocks_here + local + 1]
+                at = member * blocks_here + local
+                shifts[at, 0, :, low] = jnp.where(usable, -lse[:, low], -1e30)
+                shifts[at, 0, :, high] = jnp.broadcast_to(-lse[:, high], (8, LANES))
+                shifts[at, 1, :, low] = jnp.where(usable, -lse[:, high], -1e30)
+
+        @pl.loop(0, window)
+        def _(block):
+            k_turn[block] = kv_win[block, :, low].T
 
     unorder = reorder_matrix(True)
     lane = lax.broadcasted_iota(jnp.int32, (HALF, LANES), 1)
@@ -305,34 +308,49 @@
         local = pl.multiple_of((query_block % blocks_here) * BLOCK, BLOCK)
         dq_all[query_block // blocks_here, pl.ds(local, BLOCK)] = moved
 
-    delta = forward(0, 0)
+    def block_of(j):
+        if last:
+            return j + OUTER
+        return j + jnp.where(j < OUTER, 0, group_blocks - 2 * OUTER)
+
+    count = group_blocks - 2 * OUTER if last else 2 * OUTER
+    delta = forward(block_of(0), 0)
 
     def step(j, delta):
-        block = 2 * j
-        later = forward(block + 1, 1)
-        backward(block, 0, delta)
-        last = forward(block + 2, 0)
-        backward(block + 1, 1, later)
-        return last
-
-    delta = lax.fori_loop(0, (group_blocks - 1) // 2, step, delta)
-    if group_blocks % 2 == 0:
-        later = forward(group_blocks - 1, 1)
-        backward(group_blocks - 2, 0, delta)
-        backward(group_blocks - 1, 1, later)
+        later = forward(block_of(2 * j + 1), 1)
+        backward(block_of(2 * j), 0, delta)
+        following = forward(block_of(2 * j + 2), 0)
+        backward(block_of(2 * j + 1), 1, later)
+        return following
+
+    delta = lax.fori_loop(0, (count - 1) // 2, step, delta)
+    if count % 2 == 0:
+        later = forward(block_of(count - 1), 1)
+        backward(block_of(count - 2), 0, delta)
+        backward(block_of(count - 1), 1, later)
     else:
-        backward(group_blocks - 1, 0, delta)
+        backward(block_of(count - 1), 0, delta)
 
     groups = BLOCK // 16
-    for cols, (own_out, first_out, second_out) in ((low, key_outs), (high, value_outs)):
-        for out, start, count in (
-            (first_out, first_at, SPAN),
-            (second_out, second_at, SPAN),
-            (own_out, SPAN, group_blocks),
-        ):
-            part = acc[pl.ds(start, count), :, cols].reshape(count, 2, groups, 8, LANES)
-            out[...] = jnp.swapaxes(part, 1, 2).reshape(count, BLOCK, LANES).astype(out.dtype)
-    send_pieces(dq_outs, dq_all)
+
+    def in_token_order(part):
+        blocks = part.shape[0]
+        part = part.reshape(blocks, 2, groups, 8, 2 * LANES)
+        return jnp.swapaxes(part, 1, 2).reshape(blocks, BLOCK, 2 * LANES)
+
+    if last:
+        acc[OUTER : window - OUTER] = acc[OUTER : window - OUTER] + before[...]
+        top = window - SPAN
+        for out, side in ((first_out, 1 - odd), (second_out, odd)):
+            start = OUTER + side * (top - OUTER)
+            out[...] = in_token_order(acc[pl.ds(start, OUTER)]).astype(BF16)
+        own_out[...] = in_token_order(acc[SPAN : SPAN + group_blocks])
+        send_pieces(dq_outs, dq_all)
+    else:
+        for out, side in ((first_out, 1 - odd), (second_out, odd)):
+            start = side * (window - OUTER)
+            out[...] = in_token_order(acc[pl.ds(start, OUTER)]).astype(BF16)
+        kept_out[...] = acc[OUTER : window - OUTER]
 
 
 def owner_start(piece, half):
@@ -340,35 +358,31 @@
     return pl.multiple_of(((lax.axis_index("head") + 1 + piece) % heads) * half, half)
 
 
-def add_parts(own_ref, first_ref, second_ref, total, moved):
-    group_blocks = own_ref.shape[0]
-    first, second = exchange_start(group_blocks)
-    total[...] = own_ref[...]
+def add_arrived(total, starts, refs):
     level = lax.axis_index("var") // GROUP
     levels = lax.axis_size("var") // GROUP
     odd = below_first()
-    for other, start, ref in (
-        (level + 1 - 2 * odd, first, first_ref),
-        (level - 1 + 2 * odd, second, second_ref),
-    ):
+    for side, ref in zip((1 - odd, odd), refs):
+        other = level - 1 + 2 * side
+        start = jnp.where(side == 1, starts[1], starts[0])
 
         @pl.when((other >= 0) & (other < levels))
         def _(start=start, ref=ref):
-            at = pl.ds(start, SPAN)
+            at = pl.ds(start, OUTER)
             total[at] = total[at] + ref[...].astype(F32)
 
+
+def combine_outer_kernel(carried, own_ref, first_ref, second_ref, *refs):
+    total = refs[carried]
+    total[...] = own_ref[...]
+    add_arrived(total, (SPAN - OUTER, own_ref.shape[0] - SPAN), (first_ref, second_ref))
+
+
+def combine_kernel(own_ref, first_ref, second_ref, *rest):
+    aways, homes, (total, moved) = rest[:GROUP], rest[GROUP : 2 * GROUP], rest[2 * GROUP :]
+    total[...] = own_ref[...]
+    add_arrived(total, (0, own_ref.shape[0] - OUTER), (first_ref, second_ref))
     moved[...] = total[...].astype(BF16).reshape(moved.shape)
-
-
-def combine_kernel(own_ref, first_ref, second_ref, *rest):
-    outs, (total, moved) = rest[:GROUP], rest[GROUP:]
-    add_parts(own_ref, first_ref, second_ref, total, moved)
-    send_pieces(outs, moved)
-
-
-def combine_split_kernel(own_ref, first_ref, second_ref, *rest):
-    aways, homes, (total, moved) = rest[:GROUP], rest[GROUP : 2 * GROUP], rest[2 * GROUP :]
-    add_parts(own_ref, first_ref, second_ref, total, moved)
     half = homes[0].shape[0]
     away = aways[0].shape[0] // half
     me = lax.axis_index("var") % GROUP
@@ -381,14 +395,15 @@
         homes[distance][...] = moved[member, pl.ds(owner_start(away, half), half)]
 
 
-def gather_rows(grads, stages, start, dv_stage, dv_at):
+def gather_rows(grads, dq, start, dkv, dkv_at):
     half = grads.shape[1]
     width = grads.shape[2] // GROUP
     for member in range(GROUP):
         at = slice(member * width, (member + 1) * width)
-        for s, stage in enumerate(stages):
-            grads[s, :, at] = stage[member, pl.ds(start, half)][:, :width]
-        grads[2, :, at] = dv_stage[member, dv_at * half : (dv_at + 1) * half][:, :width]
+        both = dkv[member, dkv_at * half : (dkv_at + 1) * half]
+        grads[0, :, at] = dq[member, pl.ds(start, half)][:, :width]
+        grads[1, :, at] = both[:, :width]
+        grads[2, :, at] = both[:, LANES : LANES + width]
 
 
 def product(grads, w_ref):
@@ -399,32 +414,30 @@
 
 
 def away_kernel(*refs):
-    dqs, dks, dvs, (w_ref, *rest) = refs[:4], refs[4:8], refs[8:12], refs[12:]
-    outs, (grads, dq, dk, dv) = rest[:-4], rest[-4:]
+    dqs, dkvs, (w_ref, *rest) = refs[:4], refs[4:8], refs[8:]
+    outs, (grads, dq, dkv) = rest[:-3], rest[-3:]
     half = grads.shape[1]
     stage_pieces(dq, dqs)
-    stage_pieces(dk, dks)
-    stage_pieces(dv, dvs)
+    stage_pieces(dkv, dkvs)
     for piece, out in enumerate(outs):
-        gather_rows(grads, (dq, dk), owner_start(piece, half), dv, piece)
+        gather_rows(grads, dq, owner_start(piece, half), dkv, piece)
         out[...] = product(grads, w_ref).astype(BF16)
 
 
 def home_kernel(*refs):
-    dqs, dks, aways, homes, rest = refs[:4], refs[4:8], refs[8:12], refs[12:16], refs[16:]
-    w_ref, dq_out, dk_out, dv_out, keep_out, grads, dq, dk, away_dv, home_dv = rest
+    dqs, aways, homes, rest = refs[:4], refs[4:8], refs[8:12], refs[12:]
+    w_ref, dq_out, dk_out, dv_out, keep_out, grads, dq, away_dkv, home_dkv = rest
     half = grads.shape[1]
-    away = away_dv.shape[1] // half
+    away = away_dkv.shape[1] // half
     stage_pieces(dq, dqs)
-    stage_pieces(dk, dks)
-    stage_pieces(away_dv, aways)
-    stage_pieces(home_dv, homes)
+    stage_pieces(away_dkv, aways)
+    stage_pieces(home_dkv, homes)
     for piece in range(away + 1):
         start = owner_start(piece, half)
         if piece < away:
-            gather_rows(grads, (dq, dk), start, away_dv, piece)
+            gather_rows(grads, dq, start, away_dkv, piece)
         else:
-            gather_rows(grads, (dq, dk), start, home_dv, 0)
+            gather_rows(grads, dq, start, home_dkv, 0)
         at = pl.ds(start, half)
         dq_out[at] = grads[0]
         dk_out[at] = grads[1]
@@ -523,64 +536,75 @@
     qos = swap([None, *carried])[1:]
 
     pairs = group_blocks * slot_count * BLOCK * BLOCK * slots
-    sums = (shaped((group_blocks,) + block, F32),) + (shaped((SPAN,) + block),) * 2
-    results = pl.pallas_call(
-        functools.partial(attend_kernel, blocks_here, head_dim),
-        out_shape=sums + sums + (shaped((rows, LANES)),) * GROUP,
-        in_specs=[pl.BlockSpec(memory_space=pltpu.SMEM)] + [vmem()] * (2 + GROUP),
-        out_specs=(vmem(),) * (6 + GROUP),
-        scratch_shapes=[
-            pltpu.VMEM((window, BLOCK, wide), BF16),
-            pltpu.VMEM((window, LANES, BLOCK), BF16),
-            pltpu.VMEM((window, BLOCK, wide), F32),
-            pltpu.VMEM((group_blocks, 2, 8, wide), F32),
-            pltpu.VMEM((2, wide, LANES), BF16),
-            pltpu.VMEM((2, wide, LANES), BF16),
-            pltpu.VMEM((2, wide, wide), BF16),
-            pltpu.VMEM((2, slot_count * BLOCK, wide), F32),
-            pltpu.VMEM((2, slot_count * BLOCK, wide), F32),
-            staged(rows + LSE_ROWS, wide),
-            staged(rows),
-        ],
+    tall = (BLOCK, wide)
+    acc_scratch = pltpu.VMEM((window,) + tall, F32)
+    work = [
+        pltpu.VMEM((2, wide, LANES), BF16),
+        pltpu.VMEM((2, wide, LANES), BF16),
+        pltpu.VMEM((2, wide, wide), BF16),
+        pltpu.VMEM((2, slot_count * BLOCK, wide), F32),
+        pltpu.VMEM((2, slot_count * BLOCK, wide), F32),
+    ]
+    smem = pl.BlockSpec(memory_space=pltpu.SMEM)
+    outer = (shaped((OUTER,) + tall),) * 2
+
+    def attend_cost(part):
+        return pl.CostEstimate(
+            flops=int(40 * pairs * head_dim * part),
+            bytes_accessed=2_000_000,
+            transcendentals=int(pairs * part),
+        )
+
+    state = (
+        shaped((window,) + tall),
+        shaped((window, LANES, BLOCK)),
+        shaped((group_blocks, 2, 8, wide), F32),
+        shaped((GROUP, rows + LSE_ROWS, wide)),
+        shaped((window - 2 * OUTER,) + tall, F32),
+        shaped((GROUP, rows, LANES)),
+    )
+    first, second, *state = pl.pallas_call(
+        functools.partial(attend_kernel, False, blocks_here, head_dim),
+        out_shape=outer + state,
+        in_specs=[smem] + [vmem()] * (2 + GROUP),
+        out_specs=(vmem(),) * 8,
+        scratch_shapes=[acc_scratch] + work,
         compiler_params=params(24),
-        cost_estimate=pl.CostEstimate(
-            flops=40 * pairs * head_dim, bytes_accessed=2_000_000, transcendentals=pairs
-        ),
-    )(
-        key_blocks,
-        own,
-        first,
-        second,
-        *qos,
-    )
-    key_sum, first_part, second_part = results[:3]
-    first_back = trade_first(first_part)
-    second_back = trade_second(second_part)
-    value_sum, first_part, second_part = results[3:6]
-    first_value_back = trade_first(first_part)
-    second_value_back = trade_second(second_part)
-    dqs = swap(results[6:])
-    summing = [pltpu.VMEM((group_blocks,) + block, F32), staged(rows)]
-    dks = swap(
-        pl.pallas_call(
-            combine_kernel,
-            out_shape=(shaped((rows, LANES)),) * GROUP,
-            in_specs=[vmem()] * 3,
-            out_specs=(vmem(),) * GROUP,
-            scratch_shapes=summing,
-            compiler_params=params(8),
-            cost_estimate=cost(0, 4 * size),
-        )(key_sum, first_back, second_back)
-    )
+        cost_estimate=attend_cost(0.67),
+    )(key_blocks, own, first, second, *qos)
+    outer_back = (trade_first(first), trade_second(second))
+    own_sum, first, second, *dqs = pl.pallas_call(
+        functools.partial(attend_kernel, True, blocks_here, head_dim),
+        out_shape=(shaped((group_blocks,) + tall, F32),)
+        + outer
+        + (shaped((rows, LANES)),) * GROUP,
+        in_specs=[smem] + [vmem()] * 6,
+        out_specs=(vmem(),) * (3 + GROUP),
+        scratch_shapes=[acc_scratch] + work + [staged(rows)],
+        compiler_params=params(24),
+        cost_estimate=attend_cost(0.33),
+    )(key_blocks, *state)
+    inner_back = (trade_first(first), trade_second(second))
+    carried = tuple(dqs[1:])
+    *carried, own_sum = pl.pallas_call(
+        functools.partial(combine_outer_kernel, 2 * len(carried)),
+        out_shape=tuple(shaped(x.shape) for x in carried) + (shaped((group_blocks,) + tall, F32),),
+        in_specs=[vmem()] * 3 + [anywhere] * len(carried),
+        out_specs=(anywhere,) * len(carried) + (vmem(),),
+        input_output_aliases={3 + i: i for i in range(len(carried))},
+        compiler_params=params(8),
+        cost_estimate=cost(0, 4 * size),
+    )(own_sum, *outer_back, *carried)
+    dqs = swap([dqs[0], *carried])
     split = pl.pallas_call(
-        combine_split_kernel,
-        out_shape=(shaped((rows - half, LANES)),) * GROUP + (shaped((half, LANES)),) * GROUP,
+        combine_kernel,
+        out_shape=(shaped((rows - half, wide)),) * GROUP + (shaped((half, wide)),) * GROUP,
         in_specs=[vmem()] * 3,
         out_specs=(vmem(),) * (2 * GROUP),
-        scratch_shapes=summing,
+        scratch_shapes=[pltpu.VMEM((group_blocks,) + tall, F32), staged(rows, wide)],
         compiler_params=params(8),
-        cost_estimate=cost(0, 4 * size),
-    )(value_sum, first_value_back, second_value_back)
+        cost_estimate=cost(0, 8 * size),
+    )(own_sum, *inner_back)
     aways = swap(split[:GROUP])
     homes = swap(split[GROUP:])
 
@@ -588,25 +612,21 @@
     sends = pl.pallas_call(
         away_kernel,
         out_shape=(shaped((half, model)),) * (heads - 1),
-        in_specs=[vmem()] * (3 * GROUP + 1),
+        in_specs=[vmem()] * (2 * GROUP + 1),
         out_specs=(vmem(),) * (heads - 1),
-        scratch_shapes=[grads, staged(rows), staged(rows), staged(rows - half)],
+        scratch_shapes=[grads, staged(rows), staged(rows - half, wide)],
         compiler_params=params(12),
-        cost_estimate=pl.CostEstimate(
-            flops=6 * (rows - half) * features * model, bytes_accessed=4_000_000, transcendentals=0
-        ),
-    )(*dqs, *dks, *aways, w_qkv)
+        cost_estimate=cost(6 * (rows - half) * features * model, 4_000_000),
+    )(*dqs, *aways, w_qkv)
     dq_out, dk_out, dv_out, total = pl.pallas_call(
         home_kernel,
         out_shape=(shaped((rows, features)),) * 3 + (shaped((half, model), F32),),
-        in_specs=[vmem()] * (4 * GROUP + 1),
+        in_specs=[vmem()] * (3 * GROUP + 1),
         out_specs=(vmem(),) * 4,
-        scratch_shapes=[grads, staged(rows), staged(rows), staged(rows - half), staged(half)],
+        scratch_shapes=[grads, staged(rows), staged(rows - half, wide), staged(half, wide)],
         compiler_params=params(12),
-        cost_estimate=pl.CostEstimate(
-            flops=6 * half * features * model, bytes_accessed=6_000_000, transcendentals=0
-        ),
-    )(*dqs, *dks, *aways, *homes, w_qkv)
+        cost_estimate=cost(6 * half * features * model, 6_000_000),
+    )(*dqs, *aways, *homes, w_qkv)
     for piece, send in enumerate(sends):
         got = lax.ppermute(send, "head", [(n, (n + piece + 1) % heads) for n in range(heads)])
         total = total + got.astype(F32)

time: 83.4 us -> 79.3 us (0.951)
  waiting for transfers between devices: 33.3 us -> 29.1 us
  Pallas kernels: 21.5 us -> 23.1 us
  starting transfers between devices: 23 us -> 21.6 us
    ppermute x6, waiting for transfers between devices: 6.9 us -> 3.21 us  [trade_level(): return lax.ppermute(x, ('var', 'head'), pairs)]
    ppermute x1, waiting for transfers between devices: 2.82 us -> 0.72 us  [body(): lax.ppermute(send, 'head', [(n, (n + piece + 1) % heads) for n in range(h...]
    ppermute x18 -> x15, starting transfers between devices: 12.5 us -> 10.8 us  [trade(): return lax.ppermute(x, 'var', [(n, n ^ distance) for n in range(devices)])]
    ppermute x18 -> x15, waiting for transfers between devices: 23.6 us -> 25.2 us  [trade(): return lax.ppermute(x, 'var', [(n, n ^ distance) for n in range(devices)])]
    pallas_call x3 -> x4, Pallas kernels: 14.6 us -> 16 us  [the longest x1 10.6 us: body(): pl.pallas_call(functools.partial(attend_kernel, False, blocks_here, head_...]
  transfers between devices with their start and end apart: 25 -> 22, of which waited for: 12 -> 10; matrix products, arithmetic and copies ran while one was open for 0% -> 0% of each run, Pallas kernels for 3% -> 10%
where the time goes in v7:
time: 79.3 us; the launch traced here: 79 us
  waiting for transfers between devices  29.1 us (37%)
  Pallas kernels  23.1 us (29%)
  starting transfers between devices  21.6 us (27%)
  local copies, waits for them, and re-layouts  3.71 us (5%)
  other arithmetic  0.84 us (1%)
    ppermute x15, waiting for transfers between devices, trade(): return lax.ppermute(x, 'var', [(n, n ^ distance) for n in range(devices)])  25.2 us
    ppermute x15, starting transfers between devices, trade(): return lax.ppermute(x, 'var', [(n, n ^ distance) for n in range(devices)])  10.8 us
    pallas_call x1, Pallas kernels, body(): pl.pallas_call(functools.partial(attend_kernel, False, blocks_here, head_...  10.6 us
    ppermute x6, starting transfers between devices, trade_level(): return lax.ppermute(x, ('var', 'head'), pairs)  9.09 us
    pallas_call x1, Pallas kernels, body(): pl.pallas_call(functools.partial(attend_kernel, True, blocks_here, head_d...  4.72 us
    unnamed x13, local copies, waits for them, and re-layouts  3.71 us
    ppermute x6, waiting for transfers between devices, trade_level(): return lax.ppermute(x, ('var', 'head'), pairs)  3.21 us
    pallas_call x1, Pallas kernels, body(): pl.pallas_call(pack_kv_kernel, out_shape=(shaped((rows, wide)),) * GROUP,...  2.48 us
  transfers between devices with their start and end apart: 22, of which 10 were waited for; matrix products, arithmetic and copies ran while one was open for 0% of the time, Pallas kernels for 10%

profile of v7, /device:TPU:0, one launch (start us, length us, event | category | flops | bytes accessed | tf_op | source)
XLA Modules:
  0.0 79.0 jit_solution(8464413299008696057)
XLA Ops:
  0.6 0.0 copy-start.5
  0.6 2.5 %shard_map.102 = (bf16[384,256]{1,0:T(8,128)(2,1)}, bf16[384,256]{1,0:T(8,128)(2,1)}, bf16[384,256]{1,0:T(8,128)(2,1)}, bf16[384,256]{1,0:T(8,128)(2,1)}) custom-call(bf16[384,512]{1,0:T(8,128)(2,1)} %k_hbm.1, bf16[384,512]{1,0:T(8,128)(2,1)} %v_hbm.1), custom_call_target="tpu_custom_call" | custom-call | flops 100663296 | bytes 1966080 | tf_op jit(solution)/shard_map/pallas_call | solution.py:502
  3.1 0.5 collective-permute-start
  3.6 2.6 %collective-permute-start.1 = (bf16[384,256]{1,0:T(8,128)(2,1)}, bf16[384,256]{1,0:T(8,128)(2,1)S(1)}, u32[]{:S(2)}, u32[]{:S(2)}) collective-permute-start(bf16[384,256]{1,0:T(8,128)(2,1)} %get-tuple-element.53), channel_id=1, source_target_pairs={{0,4},{2,6},{4,0},{6,2},{8,12},{10,14},{12,8},{14,10},{16,20},{18,... | collective-permute-start | bytes 589832 | tf_op jit(solution)/shard_map/ppermute | solution.py:465
  6.2 0.1 collective-permute-start.2
  6.3 0.0 collective-permute-done.after_ref.refs_1_
  6.3 0.0 copy-start.1
  6.3 1.0 %copy-done.1 = bf16[384,512]{1,0:T(8,128)(2,1)S(1)} copy-done((bf16[384,512]{1,0:T(8,128)(2,1)S(1)}, bf16[384,512]{1,0:T(8,128)(2,1)}, u32[]{:S(2)}) %copy-start.1) | copy-done | bytes 393240
  7.3 0.0 copy-start.2
  7.3 1.0 %copy-done.2 = bf16[384,512]{1,0:T(8,128)(2,1)S(1)} copy-done((bf16[384,512]{1,0:T(8,128)(2,1)S(1)}, bf16[384,512]{1,0:T(8,128)(2,1)}, u32[]{:S(2)}) %copy-start.2) | copy-done | bytes 393240
  8.3 0.9 %copy-done.3 = bf16[384,256]{1,0:T(8,128)(2,1)S(1)} copy-done((bf16[384,256]{1,0:T(8,128)(2,1)S(1)}, bf16[384,256]{1,0:T(8,128)(2,1)}, u32[]{:S(2)}) %copy-start.3) | copy-done | bytes 196632
  9.2 0.7 copy-done.4
  9.9 0.5 shard_map.103
  10.4 1.8 %collective-permute-done.1.refs_2_ = bf16[384,256]{1,0:T(8,128)(2,1)S(1)} collective-permute-done((bf16[384,256]{1,0:T(8,128)(2,1)}, bf16[384,256]{1,0:T(8,128)(2,1)S(1)}, u32[]{:S(2)}, u32[]{:S(2)}) %collective-permute-start.1) | collective-permute-done | bytes 196640 | tf_op jit(solution)/shard_map/ppermute | solution.py:465
  12.2 3.7 %collective-permute-done.2.refs_3_ = bf16[384,256]{1,0:T(8,128)(2,1)S(1)} collective-permute-done((bf16[384,256]{1,0:T(8,128)(2,1)}, bf16[384,256]{1,0:T(8,128)(2,1)S(1)}, u32[]{:S(2)}, u32[]{:S(2)}) %collective-permute-start.2) | collective-permute-done | bytes 196640 | tf_op jit(solution)/shard_map/ppermute | solution.py:465
  15.9 0.9 %shard_map.104 = (bf16[1936,256]{1,0:T(8,128)(2,1)S(1)}, bf16[1024,256]{1,0:T(8,128)(2,1)}, bf16[1024,256]{1,0:T(8,128)(2,1)S(1)}, bf16[400,256]{1,0:T(8,128)(2,...) custom-call(bf16[384,256]{1,0:T(8,128)(2,1)S(1)} %get-tuple-element., ...), custom_call_target="tpu_custom_call", output_to_operand_aliasing={{3}: (5, {}), {4}: (6, {}), {5}: (7, {})} | custom-call | bytes 1966080 | tf_op jit(solution)/shard_map/pallas_call | solution.py:523
  16.8 1.6 %collective-permute-start.3 = (bf16[1024,256]{1,0:T(8,128)(2,1)}, bf16[1024,256]{1,0:T(8,128)(2,1)S(1)}, u32[]{:S(2)}, u32[]{:S(2)}) collective-permute-start(bf16[1024,256]{1,0:T(8,128)(2,1)} %get-tuple-element.60), channel_id=1, source_target_pairs={{0,8},{1,9},{2,3},{3,2},{4,12},{5,13},{6,7},{7,6},{8,0},{9,1},{10,... | collective-permute-start | bytes 1572872 | tf_op jit(solution)/shard_map/ppermute | solution.py:477
  18.4 1.5 %collective-permute-start.4 = (bf16[1024,256]{1,0:T(8,128)(2,1)S(1)}, bf16[1024,256]{1,0:T(8,128)(2,1)S(1)}, u32[]{:S(2)}, u32[]{:S(2)}) collective-permute-start(bf16[1024,256]{1,0:T(8,128)(2,1)S(1)} %get-tuple-element.61), channel_id=1, source_target_pairs={{0,1},{1,0},{2,10},{3,11},{4,5},{5,4},{6,14},{7,15},{8,16},{9,17},... | collective-permute-start | bytes 1572872 | tf_op jit(solution)/shard_map/ppermute | solution.py:477
  19.9 0.0 collective-permute-start.5
  19.9 1.5 %collective-permute-start.6 = (bf16[400,256]{1,0:T(8,128)(2,1)S(1)}, bf16[400,256]{1,0:T(8,128)(2,1)}, u32[]{:S(2)}, u32[]{:S(2)}) collective-permute-start(bf16[400,256]{1,0:T(8,128)(2,1)S(1)} %get-tuple-element.63), channel_id=1, source_target_pairs={{0,4},{2,6},{4,0},{6,2},{8,12},{10,14},{12,8},{14,10},{16,20},{18,... | collective-permute-start | bytes 614408 | tf_op jit(solution)/shard_map/ppermute | solution.py:465
  21.5 0.3 collective-permute-start.7
  21.8 0.0 copy-done.5
  21.8 0.1 copy.18.kb_ref
  21.9 0.0 collective-permute-done.5.refs_3_
  21.9 6.0 %collective-permute-done.6.refs_4_ = bf16[400,256]{1,0:T(8,128)(2,1)} collective-permute-done((bf16[400,256]{1,0:T(8,128)(2,1)S(1)}, bf16[400,256]{1,0:T(8,128)(2,1)}, u32[]{:S(2)}, u32[]{:S(2)}) %collective-permute-start.6) | collective-permute-done | bytes 204832 | tf_op jit(solution)/shard_map/ppermute | solution.py:465
  27.9 3.6 %collective-permute-done.7.refs_5_ = bf16[400,256]{1,0:T(8,128)(2,1)} collective-permute-done((bf16[400,256]{1,0:T(8,128)(2,1)S(1)}, bf16[400,256]{1,0:T(8,128)(2,1)}, u32[]{:S(2)}, u32[]{:S(2)}) %collective-permute-start.7) | collective-permute-done | bytes 204832 | tf_op jit(solution)/shard_map/ppermute | solution.py:465
  31.5 0.0 collective-permute-done.3.refs_1_
  31.6 0.0 collective-permute-done.4.refs_2_
  31.6 10.6 %shard_map.105 = (bf16[4,128,256]{2,1,0:T(8,128)(2,1)S(1)}, bf16[4,128,256]{2,1,0:T(8,128)(2,1)S(1)}, bf16[28,128,256]{2,1,0:T(8,128)(2,1)S(1)}, bf16[28,128,128...) custom-call(s32[48,8]{1,0:T(8,128)S(1)} %copy.18.kb_ref, ...), custom_call_target="tpu_custom_call" | custom-call | flops 5395552768 | bytes 2000000 | tf_op jit(solution)/shard_map/pallas_call | solution.py:566
  42.2 1.7 %collective-permute-start.8 = (bf16[4,128,256]{2,1,0:T(8,128)(2,1)S(1)}, bf16[4,128,256]{2,1,0:T(8,128)(2,1)S(1)}, u32[]{:S(2)}, u32[]{:S(2)}) collective-permute-start(bf16[4,128,256]{2,1,0:T(8,128)(2,1)S(1)} %get-tuple-element.73), channel_id=1, source_target_pairs={{0,8},{1,9},{2,3},{3,2},{4,12},{5,13},{6,7},{7,6},{8,0},{9,1},{10,... | collective-permute-start | bytes 786440 | tf_op jit(solution)/shard_map/ppermute | solution.py:477
  43.9 1.5 %collective-permute-start.9 = (bf16[4,128,256]{2,1,0:T(8,128)(2,1)S(1)}, bf16[4,128,256]{2,1,0:T(8,128)(2,1)S(1)}, u32[]{:S(2)}, u32[]{:S(2)}) collective-permute-start(bf16[4,128,256]{2,1,0:T(8,128)(2,1)S(1)} %get-tuple-element.74), channel_id=1, source_target_pairs={{0,1},{1,0},{2,10},{3,11},{4,5},{5,4},{6,14},{7,15},{8,16},{9,17},... | collective-permute-start | bytes 786440 | tf_op jit(solution)/shard_map/ppermute | solution.py:477
  45.4 4.7 %shard_map.106 = (f32[12,128,256]{2,1,0:T(8,128)S(1)}, bf16[4,128,256]{2,1,0:T(8,128)(2,1)S(1)}, bf16[4,128,256]{2,1,0:T(8,128)(2,1)S(1)}, bf16[384,128]{1,0:T(8...) custom-call(s32[48,8]{1,0:T(8,128)S(1)} %copy.18.kb_ref, ...), custom_call_target="tpu_custom_call" | custom-call | flops 2657510912 | bytes 2000000 | tf_op jit(solution)/shard_map/pallas_call | solution.py:576
  50.1 1.7 %collective-permute-start.13 = (bf16[4,128,256]{2,1,0:T(8,128)(2,1)S(1)}, bf16[4,128,256]{2,1,0:T(8,128)(2,1)S(1)}, u32[]{:S(2)}, u32[]{:S(2)}) collective-permute-start(bf16[4,128,256]{2,1,0:T(8,128)(2,1)S(1)} %get-tuple-element.82), channel_id=1, source_target_pairs={{0,8},{1,9},{2,3},{3,2},{4,12},{5,13},{6,7},{7,6},{8,0},{9,1},{10,... | collective-permute-start | bytes 786440 | tf_op jit(solution)/shard_map/ppermute | solution.py:477
  51.8 1.1 %collective-permute-start.14 = (bf16[4,128,256]{2,1,0:T(8,128)(2,1)S(1)}, bf16[4,128,256]{2,1,0:T(8,128)(2,1)S(1)}, u32[]{:S(2)}, u32[]{:S(2)}) collective-permute-start(bf16[4,128,256]{2,1,0:T(8,128)(2,1)S(1)} %get-tuple-element.83), channel_id=1, source_target_pairs={{0,1},{1,0},{2,10},{3,11},{4,5},{5,4},{6,14},{7,15},{8,16},{9,17},... | collective-permute-start | bytes 786440 | tf_op jit(solution)/shard_map/ppermute | solution.py:477
  52.9 0.0 collective-permute-done.8.first_ref
  52.9 0.0 collective-permute-done.9.second_ref
  52.9 0.2 shard_map.107
  53.1 0.1 collective-permute-start.10
  53.2 1.6 %collective-permute-start.11 = (bf16[384,128]{1,0:T(8,128)(2,1)S(1)}, bf16[384,128]{1,0:T(8,128)(2,1)S(1)}, u32[]{:S(2)}, u32[]{:S(2)}) collective-permute-start(bf16[384,128]{1,0:T(8,128)(2,1)S(1)} %get-tuple-element.79), channel_id=1, source_target_pairs={{0,4},{2,6},{4,0},{6,2},{8,12},{10,14},{12,8},{14,10},{16,20},{18,... | collective-permute-start | bytes 294920 | tf_op jit(solution)/shard_map/ppermute | solution.py:465
  54.8 0.3 collective-permute-start.12
  55.0 3.2 %collective-permute-done.13.first_ref = bf16[4,128,256]{2,1,0:T(8,128)(2,1)S(1)} collective-permute-done((bf16[4,128,256]{2,1,0:T(8,128)(2,1)S(1)}, bf16[4,128,256]{2,1,0:T(8,128)(2,1)S(1)}, u32[]{:S(2)}, u32[]{:S(2)}) %collective-permute-start.13) | collective-permute-done | bytes 262176 | tf_op jit(solution)/shard_map/ppermute | solution.py:477
  58.2 0.0 collective-permute-done.14.second_ref
  58.2 0.5 shard_map.108
  58.7 0.1 collective-permute-start.15
  58.8 1.6 %collective-permute-start.16 = (bf16[192,256]{1,0:T(8,128)(2,1)S(1)}, bf16[192,256]{1,0:T(8,128)(2,1)S(1)}, u32[]{:S(2)}, u32[]{:S(2)}) collective-permute-start(bf16[192,256]{1,0:T(8,128)(2,1)S(1)} %get-tuple-element.86), channel_id=1, source_target_pairs={{0,4},{2,6},{4,0},{6,2},{8,12},{10,14},{12,8},{14,10},{16,20},{18,... | collective-permute-start | bytes 294920 | tf_op jit(solution)/shard_map/ppermute | solution.py:465
  60.3 0.0 collective-permute-done.10.refs_1_
  60.4 0.3 collective-permute-start.17
  60.6 0.0 collective-permute-done.11.refs_2_
  60.6 0.0 collective-permute-done.12.refs_3_
  60.6 0.0 collective-permute-done.15.refs_5_
  60.6 3.8 %collective-permute-done.16.refs_6_ = bf16[192,256]{1,0:T(8,128)(2,1)S(1)} collective-permute-done((bf16[192,256]{1,0:T(8,128)(2,1)S(1)}, bf16[192,256]{1,0:T(8,128)(2,1)S(1)}, u32[]{:S(2)}, u32[]{:S(2)}) %collective-permute-start.16) | collective-permute-done | bytes 98336 | tf_op jit(solution)/shard_map/ppermute | solution.py:465
  64.4 1.2 %collective-permute-done.17.refs_7_ = bf16[192,256]{1,0:T(8,128)(2,1)S(1)} collective-permute-done((bf16[192,256]{1,0:T(8,128)(2,1)S(1)}, bf16[192,256]{1,0:T(8,128)(2,1)S(1)}, u32[]{:S(2)}, u32[]{:S(2)}) %collective-permute-start.17) | collective-permute-done | bytes 98336 | tf_op jit(solution)/shard_map/ppermute | solution.py:465
  65.6 0.0 copy-done
  65.6 1.2 %shard_map.110 = bf16[192,1024]{1,0:T(8,128)(2,1)S(1)} custom-call(bf16[384,128]{1,0:T(8,128)(2,1)S(1)} %get-tuple-element.71.refs_0_, bf16[384,128]{1,0:T(8,128)(2,1)S(1)} %collective-permute-done.10.refs_1_, bf16[384,128]{1,0:T(8,128)(2,1)S(1)} %collective-permute-done.11.refs_2_, bf16[384,128]{1,0:T(8,128)(2,1)S(1)} %collective-permute-done.12.refs_3_, ...), custom_call_target="tpu_custom_call" | custom-call | flops 603979776 | bytes 4000000 | tf_op jit(solution)/shard_map/pallas_call | solution.py:612
  66.8 1.7 %collective-permute-start.21 = (bf16[192,1024]{1,0:T(8,128)(2,1)S(1)}, bf16[192,1024]{1,0:T(8,128)(2,1)S(1)}, u32[]{:S(2)}, u32[]{:S(2)}) collective-permute-start(bf16[192,1024]{1,0:T(8,128)(2,1)S(1)} %shard_map.110), channel_id=1, source_target_pairs={{0,1},{1,0},{2,3},{3,2},{4,5},{5,4},{6,7},{7,6},{8,9},{9,8},{10,11... | collective-permute-start | bytes 1179656 | tf_op jit(solution)/shard_map/ppermute | solution.py:631
  68.6 0.0 collective-permute-start.18
  68.6 1.5 %collective-permute-start.19 = (bf16[192,256]{1,0:T(8,128)(2,1)S(1)}, bf16[192,256]{1,0:T(8,128)(2,1)S(1)}, u32[]{:S(2)}, u32[]{:S(2)}) collective-permute-start(bf16[192,256]{1,0:T(8,128)(2,1)S(1)} %get-tuple-element.90), channel_id=1, source_target_pairs={{0,4},{2,6},{4,0},{6,2},{8,12},{10,14},{12,8},{14,10},{16,20},{18,... | collective-permute-start | bytes 294920 | tf_op jit(solution)/shard_map/ppermute | solution.py:465
  70.1 0.3 collective-permute-start.20
  70.4 0.0 collective-permute-done.18.refs_9_
  70.4 3.7 %collective-permute-done.19.refs_10_ = bf16[192,256]{1,0:T(8,128)(2,1)S(1)} collective-permute-done((bf16[192,256]{1,0:T(8,128)(2,1)S(1)}, bf16[192,256]{1,0:T(8,128)(2,1)S(1)}, u32[]{:S(2)}, u32[]{:S(2)}) %collective-permute-start.19) | collective-permute-done | bytes 98336 | tf_op jit(solution)/shard_map/ppermute | solution.py:465
  74.2 1.3 %collective-permute-done.20.refs_11_ = bf16[192,256]{1,0:T(8,128)(2,1)S(1)} collective-permute-done((bf16[192,256]{1,0:T(8,128)(2,1)S(1)}, bf16[192,256]{1,0:T(8,128)(2,1)S(1)}, u32[]{:S(2)}, u32[]{:S(2)}) %collective-permute-start.20) | collective-permute-done | bytes 98336 | tf_op jit(solution)/shard_map/ppermute | solution.py:465
  75.5 2.0 %shard_map.109 = (bf16[384,512]{1,0:T(8,128)(2,1)}, bf16[384,512]{1,0:T(8,128)(2,1)}, bf16[384,512]{1,0:T(8,128)(2,1)}, f32[192,1024]{1,0:T(8,128)S(1)}) custom-call(bf16[384,128]{1,0:T(8,128)(2,1)S(1)} %get-tuple-element.71.refs_0_, bf16[384,128]{1,0:T(8,128)(2,1)S(1)} %collective-permute-done.10.refs_1_, ...), custom_call_target="tpu_custom_call" | custom-call | flops 603979776 | bytes 6000000 | tf_op jit(solution)/shard_map/pallas_call | solution.py:621
  77.5 0.7 collective-permute-done.21
  78.2 0.8 %add_convert_fusion = bf16[192,1024]{1,0:T(8,128)(2,1)} fusion(f32[192,1024]{1,0:T(8,128)S(1)} %get-tuple-element.95, bf16[192,1024]{1,0:T(8,128)(2,1)S(1)} %collective-permute-done.21), kind=kLoop, calls=%fused_computation | loop fusion | flops 589824 | bytes 1572864 | tf_op jit(solution)/shard_map/convert_element_type | solution.py:633
  (3 shorter events, 0.0 us)
Async XLA Ops:
  0.6 21.2 %copy-start.5 = (s32[48,8]{0,1:T(8,128)S(1)}, s32[48,8]{0,1:T(8,128)}, u32[]{:S(2)}) copy-start(s32[48,8]{0,1:T(8,128)} %param.12) | copy-start | bytes 4612
  3.1 3.2 %collective-permute-start = (bf16[384,256]{1,0:T(8,128)(2,1)}, bf16[384,256]{1,0:T(8,128)(2,1)S(1)}, u32[]{:S(2)}, u32[]{:S(2)}) collective-permute-start(bf16[384,256]{1,0:T(8,128)(2,1)} %get-tuple-element.51), channel_id=1, source_target_pairs={{0,2},{2,0},{4,6},{6,4},{8,10},{10,8},{12,14},{14,12},{16,18},{18,... | collective-permute-start | bytes 589832 | tf_op jit(solution)/shard_map/ppermute | solution.py:465
  3.6 8.6 %collective-permute-start.1 = (bf16[384,256]{1,0:T(8,128)(2,1)}, bf16[384,256]{1,0:T(8,128)(2,1)S(1)}, u32[]{:S(2)}, u32[]{:S(2)}) collective-permute-start(bf16[384,256]{1,0:T(8,128)(2,1)} %get-tuple-element.53), channel_id=1, source_target_pairs={{0,4},{2,6},{4,0},{6,2},{8,12},{10,14},{12,8},{14,10},{16,20},{18,... | collective-permute-start | bytes 589832 | tf_op jit(solution)/shard_map/ppermute | solution.py:465
  6.2 9.7 %collective-permute-start.2 = (bf16[384,256]{1,0:T(8,128)(2,1)}, bf16[384,256]{1,0:T(8,128)(2,1)S(1)}, u32[]{:S(2)}, u32[]{:S(2)}) collective-permute-start(bf16[384,256]{1,0:T(8,128)(2,1)} %get-tuple-element.54), channel_id=1, source_target_pairs={{0,6},{2,4},{4,2},{6,0},{8,14},{10,12},{12,10},{14,8},{16,22},{18,... | collective-permute-start | bytes 589832 | tf_op jit(solution)/shard_map/ppermute | solution.py:465
  6.3 1.0 %copy-start.1 = (bf16[384,512]{1,0:T(8,128)(2,1)S(1)}, bf16[384,512]{1,0:T(8,128)(2,1)}, u32[]{:S(2)}) copy-start(bf16[384,512]{1,0:T(8,128)(2,1)} %q_ref.1) | copy-start | bytes 1179652
  7.3 1.0 %copy-start.2 = (bf16[384,512]{1,0:T(8,128)(2,1)S(1)}, bf16[384,512]{1,0:T(8,128)(2,1)}, u32[]{:S(2)}) copy-start(bf16[384,512]{1,0:T(8,128)(2,1)} %g_ref.1) | copy-start | bytes 1179652
  8.3 0.9 %copy-start.3 = (bf16[384,256]{1,0:T(8,128)(2,1)S(1)}, bf16[384,256]{1,0:T(8,128)(2,1)}, u32[]{:S(2)}) copy-start(bf16[384,256]{1,0:T(8,128)(2,1)} %get-tuple-element.50.mine_ref) | copy-start | bytes 589828
  9.2 0.7 copy-start.4
  16.8 14.8 %collective-permute-start.3 = (bf16[1024,256]{1,0:T(8,128)(2,1)}, bf16[1024,256]{1,0:T(8,128)(2,1)S(1)}, u32[]{:S(2)}, u32[]{:S(2)}) collective-permute-start(bf16[1024,256]{1,0:T(8,128)(2,1)} %get-tuple-element.60), channel_id=1, source_target_pairs={{0,8},{1,9},{2,3},{3,2},{4,12},{5,13},{6,7},{7,6},{8,0},{9,1},{10,... | collective-permute-start | bytes 1572872 | tf_op jit(solution)/shard_map/ppermute | solution.py:477
  18.4 13.1 %collective-permute-start.4 = (bf16[1024,256]{1,0:T(8,128)(2,1)S(1)}, bf16[1024,256]{1,0:T(8,128)(2,1)S(1)}, u32[]{:S(2)}, u32[]{:S(2)}) collective-permute-start(bf16[1024,256]{1,0:T(8,128)(2,1)S(1)} %get-tuple-element.61), channel_id=1, source_target_pairs={{0,1},{1,0},{2,10},{3,11},{4,5},{5,4},{6,14},{7,15},{8,16},{9,17},... | collective-permute-start | bytes 1572872 | tf_op jit(solution)/shard_map/ppermute | solution.py:477
  19.9 1.9 %collective-permute-start.5 = (bf16[400,256]{1,0:T(8,128)(2,1)S(1)}, bf16[400,256]{1,0:T(8,128)(2,1)S(1)}, u32[]{:S(2)}, u32[]{:S(2)}) collective-permute-start(bf16[400,256]{1,0:T(8,128)(2,1)S(1)} %get-tuple-element.62), channel_id=1, source_target_pairs={{0,2},{2,0},{4,6},{6,4},{8,10},{10,8},{12,14},{14,12},{16,18},{18,... | collective-permute-start | bytes 614408 | tf_op jit(solution)/shard_map/ppermute | solution.py:465
  19.9 8.0 %collective-permute-start.6 = (bf16[400,256]{1,0:T(8,128)(2,1)S(1)}, bf16[400,256]{1,0:T(8,128)(2,1)}, u32[]{:S(2)}, u32[]{:S(2)}) collective-permute-start(bf16[400,256]{1,0:T(8,128)(2,1)S(1)} %get-tuple-element.63), channel_id=1, source_target_pairs={{0,4},{2,6},{4,0},{6,2},{8,12},{10,14},{12,8},{14,10},{16,20},{18,... | collective-permute-start | bytes 614408 | tf_op jit(solution)/shard_map/ppermute | solution.py:465
  21.5 10.1 %collective-permute-start.7 = (bf16[400,256]{1,0:T(8,128)(2,1)S(1)}, bf16[400,256]{1,0:T(8,128)(2,1)}, u32[]{:S(2)}, u32[]{:S(2)}) collective-permute-start(bf16[400,256]{1,0:T(8,128)(2,1)S(1)} %get-tuple-element.64), channel_id=1, source_target_pairs={{0,6},{2,4},{4,2},{6,0},{8,14},{10,12},{12,10},{14,8},{16,22},{18,... | collective-permute-start | bytes 614408 | tf_op jit(solution)/shard_map/ppermute | solution.py:465
  42.2 10.7 %collective-permute-start.8 = (bf16[4,128,256]{2,1,0:T(8,128)(2,1)S(1)}, bf16[4,128,256]{2,1,0:T(8,128)(2,1)S(1)}, u32[]{:S(2)}, u32[]{:S(2)}) collective-permute-start(bf16[4,128,256]{2,1,0:T(8,128)(2,1)S(1)} %get-tuple-element.73), channel_id=1, source_target_pairs={{0,8},{1,9},{2,3},{3,2},{4,12},{5,13},{6,7},{7,6},{8,0},{9,1},{10,... | collective-permute-start | bytes 786440 | tf_op jit(solution)/shard_map/ppermute | solution.py:477
  43.9 9.0 %collective-permute-start.9 = (bf16[4,128,256]{2,1,0:T(8,128)(2,1)S(1)}, bf16[4,128,256]{2,1,0:T(8,128)(2,1)S(1)}, u32[]{:S(2)}, u32[]{:S(2)}) collective-permute-start(bf16[4,128,256]{2,1,0:T(8,128)(2,1)S(1)} %get-tuple-element.74), channel_id=1, source_target_pairs={{0,1},{1,0},{2,10},{3,11},{4,5},{5,4},{6,14},{7,15},{8,16},{9,17},... | collective-permute-start | bytes 786440 | tf_op jit(solution)/shard_map/ppermute | solution.py:477
  50.1 8.1 %collective-permute-start.13 = (bf16[4,128,256]{2,1,0:T(8,128)(2,1)S(1)}, bf16[4,128,256]{2,1,0:T(8,128)(2,1)S(1)}, u32[]{:S(2)}, u32[]{:S(2)}) collective-permute-start(bf16[4,128,256]{2,1,0:T(8,128)(2,1)S(1)} %get-tuple-element.82), channel_id=1, source_target_pairs={{0,8},{1,9},{2,3},{3,2},{4,12},{5,13},{6,7},{7,6},{8,0},{9,1},{10,... | collective-permute-start | bytes 786440 | tf_op jit(solution)/shard_map/ppermute | solution.py:477
  51.8 6.4 %collective-permute-start.14 = (bf16[4,128,256]{2,1,0:T(8,128)(2,1)S(1)}, bf16[4,128,256]{2,1,0:T(8,128)(2,1)S(1)}, u32[]{:S(2)}, u32[]{:S(2)}) collective-permute-start(bf16[4,128,256]{2,1,0:T(8,128)(2,1)S(1)} %get-tuple-element.83), channel_id=1, source_target_pairs={{0,1},{1,0},{2,10},{3,11},{4,5},{5,4},{6,14},{7,15},{8,16},{9,17},... | collective-permute-start | bytes 786440 | tf_op jit(solution)/shard_map/ppermute | solution.py:477
  52.9 12.7 %copy-start = (bf16[3,1024,512]{2,1,0:T(8,128)(2,1)S(1)}, bf16[3,1024,512]{2,1,0:T(8,128)(2,1)}, u32[]{:S(2)}) copy-start(bf16[3,1024,512]{2,1,0:T(8,128)(2,1)} %refs_8_.1) | copy-start | bytes 9437188
  53.1 7.3 %collective-permute-start.10 = (bf16[384,128]{1,0:T(8,128)(2,1)S(1)}, bf16[384,128]{1,0:T(8,128)(2,1)S(1)}, u32[]{:S(2)}, u32[]{:S(2)}) collective-permute-start(bf16[384,128]{1,0:T(8,128)(2,1)S(1)} %get-tuple-element.78), channel_id=1, source_target_pairs={{0,2},{2,0},{4,6},{6,4},{8,10},{10,8},{12,14},{14,12},{16,18},{18,... | collective-permute-start | bytes 294920 | tf_op jit(solution)/shard_map/ppermute | solution.py:465
  53.2 7.5 %collective-permute-start.11 = (bf16[384,128]{1,0:T(8,128)(2,1)S(1)}, bf16[384,128]{1,0:T(8,128)(2,1)S(1)}, u32[]{:S(2)}, u32[]{:S(2)}) collective-permute-start(bf16[384,128]{1,0:T(8,128)(2,1)S(1)} %get-tuple-element.79), channel_id=1, source_target_pairs={{0,4},{2,6},{4,0},{6,2},{8,12},{10,14},{12,8},{14,10},{16,20},{18,... | collective-permute-start | bytes 294920 | tf_op jit(solution)/shard_map/ppermute | solution.py:465
  54.8 5.9 %collective-permute-start.12 = (bf16[384,128]{1,0:T(8,128)(2,1)S(1)}, bf16[384,128]{1,0:T(8,128)(2,1)S(1)}, u32[]{:S(2)}, u32[]{:S(2)}) collective-permute-start(bf16[384,128]{1,0:T(8,128)(2,1)S(1)} %get-tuple-element.80), channel_id=1, source_target_pairs={{0,6},{2,4},{4,2},{6,0},{8,14},{10,12},{12,10},{14,8},{16,22},{18,... | collective-permute-start | bytes 294920 | tf_op jit(solution)/shard_map/ppermute | solution.py:465
  58.7 2.0 %collective-permute-start.15 = (bf16[192,256]{1,0:T(8,128)(2,1)S(1)}, bf16[192,256]{1,0:T(8,128)(2,1)S(1)}, u32[]{:S(2)}, u32[]{:S(2)}) collective-permute-start(bf16[192,256]{1,0:T(8,128)(2,1)S(1)} %get-tuple-element.85), channel_id=1, source_target_pairs={{0,2},{2,0},{4,6},{6,4},{8,10},{10,8},{12,14},{14,12},{16,18},{18,... | collective-permute-start | bytes 294920 | tf_op jit(solution)/shard_map/ppermute | solution.py:465
  58.8 5.7 %collective-permute-start.16 = (bf16[192,256]{1,0:T(8,128)(2,1)S(1)}, bf16[192,256]{1,0:T(8,128)(2,1)S(1)}, u32[]{:S(2)}, u32[]{:S(2)}) collective-permute-start(bf16[192,256]{1,0:T(8,128)(2,1)S(1)} %get-tuple-element.86), channel_id=1, source_target_pairs={{0,4},{2,6},{4,0},{6,2},{8,12},{10,14},{12,8},{14,10},{16,20},{18,... | collective-permute-start | bytes 294920 | tf_op jit(solution)/shard_map/ppermute | solution.py:465
  60.4 5.3 %collective-permute-start.17 = (bf16[192,256]{1,0:T(8,128)(2,1)S(1)}, bf16[192,256]{1,0:T(8,128)(2,1)S(1)}, u32[]{:S(2)}, u32[]{:S(2)}) collective-permute-start(bf16[192,256]{1,0:T(8,128)(2,1)S(1)} %get-tuple-element.87), channel_id=1, source_target_pairs={{0,6},{2,4},{4,2},{6,0},{8,14},{10,12},{12,10},{14,8},{16,22},{18,... | collective-permute-start | bytes 294920 | tf_op jit(solution)/shard_map/ppermute | solution.py:465
  66.8 11.4 %collective-permute-start.21 = (bf16[192,1024]{1,0:T(8,128)(2,1)S(1)}, bf16[192,1024]{1,0:T(8,128)(2,1)S(1)}, u32[]{:S(2)}, u32[]{:S(2)}) collective-permute-start(bf16[192,1024]{1,0:T(8,128)(2,1)S(1)} %shard_map.110), channel_id=1, source_target_pairs={{0,1},{1,0},{2,3},{3,2},{4,5},{5,4},{6,7},{7,6},{8,9},{9,8},{10,11... | collective-permute-start | bytes 1179656 | tf_op jit(solution)/shard_map/ppermute | solution.py:631
  68.6 1.9 %collective-permute-start.18 = (bf16[192,256]{1,0:T(8,128)(2,1)S(1)}, bf16[192,256]{1,0:T(8,128)(2,1)S(1)}, u32[]{:S(2)}, u32[]{:S(2)}) collective-permute-start(bf16[192,256]{1,0:T(8,128)(2,1)S(1)} %get-tuple-element.89), channel_id=1, source_target_pairs={{0,2},{2,0},{4,6},{6,4},{8,10},{10,8},{12,14},{14,12},{16,18},{18,... | collective-permute-start | bytes 294920 | tf_op jit(solution)/shard_map/ppermute | solution.py:465
  68.6 5.6 %collective-permute-start.19 = (bf16[192,256]{1,0:T(8,128)(2,1)S(1)}, bf16[192,256]{1,0:T(8,128)(2,1)S(1)}, u32[]{:S(2)}, u32[]{:S(2)}) collective-permute-start(bf16[192,256]{1,0:T(8,128)(2,1)S(1)} %get-tuple-element.90), channel_id=1, source_target_pairs={{0,4},{2,6},{4,0},{6,2},{8,12},{10,14},{12,8},{14,10},{16,20},{18,... | collective-permute-start | bytes 294920 | tf_op jit(solution)/shard_map/ppermute | solution.py:465
  70.1 5.4 %collective-permute-start.20 = (bf16[192,256]{1,0:T(8,128)(2,1)S(1)}, bf16[192,256]{1,0:T(8,128)(2,1)S(1)}, u32[]{:S(2)}, u32[]{:S(2)}) collective-permute-start(bf16[192,256]{1,0:T(8,128)(2,1)S(1)} %get-tuple-element.91), channel_id=1, source_target_pairs={{0,6},{2,4},{4,2},{6,0},{8,14},{10,12},{12,10},{14,8},{16,22},{18,... | collective-permute-start | bytes 294920 | tf_op jit(solution)/shard_map/ppermute | solution.py:465

commit v8 on v7

--- a/solution.py
+++ b/solution.py
@@ -15,6 +15,7 @@
 GROUP = 4
 LANES = 128
 LSE_ROWS = 16
+PARTS = 2
 LOADS = 3
 F32 = jnp.float32
 BF16 = jnp.bfloat16
@@ -256,50 +257,57 @@
     late = slice(HALF, BLOCK)
     both_cols = slice(0, 2 * LANES)
     early_rows = slot_count * HALF
-
-    def forward(query_block, buf):
-        lay_out(query_block // blocks_here, query_block % blocks_here, buf)
-        index = picks(query_block)
-        s = dot_nt(gather(index, early, low), queries[buf])
-        g = dot_nt(gather(index, early, high), grads[buf])
-        x = dot_nt(gather(index, late, both_cols), crossed[buf])
+    part_slots = slot_count // PARTS
+    part_rows = part_slots * HALF
+
+    def forward_part(index, query_block, buf, part):
+        some = index[part * part_slots : (part + 1) * part_slots]
+        at = slice(part * part_rows, (part + 1) * part_rows)
+        after = slice(early_rows + part * part_rows, early_rows + (part + 1) * part_rows)
+        s = dot_nt(gather(some, early, low), queries[buf])
+        g = dot_nt(gather(some, early, high), grads[buf])
+        x = dot_nt(gather(some, late, both_cols), crossed[buf])
         shift = shifts[query_block, 0][None]
-        p = jnp.exp(s.reshape(early_rows // 8, 8, 2 * LANES) + shift).reshape(early_rows, 2 * LANES)
-        prob[buf, :early_rows] = p
-        slope[buf, :early_rows] = g
-        delta = jnp.sum((p * g).reshape(early_rows // 8, 8, 2 * LANES), axis=0)
+        p = jnp.exp(s.reshape(part_rows // 8, 8, 2 * LANES) + shift).reshape(part_rows, 2 * LANES)
+        prob[buf, at] = p
+        slope[buf, at] = g
+        delta = jnp.sum((p * g).reshape(part_rows // 8, 8, 2 * LANES), axis=0)
         late_shift = shifts[query_block, 1, :, low][None]
-        q = jnp.exp(x[:, low].reshape(early_rows // 8, 8, LANES) + late_shift).reshape(
-            early_rows, LANES
+        q = jnp.exp(x[:, low].reshape(part_rows // 8, 8, LANES) + late_shift).reshape(
+            part_rows, LANES
         )
-        prob[buf, early_rows:, low] = q
-        slope[buf, early_rows:, low] = x[:, high]
-        more = jnp.sum((q * x[:, high]).reshape(early_rows // 8, 8, LANES), axis=0)
-        delta_low = jnp.sum(delta[:, low], axis=0, keepdims=True)
-        delta_high = jnp.sum(delta[:, high] + more, axis=0, keepdims=True)
-        return jnp.concatenate([delta_low, delta_high], axis=1)
-
-    def backward(query_block, buf, delta):
-        index = picks(query_block)
-        p = prob[buf, :early_rows]
-        ds = (p * (slope[buf, :early_rows] - delta)).astype(BF16)
-        q = prob[buf, early_rows:, low]
-        ds_late = (q * (slope[buf, early_rows:, low] - delta[:, high])).astype(BF16)
+        prob[buf, after, low] = q
+        slope[buf, after, low] = x[:, high]
+        more = jnp.sum((q * x[:, high]).reshape(part_rows // 8, 8, LANES), axis=0)
+        return delta[:, low], delta[:, high] + more
+
+    def backward_part(index, buf, delta, part):
+        at = slice(part * part_rows, (part + 1) * part_rows)
+        after = slice(early_rows + part * part_rows, early_rows + (part + 1) * part_rows)
+        p = prob[buf, at]
+        ds = (p * (slope[buf, at] - delta)).astype(BF16)
+        q = prob[buf, after, low]
+        ds_late = (q * (slope[buf, after, low] - delta[:, high])).astype(BF16)
         dk = dot(ds, queries[buf])
         dv = dot(p.astype(BF16), grads[buf])
         r = dot(jnp.concatenate([ds_late, q.astype(BF16)], axis=1), crossed[buf])
         nothing = jnp.zeros((HALF, LANES), BF16)
         pieces = []
-        for s in range(slot_count):
+        for s in range(part_slots):
             at = slice(s * HALF, (s + 1) * HALF)
-            where = index[s]
+            where = index[part * part_slots + s]
             acc[where, early, low] = acc[where, early, low] + dk[at]
             acc[where, early, high] = acc[where, early, high] + dv[at]
             acc[where, late] = acc[where, late] + r[at]
             pieces.append(ds[at])
             pieces.append(jnp.concatenate([nothing, ds_late[at]], axis=1))
-        keys_turned = jnp.concatenate([k_turn[i] for i in index], axis=1)
-        dq = dot(keys_turned, jnp.concatenate(pieces, axis=0)) * scale
+        keys_turned = jnp.concatenate(
+            [k_turn[i] for i in index[part * part_slots : (part + 1) * part_slots]], axis=1
+        )
+        return dot(keys_turned, jnp.concatenate(pieces, axis=0))
+
+    def write_dq(query_block, dq):
+        dq = dq * scale
         halves = []
         for cols in (low, high):
             turned = dq[:, cols].T
@@ -308,28 +316,42 @@
         local = pl.multiple_of((query_block % blocks_here) * BLOCK, BLOCK)
         dq_all[query_block // blocks_here, pl.ds(local, BLOCK)] = moved
 
+    def run(ahead, ahead_buf, behind, behind_buf, delta):
+        sums, dq = None, None
+        if ahead is not None:
+            lay_out(ahead // blocks_here, ahead % blocks_here, ahead_buf)
+            ahead_index = picks(ahead)
+        if behind is not None:
+            behind_index = picks(behind)
+        for part in range(PARTS):
+            if ahead is not None:
+                more = forward_part(ahead_index, ahead, ahead_buf, part)
+                sums = more if sums is None else (sums[0] + more[0], sums[1] + more[1])
+            if behind is not None:
+                more = backward_part(behind_index, behind_buf, delta, part)
+                dq = more if dq is None else dq + more
+        if behind is not None:
+            write_dq(behind, dq)
+        if ahead is None:
+            return None
+        return jnp.concatenate([jnp.sum(x, axis=0, keepdims=True) for x in sums], axis=1)
+
     def block_of(j):
         if last:
             return j + OUTER
         return j + jnp.where(j < OUTER, 0, group_blocks - 2 * OUTER)
 
     count = group_blocks - 2 * OUTER if last else 2 * OUTER
-    delta = forward(block_of(0), 0)
+    delta = run(block_of(0), 0, None, None, None)
 
     def step(j, delta):
-        later = forward(block_of(2 * j + 1), 1)
-        backward(block_of(2 * j), 0, delta)
-        following = forward(block_of(2 * j + 2), 0)
-        backward(block_of(2 * j + 1), 1, later)
-        return following
+        delta = run(block_of(2 * j + 1), 1, block_of(2 * j), 0, delta)
+        return run(block_of(2 * j + 2), 0, block_of(2 * j + 1), 1, delta)
 
     delta = lax.fori_loop(0, (count - 1) // 2, step, delta)
     if count % 2 == 0:
-        later = forward(block_of(count - 1), 1)
-        backward(block_of(count - 2), 0, delta)
-        backward(block_of(count - 1), 1, later)
-    else:
-        backward(block_of(count - 1), 0, delta)
+        delta = run(block_of(count - 1), 1, block_of(count - 2), 0, delta)
+    run(None, None, block_of(count - 1), (count - 1) % 2, delta)
 
     groups = BLOCK // 16
 
@@ -569,7 +591,7 @@
         in_specs=[smem] + [vmem()] * (2 + GROUP),
         out_specs=(vmem(),) * 8,
         scratch_shapes=[acc_scratch] + work,
-        compiler_params=params(24),
+        compiler_params=params(16),
         cost_estimate=attend_cost(0.67),
     )(key_blocks, own, first, second, *qos)
     outer_back = (trade_first(first), trade_second(second))
@@ -581,7 +603,7 @@
         in_specs=[smem] + [vmem()] * 6,
         out_specs=(vmem(),) * (3 + GROUP),
         scratch_shapes=[acc_scratch] + work + [staged(rows)],
-        compiler_params=params(24),
+        compiler_params=params(16),
         cost_estimate=attend_cost(0.33),
     )(key_blocks, *state)
     inner_back = (trade_first(first), trade_second(second))
@@ -615,7 +637,7 @@
         in_specs=[vmem()] * (2 * GROUP + 1),
         out_specs=(vmem(),) * (heads - 1),
         scratch_shapes=[grads, staged(rows), staged(rows - half, wide)],
-        compiler_params=params(12),
+        compiler_params=params(8),
         cost_estimate=cost(6 * (rows - half) * features * model, 4_000_000),
     )(*dqs, *aways, w_qkv)
     dq_out, dk_out, dv_out, total = pl.pallas_call(
@@ -624,7 +646,7 @@
         in_specs=[vmem()] * (3 * GROUP + 1),
         out_specs=(vmem(),) * 4,
         scratch_shapes=[grads, staged(rows), staged(rows - half, wide), staged(half, wide)],
-        compiler_params=params(12),
+        compiler_params=params(8),
         cost_estimate=cost(6 * half * features * model, 6_000_000),
     )(*dqs, *aways, *homes, w_qkv)
     for piece, send in enumerate(sends):

time: 79.3 us -> 78.3 us (0.987)
  Pallas kernels: 23.1 us -> 22 us
    pallas_call x1, Pallas kernels: 10.6 us -> 9.78 us  [body(): pl.pallas_call(functools.partial(attend_kernel, False, blocks_here, head_...]
where the time goes in v8:
time: 78.3 us; the launch traced here: 78 us
  waiting for transfers between devices  29.1 us (37%)
  Pallas kernels  22 us (28%)
  starting transfers between devices  21.6 us (28%)
  local copies, waits for them, and re-layouts  3.71 us (5%)
  other arithmetic  0.84 us (1%)
    ppermute x15, waiting for transfers between devices, trade(): return lax.ppermute(x, 'var', [(n, n ^ distance) for n in range(devices)])  25.2 us
    ppermute x15, starting transfers between devices, trade(): return lax.ppermute(x, 'var', [(n, n ^ distance) for n in range(devices)])  10.8 us
    pallas_call x1, Pallas kernels, body(): pl.pallas_call(functools.partial(attend_kernel, False, blocks_here, head_...  9.78 us
    ppermute x6, starting transfers between devices, trade_level(): return lax.ppermute(x, ('var', 'head'), pairs)  9.11 us
    pallas_call x1, Pallas kernels, body(): pl.pallas_call(functools.partial(attend_kernel, True, blocks_here, head_d...  4.54 us
    unnamed x13, local copies, waits for them, and re-layouts  3.71 us
    ppermute x6, waiting for transfers between devices, trade_level(): return lax.ppermute(x, ('var', 'head'), pairs)  3.2 us
    pallas_call x1, Pallas kernels, body(): pl.pallas_call(pack_kv_kernel, out_shape=(shaped((rows, wide)),) * GROUP,...  2.48 us
  transfers between devices with their start and end apart: 22, of which 10 were waited for; matrix products, arithmetic and copies ran while one was open for 0% of the time, Pallas kernels for 10%

profile of v8, /device:TPU:0, one launch (start us, length us, event | category | flops | bytes accessed | tf_op | source)
XLA Modules:
  0.0 78.0 jit_solution(14601714852099223773)
XLA Ops:
  0.6 0.0 copy-start.5
  0.6 2.5 %shard_map.102 = (bf16[384,256]{1,0:T(8,128)(2,1)}, bf16[384,256]{1,0:T(8,128)(2,1)}, bf16[384,256]{1,0:T(8,128)(2,1)}, bf16[384,256]{1,0:T(8,128)(2,1)}) custom-call(bf16[384,512]{1,0:T(8,128)(2,1)} %k_hbm.1, bf16[384,512]{1,0:T(8,128)(2,1)} %v_hbm.1), custom_call_target="tpu_custom_call" | custom-call | flops 100663296 | bytes 1966080 | tf_op jit(solution)/shard_map/pallas_call | solution.py:524
  3.1 0.5 collective-permute-start
  3.6 2.6 %collective-permute-start.1 = (bf16[384,256]{1,0:T(8,128)(2,1)}, bf16[384,256]{1,0:T(8,128)(2,1)S(1)}, u32[]{:S(2)}, u32[]{:S(2)}) collective-permute-start(bf16[384,256]{1,0:T(8,128)(2,1)} %get-tuple-element.53), channel_id=1, source_target_pairs={{0,4},{2,6},{4,0},{6,2},{8,12},{10,14},{12,8},{14,10},{16,20},{18,... | collective-permute-start | bytes 589832 | tf_op jit(solution)/shard_map/ppermute | solution.py:487
  6.2 0.1 collective-permute-start.2
  6.3 0.0 collective-permute-done.after_ref.refs_1_
  6.3 1.0 %copy-done.1 = bf16[384,512]{1,0:T(8,128)(2,1)S(1)} copy-done((bf16[384,512]{1,0:T(8,128)(2,1)S(1)}, bf16[384,512]{1,0:T(8,128)(2,1)}, u32[]{:S(2)}) %copy-start.1) | copy-done | bytes 393240
  7.3 0.0 copy-start.2
  7.3 1.0 %copy-done.2 = bf16[384,512]{1,0:T(8,128)(2,1)S(1)} copy-done((bf16[384,512]{1,0:T(8,128)(2,1)S(1)}, bf16[384,512]{1,0:T(8,128)(2,1)}, u32[]{:S(2)}) %copy-start.2) | copy-done | bytes 393240
  8.3 0.0 copy-start.3
  8.3 0.9 %copy-done.3 = bf16[384,256]{1,0:T(8,128)(2,1)S(1)} copy-done((bf16[384,256]{1,0:T(8,128)(2,1)S(1)}, bf16[384,256]{1,0:T(8,128)(2,1)}, u32[]{:S(2)}) %copy-start.3) | copy-done | bytes 196632
  9.2 0.7 copy-done.4
  9.9 0.5 shard_map.103
  10.4 1.8 %collective-permute-done.1.refs_2_ = bf16[384,256]{1,0:T(8,128)(2,1)S(1)} collective-permute-done((bf16[384,256]{1,0:T(8,128)(2,1)}, bf16[384,256]{1,0:T(8,128)(2,1)S(1)}, u32[]{:S(2)}, u32[]{:S(2)}) %collective-permute-start.1) | collective-permute-done | bytes 196640 | tf_op jit(solution)/shard_map/ppermute | solution.py:487
  12.2 3.7 %collective-permute-done.2.refs_3_ = bf16[384,256]{1,0:T(8,128)(2,1)S(1)} collective-permute-done((bf16[384,256]{1,0:T(8,128)(2,1)}, bf16[384,256]{1,0:T(8,128)(2,1)S(1)}, u32[]{:S(2)}, u32[]{:S(2)}) %collective-permute-start.2) | collective-permute-done | bytes 196640 | tf_op jit(solution)/shard_map/ppermute | solution.py:487
  15.9 0.9 %shard_map.104 = (bf16[1936,256]{1,0:T(8,128)(2,1)S(1)}, bf16[1024,256]{1,0:T(8,128)(2,1)}, bf16[1024,256]{1,0:T(8,128)(2,1)S(1)}, bf16[400,256]{1,0:T(8,128)(2,...) custom-call(bf16[384,256]{1,0:T(8,128)(2,1)S(1)} %get-tuple-element., ...), custom_call_target="tpu_custom_call", output_to_operand_aliasing={{3}: (5, {}), {4}: (6, {}), {5}: (7, {})} | custom-call | bytes 1966080 | tf_op jit(solution)/shard_map/pallas_call | solution.py:545
  16.8 1.6 %collective-permute-start.3 = (bf16[1024,256]{1,0:T(8,128)(2,1)}, bf16[1024,256]{1,0:T(8,128)(2,1)S(1)}, u32[]{:S(2)}, u32[]{:S(2)}) collective-permute-start(bf16[1024,256]{1,0:T(8,128)(2,1)} %get-tuple-element.60), channel_id=1, source_target_pairs={{0,8},{1,9},{2,3},{3,2},{4,12},{5,13},{6,7},{7,6},{8,0},{9,1},{10,... | collective-permute-start | bytes 1572872 | tf_op jit(solution)/shard_map/ppermute | solution.py:499
  18.4 1.5 %collective-permute-start.4 = (bf16[1024,256]{1,0:T(8,128)(2,1)S(1)}, bf16[1024,256]{1,0:T(8,128)(2,1)S(1)}, u32[]{:S(2)}, u32[]{:S(2)}) collective-permute-start(bf16[1024,256]{1,0:T(8,128)(2,1)S(1)} %get-tuple-element.61), channel_id=1, source_target_pairs={{0,1},{1,0},{2,10},{3,11},{4,5},{5,4},{6,14},{7,15},{8,16},{9,17},... | collective-permute-start | bytes 1572872 | tf_op jit(solution)/shard_map/ppermute | solution.py:499
  19.9 0.0 collective-permute-start.5
  19.9 1.5 %collective-permute-start.6 = (bf16[400,256]{1,0:T(8,128)(2,1)S(1)}, bf16[400,256]{1,0:T(8,128)(2,1)}, u32[]{:S(2)}, u32[]{:S(2)}) collective-permute-start(bf16[400,256]{1,0:T(8,128)(2,1)S(1)} %get-tuple-element.63), channel_id=1, source_target_pairs={{0,4},{2,6},{4,0},{6,2},{8,12},{10,14},{12,8},{14,10},{16,20},{18,... | collective-permute-start | bytes 614408 | tf_op jit(solution)/shard_map/ppermute | solution.py:487
  21.5 0.3 collective-permute-start.7
  21.8 0.0 copy-done.5
  21.8 0.1 copy.18.kb_ref
  21.9 0.0 collective-permute-done.5.refs_3_
  21.9 6.0 %collective-permute-done.6.refs_4_ = bf16[400,256]{1,0:T(8,128)(2,1)} collective-permute-done((bf16[400,256]{1,0:T(8,128)(2,1)S(1)}, bf16[400,256]{1,0:T(8,128)(2,1)}, u32[]{:S(2)}, u32[]{:S(2)}) %collective-permute-start.6) | collective-permute-done | bytes 204832 | tf_op jit(solution)/shard_map/ppermute | solution.py:487
  27.9 3.6 %collective-permute-done.7.refs_5_ = bf16[400,256]{1,0:T(8,128)(2,1)} collective-permute-done((bf16[400,256]{1,0:T(8,128)(2,1)S(1)}, bf16[400,256]{1,0:T(8,128)(2,1)}, u32[]{:S(2)}, u32[]{:S(2)}) %collective-permute-start.7) | collective-permute-done | bytes 204832 | tf_op jit(solution)/shard_map/ppermute | solution.py:487
  31.5 0.0 collective-permute-done.3.refs_1_
  31.6 0.0 collective-permute-done.4.refs_2_
  31.6 9.8 %shard_map.105 = (bf16[4,128,256]{2,1,0:T(8,128)(2,1)S(1)}, bf16[4,128,256]{2,1,0:T(8,128)(2,1)S(1)}, bf16[28,128,256]{2,1,0:T(8,128)(2,1)S(1)}, bf16[28,128,128...) custom-call(s32[48,8]{1,0:T(8,128)S(1)} %copy.18.kb_ref, ...), custom_call_target="tpu_custom_call" | custom-call | flops 5395552768 | bytes 2000000 | tf_op jit(solution)/shard_map/pallas_call | solution.py:588
  41.4 1.7 %collective-permute-start.8 = (bf16[4,128,256]{2,1,0:T(8,128)(2,1)S(1)}, bf16[4,128,256]{2,1,0:T(8,128)(2,1)S(1)}, u32[]{:S(2)}, u32[]{:S(2)}) collective-permute-start(bf16[4,128,256]{2,1,0:T(8,128)(2,1)S(1)} %get-tuple-element.73), channel_id=1, source_target_pairs={{0,8},{1,9},{2,3},{3,2},{4,12},{5,13},{6,7},{7,6},{8,0},{9,1},{10,... | collective-permute-start | bytes 786440 | tf_op jit(solution)/shard_map/ppermute | solution.py:499
  43.0 1.5 %collective-permute-start.9 = (bf16[4,128,256]{2,1,0:T(8,128)(2,1)S(1)}, bf16[4,128,256]{2,1,0:T(8,128)(2,1)S(1)}, u32[]{:S(2)}, u32[]{:S(2)}) collective-permute-start(bf16[4,128,256]{2,1,0:T(8,128)(2,1)S(1)} %get-tuple-element.74), channel_id=1, source_target_pairs={{0,1},{1,0},{2,10},{3,11},{4,5},{5,4},{6,14},{7,15},{8,16},{9,17},... | collective-permute-start | bytes 786440 | tf_op jit(solution)/shard_map/ppermute | solution.py:499
  44.5 4.5 %shard_map.106 = (f32[12,128,256]{2,1,0:T(8,128)S(1)}, bf16[4,128,256]{2,1,0:T(8,128)(2,1)S(1)}, bf16[4,128,256]{2,1,0:T(8,128)(2,1)S(1)}, bf16[384,128]{1,0:T(8...) custom-call(s32[48,8]{1,0:T(8,128)S(1)} %copy.18.kb_ref, ...), custom_call_target="tpu_custom_call" | custom-call | flops 2657510912 | bytes 2000000 | tf_op jit(solution)/shard_map/pallas_call | solution.py:598
  49.1 1.7 %collective-permute-start.13 = (bf16[4,128,256]{2,1,0:T(8,128)(2,1)S(1)}, bf16[4,128,256]{2,1,0:T(8,128)(2,1)S(1)}, u32[]{:S(2)}, u32[]{:S(2)}) collective-permute-start(bf16[4,128,256]{2,1,0:T(8,128)(2,1)S(1)} %get-tuple-element.82), channel_id=1, source_target_pairs={{0,8},{1,9},{2,3},{3,2},{4,12},{5,13},{6,7},{7,6},{8,0},{9,1},{10,... | collective-permute-start | bytes 786440 | tf_op jit(solution)/shard_map/ppermute | solution.py:499
  50.7 1.2 %collective-permute-start.14 = (bf16[4,128,256]{2,1,0:T(8,128)(2,1)S(1)}, bf16[4,128,256]{2,1,0:T(8,128)(2,1)S(1)}, u32[]{:S(2)}, u32[]{:S(2)}) collective-permute-start(bf16[4,128,256]{2,1,0:T(8,128)(2,1)S(1)} %get-tuple-element.83), channel_id=1, source_target_pairs={{0,1},{1,0},{2,10},{3,11},{4,5},{5,4},{6,14},{7,15},{8,16},{9,17},... | collective-permute-start | bytes 786440 | tf_op jit(solution)/shard_map/ppermute | solution.py:499
  51.9 0.0 collective-permute-done.8.first_ref
  51.9 0.0 collective-permute-done.9.second_ref
  51.9 0.2 shard_map.107
  52.1 0.1 collective-permute-start.10
  52.2 1.6 %collective-permute-start.11 = (bf16[384,128]{1,0:T(8,128)(2,1)S(1)}, bf16[384,128]{1,0:T(8,128)(2,1)S(1)}, u32[]{:S(2)}, u32[]{:S(2)}) collective-permute-start(bf16[384,128]{1,0:T(8,128)(2,1)S(1)} %get-tuple-element.79), channel_id=1, source_target_pairs={{0,4},{2,6},{4,0},{6,2},{8,12},{10,14},{12,8},{14,10},{16,20},{18,... | collective-permute-start | bytes 294920 | tf_op jit(solution)/shard_map/ppermute | solution.py:487
  53.8 0.3 collective-permute-start.12
  54.0 3.2 %collective-permute-done.13.first_ref = bf16[4,128,256]{2,1,0:T(8,128)(2,1)S(1)} collective-permute-done((bf16[4,128,256]{2,1,0:T(8,128)(2,1)S(1)}, bf16[4,128,256]{2,1,0:T(8,128)(2,1)S(1)}, u32[]{:S(2)}, u32[]{:S(2)}) %collective-permute-start.13) | collective-permute-done | bytes 262176 | tf_op jit(solution)/shard_map/ppermute | solution.py:499
  57.2 0.0 collective-permute-done.14.second_ref
  57.2 0.5 shard_map.108
  57.7 0.1 collective-permute-start.15
  57.8 1.6 %collective-permute-start.16 = (bf16[192,256]{1,0:T(8,128)(2,1)S(1)}, bf16[192,256]{1,0:T(8,128)(2,1)S(1)}, u32[]{:S(2)}, u32[]{:S(2)}) collective-permute-start(bf16[192,256]{1,0:T(8,128)(2,1)S(1)} %get-tuple-element.86), channel_id=1, source_target_pairs={{0,4},{2,6},{4,0},{6,2},{8,12},{10,14},{12,8},{14,10},{16,20},{18,... | collective-permute-start | bytes 294920 | tf_op jit(solution)/shard_map/ppermute | solution.py:487
  59.3 0.0 collective-permute-done.10.refs_1_
  59.4 0.3 collective-permute-start.17
  59.6 0.0 collective-permute-done.11.refs_2_
  59.6 0.0 collective-permute-done.12.refs_3_
  59.6 0.0 collective-permute-done.15.refs_5_
  59.6 3.8 %collective-permute-done.16.refs_6_ = bf16[192,256]{1,0:T(8,128)(2,1)S(1)} collective-permute-done((bf16[192,256]{1,0:T(8,128)(2,1)S(1)}, bf16[192,256]{1,0:T(8,128)(2,1)S(1)}, u32[]{:S(2)}, u32[]{:S(2)}) %collective-permute-start.16) | collective-permute-done | bytes 98336 | tf_op jit(solution)/shard_map/ppermute | solution.py:487
  63.4 1.2 %collective-permute-done.17.refs_7_ = bf16[192,256]{1,0:T(8,128)(2,1)S(1)} collective-permute-done((bf16[192,256]{1,0:T(8,128)(2,1)S(1)}, bf16[192,256]{1,0:T(8,128)(2,1)S(1)}, u32[]{:S(2)}, u32[]{:S(2)}) %collective-permute-start.17) | collective-permute-done | bytes 98336 | tf_op jit(solution)/shard_map/ppermute | solution.py:487
  64.6 0.0 copy-done
  64.6 1.2 %shard_map.110 = bf16[192,1024]{1,0:T(8,128)(2,1)S(1)} custom-call(bf16[384,128]{1,0:T(8,128)(2,1)S(1)} %get-tuple-element.71.refs_0_, bf16[384,128]{1,0:T(8,128)(2,1)S(1)} %collective-permute-done.10.refs_1_, bf16[384,128]{1,0:T(8,128)(2,1)S(1)} %collective-permute-done.11.refs_2_, bf16[384,128]{1,0:T(8,128)(2,1)S(1)} %collective-permute-done.12.refs_3_, ...), custom_call_target="tpu_custom_call" | custom-call | flops 603979776 | bytes 4000000 | tf_op jit(solution)/shard_map/pallas_call | solution.py:634
  65.8 1.7 %collective-permute-start.21 = (bf16[192,1024]{1,0:T(8,128)(2,1)S(1)}, bf16[192,1024]{1,0:T(8,128)(2,1)S(1)}, u32[]{:S(2)}, u32[]{:S(2)}) collective-permute-start(bf16[192,1024]{1,0:T(8,128)(2,1)S(1)} %shard_map.110), channel_id=1, source_target_pairs={{0,1},{1,0},{2,3},{3,2},{4,5},{5,4},{6,7},{7,6},{8,9},{9,8},{10,11... | collective-permute-start | bytes 1179656 | tf_op jit(solution)/shard_map/ppermute | solution.py:653
  67.6 0.0 collective-permute-start.18
  67.6 1.5 %collective-permute-start.19 = (bf16[192,256]{1,0:T(8,128)(2,1)S(1)}, bf16[192,256]{1,0:T(8,128)(2,1)S(1)}, u32[]{:S(2)}, u32[]{:S(2)}) collective-permute-start(bf16[192,256]{1,0:T(8,128)(2,1)S(1)} %get-tuple-element.90), channel_id=1, source_target_pairs={{0,4},{2,6},{4,0},{6,2},{8,12},{10,14},{12,8},{14,10},{16,20},{18,... | collective-permute-start | bytes 294920 | tf_op jit(solution)/shard_map/ppermute | solution.py:487
  69.1 0.3 collective-permute-start.20
  69.4 0.0 collective-permute-done.18.refs_9_
  69.4 3.7 %collective-permute-done.19.refs_10_ = bf16[192,256]{1,0:T(8,128)(2,1)S(1)} collective-permute-done((bf16[192,256]{1,0:T(8,128)(2,1)S(1)}, bf16[192,256]{1,0:T(8,128)(2,1)S(1)}, u32[]{:S(2)}, u32[]{:S(2)}) %collective-permute-start.19) | collective-permute-done | bytes 98336 | tf_op jit(solution)/shard_map/ppermute | solution.py:487
  73.2 1.3 %collective-permute-done.20.refs_11_ = bf16[192,256]{1,0:T(8,128)(2,1)S(1)} collective-permute-done((bf16[192,256]{1,0:T(8,128)(2,1)S(1)}, bf16[192,256]{1,0:T(8,128)(2,1)S(1)}, u32[]{:S(2)}, u32[]{:S(2)}) %collective-permute-start.20) | collective-permute-done | bytes 98336 | tf_op jit(solution)/shard_map/ppermute | solution.py:487
  74.5 2.0 %shard_map.109 = (bf16[384,512]{1,0:T(8,128)(2,1)}, bf16[384,512]{1,0:T(8,128)(2,1)}, bf16[384,512]{1,0:T(8,128)(2,1)}, f32[192,1024]{1,0:T(8,128)S(1)}) custom-call(bf16[384,128]{1,0:T(8,128)(2,1)S(1)} %get-tuple-element.71.refs_0_, bf16[384,128]{1,0:T(8,128)(2,1)S(1)} %collective-permute-done.10.refs_1_, ...), custom_call_target="tpu_custom_call" | custom-call | flops 603979776 | bytes 6000000 | tf_op jit(solution)/shard_map/pallas_call | solution.py:643
  76.5 0.7 collective-permute-done.21
  77.2 0.8 %add_convert_fusion = bf16[192,1024]{1,0:T(8,128)(2,1)} fusion(f32[192,1024]{1,0:T(8,128)S(1)} %get-tuple-element.95, bf16[192,1024]{1,0:T(8,128)(2,1)S(1)} %collective-permute-done.21), kind=kLoop, calls=%fused_computation | loop fusion | flops 589824 | bytes 1572864 | tf_op jit(solution)/shard_map/convert_element_type | solution.py:655
  (3 shorter events, 0.0 us)
Async XLA Ops:
  0.6 21.2 %copy-start.5 = (s32[48,8]{0,1:T(8,128)S(1)}, s32[48,8]{0,1:T(8,128)}, u32[]{:S(2)}) copy-start(s32[48,8]{0,1:T(8,128)} %param.12) | copy-start | bytes 4612
  3.1 3.2 %collective-permute-start = (bf16[384,256]{1,0:T(8,128)(2,1)}, bf16[384,256]{1,0:T(8,128)(2,1)S(1)}, u32[]{:S(2)}, u32[]{:S(2)}) collective-permute-start(bf16[384,256]{1,0:T(8,128)(2,1)} %get-tuple-element.51), channel_id=1, source_target_pairs={{0,2},{2,0},{4,6},{6,4},{8,10},{10,8},{12,14},{14,12},{16,18},{18,... | collective-permute-start | bytes 589832 | tf_op jit(solution)/shard_map/ppermute | solution.py:487
  3.6 8.6 %collective-permute-start.1 = (bf16[384,256]{1,0:T(8,128)(2,1)}, bf16[384,256]{1,0:T(8,128)(2,1)S(1)}, u32[]{:S(2)}, u32[]{:S(2)}) collective-permute-start(bf16[384,256]{1,0:T(8,128)(2,1)} %get-tuple-element.53), channel_id=1, source_target_pairs={{0,4},{2,6},{4,0},{6,2},{8,12},{10,14},{12,8},{14,10},{16,20},{18,... | collective-permute-start | bytes 589832 | tf_op jit(solution)/shard_map/ppermute | solution.py:487
  6.2 9.7 %collective-permute-start.2 = (bf16[384,256]{1,0:T(8,128)(2,1)}, bf16[384,256]{1,0:T(8,128)(2,1)S(1)}, u32[]{:S(2)}, u32[]{:S(2)}) collective-permute-start(bf16[384,256]{1,0:T(8,128)(2,1)} %get-tuple-element.54), channel_id=1, source_target_pairs={{0,6},{2,4},{4,2},{6,0},{8,14},{10,12},{12,10},{14,8},{16,22},{18,... | collective-permute-start | bytes 589832 | tf_op jit(solution)/shard_map/ppermute | solution.py:487
  6.3 1.0 %copy-start.1 = (bf16[384,512]{1,0:T(8,128)(2,1)S(1)}, bf16[384,512]{1,0:T(8,128)(2,1)}, u32[]{:S(2)}) copy-start(bf16[384,512]{1,0:T(8,128)(2,1)} %q_ref.1) | copy-start | bytes 1179652
  7.3 1.0 %copy-start.2 = (bf16[384,512]{1,0:T(8,128)(2,1)S(1)}, bf16[384,512]{1,0:T(8,128)(2,1)}, u32[]{:S(2)}) copy-start(bf16[384,512]{1,0:T(8,128)(2,1)} %g_ref.1) | copy-start | bytes 1179652
  8.3 0.9 %copy-start.3 = (bf16[384,256]{1,0:T(8,128)(2,1)S(1)}, bf16[384,256]{1,0:T(8,128)(2,1)}, u32[]{:S(2)}) copy-start(bf16[384,256]{1,0:T(8,128)(2,1)} %get-tuple-element.50.mine_ref) | copy-start | bytes 589828
  9.2 0.7 copy-start.4
  16.8 14.8 %collective-permute-start.3 = (bf16[1024,256]{1,0:T(8,128)(2,1)}, bf16[1024,256]{1,0:T(8,128)(2,1)S(1)}, u32[]{:S(2)}, u32[]{:S(2)}) collective-permute-start(bf16[1024,256]{1,0:T(8,128)(2,1)} %get-tuple-element.60), channel_id=1, source_target_pairs={{0,8},{1,9},{2,3},{3,2},{4,12},{5,13},{6,7},{7,6},{8,0},{9,1},{10,... | collective-permute-start | bytes 1572872 | tf_op jit(solution)/shard_map/ppermute | solution.py:499
  18.4 13.1 %collective-permute-start.4 = (bf16[1024,256]{1,0:T(8,128)(2,1)S(1)}, bf16[1024,256]{1,0:T(8,128)(2,1)S(1)}, u32[]{:S(2)}, u32[]{:S(2)}) collective-permute-start(bf16[1024,256]{1,0:T(8,128)(2,1)S(1)} %get-tuple-element.61), channel_id=1, source_target_pairs={{0,1},{1,0},{2,10},{3,11},{4,5},{5,4},{6,14},{7,15},{8,16},{9,17},... | collective-permute-start | bytes 1572872 | tf_op jit(solution)/shard_map/ppermute | solution.py:499
  19.9 1.9 %collective-permute-start.5 = (bf16[400,256]{1,0:T(8,128)(2,1)S(1)}, bf16[400,256]{1,0:T(8,128)(2,1)S(1)}, u32[]{:S(2)}, u32[]{:S(2)}) collective-permute-start(bf16[400,256]{1,0:T(8,128)(2,1)S(1)} %get-tuple-element.62), channel_id=1, source_target_pairs={{0,2},{2,0},{4,6},{6,4},{8,10},{10,8},{12,14},{14,12},{16,18},{18,... | collective-permute-start | bytes 614408 | tf_op jit(solution)/shard_map/ppermute | solution.py:487
  19.9 8.0 %collective-permute-start.6 = (bf16[400,256]{1,0:T(8,128)(2,1)S(1)}, bf16[400,256]{1,0:T(8,128)(2,1)}, u32[]{:S(2)}, u32[]{:S(2)}) collective-permute-start(bf16[400,256]{1,0:T(8,128)(2,1)S(1)} %get-tuple-element.63), channel_id=1, source_target_pairs={{0,4},{2,6},{4,0},{6,2},{8,12},{10,14},{12,8},{14,10},{16,20},{18,... | collective-permute-start | bytes 614408 | tf_op jit(solution)/shard_map/ppermute | solution.py:487
  21.5 10.1 %collective-permute-start.7 = (bf16[400,256]{1,0:T(8,128)(2,1)S(1)}, bf16[400,256]{1,0:T(8,128)(2,1)}, u32[]{:S(2)}, u32[]{:S(2)}) collective-permute-start(bf16[400,256]{1,0:T(8,128)(2,1)S(1)} %get-tuple-element.64), channel_id=1, source_target_pairs={{0,6},{2,4},{4,2},{6,0},{8,14},{10,12},{12,10},{14,8},{16,22},{18,... | collective-permute-start | bytes 614408 | tf_op jit(solution)/shard_map/ppermute | solution.py:487
  41.4 10.5 %collective-permute-start.8 = (bf16[4,128,256]{2,1,0:T(8,128)(2,1)S(1)}, bf16[4,128,256]{2,1,0:T(8,128)(2,1)S(1)}, u32[]{:S(2)}, u32[]{:S(2)}) collective-permute-start(bf16[4,128,256]{2,1,0:T(8,128)(2,1)S(1)} %get-tuple-element.73), channel_id=1, source_target_pairs={{0,8},{1,9},{2,3},{3,2},{4,12},{5,13},{6,7},{7,6},{8,0},{9,1},{10,... | collective-permute-start | bytes 786440 | tf_op jit(solution)/shard_map/ppermute | solution.py:499
  43.0 8.9 %collective-permute-start.9 = (bf16[4,128,256]{2,1,0:T(8,128)(2,1)S(1)}, bf16[4,128,256]{2,1,0:T(8,128)(2,1)S(1)}, u32[]{:S(2)}, u32[]{:S(2)}) collective-permute-start(bf16[4,128,256]{2,1,0:T(8,128)(2,1)S(1)} %get-tuple-element.74), channel_id=1, source_target_pairs={{0,1},{1,0},{2,10},{3,11},{4,5},{5,4},{6,14},{7,15},{8,16},{9,17},... | collective-permute-start | bytes 786440 | tf_op jit(solution)/shard_map/ppermute | solution.py:499
  49.1 8.1 %collective-permute-start.13 = (bf16[4,128,256]{2,1,0:T(8,128)(2,1)S(1)}, bf16[4,128,256]{2,1,0:T(8,128)(2,1)S(1)}, u32[]{:S(2)}, u32[]{:S(2)}) collective-permute-start(bf16[4,128,256]{2,1,0:T(8,128)(2,1)S(1)} %get-tuple-element.82), channel_id=1, source_target_pairs={{0,8},{1,9},{2,3},{3,2},{4,12},{5,13},{6,7},{7,6},{8,0},{9,1},{10,... | collective-permute-start | bytes 786440 | tf_op jit(solution)/shard_map/ppermute | solution.py:499
  50.7 6.5 %collective-permute-start.14 = (bf16[4,128,256]{2,1,0:T(8,128)(2,1)S(1)}, bf16[4,128,256]{2,1,0:T(8,128)(2,1)S(1)}, u32[]{:S(2)}, u32[]{:S(2)}) collective-permute-start(bf16[4,128,256]{2,1,0:T(8,128)(2,1)S(1)} %get-tuple-element.83), channel_id=1, source_target_pairs={{0,1},{1,0},{2,10},{3,11},{4,5},{5,4},{6,14},{7,15},{8,16},{9,17},... | collective-permute-start | bytes 786440 | tf_op jit(solution)/shard_map/ppermute | solution.py:499
  51.9 12.7 %copy-start = (bf16[3,1024,512]{2,1,0:T(8,128)(2,1)S(1)}, bf16[3,1024,512]{2,1,0:T(8,128)(2,1)}, u32[]{:S(2)}) copy-start(bf16[3,1024,512]{2,1,0:T(8,128)(2,1)} %refs_8_.1) | copy-start | bytes 9437188
  52.1 7.2 %collective-permute-start.10 = (bf16[384,128]{1,0:T(8,128)(2,1)S(1)}, bf16[384,128]{1,0:T(8,128)(2,1)S(1)}, u32[]{:S(2)}, u32[]{:S(2)}) collective-permute-start(bf16[384,128]{1,0:T(8,128)(2,1)S(1)} %get-tuple-element.78), channel_id=1, source_target_pairs={{0,2},{2,0},{4,6},{6,4},{8,10},{10,8},{12,14},{14,12},{16,18},{18,... | collective-permute-start | bytes 294920 | tf_op jit(solution)/shard_map/ppermute | solution.py:487
  52.2 7.5 %collective-permute-start.11 = (bf16[384,128]{1,0:T(8,128)(2,1)S(1)}, bf16[384,128]{1,0:T(8,128)(2,1)S(1)}, u32[]{:S(2)}, u32[]{:S(2)}) collective-permute-start(bf16[384,128]{1,0:T(8,128)(2,1)S(1)} %get-tuple-element.79), channel_id=1, source_target_pairs={{0,4},{2,6},{4,0},{6,2},{8,12},{10,14},{12,8},{14,10},{16,20},{18,... | collective-permute-start | bytes 294920 | tf_op jit(solution)/shard_map/ppermute | solution.py:487
  53.8 5.9 %collective-permute-start.12 = (bf16[384,128]{1,0:T(8,128)(2,1)S(1)}, bf16[384,128]{1,0:T(8,128)(2,1)S(1)}, u32[]{:S(2)}, u32[]{:S(2)}) collective-permute-start(bf16[384,128]{1,0:T(8,128)(2,1)S(1)} %get-tuple-element.80), channel_id=1, source_target_pairs={{0,6},{2,4},{4,2},{6,0},{8,14},{10,12},{12,10},{14,8},{16,22},{18,... | collective-permute-start | bytes 294920 | tf_op jit(solution)/shard_map/ppermute | solution.py:487
  57.7 2.0 %collective-permute-start.15 = (bf16[192,256]{1,0:T(8,128)(2,1)S(1)}, bf16[192,256]{1,0:T(8,128)(2,1)S(1)}, u32[]{:S(2)}, u32[]{:S(2)}) collective-permute-start(bf16[192,256]{1,0:T(8,128)(2,1)S(1)} %get-tuple-element.85), channel_id=1, source_target_pairs={{0,2},{2,0},{4,6},{6,4},{8,10},{10,8},{12,14},{14,12},{16,18},{18,... | collective-permute-start | bytes 294920 | tf_op jit(solution)/shard_map/ppermute | solution.py:487
  57.8 5.7 %collective-permute-start.16 = (bf16[192,256]{1,0:T(8,128)(2,1)S(1)}, bf16[192,256]{1,0:T(8,128)(2,1)S(1)}, u32[]{:S(2)}, u32[]{:S(2)}) collective-permute-start(bf16[192,256]{1,0:T(8,128)(2,1)S(1)} %get-tuple-element.86), channel_id=1, source_target_pairs={{0,4},{2,6},{4,0},{6,2},{8,12},{10,14},{12,8},{14,10},{16,20},{18,... | collective-permute-start | bytes 294920 | tf_op jit(solution)/shard_map/ppermute | solution.py:487
  59.4 5.3 %collective-permute-start.17 = (bf16[192,256]{1,0:T(8,128)(2,1)S(1)}, bf16[192,256]{1,0:T(8,128)(2,1)S(1)}, u32[]{:S(2)}, u32[]{:S(2)}) collective-permute-start(bf16[192,256]{1,0:T(8,128)(2,1)S(1)} %get-tuple-element.87), channel_id=1, source_target_pairs={{0,6},{2,4},{4,2},{6,0},{8,14},{10,12},{12,10},{14,8},{16,22},{18,... | collective-permute-start | bytes 294920 | tf_op jit(solution)/shard_map/ppermute | solution.py:487
  65.8 11.4 %collective-permute-start.21 = (bf16[192,1024]{1,0:T(8,128)(2,1)S(1)}, bf16[192,1024]{1,0:T(8,128)(2,1)S(1)}, u32[]{:S(2)}, u32[]{:S(2)}) collective-permute-start(bf16[192,1024]{1,0:T(8,128)(2,1)S(1)} %shard_map.110), channel_id=1, source_target_pairs={{0,1},{1,0},{2,3},{3,2},{4,5},{5,4},{6,7},{7,6},{8,9},{9,8},{10,11... | collective-permute-start | bytes 1179656 | tf_op jit(solution)/shard_map/ppermute | solution.py:653
  67.6 1.9 %collective-permute-start.18 = (bf16[192,256]{1,0:T(8,128)(2,1)S(1)}, bf16[192,256]{1,0:T(8,128)(2,1)S(1)}, u32[]{:S(2)}, u32[]{:S(2)}) collective-permute-start(bf16[192,256]{1,0:T(8,128)(2,1)S(1)} %get-tuple-element.89), channel_id=1, source_target_pairs={{0,2},{2,0},{4,6},{6,4},{8,10},{10,8},{12,14},{14,12},{16,18},{18,... | collective-permute-start | bytes 294920 | tf_op jit(solution)/shard_map/ppermute | solution.py:487
  67.6 5.6 %collective-permute-start.19 = (bf16[192,256]{1,0:T(8,128)(2,1)S(1)}, bf16[192,256]{1,0:T(8,128)(2,1)S(1)}, u32[]{:S(2)}, u32[]{:S(2)}) collective-permute-start(bf16[192,256]{1,0:T(8,128)(2,1)S(1)} %get-tuple-element.90), channel_id=1, source_target_pairs={{0,4},{2,6},{4,0},{6,2},{8,12},{10,14},{12,8},{14,10},{16,20},{18,... | collective-permute-start | bytes 294920 | tf_op jit(solution)/shard_map/ppermute | solution.py:487
  69.1 5.4 %collective-permute-start.20 = (bf16[192,256]{1,0:T(8,128)(2,1)S(1)}, bf16[192,256]{1,0:T(8,128)(2,1)S(1)}, u32[]{:S(2)}, u32[]{:S(2)}) collective-permute-start(bf16[192,256]{1,0:T(8,128)(2,1)S(1)} %get-tuple-element.91), channel_id=1, source_target_pairs={{0,6},{2,4},{4,2},{6,0},{8,14},{10,12},{12,10},{14,8},{16,22},{18,... | collective-permute-start | bytes 294920 | tf_op jit(solution)/shard_map/ppermute | solution.py:487

commit v9 on v8

--- a/solution.py
+++ b/solution.py
@@ -111,18 +111,19 @@
 
 
 def pack_kv_kernel(k_hbm, v_hbm, *rest):
-    outs, (k_ref, v_ref, turned, sems) = rest[:GROUP], rest[GROUP:]
+    outs, (k_ref, v_ref, turned, sems) = rest[: 2 * GROUP], rest[2 * GROUP :]
     arrivals = load_all([(k_hbm, k_ref), (v_hbm, v_ref)], sems)
-    for half, ref in enumerate((k_ref, v_ref)):
-        for copy in arrivals[half]:
+    for i, ref in enumerate((k_ref, v_ref)):
+        for copy in arrivals[i]:
             copy.wait()
-        reorder_into(turned, half, ref)
-    send_pieces(outs, turned)
-
-
-def pack_qo_kernel(slots, head_dim, q_ref, g_ref, lse_ref, mine_ref, after_ref, *rest):
-    outs, (hold, qo_ref) = rest[:GROUP], rest[GROUP:]
-    hold[...] = mine_ref[...]
+        reorder_into(turned.at[i], 0, ref)
+        send_pieces(outs[i * GROUP : (i + 1) * GROUP], turned.at[i])
+
+
+def pack_qo_kernel(slots, head_dim, q_ref, g_ref, lse_ref, key_ref, value_ref, after_ref, *rest):
+    outs, (hold_key, hold_value, qo_ref) = rest[:GROUP], rest[GROUP:]
+    hold_key[...] = key_ref[...]
+    hold_value[...] = value_ref[...]
     rows = q_ref.shape[0]
     blocks = rows // BLOCK
     reorder_into(qo_ref, 0, q_ref, head_dim ** (-0.5))
@@ -161,11 +162,18 @@
 
 
 def line_kernel(carried, *refs):
-    pieces, query_piece, refs = refs[:GROUP], refs[GROUP], refs[GROUP + 1 + carried :]
+    pieces, refs = refs[:GROUP], refs[GROUP:]
+    rows = pieces[0].shape[0]
+    blocks = rows // BLOCK
+    if carried:
+        query_piece, refs = refs[0], refs[2 + carried :]
+        tail = GROUP * rows
+        for cols in (slice(0, LANES), slice(LANES, 2 * LANES)):
+            refs[0][tail : tail + rows + LSE_ROWS] = query_piece[:, cols]
+            tail += rows + LSE_ROWS
+    else:
+        refs = refs[2:]
     own, first_out, second_out = refs[:3]
-    rows = pieces[0].shape[0]
-    own[GROUP * rows :] = query_piece[...]
-    blocks = rows // BLOCK
     me = lax.axis_index("var") % GROUP
     for distance in range(GROUP):
         at = pl.ds(pl.multiple_of((me ^ distance) * rows, rows), rows)
@@ -175,6 +183,10 @@
         out[...] = own[pl.ds(pl.multiple_of(start * BLOCK, BLOCK), SPAN * BLOCK)]
 
 
+def gate_kernel(*refs):
+    pass
+
+
 def attend_kernel(last, blocks_here, head_dim, kb_ref, *refs):
     if last:
         kv_win, k_turn, shifts, qo_ref, before, dq_before, *refs = refs
@@ -182,7 +194,7 @@
         dq_outs, refs = refs[:GROUP], refs[GROUP:]
         acc, queries, grads, crossed, prob, slope, dq_all = refs
     else:
-        kv_refs, refs = refs[:3], refs[3:]
+        key_refs, value_refs, refs = refs[:3], refs[3:6], refs[6:]
         qo_pieces, refs = refs[: GROUP - 1], refs[GROUP - 1 :]
         first_out, second_out, kv_win, k_turn, shifts, qo_ref, kept_out, dq_all, *refs = refs
         acc, queries, grads, crossed, prob, slope = refs
@@ -202,12 +214,20 @@
         dq_all[...] = dq_before[...]
     else:
         top = window - SPAN
-        for ref, start, count in zip(
-            kv_refs, (SPAN, (1 - odd) * top, odd * top), (group_blocks, SPAN, SPAN)
-        ):
-            kv_win[pl.ds(start, count)] = ref[: count * BLOCK].reshape(count, BLOCK, 2 * LANES)
-        own_queries = kv_refs[0].at[pl.ds(group_blocks * BLOCK, rows + LSE_ROWS)]
-        stage_pieces(qo_ref, (own_queries, *qo_pieces))
+        for cols, kv_refs in ((low, key_refs), (high, value_refs)):
+            for ref, start, count in zip(
+                kv_refs, (SPAN, (1 - odd) * top, odd * top), (group_blocks, SPAN, SPAN)
+            ):
+                kv_win[pl.ds(start, count), :, cols] = ref[: count * BLOCK].reshape(
+                    count, BLOCK, LANES
+                )
+        me = lax.axis_index("var") % GROUP
+        tail = group_blocks * BLOCK
+        for cols in (low, high):
+            qo_ref[me, :, cols] = value_refs[0][tail : tail + rows + LSE_ROWS]
+            tail += rows + LSE_ROWS
+        for distance, piece in enumerate(qo_pieces):
+            qo_ref[me ^ (distance + 1)] = piece[...]
         key_patch = lax.broadcasted_iota(jnp.int32, (8, LANES), 0)
         query_patch = lax.broadcasted_iota(jnp.int32, (8, LANES), 1) & 7
         usable = key_patch <= query_patch
@@ -521,40 +541,62 @@
 
     size = rows * features * 2
 
-    kvs = pl.pallas_call(
+    packed = pl.pallas_call(
         pack_kv_kernel,
-        out_shape=(shaped((rows, wide)),) * GROUP,
+        out_shape=(shaped((rows, LANES)),) * (2 * GROUP),
         in_specs=[hbm] * 2,
-        out_specs=(vmem(),) * GROUP,
+        out_specs=(vmem(),) * (2 * GROUP),
         scratch_shapes=[pltpu.VMEM((rows, features), BF16)] * 2
-        + [staged(rows, wide), pltpu.SemaphoreType.DMA((2, LOADS))],
+        + [pltpu.VMEM((2, GROUP, rows, LANES), BF16), pltpu.SemaphoreType.DMA((2, LOADS))],
         compiler_params=params(PACK_MIB),
         cost_estimate=cost(4 * rows * features * BLOCK, 5 * size),
     )(keys, values)
-    kvs = swap(kvs)
-    *qos, kvs[0] = pl.pallas_call(
+    key_pieces = swap(packed[:GROUP])
+    value_pieces = swap(packed[GROUP:])
+    *qos, key_pieces[0], value_pieces[0] = pl.pallas_call(
         functools.partial(pack_qo_kernel, slots, head_dim),
-        out_shape=(shaped((rows + LSE_ROWS, wide)),) * GROUP + (shaped((rows, wide)),),
-        in_specs=[vmem()] * 4 + [anywhere],
-        out_specs=(vmem(),) * (GROUP + 1),
+        out_shape=(shaped((rows + LSE_ROWS, wide)),) * GROUP + (shaped((rows, LANES)),) * 2,
+        in_specs=[vmem()] * 5 + [anywhere],
+        out_specs=(vmem(),) * (GROUP + 2),
         scratch_shapes=[staged(rows + LSE_ROWS, wide)],
         compiler_params=params(8),
         cost_estimate=cost(4 * rows * features * BLOCK, 10 * size),
-    )(queries, out_grad, log_sum_exp, kvs[0], kvs[1])
+    )(queries, out_grad, log_sum_exp, packed[0], packed[GROUP], key_pieces[1])
+    sends_shape = (shaped((SPAN * BLOCK, LANES)),) * 2
+    own_keys, first_keys, second_keys = pl.pallas_call(
+        functools.partial(line_kernel, 0),
+        out_shape=(shaped((GROUP * rows, LANES)),) + sends_shape,
+        in_specs=[vmem()] * GROUP + [anywhere] * 2,
+        out_specs=(vmem(),) * 3,
+        compiler_params=params(8),
+        cost_estimate=cost(0, 3 * size),
+    )(*key_pieces, value_pieces[1], value_pieces[2])
+    first_keys = trade_first(first_keys)
+    second_keys = trade_second(second_keys)
     carried = tuple(qos[1:])
-    own, first, second, *carried = pl.pallas_call(
-        functools.partial(line_kernel, len(carried)),
-        out_shape=(shaped((GROUP * rows + rows + LSE_ROWS, wide)),)
-        + (shaped((SPAN * BLOCK, wide)),) * 2
+    count = len(carried)
+    own_values, first_values, second_values, *carried = pl.pallas_call(
+        functools.partial(line_kernel, count),
+        out_shape=(shaped((GROUP * rows + 2 * (rows + LSE_ROWS), LANES)),)
+        + sends_shape
         + tuple(shaped(x.shape) for x in carried),
-        in_specs=[vmem()] * (GROUP + 1) + [anywhere] * len(carried),
-        out_specs=(vmem(),) * 3 + (anywhere,) * len(carried),
-        input_output_aliases={GROUP + 1 + i: 3 + i for i in range(len(carried))},
+        in_specs=[vmem()] * (GROUP + 1) + [anywhere] * (count + 1),
+        out_specs=(vmem(),) * 3 + (anywhere,) * count,
+        input_output_aliases={GROUP + 2 + i: 3 + i for i in range(count)},
         compiler_params=params(8),
         cost_estimate=cost(0, 5 * size),
-    )(*kvs, qos[0], *carried)
-    first = trade_first(first)
-    second = trade_second(second)
+    )(*value_pieces, qos[0], own_keys, *carried)
+    first_values = trade_first(first_values)
+    second_values = trade_second(second_values)
+    carried[-1] = pl.pallas_call(
+        gate_kernel,
+        out_shape=shaped(carried[-1].shape),
+        in_specs=[anywhere] * 3,
+        out_specs=anywhere,
+        input_output_aliases={0: 0},
+        compiler_params=params(4),
+        cost_estimate=cost(0, 1024),
+    )(carried[-1], first_keys, second_keys)
     qos = swap([None, *carried])[1:]
 
     pairs = group_blocks * slot_count * BLOCK * BLOCK * slots
@@ -588,12 +630,21 @@
     first, second, *state = pl.pallas_call(
         functools.partial(attend_kernel, False, blocks_here, head_dim),
         out_shape=outer + state,
-        in_specs=[smem] + [vmem()] * (2 + GROUP),
+        in_specs=[smem] + [vmem()] * (5 + GROUP),
         out_specs=(vmem(),) * 8,
         scratch_shapes=[acc_scratch] + work,
         compiler_params=params(16),
         cost_estimate=attend_cost(0.67),
-    )(key_blocks, own, first, second, *qos)
+    )(
+        key_blocks,
+        own_keys,
+        first_keys,
+        second_keys,
+        own_values,
+        first_values,
+        second_values,
+        *qos,
+    )
     outer_back = (trade_first(first), trade_second(second))
     own_sum, first, second, *dqs = pl.pallas_call(
         functools.partial(attend_kernel, True, blocks_here, head_dim),

time: 78.3 us -> 83.3 us (1.064)
  waiting for transfers between devices: 29.1 us -> 32 us
  starting transfers between devices: 21.6 us -> 23.4 us
  local copies, waits for them, and re-layouts: 3.71 us -> 4.57 us
    ppermute x15 -> x18, starting transfers between devices: 10.8 us -> 13.1 us  [trade(): return lax.ppermute(x, 'var', [(n, n ^ distance) for n in range(devices)])]
    ppermute x6 -> x8, waiting for transfers between devices: 3.2 us -> 5.17 us  [trade_level(): return lax.ppermute(x, ('var', 'head'), pairs)]
    pallas_call x2 -> x4, Pallas kernels: 3.41 us -> 2.54 us  [the longest x1 2.36 us: body(): pl.pallas_call(pack_kv_kernel, out_shape=(shaped((rows, LANES)),) * (2 *...]
    unnamed x13 -> x15, local copies, waits for them, and re-layouts: 3.71 us -> 4.57 us
    ppermute x6 -> x8, starting transfers between devices: 9.11 us -> 9.31 us  [trade_level(): return lax.ppermute(x, ('var', 'head'), pairs)]
    ppermute x15 -> x18, waiting for transfers between devices: 25.2 us -> 25.3 us  [trade(): return lax.ppermute(x, 'var', [(n, n ^ distance) for n in range(devices)])]
  transfers between devices with their start and end apart: 22 -> 27, of which waited for: 10 -> 12; matrix products, arithmetic and copies ran while one was open for 0% -> 0% of each run, Pallas kernels for 10% -> 9%
where the time goes in v9:
time: 83.3 us; the launch traced here: 82.9 us
  waiting for transfers between devices  32 us (38%)
  starting transfers between devices  23.4 us (28%)
  Pallas kernels  21.4 us (26%)
  local copies, waits for them, and re-layouts  4.57 us (5%)
  other arithmetic  0.84 us (1%)
    ppermute x18, waiting for transfers between devices, trade(): return lax.ppermute(x, 'var', [(n, n ^ distance) for n in range(devices)])  25.3 us
    ppermute x18, starting transfers between devices, trade(): return lax.ppermute(x, 'var', [(n, n ^ distance) for n in range(devices)])  13.1 us
    pallas_call x1, Pallas kernels, body(): pl.pallas_call(functools.partial(attend_kernel, False, blocks_here, head_...  9.98 us
    ppermute x8, starting transfers between devices, trade_level(): return lax.ppermute(x, ('var', 'head'), pairs)  9.31 us
    ppermute x8, waiting for transfers between devices, trade_level(): return lax.ppermute(x, ('var', 'head'), pairs)  5.17 us
    unnamed x15, local copies, waits for them, and re-layouts  4.57 us
    pallas_call x1, Pallas kernels, body(): pl.pallas_call(functools.partial(attend_kernel, True, blocks_here, head_d...  4.54 us
    pallas_call x1, Pallas kernels, body(): pl.pallas_call(pack_kv_kernel, out_shape=(shaped((rows, LANES)),) * (2 *...  2.36 us
  transfers between devices with their start and end apart: 27, of which 12 were waited for; matrix products, arithmetic and copies ran while one was open for 0% of the time, Pallas kernels for 9%

profile of v9, /device:TPU:0, one launch (start us, length us, event | category | flops | bytes accessed | tf_op | source)
XLA Modules:
  0.0 82.9 jit_solution(10149766731536293766)
XLA Ops:
  0.6 2.4 %shard_map.102 = (bf16[384,128]{1,0:T(8,128)(2,1)}, bf16[384,128]{1,0:T(8,128)(2,1)}, bf16[384,128]{1,0:T(8,128)(2,1)}, bf16[384,128]{1,0:T(8,128)(2,1)}, bf16[3...) custom-call(bf16[384,512]{1,0:T(8,128)(2,1)} %k_hbm.1, ...), custom_call_target="tpu_custom_call" | custom-call | flops 100663296 | bytes 1966080 | tf_op jit(solution)/shard_map/pallas_call | solution.py:544
  3.0 0.5 collective-permute-start
  3.5 2.6 %collective-permute-start.1 = (bf16[384,128]{1,0:T(8,128)(2,1)}, bf16[384,128]{1,0:T(8,128)(2,1)S(1)}, u32[]{:S(2)}, u32[]{:S(2)}) collective-permute-start(bf16[384,128]{1,0:T(8,128)(2,1)} %get-tuple-element.62), channel_id=1, source_target_pairs={{0,4},{2,6},{4,0},{6,2},{8,12},{10,14},{12,8},{14,10},{16,20},{18,... | collective-permute-start | bytes 294920 | tf_op jit(solution)/shard_map/ppermute | solution.py:507
  6.1 0.1 collective-permute-start.2
  6.2 0.1 collective-permute-start.3
  6.3 1.9 %collective-permute-start.4 = (bf16[384,128]{1,0:T(8,128)(2,1)}, bf16[384,128]{1,0:T(8,128)(2,1)S(1)}, u32[]{:S(2)}, u32[]{:S(2)}) collective-permute-start(bf16[384,128]{1,0:T(8,128)(2,1)} %get-tuple-element.65), channel_id=1, source_target_pairs={{0,4},{2,6},{4,0},{6,2},{8,12},{10,14},{12,8},{14,10},{16,20},{18,... | collective-permute-start | bytes 294920 | tf_op jit(solution)/shard_map/ppermute | solution.py:507
  8.3 0.0 collective-permute-done.after_ref.refs_1_
  8.3 1.0 %copy-done.1 = bf16[384,512]{1,0:T(8,128)(2,1)S(1)} copy-done((bf16[384,512]{1,0:T(8,128)(2,1)S(1)}, bf16[384,512]{1,0:T(8,128)(2,1)}, u32[]{:S(2)}) %copy-start.1) | copy-done | bytes 393240
  9.3 1.0 %copy-done.2 = bf16[384,512]{1,0:T(8,128)(2,1)S(1)} copy-done((bf16[384,512]{1,0:T(8,128)(2,1)S(1)}, bf16[384,512]{1,0:T(8,128)(2,1)}, u32[]{:S(2)}) %copy-start.2) | copy-done | bytes 393240
  10.3 0.9 %copy-done.3 = bf16[384,128]{1,0:T(8,128)(2,1)S(1)} copy-done((bf16[384,128]{1,0:T(8,128)(2,1)S(1)}, bf16[384,128]{1,0:T(8,128)(2,1)}, u32[]{:S(2)}) %copy-start.3) | copy-done | bytes 98328
  11.1 0.9 %copy-done.4 = bf16[384,128]{1,0:T(8,128)(2,1)S(1)} copy-done((bf16[384,128]{1,0:T(8,128)(2,1)S(1)}, bf16[384,128]{1,0:T(8,128)(2,1)}, u32[]{:S(2)}) %copy-start.4) | copy-done | bytes 98328
  12.0 0.7 copy-done.5
  12.7 0.5 shard_map.103
  13.2 0.0 copy-start.6
  13.2 0.0 collective-permute-done.1.refs_2_
  13.3 0.6 collective-permute-done.4.refs_5_.refs_2_
  13.9 0.1 shard_map.104
  14.0 1.9 %collective-permute-start.5 = (bf16[1024,128]{1,0:T(8,128)(2,1)S(1)}, bf16[1024,128]{1,0:T(8,128)(2,1)S(1)}, u32[]{:S(2)}, u32[]{:S(2)}) collective-permute-start(bf16[1024,128]{1,0:T(8,128)(2,1)S(1)} %get-tuple-element.67), channel_id=1, source_target_pairs={{0,8},{1,9},{2,3},{3,2},{4,12},{5,13},{6,7},{7,6},{8,0},{9,1},{10,... | collective-permute-start | bytes 786440 | tf_op jit(solution)/shard_map/ppermute | solution.py:519
  15.9 1.5 %collective-permute-start.6 = (bf16[1024,128]{1,0:T(8,128)(2,1)S(1)}, bf16[1024,128]{1,0:T(8,128)(2,1)S(1)}, u32[]{:S(2)}, u32[]{:S(2)}) collective-permute-start(bf16[1024,128]{1,0:T(8,128)(2,1)S(1)} %get-tuple-element.68), channel_id=1, source_target_pairs={{0,1},{1,0},{2,10},{3,11},{4,5},{5,4},{6,14},{7,15},{8,16},{9,17},... | collective-permute-start | bytes 786440 | tf_op jit(solution)/shard_map/ppermute | solution.py:519
  17.4 0.3 collective-permute-start.7
  17.7 4.9 %collective-permute-done.7.refs_3_ = bf16[384,128]{1,0:T(8,128)(2,1)S(1)} collective-permute-done((bf16[384,128]{1,0:T(8,128)(2,1)}, bf16[384,128]{1,0:T(8,128)(2,1)S(1)}, u32[]{:S(2)}, u32[]{:S(2)}) %collective-permute-start.7) | collective-permute-done | bytes 98336 | tf_op jit(solution)/shard_map/ppermute | solution.py:507
  22.6 0.1 shard_map.105
  22.7 1.7 %collective-permute-start.8 = (bf16[1024,128]{1,0:T(8,128)(2,1)S(1)}, bf16[1024,128]{1,0:T(8,128)(2,1)S(1)}, u32[]{:S(2)}, u32[]{:S(2)}) collective-permute-start(bf16[1024,128]{1,0:T(8,128)(2,1)S(1)} %get-tuple-element.76), channel_id=1, source_target_pairs={{0,8},{1,9},{2,3},{3,2},{4,12},{5,13},{6,7},{7,6},{8,0},{9,1},{10,... | collective-permute-start | bytes 786440 | tf_op jit(solution)/shard_map/ppermute | solution.py:519
  24.4 1.5 %collective-permute-start.9 = (bf16[1024,128]{1,0:T(8,128)(2,1)S(1)}, bf16[1024,128]{1,0:T(8,128)(2,1)S(1)}, u32[]{:S(2)}, u32[]{:S(2)}) collective-permute-start(bf16[1024,128]{1,0:T(8,128)(2,1)S(1)} %get-tuple-element.77), channel_id=1, source_target_pairs={{0,1},{1,0},{2,10},{3,11},{4,5},{5,4},{6,14},{7,15},{8,16},{9,17},... | collective-permute-start | bytes 786440 | tf_op jit(solution)/shard_map/ppermute | solution.py:519
  25.9 0.0 collective-permute-start.10
  25.9 0.0 collective-permute-done.5.refs_1_
  25.9 0.7 collective-permute-start.11
  26.6 1.2 %collective-permute-start.12 = (bf16[400,256]{1,0:T(8,128)(2,1)S(1)}, bf16[400,256]{1,0:T(8,128)(2,1)}, u32[]{:S(2)}, u32[]{:S(2)}) collective-permute-start(bf16[400,256]{1,0:T(8,128)(2,1)S(1)} %shard_map.106), channel_id=1, source_target_pairs={{0,6},{2,4},{4,2},{6,0},{8,14},{10,12},{12,10},{14,8},{16,22},{18,... | collective-permute-start | bytes 614408 | tf_op jit(solution)/shard_map/ppermute | solution.py:507
  27.8 0.1 copy.19.kb_ref
  27.9 0.0 collective-permute-done.10.refs_6_
  27.9 6.0 %collective-permute-done.11.refs_7_ = bf16[400,256]{1,0:T(8,128)(2,1)} collective-permute-done((bf16[400,256]{1,0:T(8,128)(2,1)S(1)}, bf16[400,256]{1,0:T(8,128)(2,1)}, u32[]{:S(2)}, u32[]{:S(2)}) %collective-permute-start.11) | collective-permute-done | bytes 204832 | tf_op jit(solution)/shard_map/ppermute | solution.py:507
  33.9 0.0 collective-permute-done.8.refs_4_
  33.9 0.0 collective-permute-done.9.refs_5_
  33.9 3.6 %collective-permute-done.12.refs_8_ = bf16[400,256]{1,0:T(8,128)(2,1)} collective-permute-done((bf16[400,256]{1,0:T(8,128)(2,1)S(1)}, bf16[400,256]{1,0:T(8,128)(2,1)}, u32[]{:S(2)}, u32[]{:S(2)}) %collective-permute-start.12) | collective-permute-done | bytes 204832 | tf_op jit(solution)/shard_map/ppermute | solution.py:507
  37.5 10.0 %shard_map.107 = (bf16[4,128,256]{2,1,0:T(8,128)(2,1)S(1)}, bf16[4,128,256]{2,1,0:T(8,128)(2,1)S(1)}, bf16[28,128,256]{2,1,0:T(8,128)(2,1)S(1)}, bf16[28,128,128...) custom-call(s32[48,8]{1,0:T(8,128)S(1)} %copy.19.kb_ref, ...), custom_call_target="tpu_custom_call" | custom-call | flops 5395552768 | bytes 2000000 | tf_op jit(solution)/shard_map/pallas_call | solution.py:630
  47.5 0.6 collective-permute-start.13
  48.1 0.5 collective-permute-start.14
  48.6 4.5 %shard_map.108 = (f32[12,128,256]{2,1,0:T(8,128)S(1)}, bf16[4,128,256]{2,1,0:T(8,128)(2,1)S(1)}, bf16[4,128,256]{2,1,0:T(8,128)(2,1)S(1)}, bf16[384,128]{1,0:T(8...) custom-call(s32[48,8]{1,0:T(8,128)S(1)} %copy.19.kb_ref, ...), custom_call_target="tpu_custom_call" | custom-call | flops 2657510912 | bytes 2000000 | tf_op jit(solution)/shard_map/pallas_call | solution.py:649
  53.1 1.1 %collective-permute-start.18 = (bf16[4,128,256]{2,1,0:T(8,128)(2,1)S(1)}, bf16[4,128,256]{2,1,0:T(8,128)(2,1)S(1)}, u32[]{:S(2)}, u32[]{:S(2)}) collective-permute-start(bf16[4,128,256]{2,1,0:T(8,128)(2,1)S(1)} %get-tuple-element.98), channel_id=1, source_target_pairs={{0,8},{1,9},{2,3},{3,2},{4,12},{5,13},{6,7},{7,6},{8,0},{9,1},{10,... | collective-permute-start | bytes 786440 | tf_op jit(solution)/shard_map/ppermute | solution.py:519
  54.2 0.6 collective-permute-start.19
  54.8 1.5 %collective-permute-done.13.first_ref = bf16[4,128,256]{2,1,0:T(8,128)(2,1)S(1)} collective-permute-done((bf16[4,128,256]{2,1,0:T(8,128)(2,1)S(1)}, bf16[4,128,256]{2,1,0:T(8,128)(2,1)S(1)}, u32[]{:S(2)}, u32[]{:S(2)}) %collective-permute-start.13) | collective-permute-done | bytes 262176 | tf_op jit(solution)/shard_map/ppermute | solution.py:519
  56.3 0.3 collective-permute-done.14.second_ref
  56.6 0.2 shard_map.109
  56.7 0.1 collective-permute-start.15
  56.8 0.5 collective-permute-start.16
  57.3 1.4 %collective-permute-start.17 = (bf16[384,128]{1,0:T(8,128)(2,1)S(1)}, bf16[384,128]{1,0:T(8,128)(2,1)S(1)}, u32[]{:S(2)}, u32[]{:S(2)}) collective-permute-start(bf16[384,128]{1,0:T(8,128)(2,1)S(1)} %get-tuple-element.96), channel_id=1, source_target_pairs={{0,6},{2,4},{4,2},{6,0},{8,14},{10,12},{12,10},{14,8},{16,22},{18,... | collective-permute-start | bytes 294920 | tf_op jit(solution)/shard_map/ppermute | solution.py:507
  58.7 3.4 %collective-permute-done.18.first_ref = bf16[4,128,256]{2,1,0:T(8,128)(2,1)S(1)} collective-permute-done((bf16[4,128,256]{2,1,0:T(8,128)(2,1)S(1)}, bf16[4,128,256]{2,1,0:T(8,128)(2,1)S(1)}, u32[]{:S(2)}, u32[]{:S(2)}) %collective-permute-start.18) | collective-permute-done | bytes 262176 | tf_op jit(solution)/shard_map/ppermute | solution.py:519
  62.1 0.0 collective-permute-done.19.second_ref
  62.1 0.5 shard_map.110
  62.6 0.1 collective-permute-start.20
  62.6 0.8 collective-permute-start.21
  63.4 1.1 %collective-permute-start.22 = (bf16[192,256]{1,0:T(8,128)(2,1)S(1)}, bf16[192,256]{1,0:T(8,128)(2,1)S(1)}, u32[]{:S(2)}, u32[]{:S(2)}) collective-permute-start(bf16[192,256]{1,0:T(8,128)(2,1)S(1)} %get-tuple-element.103), channel_id=1, source_target_pairs={{0,6},{2,4},{4,2},{6,0},{8,14},{10,12},{12,10},{14,8},{16,22},{18,... | collective-permute-start | bytes 294920 | tf_op jit(solution)/shard_map/ppermute | solution.py:507
  64.5 0.0 collective-permute-done.16.refs_2_
  64.5 3.8 %collective-permute-done.21.refs_6_ = bf16[192,256]{1,0:T(8,128)(2,1)S(1)} collective-permute-done((bf16[192,256]{1,0:T(8,128)(2,1)S(1)}, bf16[192,256]{1,0:T(8,128)(2,1)S(1)}, u32[]{:S(2)}, u32[]{:S(2)}) %collective-permute-start.21) | collective-permute-done | bytes 98336 | tf_op jit(solution)/shard_map/ppermute | solution.py:507
  68.3 1.2 %collective-permute-done.22.refs_7_ = bf16[192,256]{1,0:T(8,128)(2,1)S(1)} collective-permute-done((bf16[192,256]{1,0:T(8,128)(2,1)S(1)}, bf16[192,256]{1,0:T(8,128)(2,1)S(1)}, u32[]{:S(2)}, u32[]{:S(2)}) %collective-permute-start.22) | collective-permute-done | bytes 98336 | tf_op jit(solution)/shard_map/ppermute | solution.py:507
  69.5 1.2 %shard_map.112 = bf16[192,1024]{1,0:T(8,128)(2,1)S(1)} custom-call(bf16[384,128]{1,0:T(8,128)(2,1)S(1)} %get-tuple-element.87.refs_0_, bf16[384,128]{1,0:T(8,128)(2,1)S(1)} %collective-permute-done.15.refs_1_, bf16[384,128]{1,0:T(8,128)(2,1)S(1)} %collective-permute-done.16.refs_2_, bf16[384,128]{1,0:T(8,128)(2,1)S(1)} %collective-permute-done.17.refs_3_, ...), custom_call_target="tpu_custom_call" | custom-call | flops 603979776 | bytes 4000000 | tf_op jit(solution)/shard_map/pallas_call | solution.py:685
  70.7 0.9 %collective-permute-start.26 = (bf16[192,1024]{1,0:T(8,128)(2,1)S(1)}, bf16[192,1024]{1,0:T(8,128)(2,1)S(1)}, u32[]{:S(2)}, u32[]{:S(2)}) collective-permute-start(bf16[192,1024]{1,0:T(8,128)(2,1)S(1)} %shard_map.112), channel_id=1, source_target_pairs={{0,1},{1,0},{2,3},{3,2},{4,5},{5,4},{6,7},{7,6},{8,9},{9,8},{10,11... | collective-permute-start | bytes 1179656 | tf_op jit(solution)/shard_map/ppermute | solution.py:704
  71.6 0.8 collective-permute-start.24
  72.4 1.1 %collective-permute-start.25 = (bf16[192,256]{1,0:T(8,128)(2,1)S(1)}, bf16[192,256]{1,0:T(8,128)(2,1)S(1)}, u32[]{:S(2)}, u32[]{:S(2)}) collective-permute-start(bf16[192,256]{1,0:T(8,128)(2,1)S(1)} %get-tuple-element.107), channel_id=1, source_target_pairs={{0,6},{2,4},{4,2},{6,0},{8,14},{10,12},{12,10},{14,8},{16,22},{18,... | collective-permute-start | bytes 294920 | tf_op jit(solution)/shard_map/ppermute | solution.py:507
  73.5 3.7 %collective-permute-done.24.refs_10_ = bf16[192,256]{1,0:T(8,128)(2,1)S(1)} collective-permute-done((bf16[192,256]{1,0:T(8,128)(2,1)S(1)}, bf16[192,256]{1,0:T(8,128)(2,1)S(1)}, u32[]{:S(2)}, u32[]{:S(2)}) %collective-permute-start.24) | collective-permute-done | bytes 98336 | tf_op jit(solution)/shard_map/ppermute | solution.py:507
  77.2 1.3 %collective-permute-done.25.refs_11_ = bf16[192,256]{1,0:T(8,128)(2,1)S(1)} collective-permute-done((bf16[192,256]{1,0:T(8,128)(2,1)S(1)}, bf16[192,256]{1,0:T(8,128)(2,1)S(1)}, u32[]{:S(2)}, u32[]{:S(2)}) %collective-permute-start.25) | collective-permute-done | bytes 98336 | tf_op jit(solution)/shard_map/ppermute | solution.py:507
  78.6 2.0 %shard_map.111 = (bf16[384,512]{1,0:T(8,128)(2,1)}, bf16[384,512]{1,0:T(8,128)(2,1)}, bf16[384,512]{1,0:T(8,128)(2,1)}, f32[192,1024]{1,0:T(8,128)S(1)}) custom-call(bf16[384,128]{1,0:T(8,128)(2,1)S(1)} %get-tuple-element.87.refs_0_, bf16[384,128]{1,0:T(8,128)(2,1)S(1)} %collective-permute-done.15.refs_1_, ...), custom_call_target="tpu_custom_call" | custom-call | flops 603979776 | bytes 6000000 | tf_op jit(solution)/shard_map/pallas_call | solution.py:694
  80.5 1.5 %collective-permute-done.26 = bf16[192,1024]{1,0:T(8,128)(2,1)S(1)} collective-permute-done((bf16[192,1024]{1,0:T(8,128)(2,1)S(1)}, bf16[192,1024]{1,0:T(8,128)(2,1)S(1)}, u32[]{:S(2)}, u32[]{:S(2)}) %collective-permute-start.26) | collective-permute-done | bytes 393248 | tf_op jit(solution)/shard_map/ppermute | solution.py:704
  82.1 0.8 %add_convert_fusion = bf16[192,1024]{1,0:T(8,128)(2,1)} fusion(f32[192,1024]{1,0:T(8,128)S(1)} %get-tuple-element.111, bf16[192,1024]{1,0:T(8,128)(2,1)S(1)} %collective-permute-done.26), kind=kLoop, calls=%fused_computation | loop fusion | flops 589824 | bytes 1572864 | tf_op jit(solution)/shard_map/convert_element_type | solution.py:706
  (17 shorter events, 0.0 us)
Async XLA Ops:
  3.0 5.3 %collective-permute-start = (bf16[384,128]{1,0:T(8,128)(2,1)}, bf16[384,128]{1,0:T(8,128)(2,1)S(1)}, u32[]{:S(2)}, u32[]{:S(2)}) collective-permute-start(bf16[384,128]{1,0:T(8,128)(2,1)} %get-tuple-element.60), channel_id=1, source_target_pairs={{0,2},{2,0},{4,6},{6,4},{8,10},{10,8},{12,14},{14,12},{16,18},{18,... | collective-permute-start | bytes 294920 | tf_op jit(solution)/shard_map/ppermute | solution.py:507
  3.5 9.7 %collective-permute-start.1 = (bf16[384,128]{1,0:T(8,128)(2,1)}, bf16[384,128]{1,0:T(8,128)(2,1)S(1)}, u32[]{:S(2)}, u32[]{:S(2)}) collective-permute-start(bf16[384,128]{1,0:T(8,128)(2,1)} %get-tuple-element.62), channel_id=1, source_target_pairs={{0,4},{2,6},{4,0},{6,2},{8,12},{10,14},{12,8},{14,10},{16,20},{18,... | collective-permute-start | bytes 294920 | tf_op jit(solution)/shard_map/ppermute | solution.py:507
  6.1 7.2 %collective-permute-start.2 = (bf16[384,128]{1,0:T(8,128)(2,1)}, bf16[384,128]{1,0:T(8,128)(2,1)S(1)}, u32[]{:S(2)}, u32[]{:S(2)}) collective-permute-start(bf16[384,128]{1,0:T(8,128)(2,1)} %get-tuple-element.63), channel_id=1, source_target_pairs={{0,6},{2,4},{4,2},{6,0},{8,14},{10,12},{12,10},{14,8},{16,22},{18,... | collective-permute-start | bytes 294920 | tf_op jit(solution)/shard_map/ppermute | solution.py:507
  6.2 7.1 %collective-permute-start.3 = (bf16[384,128]{1,0:T(8,128)(2,1)}, bf16[384,128]{1,0:T(8,128)(2,1)S(1)}, u32[]{:S(2)}, u32[]{:S(2)}) collective-permute-start(bf16[384,128]{1,0:T(8,128)(2,1)} %get-tuple-element.64), channel_id=1, source_target_pairs={{0,2},{2,0},{4,6},{6,4},{8,10},{10,8},{12,14},{14,12},{16,18},{18,... | collective-permute-start | bytes 294920 | tf_op jit(solution)/shard_map/ppermute | solution.py:507
  6.3 7.6 %collective-permute-start.4 = (bf16[384,128]{1,0:T(8,128)(2,1)}, bf16[384,128]{1,0:T(8,128)(2,1)S(1)}, u32[]{:S(2)}, u32[]{:S(2)}) collective-permute-start(bf16[384,128]{1,0:T(8,128)(2,1)} %get-tuple-element.65), channel_id=1, source_target_pairs={{0,4},{2,6},{4,0},{6,2},{8,12},{10,14},{12,8},{14,10},{16,20},{18,... | collective-permute-start | bytes 294920 | tf_op jit(solution)/shard_map/ppermute | solution.py:507
  8.3 1.0 %copy-start.1 = (bf16[384,512]{1,0:T(8,128)(2,1)S(1)}, bf16[384,512]{1,0:T(8,128)(2,1)}, u32[]{:S(2)}) copy-start(bf16[384,512]{1,0:T(8,128)(2,1)} %q_ref.1) | copy-start | bytes 1179652
  9.3 1.0 %copy-start.2 = (bf16[384,512]{1,0:T(8,128)(2,1)S(1)}, bf16[384,512]{1,0:T(8,128)(2,1)}, u32[]{:S(2)}) copy-start(bf16[384,512]{1,0:T(8,128)(2,1)} %g_ref.1) | copy-start | bytes 1179652
  10.2 0.9 %copy-start.3 = (bf16[384,128]{1,0:T(8,128)(2,1)S(1)}, bf16[384,128]{1,0:T(8,128)(2,1)}, u32[]{:S(2)}) copy-start(bf16[384,128]{1,0:T(8,128)(2,1)} %get-tuple-element.58.key_ref) | copy-start | bytes 294916
  11.1 0.9 %copy-start.4 = (bf16[384,128]{1,0:T(8,128)(2,1)S(1)}, bf16[384,128]{1,0:T(8,128)(2,1)}, u32[]{:S(2)}) copy-start(bf16[384,128]{1,0:T(8,128)(2,1)} %get-tuple-element.59.value_ref) | copy-start | bytes 294916
  12.0 0.7 copy-start.5
  13.2 14.6 %copy-start.6 = (s32[48,8]{0,1:T(8,128)S(1)}, s32[48,8]{0,1:T(8,128)}, u32[]{:S(2)}) copy-start(s32[48,8]{0,1:T(8,128)} %param.12) | copy-start | bytes 4612
  14.0 11.9 %collective-permute-start.5 = (bf16[1024,128]{1,0:T(8,128)(2,1)S(1)}, bf16[1024,128]{1,0:T(8,128)(2,1)S(1)}, u32[]{:S(2)}, u32[]{:S(2)}) collective-permute-start(bf16[1024,128]{1,0:T(8,128)(2,1)S(1)} %get-tuple-element.67), channel_id=1, source_target_pairs={{0,8},{1,9},{2,3},{3,2},{4,12},{5,13},{6,7},{7,6},{8,0},{9,1},{10,... | collective-permute-start | bytes 786440 | tf_op jit(solution)/shard_map/ppermute | solution.py:519
  15.9 10.8 %collective-permute-start.6 = (bf16[1024,128]{1,0:T(8,128)(2,1)S(1)}, bf16[1024,128]{1,0:T(8,128)(2,1)S(1)}, u32[]{:S(2)}, u32[]{:S(2)}) collective-permute-start(bf16[1024,128]{1,0:T(8,128)(2,1)S(1)} %get-tuple-element.68), channel_id=1, source_target_pairs={{0,1},{1,0},{2,10},{3,11},{4,5},{5,4},{6,14},{7,15},{8,16},{9,17},... | collective-permute-start | bytes 786440 | tf_op jit(solution)/shard_map/ppermute | solution.py:519
  17.4 5.2 %collective-permute-start.7 = (bf16[384,128]{1,0:T(8,128)(2,1)}, bf16[384,128]{1,0:T(8,128)(2,1)S(1)}, u32[]{:S(2)}, u32[]{:S(2)}) collective-permute-start(bf16[384,128]{1,0:T(8,128)(2,1)} %get-tuple-element.70), channel_id=1, source_target_pairs={{0,6},{2,4},{4,2},{6,0},{8,14},{10,12},{12,10},{14,8},{16,22},{18,... | collective-permute-start | bytes 294920 | tf_op jit(solution)/shard_map/ppermute | solution.py:507
  22.7 11.2 %collective-permute-start.8 = (bf16[1024,128]{1,0:T(8,128)(2,1)S(1)}, bf16[1024,128]{1,0:T(8,128)(2,1)S(1)}, u32[]{:S(2)}, u32[]{:S(2)}) collective-permute-start(bf16[1024,128]{1,0:T(8,128)(2,1)S(1)} %get-tuple-element.76), channel_id=1, source_target_pairs={{0,8},{1,9},{2,3},{3,2},{4,12},{5,13},{6,7},{7,6},{8,0},{9,1},{10,... | collective-permute-start | bytes 786440 | tf_op jit(solution)/shard_map/ppermute | solution.py:519
  24.4 9.5 %collective-permute-start.9 = (bf16[1024,128]{1,0:T(8,128)(2,1)S(1)}, bf16[1024,128]{1,0:T(8,128)(2,1)S(1)}, u32[]{:S(2)}, u32[]{:S(2)}) collective-permute-start(bf16[1024,128]{1,0:T(8,128)(2,1)S(1)} %get-tuple-element.77), channel_id=1, source_target_pairs={{0,1},{1,0},{2,10},{3,11},{4,5},{5,4},{6,14},{7,15},{8,16},{9,17},... | collective-permute-start | bytes 786440 | tf_op jit(solution)/shard_map/ppermute | solution.py:519
  25.9 2.0 %collective-permute-start.10 = (bf16[400,256]{1,0:T(8,128)(2,1)S(1)}, bf16[400,256]{1,0:T(8,128)(2,1)S(1)}, u32[]{:S(2)}, u32[]{:S(2)}) collective-permute-start(bf16[400,256]{1,0:T(8,128)(2,1)S(1)} %get-tuple-element.78), channel_id=1, source_target_pairs={{0,2},{2,0},{4,6},{6,4},{8,10},{10,8},{12,14},{14,12},{16,18},{18,... | collective-permute-start | bytes 614408 | tf_op jit(solution)/shard_map/ppermute | solution.py:507
  25.9 8.0 %collective-permute-start.11 = (bf16[400,256]{1,0:T(8,128)(2,1)S(1)}, bf16[400,256]{1,0:T(8,128)(2,1)}, u32[]{:S(2)}, u32[]{:S(2)}) collective-permute-start(bf16[400,256]{1,0:T(8,128)(2,1)S(1)} %get-tuple-element.79), channel_id=1, source_target_pairs={{0,4},{2,6},{4,0},{6,2},{8,12},{10,14},{12,8},{14,10},{16,20},{18,... | collective-permute-start | bytes 614408 | tf_op jit(solution)/shard_map/ppermute | solution.py:507
  26.6 10.9 %collective-permute-start.12 = (bf16[400,256]{1,0:T(8,128)(2,1)S(1)}, bf16[400,256]{1,0:T(8,128)(2,1)}, u32[]{:S(2)}, u32[]{:S(2)}) collective-permute-start(bf16[400,256]{1,0:T(8,128)(2,1)S(1)} %shard_map.106), channel_id=1, source_target_pairs={{0,6},{2,4},{4,2},{6,0},{8,14},{10,12},{12,10},{14,8},{16,22},{18,... | collective-permute-start | bytes 614408 | tf_op jit(solution)/shard_map/ppermute | solution.py:507
  47.5 8.8 %collective-permute-start.13 = (bf16[4,128,256]{2,1,0:T(8,128)(2,1)S(1)}, bf16[4,128,256]{2,1,0:T(8,128)(2,1)S(1)}, u32[]{:S(2)}, u32[]{:S(2)}) collective-permute-start(bf16[4,128,256]{2,1,0:T(8,128)(2,1)S(1)} %get-tuple-element.89), channel_id=1, source_target_pairs={{0,8},{1,9},{2,3},{3,2},{4,12},{5,13},{6,7},{7,6},{8,0},{9,1},{10,... | collective-permute-start | bytes 786440 | tf_op jit(solution)/shard_map/ppermute | solution.py:519
  48.1 8.5 %collective-permute-start.14 = (bf16[4,128,256]{2,1,0:T(8,128)(2,1)S(1)}, bf16[4,128,256]{2,1,0:T(8,128)(2,1)S(1)}, u32[]{:S(2)}, u32[]{:S(2)}) collective-permute-start(bf16[4,128,256]{2,1,0:T(8,128)(2,1)S(1)} %get-tuple-element.90), channel_id=1, source_target_pairs={{0,1},{1,0},{2,10},{3,11},{4,5},{5,4},{6,14},{7,15},{8,16},{9,17},... | collective-permute-start | bytes 786440 | tf_op jit(solution)/shard_map/ppermute | solution.py:519
  53.1 9.0 %collective-permute-start.18 = (bf16[4,128,256]{2,1,0:T(8,128)(2,1)S(1)}, bf16[4,128,256]{2,1,0:T(8,128)(2,1)S(1)}, u32[]{:S(2)}, u32[]{:S(2)}) collective-permute-start(bf16[4,128,256]{2,1,0:T(8,128)(2,1)S(1)} %get-tuple-element.98), channel_id=1, source_target_pairs={{0,8},{1,9},{2,3},{3,2},{4,12},{5,13},{6,7},{7,6},{8,0},{9,1},{10,... | collective-permute-start | bytes 786440 | tf_op jit(solution)/shard_map/ppermute | solution.py:519
  54.2 7.9 %collective-permute-start.19 = (bf16[4,128,256]{2,1,0:T(8,128)(2,1)S(1)}, bf16[4,128,256]{2,1,0:T(8,128)(2,1)S(1)}, u32[]{:S(2)}, u32[]{:S(2)}) collective-permute-start(bf16[4,128,256]{2,1,0:T(8,128)(2,1)S(1)} %get-tuple-element.99), channel_id=1, source_target_pairs={{0,1},{1,0},{2,10},{3,11},{4,5},{5,4},{6,14},{7,15},{8,16},{9,17},... | collective-permute-start | bytes 786440 | tf_op jit(solution)/shard_map/ppermute | solution.py:519
  56.6 12.9 %copy-start = (bf16[3,1024,512]{2,1,0:T(8,128)(2,1)S(1)}, bf16[3,1024,512]{2,1,0:T(8,128)(2,1)}, u32[]{:S(2)}) copy-start(bf16[3,1024,512]{2,1,0:T(8,128)(2,1)} %refs_8_.1) | copy-start | bytes 9437188
  56.7 6.7 %collective-permute-start.15 = (bf16[384,128]{1,0:T(8,128)(2,1)S(1)}, bf16[384,128]{1,0:T(8,128)(2,1)S(1)}, u32[]{:S(2)}, u32[]{:S(2)}) collective-permute-start(bf16[384,128]{1,0:T(8,128)(2,1)S(1)} %get-tuple-element.94), channel_id=1, source_target_pairs={{0,2},{2,0},{4,6},{6,4},{8,10},{10,8},{12,14},{14,12},{16,18},{18,... | collective-permute-start | bytes 294920 | tf_op jit(solution)/shard_map/ppermute | solution.py:507
  56.8 7.7 %collective-permute-start.16 = (bf16[384,128]{1,0:T(8,128)(2,1)S(1)}, bf16[384,128]{1,0:T(8,128)(2,1)S(1)}, u32[]{:S(2)}, u32[]{:S(2)}) collective-permute-start(bf16[384,128]{1,0:T(8,128)(2,1)S(1)} %get-tuple-element.95), channel_id=1, source_target_pairs={{0,4},{2,6},{4,0},{6,2},{8,12},{10,14},{12,8},{14,10},{16,20},{18,... | collective-permute-start | bytes 294920 | tf_op jit(solution)/shard_map/ppermute | solution.py:507
  57.3 7.2 %collective-permute-start.17 = (bf16[384,128]{1,0:T(8,128)(2,1)S(1)}, bf16[384,128]{1,0:T(8,128)(2,1)S(1)}, u32[]{:S(2)}, u32[]{:S(2)}) collective-permute-start(bf16[384,128]{1,0:T(8,128)(2,1)S(1)} %get-tuple-element.96), channel_id=1, source_target_pairs={{0,6},{2,4},{4,2},{6,0},{8,14},{10,12},{12,10},{14,8},{16,22},{18,... | collective-permute-start | bytes 294920 | tf_op jit(solution)/shard_map/ppermute | solution.py:507
  62.6 2.0 %collective-permute-start.20 = (bf16[192,256]{1,0:T(8,128)(2,1)S(1)}, bf16[192,256]{1,0:T(8,128)(2,1)S(1)}, u32[]{:S(2)}, u32[]{:S(2)}) collective-permute-start(bf16[192,256]{1,0:T(8,128)(2,1)S(1)} %get-tuple-element.101), channel_id=1, source_target_pairs={{0,2},{2,0},{4,6},{6,4},{8,10},{10,8},{12,14},{14,12},{16,18},{18,... | collective-permute-start | bytes 294920 | tf_op jit(solution)/shard_map/ppermute | solution.py:507
  62.6 5.7 %collective-permute-start.21 = (bf16[192,256]{1,0:T(8,128)(2,1)S(1)}, bf16[192,256]{1,0:T(8,128)(2,1)S(1)}, u32[]{:S(2)}, u32[]{:S(2)}) collective-permute-start(bf16[192,256]{1,0:T(8,128)(2,1)S(1)} %get-tuple-element.102), channel_id=1, source_target_pairs={{0,4},{2,6},{4,0},{6,2},{8,12},{10,14},{12,8},{14,10},{16,20},{18,... | collective-permute-start | bytes 294920 | tf_op jit(solution)/shard_map/ppermute | solution.py:507
  63.4 6.1 %collective-permute-start.22 = (bf16[192,256]{1,0:T(8,128)(2,1)S(1)}, bf16[192,256]{1,0:T(8,128)(2,1)S(1)}, u32[]{:S(2)}, u32[]{:S(2)}) collective-permute-start(bf16[192,256]{1,0:T(8,128)(2,1)S(1)} %get-tuple-element.103), channel_id=1, source_target_pairs={{0,6},{2,4},{4,2},{6,0},{8,14},{10,12},{12,10},{14,8},{16,22},{18,... | collective-permute-start | bytes 294920 | tf_op jit(solution)/shard_map/ppermute | solution.py:507
  70.7 11.4 %collective-permute-start.26 = (bf16[192,1024]{1,0:T(8,128)(2,1)S(1)}, bf16[192,1024]{1,0:T(8,128)(2,1)S(1)}, u32[]{:S(2)}, u32[]{:S(2)}) collective-permute-start(bf16[192,1024]{1,0:T(8,128)(2,1)S(1)} %shard_map.112), channel_id=1, source_target_pairs={{0,1},{1,0},{2,3},{3,2},{4,5},{5,4},{6,7},{7,6},{8,9},{9,8},{10,11... | collective-permute-start | bytes 1179656 | tf_op jit(solution)/shard_map/ppermute | solution.py:704
  71.6 1.9 %collective-permute-start.23 = (bf16[192,256]{1,0:T(8,128)(2,1)S(1)}, bf16[192,256]{1,0:T(8,128)(2,1)S(1)}, u32[]{:S(2)}, u32[]{:S(2)}) collective-permute-start(bf16[192,256]{1,0:T(8,128)(2,1)S(1)} %get-tuple-element.105), channel_id=1, source_target_pairs={{0,2},{2,0},{4,6},{6,4},{8,10},{10,8},{12,14},{14,12},{16,18},{18,... | collective-permute-start | bytes 294920 | tf_op jit(solution)/shard_map/ppermute | solution.py:507
  71.6 5.6 %collective-permute-start.24 = (bf16[192,256]{1,0:T(8,128)(2,1)S(1)}, bf16[192,256]{1,0:T(8,128)(2,1)S(1)}, u32[]{:S(2)}, u32[]{:S(2)}) collective-permute-start(bf16[192,256]{1,0:T(8,128)(2,1)S(1)} %get-tuple-element.106), channel_id=1, source_target_pairs={{0,4},{2,6},{4,0},{6,2},{8,12},{10,14},{12,8},{14,10},{16,20},{18,... | collective-permute-start | bytes 294920 | tf_op jit(solution)/shard_map/ppermute | solution.py:507
  72.4 6.2 %collective-permute-start.25 = (bf16[192,256]{1,0:T(8,128)(2,1)S(1)}, bf16[192,256]{1,0:T(8,128)(2,1)S(1)}, u32[]{:S(2)}, u32[]{:S(2)}) collective-permute-start(bf16[192,256]{1,0:T(8,128)(2,1)S(1)} %get-tuple-element.107), channel_id=1, source_target_pairs={{0,6},{2,4},{4,2},{6,0},{8,14},{10,12},{12,10},{14,8},{16,22},{18,... | collective-permute-start | bytes 294920 | tf_op jit(solution)/shard_map/ppermute | solution.py:507

commit v10 on v8

--- a/solution.py
+++ b/solution.py
@@ -16,6 +16,7 @@
 LANES = 128
 LSE_ROWS = 16
 PARTS = 2
+CHUNKS = 2
 LOADS = 3
 F32 = jnp.float32
 BF16 = jnp.bfloat16
@@ -401,20 +402,29 @@
 
 
 def combine_kernel(own_ref, first_ref, second_ref, *rest):
-    aways, homes, (total, moved) = rest[:GROUP], rest[GROUP : 2 * GROUP], rest[2 * GROUP :]
+    rest = rest[GROUP - 1 :]
+    chunks, rest = rest[: CHUNKS * GROUP], rest[CHUNKS * GROUP :]
+    homes, (total, moved) = rest[:GROUP], rest[GROUP:]
     total[...] = own_ref[...]
     add_arrived(total, (0, own_ref.shape[0] - OUTER), (first_ref, second_ref))
     moved[...] = total[...].astype(BF16).reshape(moved.shape)
     half = homes[0].shape[0]
-    away = aways[0].shape[0] // half
+    small = half // CHUNKS
+    away = chunks[0].shape[0] // small
     me = lax.axis_index("var") % GROUP
     for distance in range(GROUP):
         member = me ^ distance
-        for piece in range(away):
-            aways[distance][piece * half : (piece + 1) * half] = moved[
-                member, pl.ds(owner_start(piece, half), half)
-            ]
+        for chunk in range(CHUNKS):
+            for piece in range(away):
+                chunks[chunk * GROUP + distance][piece * small : (piece + 1) * small] = moved[
+                    member, pl.ds(chunk_start(piece, half, chunk), small)
+                ]
         homes[distance][...] = moved[member, pl.ds(owner_start(away, half), half)]
+
+
+def chunk_start(piece, half, chunk):
+    small = half // CHUNKS
+    return pl.multiple_of(owner_start(piece, half) + chunk * small, small)
 
 
 def gather_rows(grads, dq, start, dkv, dkv_at):
@@ -435,36 +445,56 @@
     return total
 
 
-def away_kernel(*refs):
-    dqs, dkvs, (w_ref, *rest) = refs[:4], refs[4:8], refs[8:]
+def away_kernel(chunk, *refs):
+    dqs, dkvs, w_ref, rest = refs[:4], refs[4:8], refs[8], refs[9 + (chunk > 0) :]
     outs, (grads, dq, dkv) = rest[:-3], rest[-3:]
-    half = grads.shape[1]
+    half = grads.shape[1] * CHUNKS
     stage_pieces(dq, dqs)
     stage_pieces(dkv, dkvs)
     for piece, out in enumerate(outs):
-        gather_rows(grads, dq, owner_start(piece, half), dkv, piece)
+        gather_rows(grads, dq, chunk_start(piece, half, chunk), dkv, piece)
         out[...] = product(grads, w_ref).astype(BF16)
 
 
 def home_kernel(*refs):
-    dqs, aways, homes, rest = refs[:4], refs[4:8], refs[8:12], refs[12:]
-    w_ref, dq_out, dk_out, dv_out, keep_out, grads, dq, away_dkv, home_dkv = rest
+    dqs, aways, refs = refs[:4], refs[4 : 4 + 4 * CHUNKS], refs[4 + 4 * CHUNKS :]
+    homes, w_ref, gots, refs = refs[:4], refs[4], refs[5:-9], refs[-9:]
+    dq_out, dk_out, dv_out, keep_out, grads, small_grads, dq, away_dkv, home_dkv = refs
     half = grads.shape[1]
-    away = away_dkv.shape[1] // half
+    small = half // CHUNKS
+    away = away_dkv.shape[1] // small
     stage_pieces(dq, dqs)
-    stage_pieces(away_dkv, aways)
     stage_pieces(home_dkv, homes)
-    for piece in range(away + 1):
-        start = owner_start(piece, half)
-        if piece < away:
-            gather_rows(grads, dq, start, away_dkv, piece)
-        else:
-            gather_rows(grads, dq, start, home_dkv, 0)
-        at = pl.ds(start, half)
-        dq_out[at] = grads[0]
-        dk_out[at] = grads[1]
-        dv_out[at] = grads[2]
+
+    def write(rows_at, some):
+        dq_out[rows_at] = some[0]
+        dk_out[rows_at] = some[1]
+        dv_out[rows_at] = some[2]
+
+    for chunk in range(CHUNKS):
+        stage_pieces(away_dkv, aways[chunk * GROUP : (chunk + 1) * GROUP])
+        for piece in range(away):
+            start = chunk_start(piece, half, chunk)
+            gather_rows(small_grads, dq, start, away_dkv, piece)
+            write(pl.ds(start, small), small_grads)
+    start = owner_start(away, half)
+    gather_rows(grads, dq, start, home_dkv, 0)
+    write(pl.ds(start, half), grads)
     keep_out[...] = product(grads, w_ref)
+    for i, got in enumerate(gots):
+        chunk = i // away
+        at = slice(chunk * small, (chunk + 1) * small)
+        keep_out[at] = keep_out[at] + got[...].astype(F32)
+
+
+def add_kernel(keep_ref, *refs):
+    gots, out = refs[:-1], refs[-1]
+    begin = keep_ref.shape[0] - gots[0].shape[0]
+    out[:begin] = keep_ref[:begin].astype(BF16)
+    total = keep_ref[begin:]
+    for got in gots:
+        total = total + got[...].astype(F32)
+    out[begin:] = total.astype(BF16)
 
 
 def body(queries, keys, values, out_grad, log_sum_exp, key_blocks, w_qkv):
@@ -620,39 +650,56 @@
     dqs = swap([dqs[0], *carried])
     split = pl.pallas_call(
         combine_kernel,
-        out_shape=(shaped((rows - half, wide)),) * GROUP + (shaped((half, wide)),) * GROUP,
-        in_specs=[vmem()] * 3,
-        out_specs=(vmem(),) * (2 * GROUP),
+        out_shape=(shaped(((rows - half) // CHUNKS, wide)),) * (CHUNKS * GROUP)
+        + (shaped((half, wide)),) * GROUP,
+        in_specs=[vmem()] * 3 + [anywhere] * (GROUP - 1),
+        out_specs=(vmem(),) * ((CHUNKS + 1) * GROUP),
         scratch_shapes=[pltpu.VMEM((group_blocks,) + tall, F32), staged(rows, wide)],
         compiler_params=params(8),
         cost_estimate=cost(0, 8 * size),
-    )(own_sum, *inner_back)
-    aways = swap(split[:GROUP])
-    homes = swap(split[GROUP:])
-
+    )(own_sum, *inner_back, *dqs[1:])
+    aways = [swap(split[c * GROUP : (c + 1) * GROUP]) for c in range(CHUNKS)]
+    homes = swap(split[CHUNKS * GROUP :])
+
+    small = half // CHUNKS
     grads = pltpu.VMEM((3, half, features), BF16)
-    sends = pl.pallas_call(
-        away_kernel,
-        out_shape=(shaped((half, model)),) * (heads - 1),
-        in_specs=[vmem()] * (2 * GROUP + 1),
-        out_specs=(vmem(),) * (heads - 1),
-        scratch_shapes=[grads, staged(rows), staged(rows - half, wide)],
-        compiler_params=params(8),
-        cost_estimate=cost(6 * (rows - half) * features * model, 4_000_000),
-    )(*dqs, *aways, w_qkv)
-    dq_out, dk_out, dv_out, total = pl.pallas_call(
+    small_grads = pltpu.VMEM((3, small, features), BF16)
+    away_stage = staged((rows - half) // CHUNKS, wide)
+    sends, after = [], ()
+    for chunk in range(CHUNKS):
+        sent = pl.pallas_call(
+            functools.partial(away_kernel, chunk),
+            out_shape=(shaped((small, model)),) * (heads - 1),
+            in_specs=[vmem()] * (2 * GROUP + 1) + [anywhere] * len(after),
+            out_specs=(vmem(),) * (heads - 1),
+            scratch_shapes=[small_grads, staged(rows), away_stage],
+            compiler_params=params(8),
+            cost_estimate=cost(6 * (rows - half) * features * model // CHUNKS, 4_000_000),
+        )(*dqs, *aways[chunk], w_qkv, *after)
+        after = (sent[0],)
+        got = []
+        for piece, send in enumerate(sent):
+            turn = [(n, (n + piece + 1) % heads) for n in range(heads)]
+            got.append(lax.ppermute(send, "head", turn))
+        sends.append(got)
+    early = [x for got in sends[:-1] for x in got]
+    dq_out, dk_out, dv_out, keep = pl.pallas_call(
         home_kernel,
         out_shape=(shaped((rows, features)),) * 3 + (shaped((half, model), F32),),
-        in_specs=[vmem()] * (3 * GROUP + 1),
+        in_specs=[vmem()] * ((2 + CHUNKS) * GROUP + 1 + len(early)),
         out_specs=(vmem(),) * 4,
-        scratch_shapes=[grads, staged(rows), staged(rows - half, wide), staged(half, wide)],
+        scratch_shapes=[grads, small_grads, staged(rows), away_stage, staged(half, wide)],
         compiler_params=params(8),
         cost_estimate=cost(6 * half * features * model, 6_000_000),
-    )(*dqs, *aways, *homes, w_qkv)
-    for piece, send in enumerate(sends):
-        got = lax.ppermute(send, "head", [(n, (n + piece + 1) % heads) for n in range(heads)])
-        total = total + got.astype(F32)
-    return dq_out, dk_out, dv_out, total.astype(BF16)
+    )(*dqs, *[x for pieces in aways for x in pieces], *homes, w_qkv, *early)
+    total = pl.pallas_call(
+        add_kernel,
+        out_shape=shaped((half, model)),
+        in_specs=[vmem()] * heads,
+        out_specs=vmem(),
+        compiler_params=params(8),
+    )(keep, *sends[-1])
+    return dq_out, dk_out, dv_out, total
 
 
 def solution(mesh):

time: 78.3 us -> 79.4 us (1.014)
  starting transfers between devices: 21.6 us -> 24 us
  waiting for transfers between devices: 29.1 us -> 27.2 us
  Pallas kernels: 22 us -> 23.5 us
  other arithmetic: 0.84 us -> 0 us
    ppermute x15 -> x18, starting transfers between devices: 10.8 us -> 12.8 us  [trade(): return lax.ppermute(x, 'var', [(n, n ^ distance) for n in range(devices)])]
    pallas_call x2 -> x4, Pallas kernels: 1.67 us -> 3.43 us  [the longest x2 2.16 us: body(): pl.pallas_call(functools.partial(away_kernel, chunk), out_shape=(shaped((...]
    ppermute x15 -> x18, waiting for transfers between devices: 25.2 us -> 24 us  [trade(): return lax.ppermute(x, 'var', [(n, n ^ distance) for n in range(devices)])]
    convert_element_type x1 -> x0, other arithmetic: 0.84 us -> none  [body(): return (dq_out, dk_out, dv_out, total.astype(BF16))]
    ppermute x1 -> x2, starting transfers between devices: 1.73 us -> 1.99 us  [body(): got.append(lax.ppermute(send, 'head', turn))]
  transfers between devices with their start and end apart: 22 -> 26, of which waited for: 10 -> 12; matrix products, arithmetic and copies ran while one was open for 0% -> 0% of each run, Pallas kernels for 10% -> 11%
where the time goes in v10:
time: 79.4 us; the launch traced here: 79.1 us
  waiting for transfers between devices  27.2 us (34%)
  starting transfers between devices  24 us (30%)
  Pallas kernels  23.5 us (30%)
  local copies, waits for them, and re-layouts  3.71 us (5%)
    ppermute x18, waiting for transfers between devices, trade(): return lax.ppermute(x, 'var', [(n, n ^ distance) for n in range(devices)])  24 us
    ppermute x18, starting transfers between devices, trade(): return lax.ppermute(x, 'var', [(n, n ^ distance) for n in range(devices)])  12.8 us
    pallas_call x1, Pallas kernels, body(): pl.pallas_call(functools.partial(attend_kernel, False, blocks_here, head_...  9.78 us
    ppermute x6, starting transfers between devices, trade_level(): return lax.ppermute(x, ('var', 'head'), pairs)  9.11 us
    pallas_call x1, Pallas kernels, body(): pl.pallas_call(functools.partial(attend_kernel, True, blocks_here, head_d...  4.54 us
    unnamed x13, local copies, waits for them, and re-layouts  3.71 us
    ppermute x6, waiting for transfers between devices, trade_level(): return lax.ppermute(x, ('var', 'head'), pairs)  3.19 us
    pallas_call x1, Pallas kernels, body(): pl.pallas_call(pack_kv_kernel, out_shape=(shaped((rows, wide)),) * GROUP,...  2.48 us
  transfers between devices with their start and end apart: 26, of which 12 were waited for; matrix products, arithmetic and copies ran while one was open for 0% of the time, Pallas kernels for 11%

profile of v10, /device:TPU:0, one launch (start us, length us, event | category | flops | bytes accessed | tf_op | source)
XLA Modules:
  0.0 79.1 jit_solution(17572362771824921333)
XLA Ops:
  0.6 2.5 %shard_map.102 = (bf16[384,256]{1,0:T(8,128)(2,1)}, bf16[384,256]{1,0:T(8,128)(2,1)}, bf16[384,256]{1,0:T(8,128)(2,1)}, bf16[384,256]{1,0:T(8,128)(2,1)}) custom-call(bf16[384,512]{1,0:T(8,128)(2,1)} %k_hbm.1, bf16[384,512]{1,0:T(8,128)(2,1)} %v_hbm.1), custom_call_target="tpu_custom_call" | custom-call | flops 100663296 | bytes 1966080 | tf_op jit(solution)/shard_map/pallas_call | solution.py:554
  3.1 0.5 collective-permute-start
  3.6 2.6 %collective-permute-start.1 = (bf16[384,256]{1,0:T(8,128)(2,1)}, bf16[384,256]{1,0:T(8,128)(2,1)S(1)}, u32[]{:S(2)}, u32[]{:S(2)}) collective-permute-start(bf16[384,256]{1,0:T(8,128)(2,1)} %get-tuple-element.57), channel_id=1, source_target_pairs={{0,4},{2,6},{4,0},{6,2},{8,12},{10,14},{12,8},{14,10},{16,20},{18,... | collective-permute-start | bytes 589832 | tf_op jit(solution)/shard_map/ppermute | solution.py:517
  6.2 0.1 collective-permute-start.2
  6.3 0.0 collective-permute-done.after_ref.refs_1_
  6.3 1.0 %copy-done.1 = bf16[384,512]{1,0:T(8,128)(2,1)S(1)} copy-done((bf16[384,512]{1,0:T(8,128)(2,1)S(1)}, bf16[384,512]{1,0:T(8,128)(2,1)}, u32[]{:S(2)}) %copy-start.1) | copy-done | bytes 393240
  7.3 1.0 %copy-done.2 = bf16[384,512]{1,0:T(8,128)(2,1)S(1)} copy-done((bf16[384,512]{1,0:T(8,128)(2,1)S(1)}, bf16[384,512]{1,0:T(8,128)(2,1)}, u32[]{:S(2)}) %copy-start.2) | copy-done | bytes 393240
  8.3 0.9 %copy-done.3 = bf16[384,256]{1,0:T(8,128)(2,1)S(1)} copy-done((bf16[384,256]{1,0:T(8,128)(2,1)S(1)}, bf16[384,256]{1,0:T(8,128)(2,1)}, u32[]{:S(2)}) %copy-start.3) | copy-done | bytes 196632
  9.2 0.7 copy-done.4
  9.9 0.5 shard_map.103
  10.4 1.8 %collective-permute-done.1.refs_2_ = bf16[384,256]{1,0:T(8,128)(2,1)S(1)} collective-permute-done((bf16[384,256]{1,0:T(8,128)(2,1)}, bf16[384,256]{1,0:T(8,128)(2,1)S(1)}, u32[]{:S(2)}, u32[]{:S(2)}) %collective-permute-start.1) | collective-permute-done | bytes 196640 | tf_op jit(solution)/shard_map/ppermute | solution.py:517
  12.2 3.7 %collective-permute-done.2.refs_3_ = bf16[384,256]{1,0:T(8,128)(2,1)S(1)} collective-permute-done((bf16[384,256]{1,0:T(8,128)(2,1)}, bf16[384,256]{1,0:T(8,128)(2,1)S(1)}, u32[]{:S(2)}, u32[]{:S(2)}) %collective-permute-start.2) | collective-permute-done | bytes 196640 | tf_op jit(solution)/shard_map/ppermute | solution.py:517
  15.9 0.9 %shard_map.104 = (bf16[1936,256]{1,0:T(8,128)(2,1)S(1)}, bf16[1024,256]{1,0:T(8,128)(2,1)}, bf16[1024,256]{1,0:T(8,128)(2,1)S(1)}, bf16[400,256]{1,0:T(8,128)(2,...) custom-call(bf16[384,256]{1,0:T(8,128)(2,1)S(1)} %get-tuple-element., ...), custom_call_target="tpu_custom_call", output_to_operand_aliasing={{3}: (5, {}), {4}: (6, {}), {5}: (7, {})} | custom-call | bytes 1966080 | tf_op jit(solution)/shard_map/pallas_call | solution.py:575
  16.8 1.6 %collective-permute-start.3 = (bf16[1024,256]{1,0:T(8,128)(2,1)}, bf16[1024,256]{1,0:T(8,128)(2,1)S(1)}, u32[]{:S(2)}, u32[]{:S(2)}) collective-permute-start(bf16[1024,256]{1,0:T(8,128)(2,1)} %get-tuple-element.64), channel_id=1, source_target_pairs={{0,8},{1,9},{2,3},{3,2},{4,12},{5,13},{6,7},{7,6},{8,0},{9,1},{10,... | collective-permute-start | bytes 1572872 | tf_op jit(solution)/shard_map/ppermute | solution.py:529
  18.4 1.5 %collective-permute-start.4 = (bf16[1024,256]{1,0:T(8,128)(2,1)S(1)}, bf16[1024,256]{1,0:T(8,128)(2,1)S(1)}, u32[]{:S(2)}, u32[]{:S(2)}) collective-permute-start(bf16[1024,256]{1,0:T(8,128)(2,1)S(1)} %get-tuple-element.65), channel_id=1, source_target_pairs={{0,1},{1,0},{2,10},{3,11},{4,5},{5,4},{6,14},{7,15},{8,16},{9,17},... | collective-permute-start | bytes 1572872 | tf_op jit(solution)/shard_map/ppermute | solution.py:529
  19.9 0.0 collective-permute-start.5
  19.9 1.5 %collective-permute-start.6 = (bf16[400,256]{1,0:T(8,128)(2,1)S(1)}, bf16[400,256]{1,0:T(8,128)(2,1)}, u32[]{:S(2)}, u32[]{:S(2)}) collective-permute-start(bf16[400,256]{1,0:T(8,128)(2,1)S(1)} %get-tuple-element.67), channel_id=1, source_target_pairs={{0,4},{2,6},{4,0},{6,2},{8,12},{10,14},{12,8},{14,10},{16,20},{18,... | collective-permute-start | bytes 614408 | tf_op jit(solution)/shard_map/ppermute | solution.py:517
  21.5 0.3 collective-permute-start.7
  21.8 0.1 copy.18.kb_ref
  21.9 0.0 collective-permute-done.5.refs_3_
  21.9 6.0 %collective-permute-done.6.refs_4_ = bf16[400,256]{1,0:T(8,128)(2,1)} collective-permute-done((bf16[400,256]{1,0:T(8,128)(2,1)S(1)}, bf16[400,256]{1,0:T(8,128)(2,1)}, u32[]{:S(2)}, u32[]{:S(2)}) %collective-permute-start.6) | collective-permute-done | bytes 204832 | tf_op jit(solution)/shard_map/ppermute | solution.py:517
  27.9 3.6 %collective-permute-done.7.refs_5_ = bf16[400,256]{1,0:T(8,128)(2,1)} collective-permute-done((bf16[400,256]{1,0:T(8,128)(2,1)S(1)}, bf16[400,256]{1,0:T(8,128)(2,1)}, u32[]{:S(2)}, u32[]{:S(2)}) %collective-permute-start.7) | collective-permute-done | bytes 204832 | tf_op jit(solution)/shard_map/ppermute | solution.py:517
  31.5 0.0 collective-permute-done.3.refs_1_
  31.6 0.0 collective-permute-done.4.refs_2_
  31.6 9.8 %shard_map.105 = (bf16[4,128,256]{2,1,0:T(8,128)(2,1)S(1)}, bf16[4,128,256]{2,1,0:T(8,128)(2,1)S(1)}, bf16[28,128,256]{2,1,0:T(8,128)(2,1)S(1)}, bf16[28,128,128...) custom-call(s32[48,8]{1,0:T(8,128)S(1)} %copy.18.kb_ref, ...), custom_call_target="tpu_custom_call" | custom-call | flops 5395552768 | bytes 2000000 | tf_op jit(solution)/shard_map/pallas_call | solution.py:618
  41.4 1.7 %collective-permute-start.8 = (bf16[4,128,256]{2,1,0:T(8,128)(2,1)S(1)}, bf16[4,128,256]{2,1,0:T(8,128)(2,1)S(1)}, u32[]{:S(2)}, u32[]{:S(2)}) collective-permute-start(bf16[4,128,256]{2,1,0:T(8,128)(2,1)S(1)} %get-tuple-element.77), channel_id=1, source_target_pairs={{0,8},{1,9},{2,3},{3,2},{4,12},{5,13},{6,7},{7,6},{8,0},{9,1},{10,... | collective-permute-start | bytes 786440 | tf_op jit(solution)/shard_map/ppermute | solution.py:529
  43.1 1.5 %collective-permute-start.9 = (bf16[4,128,256]{2,1,0:T(8,128)(2,1)S(1)}, bf16[4,128,256]{2,1,0:T(8,128)(2,1)S(1)}, u32[]{:S(2)}, u32[]{:S(2)}) collective-permute-start(bf16[4,128,256]{2,1,0:T(8,128)(2,1)S(1)} %get-tuple-element.78), channel_id=1, source_target_pairs={{0,1},{1,0},{2,10},{3,11},{4,5},{5,4},{6,14},{7,15},{8,16},{9,17},... | collective-permute-start | bytes 786440 | tf_op jit(solution)/shard_map/ppermute | solution.py:529
  44.6 4.5 %shard_map.106 = (f32[12,128,256]{2,1,0:T(8,128)S(1)}, bf16[4,128,256]{2,1,0:T(8,128)(2,1)S(1)}, bf16[4,128,256]{2,1,0:T(8,128)(2,1)S(1)}, bf16[384,128]{1,0:T(8...) custom-call(s32[48,8]{1,0:T(8,128)S(1)} %copy.18.kb_ref, ...), custom_call_target="tpu_custom_call" | custom-call | flops 2657510912 | bytes 2000000 | tf_op jit(solution)/shard_map/pallas_call | solution.py:628
  49.1 1.7 %collective-permute-start.13 = (bf16[4,128,256]{2,1,0:T(8,128)(2,1)S(1)}, bf16[4,128,256]{2,1,0:T(8,128)(2,1)S(1)}, u32[]{:S(2)}, u32[]{:S(2)}) collective-permute-start(bf16[4,128,256]{2,1,0:T(8,128)(2,1)S(1)} %get-tuple-element.86), channel_id=1, source_target_pairs={{0,8},{1,9},{2,3},{3,2},{4,12},{5,13},{6,7},{7,6},{8,0},{9,1},{10,... | collective-permute-start | bytes 786440 | tf_op jit(solution)/shard_map/ppermute | solution.py:529
  50.8 1.2 %collective-permute-start.14 = (bf16[4,128,256]{2,1,0:T(8,128)(2,1)S(1)}, bf16[4,128,256]{2,1,0:T(8,128)(2,1)S(1)}, u32[]{:S(2)}, u32[]{:S(2)}) collective-permute-start(bf16[4,128,256]{2,1,0:T(8,128)(2,1)S(1)} %get-tuple-element.87), channel_id=1, source_target_pairs={{0,1},{1,0},{2,10},{3,11},{4,5},{5,4},{6,14},{7,15},{8,16},{9,17},... | collective-permute-start | bytes 786440 | tf_op jit(solution)/shard_map/ppermute | solution.py:529
  51.9 0.0 collective-permute-done.8.first_ref
  51.9 0.0 collective-permute-done.9.second_ref
  51.9 0.2 shard_map.107
  52.1 0.1 collective-permute-start.10
  52.2 1.6 %collective-permute-start.11 = (bf16[384,128]{1,0:T(8,128)(2,1)S(1)}, bf16[384,128]{1,0:T(8,128)(2,1)S(1)}, u32[]{:S(2)}, u32[]{:S(2)}) collective-permute-start(bf16[384,128]{1,0:T(8,128)(2,1)S(1)} %get-tuple-element.83), channel_id=1, source_target_pairs={{0,4},{2,6},{4,0},{6,2},{8,12},{10,14},{12,8},{14,10},{16,20},{18,... | collective-permute-start | bytes 294920 | tf_op jit(solution)/shard_map/ppermute | solution.py:517
  53.8 0.3 collective-permute-start.12
  54.0 3.1 %collective-permute-done.13.first_ref = bf16[4,128,256]{2,1,0:T(8,128)(2,1)S(1)} collective-permute-done((bf16[4,128,256]{2,1,0:T(8,128)(2,1)S(1)}, bf16[4,128,256]{2,1,0:T(8,128)(2,1)S(1)}, u32[]{:S(2)}, u32[]{:S(2)}) %collective-permute-start.13) | collective-permute-done | bytes 262176 | tf_op jit(solution)/shard_map/ppermute | solution.py:529
  57.2 0.0 collective-permute-done.14.second_ref
  57.2 0.0 collective-permute-done.10.rest_0_.refs_1_
  57.2 0.6 collective-permute-done.11.rest_1_.refs_2_
  57.8 1.2 %collective-permute-done.12.rest_2_.refs_3_ = bf16[384,128]{1,0:T(8,128)(2,1)S(1)} collective-permute-done((bf16[384,128]{1,0:T(8,128)(2,1)S(1)}, bf16[384,128]{1,0:T(8,128)(2,1)S(1)}, u32[]{:S(2)}, u32[]{:S(2)}) %collective-permute-start.12) | collective-permute-done | bytes 98336 | tf_op jit(solution)/shard_map/ppermute | solution.py:517
  59.0 0.5 shard_map.108
  59.5 0.3 collective-permute-start.15
  59.9 1.5 %collective-permute-start.16 = (bf16[96,256]{1,0:T(8,128)(2,1)S(1)}, bf16[96,256]{1,0:T(8,128)(2,1)S(1)}, u32[]{:S(2)}, u32[]{:S(2)}) collective-permute-start(bf16[96,256]{1,0:T(8,128)(2,1)S(1)} %get-tuple-element.90), channel_id=1, source_target_pairs={{0,4},{2,6},{4,0},{6,2},{8,12},{10,14},{12,8},{14,10},{16,20},{18,... | collective-permute-start | bytes 147464 | tf_op jit(solution)/shard_map/ppermute | solution.py:517
  61.4 0.1 collective-permute-start.17
  61.4 0.6 collective-permute-start.18
  62.0 1.5 %collective-permute-start.19 = (bf16[96,256]{1,0:T(8,128)(2,1)S(1)}, bf16[96,256]{1,0:T(8,128)(2,1)S(1)}, u32[]{:S(2)}, u32[]{:S(2)}) collective-permute-start(bf16[96,256]{1,0:T(8,128)(2,1)S(1)} %get-tuple-element.94), channel_id=1, source_target_pairs={{0,4},{2,6},{4,0},{6,2},{8,12},{10,14},{12,8},{14,10},{16,20},{18,... | collective-permute-start | bytes 147464 | tf_op jit(solution)/shard_map/ppermute | solution.py:517
  63.5 0.0 collective-permute-done.15.refs_5_
  63.5 0.0 collective-permute-start.20
  63.5 0.4 collective-permute-done.16.refs_6_
  64.0 1.3 %collective-permute-done.17.refs_7_ = bf16[96,256]{1,0:T(8,128)(2,1)S(1)} collective-permute-done((bf16[96,256]{1,0:T(8,128)(2,1)S(1)}, bf16[96,256]{1,0:T(8,128)(2,1)S(1)}, u32[]{:S(2)}, u32[]{:S(2)}) %collective-permute-start.17) | collective-permute-done | bytes 49184 | tf_op jit(solution)/shard_map/ppermute | solution.py:517
  65.3 1.1 %shard_map.109.refs_9_ = bf16[96,1024]{1,0:T(8,128)(2,1)S(1)} custom-call(bf16[384,128]{1,0:T(8,128)(2,1)S(1)} %get-tuple-element.75.refs_0_, bf16[384,128]{1,0:T(8,128)(2,1)S(1)} %collective-permute-done.10.rest_0_.refs_1_, bf16[384,128]{1,0:T(8,128)(2,1)S(1)} %collective-permute-done.11.rest_1_.refs_2_, ...), custom_call_target="tpu_custom_call" | custom-call | flops 301989888 | bytes 4000000 | tf_op jit(solution)/shard_map/pallas_call | solution.py:670
  66.4 1.0 %collective-permute-start.24 = (bf16[96,1024]{1,0:T(8,128)(2,1)S(1)}, bf16[96,1024]{1,0:T(8,128)(2,1)S(1)}, u32[]{:S(2)}, u32[]{:S(2)}) collective-permute-start(bf16[96,1024]{1,0:T(8,128)(2,1)S(1)} %shard_map.109.refs_9_), channel_id=1, source_target_pairs={{0,1},{1,0},{2,3},{3,2},{4,5},{5,4},{6,7},{7,6},{8,9},{9,8},{10,11... | collective-permute-start | bytes 589832 | tf_op jit(solution)/shard_map/ppermute | solution.py:683
  67.4 0.0 collective-permute-done.18.refs_9_.refs_5_
  67.4 0.0 collective-permute-done.19.refs_10_.refs_6_
  67.4 0.2 collective-permute-done.20.refs_11_.refs_7_
  67.5 1.1 %shard_map.111 = bf16[96,1024]{1,0:T(8,128)(2,1)S(1)} custom-call(bf16[384,128]{1,0:T(8,128)(2,1)S(1)} %get-tuple-element.75.refs_0_, bf16[384,128]{1,0:T(8,128)(2,1)S(1)} %collective-permute-done.10.rest_0_.refs_1_, bf16[384,128]{1,0:T(8,128)(2,1)S(1)} %collective-permute-done.11.rest_1_.refs_2_, ...), custom_call_target="tpu_custom_call" | custom-call | flops 301989888 | bytes 4000000 | tf_op jit(solution)/shard_map/pallas_call | solution.py:670
  68.6 1.0 %collective-permute-start.25 = (bf16[96,1024]{1,0:T(8,128)(2,1)S(1)}, bf16[96,1024]{1,0:T(8,128)(2,1)S(1)}, u32[]{:S(2)}, u32[]{:S(2)}) collective-permute-start(bf16[96,1024]{1,0:T(8,128)(2,1)S(1)} %shard_map.111), channel_id=1, source_target_pairs={{0,1},{1,0},{2,3},{3,2},{4,5},{5,4},{6,7},{7,6},{8,9},{9,8},{10,11... | collective-permute-start | bytes 589832 | tf_op jit(solution)/shard_map/ppermute | solution.py:683
  69.7 0.7 collective-permute-start.22
  70.4 1.1 %collective-permute-start.23 = (bf16[192,256]{1,0:T(8,128)(2,1)S(1)}, bf16[192,256]{1,0:T(8,128)(2,1)S(1)}, u32[]{:S(2)}, u32[]{:S(2)}) collective-permute-start(bf16[192,256]{1,0:T(8,128)(2,1)S(1)} %get-tuple-element.99), channel_id=1, source_target_pairs={{0,6},{2,4},{4,2},{6,0},{8,14},{10,12},{12,10},{14,8},{16,22},{18,... | collective-permute-start | bytes 294920 | tf_op jit(solution)/shard_map/ppermute | solution.py:517
  71.5 3.7 %collective-permute-done.22.refs_14_ = bf16[192,256]{1,0:T(8,128)(2,1)S(1)} collective-permute-done((bf16[192,256]{1,0:T(8,128)(2,1)S(1)}, bf16[192,256]{1,0:T(8,128)(2,1)S(1)}, u32[]{:S(2)}, u32[]{:S(2)}) %collective-permute-start.22) | collective-permute-done | bytes 98336 | tf_op jit(solution)/shard_map/ppermute | solution.py:517
  75.3 1.3 %collective-permute-done.23.refs_15_ = bf16[192,256]{1,0:T(8,128)(2,1)S(1)} collective-permute-done((bf16[192,256]{1,0:T(8,128)(2,1)S(1)}, bf16[192,256]{1,0:T(8,128)(2,1)S(1)}, u32[]{:S(2)}, u32[]{:S(2)}) %collective-permute-start.23) | collective-permute-done | bytes 98336 | tf_op jit(solution)/shard_map/ppermute | solution.py:517
  76.6 1.7 %shard_map.110 = (bf16[384,512]{1,0:T(8,128)(2,1)}, bf16[384,512]{1,0:T(8,128)(2,1)}, bf16[384,512]{1,0:T(8,128)(2,1)}, f32[192,1024]{1,0:T(8,128)S(1)}) custom-call(bf16[384,128]{1,0:T(8,128)(2,1)S(1)} %get-tuple-element.75.refs_0_, bf16[384,128]{1,0:T(8,128)(2,1)S(1)} %collective-permute-done.10.rest_0_.refs_1_, ...), custom_call_target="tpu_custom_call" | custom-call | flops 603979776 | bytes 6000000 | tf_op jit(solution)/shard_map/pallas_call | solution.py:686
  78.3 0.8 %shard_map.112 = bf16[192,1024]{1,0:T(8,128)(2,1)} custom-call(f32[192,1024]{1,0:T(8,128)S(1)} %get-tuple-element.103.keep_ref, bf16[96,1024]{1,0:T(8,128)(2,1)S(1)} %collective-permute-done.25.refs_0_), custom_call_target="tpu_custom_call" | custom-call | tf_op jit(solution)/shard_map/pallas_call | solution.py:695
  (12 shorter events, 0.0 us)
Async XLA Ops:
  0.6 21.2 %copy-start.5 = (s32[48,8]{0,1:T(8,128)S(1)}, s32[48,8]{0,1:T(8,128)}, u32[]{:S(2)}) copy-start(s32[48,8]{0,1:T(8,128)} %param.12) | copy-start | bytes 4612
  3.1 3.2 %collective-permute-start = (bf16[384,256]{1,0:T(8,128)(2,1)}, bf16[384,256]{1,0:T(8,128)(2,1)S(1)}, u32[]{:S(2)}, u32[]{:S(2)}) collective-permute-start(bf16[384,256]{1,0:T(8,128)(2,1)} %get-tuple-element.55), channel_id=1, source_target_pairs={{0,2},{2,0},{4,6},{6,4},{8,10},{10,8},{12,14},{14,12},{16,18},{18,... | collective-permute-start | bytes 589832 | tf_op jit(solution)/shard_map/ppermute | solution.py:517
  3.6 8.6 %collective-permute-start.1 = (bf16[384,256]{1,0:T(8,128)(2,1)}, bf16[384,256]{1,0:T(8,128)(2,1)S(1)}, u32[]{:S(2)}, u32[]{:S(2)}) collective-permute-start(bf16[384,256]{1,0:T(8,128)(2,1)} %get-tuple-element.57), channel_id=1, source_target_pairs={{0,4},{2,6},{4,0},{6,2},{8,12},{10,14},{12,8},{14,10},{16,20},{18,... | collective-permute-start | bytes 589832 | tf_op jit(solution)/shard_map/ppermute | solution.py:517
  6.2 9.7 %collective-permute-start.2 = (bf16[384,256]{1,0:T(8,128)(2,1)}, bf16[384,256]{1,0:T(8,128)(2,1)S(1)}, u32[]{:S(2)}, u32[]{:S(2)}) collective-permute-start(bf16[384,256]{1,0:T(8,128)(2,1)} %get-tuple-element.58), channel_id=1, source_target_pairs={{0,6},{2,4},{4,2},{6,0},{8,14},{10,12},{12,10},{14,8},{16,22},{18,... | collective-permute-start | bytes 589832 | tf_op jit(solution)/shard_map/ppermute | solution.py:517
  6.3 1.0 %copy-start.1 = (bf16[384,512]{1,0:T(8,128)(2,1)S(1)}, bf16[384,512]{1,0:T(8,128)(2,1)}, u32[]{:S(2)}) copy-start(bf16[384,512]{1,0:T(8,128)(2,1)} %q_ref.1) | copy-start | bytes 1179652
  7.3 1.0 %copy-start.2 = (bf16[384,512]{1,0:T(8,128)(2,1)S(1)}, bf16[384,512]{1,0:T(8,128)(2,1)}, u32[]{:S(2)}) copy-start(bf16[384,512]{1,0:T(8,128)(2,1)} %g_ref.1) | copy-start | bytes 1179652
  8.3 0.9 %copy-start.3 = (bf16[384,256]{1,0:T(8,128)(2,1)S(1)}, bf16[384,256]{1,0:T(8,128)(2,1)}, u32[]{:S(2)}) copy-start(bf16[384,256]{1,0:T(8,128)(2,1)} %get-tuple-element.54.mine_ref) | copy-start | bytes 589828
  9.2 0.7 copy-start.4
  16.8 14.8 %collective-permute-start.3 = (bf16[1024,256]{1,0:T(8,128)(2,1)}, bf16[1024,256]{1,0:T(8,128)(2,1)S(1)}, u32[]{:S(2)}, u32[]{:S(2)}) collective-permute-start(bf16[1024,256]{1,0:T(8,128)(2,1)} %get-tuple-element.64), channel_id=1, source_target_pairs={{0,8},{1,9},{2,3},{3,2},{4,12},{5,13},{6,7},{7,6},{8,0},{9,1},{10,... | collective-permute-start | bytes 1572872 | tf_op jit(solution)/shard_map/ppermute | solution.py:529
  18.4 13.1 %collective-permute-start.4 = (bf16[1024,256]{1,0:T(8,128)(2,1)S(1)}, bf16[1024,256]{1,0:T(8,128)(2,1)S(1)}, u32[]{:S(2)}, u32[]{:S(2)}) collective-permute-start(bf16[1024,256]{1,0:T(8,128)(2,1)S(1)} %get-tuple-element.65), channel_id=1, source_target_pairs={{0,1},{1,0},{2,10},{3,11},{4,5},{5,4},{6,14},{7,15},{8,16},{9,17},... | collective-permute-start | bytes 1572872 | tf_op jit(solution)/shard_map/ppermute | solution.py:529
  19.9 1.9 %collective-permute-start.5 = (bf16[400,256]{1,0:T(8,128)(2,1)S(1)}, bf16[400,256]{1,0:T(8,128)(2,1)S(1)}, u32[]{:S(2)}, u32[]{:S(2)}) collective-permute-start(bf16[400,256]{1,0:T(8,128)(2,1)S(1)} %get-tuple-element.66), channel_id=1, source_target_pairs={{0,2},{2,0},{4,6},{6,4},{8,10},{10,8},{12,14},{14,12},{16,18},{18,... | collective-permute-start | bytes 614408 | tf_op jit(solution)/shard_map/ppermute | solution.py:517
  19.9 8.0 %collective-permute-start.6 = (bf16[400,256]{1,0:T(8,128)(2,1)S(1)}, bf16[400,256]{1,0:T(8,128)(2,1)}, u32[]{:S(2)}, u32[]{:S(2)}) collective-permute-start(bf16[400,256]{1,0:T(8,128)(2,1)S(1)} %get-tuple-element.67), channel_id=1, source_target_pairs={{0,4},{2,6},{4,0},{6,2},{8,12},{10,14},{12,8},{14,10},{16,20},{18,... | collective-permute-start | bytes 614408 | tf_op jit(solution)/shard_map/ppermute | solution.py:517
  21.5 10.1 %collective-permute-start.7 = (bf16[400,256]{1,0:T(8,128)(2,1)S(1)}, bf16[400,256]{1,0:T(8,128)(2,1)}, u32[]{:S(2)}, u32[]{:S(2)}) collective-permute-start(bf16[400,256]{1,0:T(8,128)(2,1)S(1)} %get-tuple-element.68), channel_id=1, source_target_pairs={{0,6},{2,4},{4,2},{6,0},{8,14},{10,12},{12,10},{14,8},{16,22},{18,... | collective-permute-start | bytes 614408 | tf_op jit(solution)/shard_map/ppermute | solution.py:517
  41.4 10.5 %collective-permute-start.8 = (bf16[4,128,256]{2,1,0:T(8,128)(2,1)S(1)}, bf16[4,128,256]{2,1,0:T(8,128)(2,1)S(1)}, u32[]{:S(2)}, u32[]{:S(2)}) collective-permute-start(bf16[4,128,256]{2,1,0:T(8,128)(2,1)S(1)} %get-tuple-element.77), channel_id=1, source_target_pairs={{0,8},{1,9},{2,3},{3,2},{4,12},{5,13},{6,7},{7,6},{8,0},{9,1},{10,... | collective-permute-start | bytes 786440 | tf_op jit(solution)/shard_map/ppermute | solution.py:529
  43.1 8.9 %collective-permute-start.9 = (bf16[4,128,256]{2,1,0:T(8,128)(2,1)S(1)}, bf16[4,128,256]{2,1,0:T(8,128)(2,1)S(1)}, u32[]{:S(2)}, u32[]{:S(2)}) collective-permute-start(bf16[4,128,256]{2,1,0:T(8,128)(2,1)S(1)} %get-tuple-element.78), channel_id=1, source_target_pairs={{0,1},{1,0},{2,10},{3,11},{4,5},{5,4},{6,14},{7,15},{8,16},{9,17},... | collective-permute-start | bytes 786440 | tf_op jit(solution)/shard_map/ppermute | solution.py:529
  49.1 8.1 %collective-permute-start.13 = (bf16[4,128,256]{2,1,0:T(8,128)(2,1)S(1)}, bf16[4,128,256]{2,1,0:T(8,128)(2,1)S(1)}, u32[]{:S(2)}, u32[]{:S(2)}) collective-permute-start(bf16[4,128,256]{2,1,0:T(8,128)(2,1)S(1)} %get-tuple-element.86), channel_id=1, source_target_pairs={{0,8},{1,9},{2,3},{3,2},{4,12},{5,13},{6,7},{7,6},{8,0},{9,1},{10,... | collective-permute-start | bytes 786440 | tf_op jit(solution)/shard_map/ppermute | solution.py:529
  50.8 6.4 %collective-permute-start.14 = (bf16[4,128,256]{2,1,0:T(8,128)(2,1)S(1)}, bf16[4,128,256]{2,1,0:T(8,128)(2,1)S(1)}, u32[]{:S(2)}, u32[]{:S(2)}) collective-permute-start(bf16[4,128,256]{2,1,0:T(8,128)(2,1)S(1)} %get-tuple-element.87), channel_id=1, source_target_pairs={{0,1},{1,0},{2,10},{3,11},{4,5},{5,4},{6,14},{7,15},{8,16},{9,17},... | collective-permute-start | bytes 786440 | tf_op jit(solution)/shard_map/ppermute | solution.py:529
  51.9 13.4 %copy-start = (bf16[3,1024,512]{2,1,0:T(8,128)(2,1)S(1)}, bf16[3,1024,512]{2,1,0:T(8,128)(2,1)}, u32[]{:S(2)}) copy-start(bf16[3,1024,512]{2,1,0:T(8,128)(2,1)} %refs_8_.3) | copy-start | bytes 9437188
  52.1 5.1 %collective-permute-start.10 = (bf16[384,128]{1,0:T(8,128)(2,1)S(1)}, bf16[384,128]{1,0:T(8,128)(2,1)S(1)}, u32[]{:S(2)}, u32[]{:S(2)}) collective-permute-start(bf16[384,128]{1,0:T(8,128)(2,1)S(1)} %get-tuple-element.82), channel_id=1, source_target_pairs={{0,2},{2,0},{4,6},{6,4},{8,10},{10,8},{12,14},{14,12},{16,18},{18,... | collective-permute-start | bytes 294920 | tf_op jit(solution)/shard_map/ppermute | solution.py:517
  52.2 5.7 %collective-permute-start.11 = (bf16[384,128]{1,0:T(8,128)(2,1)S(1)}, bf16[384,128]{1,0:T(8,128)(2,1)S(1)}, u32[]{:S(2)}, u32[]{:S(2)}) collective-permute-start(bf16[384,128]{1,0:T(8,128)(2,1)S(1)} %get-tuple-element.83), channel_id=1, source_target_pairs={{0,4},{2,6},{4,0},{6,2},{8,12},{10,14},{12,8},{14,10},{16,20},{18,... | collective-permute-start | bytes 294920 | tf_op jit(solution)/shard_map/ppermute | solution.py:517
  53.8 5.3 %collective-permute-start.12 = (bf16[384,128]{1,0:T(8,128)(2,1)S(1)}, bf16[384,128]{1,0:T(8,128)(2,1)S(1)}, u32[]{:S(2)}, u32[]{:S(2)}) collective-permute-start(bf16[384,128]{1,0:T(8,128)(2,1)S(1)} %get-tuple-element.84), channel_id=1, source_target_pairs={{0,6},{2,4},{4,2},{6,0},{8,14},{10,12},{12,10},{14,8},{16,22},{18,... | collective-permute-start | bytes 294920 | tf_op jit(solution)/shard_map/ppermute | solution.py:517
  59.5 4.0 %collective-permute-start.15 = (bf16[96,256]{1,0:T(8,128)(2,1)S(1)}, bf16[96,256]{1,0:T(8,128)(2,1)S(1)}, u32[]{:S(2)}, u32[]{:S(2)}) collective-permute-start(bf16[96,256]{1,0:T(8,128)(2,1)S(1)} %get-tuple-element.89), channel_id=1, source_target_pairs={{0,2},{2,0},{4,6},{6,4},{8,10},{10,8},{12,14},{14,12},{16,18},{18,... | collective-permute-start | bytes 147464 | tf_op jit(solution)/shard_map/ppermute | solution.py:517
  59.9 4.1 %collective-permute-start.16 = (bf16[96,256]{1,0:T(8,128)(2,1)S(1)}, bf16[96,256]{1,0:T(8,128)(2,1)S(1)}, u32[]{:S(2)}, u32[]{:S(2)}) collective-permute-start(bf16[96,256]{1,0:T(8,128)(2,1)S(1)} %get-tuple-element.90), channel_id=1, source_target_pairs={{0,4},{2,6},{4,0},{6,2},{8,12},{10,14},{12,8},{14,10},{16,20},{18,... | collective-permute-start | bytes 147464 | tf_op jit(solution)/shard_map/ppermute | solution.py:517
  61.4 3.9 %collective-permute-start.17 = (bf16[96,256]{1,0:T(8,128)(2,1)S(1)}, bf16[96,256]{1,0:T(8,128)(2,1)S(1)}, u32[]{:S(2)}, u32[]{:S(2)}) collective-permute-start(bf16[96,256]{1,0:T(8,128)(2,1)S(1)} %get-tuple-element.91), channel_id=1, source_target_pairs={{0,6},{2,4},{4,2},{6,0},{8,14},{10,12},{12,10},{14,8},{16,22},{18,... | collective-permute-start | bytes 147464 | tf_op jit(solution)/shard_map/ppermute | solution.py:517
  61.4 5.9 %collective-permute-start.18 = (bf16[96,256]{1,0:T(8,128)(2,1)S(1)}, bf16[96,256]{1,0:T(8,128)(2,1)S(1)}, u32[]{:S(2)}, u32[]{:S(2)}) collective-permute-start(bf16[96,256]{1,0:T(8,128)(2,1)S(1)} %get-tuple-element.93), channel_id=1, source_target_pairs={{0,2},{2,0},{4,6},{6,4},{8,10},{10,8},{12,14},{14,12},{16,18},{18,... | collective-permute-start | bytes 147464 | tf_op jit(solution)/shard_map/ppermute | solution.py:517
  62.0 5.4 %collective-permute-start.19 = (bf16[96,256]{1,0:T(8,128)(2,1)S(1)}, bf16[96,256]{1,0:T(8,128)(2,1)S(1)}, u32[]{:S(2)}, u32[]{:S(2)}) collective-permute-start(bf16[96,256]{1,0:T(8,128)(2,1)S(1)} %get-tuple-element.94), channel_id=1, source_target_pairs={{0,4},{2,6},{4,0},{6,2},{8,12},{10,14},{12,8},{14,10},{16,20},{18,... | collective-permute-start | bytes 147464 | tf_op jit(solution)/shard_map/ppermute | solution.py:517
  63.5 4.0 %collective-permute-start.20 = (bf16[96,256]{1,0:T(8,128)(2,1)S(1)}, bf16[96,256]{1,0:T(8,128)(2,1)S(1)}, u32[]{:S(2)}, u32[]{:S(2)}) collective-permute-start(bf16[96,256]{1,0:T(8,128)(2,1)S(1)} %get-tuple-element.95), channel_id=1, source_target_pairs={{0,6},{2,4},{4,2},{6,0},{8,14},{10,12},{12,10},{14,8},{16,22},{18,... | collective-permute-start | bytes 147464 | tf_op jit(solution)/shard_map/ppermute | solution.py:517
  66.4 10.2 %collective-permute-start.24 = (bf16[96,1024]{1,0:T(8,128)(2,1)S(1)}, bf16[96,1024]{1,0:T(8,128)(2,1)S(1)}, u32[]{:S(2)}, u32[]{:S(2)}) collective-permute-start(bf16[96,1024]{1,0:T(8,128)(2,1)S(1)} %shard_map.109.refs_9_), channel_id=1, source_target_pairs={{0,1},{1,0},{2,3},{3,2},{4,5},{5,4},{6,7},{7,6},{8,9},{9,8},{10,11... | collective-permute-start | bytes 589832 | tf_op jit(solution)/shard_map/ppermute | solution.py:683
  68.6 9.7 %collective-permute-start.25 = (bf16[96,1024]{1,0:T(8,128)(2,1)S(1)}, bf16[96,1024]{1,0:T(8,128)(2,1)S(1)}, u32[]{:S(2)}, u32[]{:S(2)}) collective-permute-start(bf16[96,1024]{1,0:T(8,128)(2,1)S(1)} %shard_map.111), channel_id=1, source_target_pairs={{0,1},{1,0},{2,3},{3,2},{4,5},{5,4},{6,7},{7,6},{8,9},{9,8},{10,11... | collective-permute-start | bytes 589832 | tf_op jit(solution)/shard_map/ppermute | solution.py:683
  69.7 1.9 %collective-permute-start.21 = (bf16[192,256]{1,0:T(8,128)(2,1)S(1)}, bf16[192,256]{1,0:T(8,128)(2,1)S(1)}, u32[]{:S(2)}, u32[]{:S(2)}) collective-permute-start(bf16[192,256]{1,0:T(8,128)(2,1)S(1)} %get-tuple-element.97), channel_id=1, source_target_pairs={{0,2},{2,0},{4,6},{6,4},{8,10},{10,8},{12,14},{14,12},{16,18},{18,... | collective-permute-start | bytes 294920 | tf_op jit(solution)/shard_map/ppermute | solution.py:517
  69.7 5.6 %collective-permute-start.22 = (bf16[192,256]{1,0:T(8,128)(2,1)S(1)}, bf16[192,256]{1,0:T(8,128)(2,1)S(1)}, u32[]{:S(2)}, u32[]{:S(2)}) collective-permute-start(bf16[192,256]{1,0:T(8,128)(2,1)S(1)} %get-tuple-element.98), channel_id=1, source_target_pairs={{0,4},{2,6},{4,0},{6,2},{8,12},{10,14},{12,8},{14,10},{16,20},{18,... | collective-permute-start | bytes 294920 | tf_op jit(solution)/shard_map/ppermute | solution.py:517
  70.4 6.2 %collective-permute-start.23 = (bf16[192,256]{1,0:T(8,128)(2,1)S(1)}, bf16[192,256]{1,0:T(8,128)(2,1)S(1)}, u32[]{:S(2)}, u32[]{:S(2)}) collective-permute-start(bf16[192,256]{1,0:T(8,128)(2,1)S(1)} %get-tuple-element.99), channel_id=1, source_target_pairs={{0,6},{2,4},{4,2},{6,0},{8,14},{10,12},{12,10},{14,8},{16,22},{18,... | collective-permute-start | bytes 294920 | tf_op jit(solution)/shard_map/ppermute | solution.py:517

commit v11 on v8

--- a/solution.py
+++ b/solution.py
@@ -15,7 +15,7 @@
 GROUP = 4
 LANES = 128
 LSE_ROWS = 16
-PARTS = 2
+PARTS = 4
 LOADS = 3
 F32 = jnp.float32
 BF16 = jnp.bfloat16

time: 78.3 us -> 80.5 us (1.028)
  Pallas kernels: 22 us -> 24.2 us
    pallas_call x1, Pallas kernels: 9.78 us -> 11.1 us  [body(): pl.pallas_call(functools.partial(attend_kernel, False, blocks_here, head_...]
    pallas_call x1, Pallas kernels: 4.54 us -> 5.36 us  [body(): pl.pallas_call(functools.partial(attend_kernel, True, blocks_here, head_d...]
  transfers between devices with their start and end apart: 22 -> 22, of which waited for: 10 -> 10; matrix products, arithmetic and copies ran while one was open for 0% -> 0% of each run, Pallas kernels for 10% -> 11%
where the time goes in v11:
time: 80.5 us; the launch traced here: 80.2 us
  waiting for transfers between devices  29.1 us (36%)
  Pallas kernels  24.2 us (30%)
  starting transfers between devices  21.6 us (27%)
  local copies, waits for them, and re-layouts  3.71 us (5%)
  other arithmetic  0.84 us (1%)
    ppermute x15, waiting for transfers between devices, trade(): return lax.ppermute(x, 'var', [(n, n ^ distance) for n in range(devices)])  25.2 us
    pallas_call x1, Pallas kernels, body(): pl.pallas_call(functools.partial(attend_kernel, False, blocks_here, head_...  11.1 us
    ppermute x15, starting transfers between devices, trade(): return lax.ppermute(x, 'var', [(n, n ^ distance) for n in range(devices)])  10.8 us
    ppermute x6, starting transfers between devices, trade_level(): return lax.ppermute(x, ('var', 'head'), pairs)  9.11 us
    pallas_call x1, Pallas kernels, body(): pl.pallas_call(functools.partial(attend_kernel, True, blocks_here, head_d...  5.36 us
    unnamed x13, local copies, waits for them, and re-layouts  3.71 us
    ppermute x6, waiting for transfers between devices, trade_level(): return lax.ppermute(x, ('var', 'head'), pairs)  3.2 us
    pallas_call x1, Pallas kernels, body(): pl.pallas_call(pack_kv_kernel, out_shape=(shaped((rows, wide)),) * GROUP,...  2.48 us
  transfers between devices with their start and end apart: 22, of which 10 were waited for; matrix products, arithmetic and copies ran while one was open for 0% of the time, Pallas kernels for 11%

profile of v11, /device:TPU:0, one launch (start us, length us, event | category | flops | bytes accessed | tf_op | source)
XLA Modules:
  0.0 80.2 jit_solution(4380398959189813976)
XLA Ops:
  0.6 0.0 copy-start.5
  0.6 2.5 %shard_map.102 = (bf16[384,256]{1,0:T(8,128)(2,1)}, bf16[384,256]{1,0:T(8,128)(2,1)}, bf16[384,256]{1,0:T(8,128)(2,1)}, bf16[384,256]{1,0:T(8,128)(2,1)}) custom-call(bf16[384,512]{1,0:T(8,128)(2,1)} %k_hbm.1, bf16[384,512]{1,0:T(8,128)(2,1)} %v_hbm.1), custom_call_target="tpu_custom_call" | custom-call | flops 100663296 | bytes 1966080 | tf_op jit(solution)/shard_map/pallas_call | solution.py:524
  3.1 0.5 collective-permute-start
  3.6 2.6 %collective-permute-start.1 = (bf16[384,256]{1,0:T(8,128)(2,1)}, bf16[384,256]{1,0:T(8,128)(2,1)S(1)}, u32[]{:S(2)}, u32[]{:S(2)}) collective-permute-start(bf16[384,256]{1,0:T(8,128)(2,1)} %get-tuple-element.53), channel_id=1, source_target_pairs={{0,4},{2,6},{4,0},{6,2},{8,12},{10,14},{12,8},{14,10},{16,20},{18,... | collective-permute-start | bytes 589832 | tf_op jit(solution)/shard_map/ppermute | solution.py:487
  6.2 0.1 collective-permute-start.2
  6.3 0.0 collective-permute-done.after_ref.refs_1_
  6.3 0.0 copy-start.1
  6.3 1.0 %copy-done.1 = bf16[384,512]{1,0:T(8,128)(2,1)S(1)} copy-done((bf16[384,512]{1,0:T(8,128)(2,1)S(1)}, bf16[384,512]{1,0:T(8,128)(2,1)}, u32[]{:S(2)}) %copy-start.1) | copy-done | bytes 393240
  7.3 0.0 copy-start.2
  7.3 1.0 %copy-done.2 = bf16[384,512]{1,0:T(8,128)(2,1)S(1)} copy-done((bf16[384,512]{1,0:T(8,128)(2,1)S(1)}, bf16[384,512]{1,0:T(8,128)(2,1)}, u32[]{:S(2)}) %copy-start.2) | copy-done | bytes 393240
  8.3 0.9 %copy-done.3 = bf16[384,256]{1,0:T(8,128)(2,1)S(1)} copy-done((bf16[384,256]{1,0:T(8,128)(2,1)S(1)}, bf16[384,256]{1,0:T(8,128)(2,1)}, u32[]{:S(2)}) %copy-start.3) | copy-done | bytes 196632
  9.2 0.7 copy-done.4
  9.9 0.5 shard_map.103
  10.4 1.8 %collective-permute-done.1.refs_2_ = bf16[384,256]{1,0:T(8,128)(2,1)S(1)} collective-permute-done((bf16[384,256]{1,0:T(8,128)(2,1)}, bf16[384,256]{1,0:T(8,128)(2,1)S(1)}, u32[]{:S(2)}, u32[]{:S(2)}) %collective-permute-start.1) | collective-permute-done | bytes 196640 | tf_op jit(solution)/shard_map/ppermute | solution.py:487
  12.2 3.7 %collective-permute-done.2.refs_3_ = bf16[384,256]{1,0:T(8,128)(2,1)S(1)} collective-permute-done((bf16[384,256]{1,0:T(8,128)(2,1)}, bf16[384,256]{1,0:T(8,128)(2,1)S(1)}, u32[]{:S(2)}, u32[]{:S(2)}) %collective-permute-start.2) | collective-permute-done | bytes 196640 | tf_op jit(solution)/shard_map/ppermute | solution.py:487
  15.9 0.9 %shard_map.104 = (bf16[1936,256]{1,0:T(8,128)(2,1)S(1)}, bf16[1024,256]{1,0:T(8,128)(2,1)}, bf16[1024,256]{1,0:T(8,128)(2,1)S(1)}, bf16[400,256]{1,0:T(8,128)(2,...) custom-call(bf16[384,256]{1,0:T(8,128)(2,1)S(1)} %get-tuple-element., ...), custom_call_target="tpu_custom_call", output_to_operand_aliasing={{3}: (5, {}), {4}: (6, {}), {5}: (7, {})} | custom-call | bytes 1966080 | tf_op jit(solution)/shard_map/pallas_call | solution.py:545
  16.8 1.6 %collective-permute-start.3 = (bf16[1024,256]{1,0:T(8,128)(2,1)}, bf16[1024,256]{1,0:T(8,128)(2,1)S(1)}, u32[]{:S(2)}, u32[]{:S(2)}) collective-permute-start(bf16[1024,256]{1,0:T(8,128)(2,1)} %get-tuple-element.60), channel_id=1, source_target_pairs={{0,8},{1,9},{2,3},{3,2},{4,12},{5,13},{6,7},{7,6},{8,0},{9,1},{10,... | collective-permute-start | bytes 1572872 | tf_op jit(solution)/shard_map/ppermute | solution.py:499
  18.4 1.5 %collective-permute-start.4 = (bf16[1024,256]{1,0:T(8,128)(2,1)S(1)}, bf16[1024,256]{1,0:T(8,128)(2,1)S(1)}, u32[]{:S(2)}, u32[]{:S(2)}) collective-permute-start(bf16[1024,256]{1,0:T(8,128)(2,1)S(1)} %get-tuple-element.61), channel_id=1, source_target_pairs={{0,1},{1,0},{2,10},{3,11},{4,5},{5,4},{6,14},{7,15},{8,16},{9,17},... | collective-permute-start | bytes 1572872 | tf_op jit(solution)/shard_map/ppermute | solution.py:499
  19.9 0.0 collective-permute-start.5
  19.9 1.5 %collective-permute-start.6 = (bf16[400,256]{1,0:T(8,128)(2,1)S(1)}, bf16[400,256]{1,0:T(8,128)(2,1)}, u32[]{:S(2)}, u32[]{:S(2)}) collective-permute-start(bf16[400,256]{1,0:T(8,128)(2,1)S(1)} %get-tuple-element.63), channel_id=1, source_target_pairs={{0,4},{2,6},{4,0},{6,2},{8,12},{10,14},{12,8},{14,10},{16,20},{18,... | collective-permute-start | bytes 614408 | tf_op jit(solution)/shard_map/ppermute | solution.py:487
  21.5 0.3 collective-permute-start.7
  21.8 0.0 copy-done.5
  21.8 0.1 copy.18.kb_ref
  21.9 0.0 collective-permute-done.5.refs_3_
  21.9 6.0 %collective-permute-done.6.refs_4_ = bf16[400,256]{1,0:T(8,128)(2,1)} collective-permute-done((bf16[400,256]{1,0:T(8,128)(2,1)S(1)}, bf16[400,256]{1,0:T(8,128)(2,1)}, u32[]{:S(2)}, u32[]{:S(2)}) %collective-permute-start.6) | collective-permute-done | bytes 204832 | tf_op jit(solution)/shard_map/ppermute | solution.py:487
  27.9 3.6 %collective-permute-done.7.refs_5_ = bf16[400,256]{1,0:T(8,128)(2,1)} collective-permute-done((bf16[400,256]{1,0:T(8,128)(2,1)S(1)}, bf16[400,256]{1,0:T(8,128)(2,1)}, u32[]{:S(2)}, u32[]{:S(2)}) %collective-permute-start.7) | collective-permute-done | bytes 204832 | tf_op jit(solution)/shard_map/ppermute | solution.py:487
  31.5 0.0 collective-permute-done.3.refs_1_
  31.6 0.0 collective-permute-done.4.refs_2_
  31.6 11.1 %shard_map.105 = (bf16[4,128,256]{2,1,0:T(8,128)(2,1)S(1)}, bf16[4,128,256]{2,1,0:T(8,128)(2,1)S(1)}, bf16[28,128,256]{2,1,0:T(8,128)(2,1)S(1)}, bf16[28,128,128...) custom-call(s32[48,8]{1,0:T(8,128)S(1)} %copy.18.kb_ref, ...), custom_call_target="tpu_custom_call" | custom-call | flops 5395552768 | bytes 2000000 | tf_op jit(solution)/shard_map/pallas_call | solution.py:588
  42.7 1.7 %collective-permute-start.8 = (bf16[4,128,256]{2,1,0:T(8,128)(2,1)S(1)}, bf16[4,128,256]{2,1,0:T(8,128)(2,1)S(1)}, u32[]{:S(2)}, u32[]{:S(2)}) collective-permute-start(bf16[4,128,256]{2,1,0:T(8,128)(2,1)S(1)} %get-tuple-element.73), channel_id=1, source_target_pairs={{0,8},{1,9},{2,3},{3,2},{4,12},{5,13},{6,7},{7,6},{8,0},{9,1},{10,... | collective-permute-start | bytes 786440 | tf_op jit(solution)/shard_map/ppermute | solution.py:499
  44.4 1.5 %collective-permute-start.9 = (bf16[4,128,256]{2,1,0:T(8,128)(2,1)S(1)}, bf16[4,128,256]{2,1,0:T(8,128)(2,1)S(1)}, u32[]{:S(2)}, u32[]{:S(2)}) collective-permute-start(bf16[4,128,256]{2,1,0:T(8,128)(2,1)S(1)} %get-tuple-element.74), channel_id=1, source_target_pairs={{0,1},{1,0},{2,10},{3,11},{4,5},{5,4},{6,14},{7,15},{8,16},{9,17},... | collective-permute-start | bytes 786440 | tf_op jit(solution)/shard_map/ppermute | solution.py:499
  45.9 5.4 %shard_map.106 = (f32[12,128,256]{2,1,0:T(8,128)S(1)}, bf16[4,128,256]{2,1,0:T(8,128)(2,1)S(1)}, bf16[4,128,256]{2,1,0:T(8,128)(2,1)S(1)}, bf16[384,128]{1,0:T(8...) custom-call(s32[48,8]{1,0:T(8,128)S(1)} %copy.18.kb_ref, ...), custom_call_target="tpu_custom_call" | custom-call | flops 2657510912 | bytes 2000000 | tf_op jit(solution)/shard_map/pallas_call | solution.py:598
  51.2 1.7 %collective-permute-start.13 = (bf16[4,128,256]{2,1,0:T(8,128)(2,1)S(1)}, bf16[4,128,256]{2,1,0:T(8,128)(2,1)S(1)}, u32[]{:S(2)}, u32[]{:S(2)}) collective-permute-start(bf16[4,128,256]{2,1,0:T(8,128)(2,1)S(1)} %get-tuple-element.82), channel_id=1, source_target_pairs={{0,8},{1,9},{2,3},{3,2},{4,12},{5,13},{6,7},{7,6},{8,0},{9,1},{10,... | collective-permute-start | bytes 786440 | tf_op jit(solution)/shard_map/ppermute | solution.py:499
  52.9 1.1 %collective-permute-start.14 = (bf16[4,128,256]{2,1,0:T(8,128)(2,1)S(1)}, bf16[4,128,256]{2,1,0:T(8,128)(2,1)S(1)}, u32[]{:S(2)}, u32[]{:S(2)}) collective-permute-start(bf16[4,128,256]{2,1,0:T(8,128)(2,1)S(1)} %get-tuple-element.83), channel_id=1, source_target_pairs={{0,1},{1,0},{2,10},{3,11},{4,5},{5,4},{6,14},{7,15},{8,16},{9,17},... | collective-permute-start | bytes 786440 | tf_op jit(solution)/shard_map/ppermute | solution.py:499
  54.1 0.0 collective-permute-done.8.first_ref
  54.1 0.0 collective-permute-done.9.second_ref
  54.1 0.2 shard_map.107
  54.3 0.1 collective-permute-start.10
  54.3 1.6 %collective-permute-start.11 = (bf16[384,128]{1,0:T(8,128)(2,1)S(1)}, bf16[384,128]{1,0:T(8,128)(2,1)S(1)}, u32[]{:S(2)}, u32[]{:S(2)}) collective-permute-start(bf16[384,128]{1,0:T(8,128)(2,1)S(1)} %get-tuple-element.79), channel_id=1, source_target_pairs={{0,4},{2,6},{4,0},{6,2},{8,12},{10,14},{12,8},{14,10},{16,20},{18,... | collective-permute-start | bytes 294920 | tf_op jit(solution)/shard_map/ppermute | solution.py:487
  55.9 0.3 collective-permute-start.12
  56.2 3.2 %collective-permute-done.13.first_ref = bf16[4,128,256]{2,1,0:T(8,128)(2,1)S(1)} collective-permute-done((bf16[4,128,256]{2,1,0:T(8,128)(2,1)S(1)}, bf16[4,128,256]{2,1,0:T(8,128)(2,1)S(1)}, u32[]{:S(2)}, u32[]{:S(2)}) %collective-permute-start.13) | collective-permute-done | bytes 262176 | tf_op jit(solution)/shard_map/ppermute | solution.py:499
  59.4 0.0 collective-permute-done.14.second_ref
  59.4 0.5 shard_map.108
  59.8 0.1 collective-permute-start.15
  59.9 1.6 %collective-permute-start.16 = (bf16[192,256]{1,0:T(8,128)(2,1)S(1)}, bf16[192,256]{1,0:T(8,128)(2,1)S(1)}, u32[]{:S(2)}, u32[]{:S(2)}) collective-permute-start(bf16[192,256]{1,0:T(8,128)(2,1)S(1)} %get-tuple-element.86), channel_id=1, source_target_pairs={{0,4},{2,6},{4,0},{6,2},{8,12},{10,14},{12,8},{14,10},{16,20},{18,... | collective-permute-start | bytes 294920 | tf_op jit(solution)/shard_map/ppermute | solution.py:487
  61.5 0.0 collective-permute-done.10.refs_1_
  61.5 0.3 collective-permute-start.17
  61.8 0.0 collective-permute-done.11.refs_2_
  61.8 0.0 collective-permute-done.12.refs_3_
  61.8 0.0 collective-permute-done.15.refs_5_
  61.8 3.8 %collective-permute-done.16.refs_6_ = bf16[192,256]{1,0:T(8,128)(2,1)S(1)} collective-permute-done((bf16[192,256]{1,0:T(8,128)(2,1)S(1)}, bf16[192,256]{1,0:T(8,128)(2,1)S(1)}, u32[]{:S(2)}, u32[]{:S(2)}) %collective-permute-start.16) | collective-permute-done | bytes 98336 | tf_op jit(solution)/shard_map/ppermute | solution.py:487
  65.6 1.2 %collective-permute-done.17.refs_7_ = bf16[192,256]{1,0:T(8,128)(2,1)S(1)} collective-permute-done((bf16[192,256]{1,0:T(8,128)(2,1)S(1)}, bf16[192,256]{1,0:T(8,128)(2,1)S(1)}, u32[]{:S(2)}, u32[]{:S(2)}) %collective-permute-start.17) | collective-permute-done | bytes 98336 | tf_op jit(solution)/shard_map/ppermute | solution.py:487
  66.8 0.0 copy-done
  66.8 1.2 %shard_map.110 = bf16[192,1024]{1,0:T(8,128)(2,1)S(1)} custom-call(bf16[384,128]{1,0:T(8,128)(2,1)S(1)} %get-tuple-element.71.refs_0_, bf16[384,128]{1,0:T(8,128)(2,1)S(1)} %collective-permute-done.10.refs_1_, bf16[384,128]{1,0:T(8,128)(2,1)S(1)} %collective-permute-done.11.refs_2_, bf16[384,128]{1,0:T(8,128)(2,1)S(1)} %collective-permute-done.12.refs_3_, ...), custom_call_target="tpu_custom_call" | custom-call | flops 603979776 | bytes 4000000 | tf_op jit(solution)/shard_map/pallas_call | solution.py:634
  68.0 1.7 %collective-permute-start.21 = (bf16[192,1024]{1,0:T(8,128)(2,1)S(1)}, bf16[192,1024]{1,0:T(8,128)(2,1)S(1)}, u32[]{:S(2)}, u32[]{:S(2)}) collective-permute-start(bf16[192,1024]{1,0:T(8,128)(2,1)S(1)} %shard_map.110), channel_id=1, source_target_pairs={{0,1},{1,0},{2,3},{3,2},{4,5},{5,4},{6,7},{7,6},{8,9},{9,8},{10,11... | collective-permute-start | bytes 1179656 | tf_op jit(solution)/shard_map/ppermute | solution.py:653
  69.7 0.0 collective-permute-start.18
  69.7 1.5 %collective-permute-start.19 = (bf16[192,256]{1,0:T(8,128)(2,1)S(1)}, bf16[192,256]{1,0:T(8,128)(2,1)S(1)}, u32[]{:S(2)}, u32[]{:S(2)}) collective-permute-start(bf16[192,256]{1,0:T(8,128)(2,1)S(1)} %get-tuple-element.90), channel_id=1, source_target_pairs={{0,4},{2,6},{4,0},{6,2},{8,12},{10,14},{12,8},{14,10},{16,20},{18,... | collective-permute-start | bytes 294920 | tf_op jit(solution)/shard_map/ppermute | solution.py:487
  71.2 0.3 collective-permute-start.20
  71.6 0.0 collective-permute-done.18.refs_9_
  71.6 3.7 %collective-permute-done.19.refs_10_ = bf16[192,256]{1,0:T(8,128)(2,1)S(1)} collective-permute-done((bf16[192,256]{1,0:T(8,128)(2,1)S(1)}, bf16[192,256]{1,0:T(8,128)(2,1)S(1)}, u32[]{:S(2)}, u32[]{:S(2)}) %collective-permute-start.19) | collective-permute-done | bytes 98336 | tf_op jit(solution)/shard_map/ppermute | solution.py:487
  75.3 1.3 %collective-permute-done.20.refs_11_ = bf16[192,256]{1,0:T(8,128)(2,1)S(1)} collective-permute-done((bf16[192,256]{1,0:T(8,128)(2,1)S(1)}, bf16[192,256]{1,0:T(8,128)(2,1)S(1)}, u32[]{:S(2)}, u32[]{:S(2)}) %collective-permute-start.20) | collective-permute-done | bytes 98336 | tf_op jit(solution)/shard_map/ppermute | solution.py:487
  76.7 2.0 %shard_map.109 = (bf16[384,512]{1,0:T(8,128)(2,1)}, bf16[384,512]{1,0:T(8,128)(2,1)}, bf16[384,512]{1,0:T(8,128)(2,1)}, f32[192,1024]{1,0:T(8,128)S(1)}) custom-call(bf16[384,128]{1,0:T(8,128)(2,1)S(1)} %get-tuple-element.71.refs_0_, bf16[384,128]{1,0:T(8,128)(2,1)S(1)} %collective-permute-done.10.refs_1_, ...), custom_call_target="tpu_custom_call" | custom-call | flops 603979776 | bytes 6000000 | tf_op jit(solution)/shard_map/pallas_call | solution.py:643
  78.6 0.7 collective-permute-done.21
  79.4 0.8 %add_convert_fusion = bf16[192,1024]{1,0:T(8,128)(2,1)} fusion(f32[192,1024]{1,0:T(8,128)S(1)} %get-tuple-element.95, bf16[192,1024]{1,0:T(8,128)(2,1)S(1)} %collective-permute-done.21), kind=kLoop, calls=%fused_computation | loop fusion | flops 589824 | bytes 1572864 | tf_op jit(solution)/shard_map/convert_element_type | solution.py:655
  (3 shorter events, 0.0 us)
Async XLA Ops:
  0.6 21.2 %copy-start.5 = (s32[48,8]{0,1:T(8,128)S(1)}, s32[48,8]{0,1:T(8,128)}, u32[]{:S(2)}) copy-start(s32[48,8]{0,1:T(8,128)} %param.12) | copy-start | bytes 4612
  3.1 3.2 %collective-permute-start = (bf16[384,256]{1,0:T(8,128)(2,1)}, bf16[384,256]{1,0:T(8,128)(2,1)S(1)}, u32[]{:S(2)}, u32[]{:S(2)}) collective-permute-start(bf16[384,256]{1,0:T(8,128)(2,1)} %get-tuple-element.51), channel_id=1, source_target_pairs={{0,2},{2,0},{4,6},{6,4},{8,10},{10,8},{12,14},{14,12},{16,18},{18,... | collective-permute-start | bytes 589832 | tf_op jit(solution)/shard_map/ppermute | solution.py:487
  3.6 8.6 %collective-permute-start.1 = (bf16[384,256]{1,0:T(8,128)(2,1)}, bf16[384,256]{1,0:T(8,128)(2,1)S(1)}, u32[]{:S(2)}, u32[]{:S(2)}) collective-permute-start(bf16[384,256]{1,0:T(8,128)(2,1)} %get-tuple-element.53), channel_id=1, source_target_pairs={{0,4},{2,6},{4,0},{6,2},{8,12},{10,14},{12,8},{14,10},{16,20},{18,... | collective-permute-start | bytes 589832 | tf_op jit(solution)/shard_map/ppermute | solution.py:487
  6.2 9.7 %collective-permute-start.2 = (bf16[384,256]{1,0:T(8,128)(2,1)}, bf16[384,256]{1,0:T(8,128)(2,1)S(1)}, u32[]{:S(2)}, u32[]{:S(2)}) collective-permute-start(bf16[384,256]{1,0:T(8,128)(2,1)} %get-tuple-element.54), channel_id=1, source_target_pairs={{0,6},{2,4},{4,2},{6,0},{8,14},{10,12},{12,10},{14,8},{16,22},{18,... | collective-permute-start | bytes 589832 | tf_op jit(solution)/shard_map/ppermute | solution.py:487
  6.3 1.0 %copy-start.1 = (bf16[384,512]{1,0:T(8,128)(2,1)S(1)}, bf16[384,512]{1,0:T(8,128)(2,1)}, u32[]{:S(2)}) copy-start(bf16[384,512]{1,0:T(8,128)(2,1)} %q_ref.1) | copy-start | bytes 1179652
  7.3 1.0 %copy-start.2 = (bf16[384,512]{1,0:T(8,128)(2,1)S(1)}, bf16[384,512]{1,0:T(8,128)(2,1)}, u32[]{:S(2)}) copy-start(bf16[384,512]{1,0:T(8,128)(2,1)} %g_ref.1) | copy-start | bytes 1179652
  8.3 0.9 %copy-start.3 = (bf16[384,256]{1,0:T(8,128)(2,1)S(1)}, bf16[384,256]{1,0:T(8,128)(2,1)}, u32[]{:S(2)}) copy-start(bf16[384,256]{1,0:T(8,128)(2,1)} %get-tuple-element.50.mine_ref) | copy-start | bytes 589828
  9.2 0.7 copy-start.4
  16.8 14.8 %collective-permute-start.3 = (bf16[1024,256]{1,0:T(8,128)(2,1)}, bf16[1024,256]{1,0:T(8,128)(2,1)S(1)}, u32[]{:S(2)}, u32[]{:S(2)}) collective-permute-start(bf16[1024,256]{1,0:T(8,128)(2,1)} %get-tuple-element.60), channel_id=1, source_target_pairs={{0,8},{1,9},{2,3},{3,2},{4,12},{5,13},{6,7},{7,6},{8,0},{9,1},{10,... | collective-permute-start | bytes 1572872 | tf_op jit(solution)/shard_map/ppermute | solution.py:499
  18.4 13.1 %collective-permute-start.4 = (bf16[1024,256]{1,0:T(8,128)(2,1)S(1)}, bf16[1024,256]{1,0:T(8,128)(2,1)S(1)}, u32[]{:S(2)}, u32[]{:S(2)}) collective-permute-start(bf16[1024,256]{1,0:T(8,128)(2,1)S(1)} %get-tuple-element.61), channel_id=1, source_target_pairs={{0,1},{1,0},{2,10},{3,11},{4,5},{5,4},{6,14},{7,15},{8,16},{9,17},... | collective-permute-start | bytes 1572872 | tf_op jit(solution)/shard_map/ppermute | solution.py:499
  19.9 1.9 %collective-permute-start.5 = (bf16[400,256]{1,0:T(8,128)(2,1)S(1)}, bf16[400,256]{1,0:T(8,128)(2,1)S(1)}, u32[]{:S(2)}, u32[]{:S(2)}) collective-permute-start(bf16[400,256]{1,0:T(8,128)(2,1)S(1)} %get-tuple-element.62), channel_id=1, source_target_pairs={{0,2},{2,0},{4,6},{6,4},{8,10},{10,8},{12,14},{14,12},{16,18},{18,... | collective-permute-start | bytes 614408 | tf_op jit(solution)/shard_map/ppermute | solution.py:487
  19.9 8.0 %collective-permute-start.6 = (bf16[400,256]{1,0:T(8,128)(2,1)S(1)}, bf16[400,256]{1,0:T(8,128)(2,1)}, u32[]{:S(2)}, u32[]{:S(2)}) collective-permute-start(bf16[400,256]{1,0:T(8,128)(2,1)S(1)} %get-tuple-element.63), channel_id=1, source_target_pairs={{0,4},{2,6},{4,0},{6,2},{8,12},{10,14},{12,8},{14,10},{16,20},{18,... | collective-permute-start | bytes 614408 | tf_op jit(solution)/shard_map/ppermute | solution.py:487
  21.5 10.1 %collective-permute-start.7 = (bf16[400,256]{1,0:T(8,128)(2,1)S(1)}, bf16[400,256]{1,0:T(8,128)(2,1)}, u32[]{:S(2)}, u32[]{:S(2)}) collective-permute-start(bf16[400,256]{1,0:T(8,128)(2,1)S(1)} %get-tuple-element.64), channel_id=1, source_target_pairs={{0,6},{2,4},{4,2},{6,0},{8,14},{10,12},{12,10},{14,8},{16,22},{18,... | collective-permute-start | bytes 614408 | tf_op jit(solution)/shard_map/ppermute | solution.py:487
  42.7 11.4 %collective-permute-start.8 = (bf16[4,128,256]{2,1,0:T(8,128)(2,1)S(1)}, bf16[4,128,256]{2,1,0:T(8,128)(2,1)S(1)}, u32[]{:S(2)}, u32[]{:S(2)}) collective-permute-start(bf16[4,128,256]{2,1,0:T(8,128)(2,1)S(1)} %get-tuple-element.73), channel_id=1, source_target_pairs={{0,8},{1,9},{2,3},{3,2},{4,12},{5,13},{6,7},{7,6},{8,0},{9,1},{10,... | collective-permute-start | bytes 786440 | tf_op jit(solution)/shard_map/ppermute | solution.py:499
  44.4 9.7 %collective-permute-start.9 = (bf16[4,128,256]{2,1,0:T(8,128)(2,1)S(1)}, bf16[4,128,256]{2,1,0:T(8,128)(2,1)S(1)}, u32[]{:S(2)}, u32[]{:S(2)}) collective-permute-start(bf16[4,128,256]{2,1,0:T(8,128)(2,1)S(1)} %get-tuple-element.74), channel_id=1, source_target_pairs={{0,1},{1,0},{2,10},{3,11},{4,5},{5,4},{6,14},{7,15},{8,16},{9,17},... | collective-permute-start | bytes 786440 | tf_op jit(solution)/shard_map/ppermute | solution.py:499
  51.2 8.1 %collective-permute-start.13 = (bf16[4,128,256]{2,1,0:T(8,128)(2,1)S(1)}, bf16[4,128,256]{2,1,0:T(8,128)(2,1)S(1)}, u32[]{:S(2)}, u32[]{:S(2)}) collective-permute-start(bf16[4,128,256]{2,1,0:T(8,128)(2,1)S(1)} %get-tuple-element.82), channel_id=1, source_target_pairs={{0,8},{1,9},{2,3},{3,2},{4,12},{5,13},{6,7},{7,6},{8,0},{9,1},{10,... | collective-permute-start | bytes 786440 | tf_op jit(solution)/shard_map/ppermute | solution.py:499
  52.9 6.4 %collective-permute-start.14 = (bf16[4,128,256]{2,1,0:T(8,128)(2,1)S(1)}, bf16[4,128,256]{2,1,0:T(8,128)(2,1)S(1)}, u32[]{:S(2)}, u32[]{:S(2)}) collective-permute-start(bf16[4,128,256]{2,1,0:T(8,128)(2,1)S(1)} %get-tuple-element.83), channel_id=1, source_target_pairs={{0,1},{1,0},{2,10},{3,11},{4,5},{5,4},{6,14},{7,15},{8,16},{9,17},... | collective-permute-start | bytes 786440 | tf_op jit(solution)/shard_map/ppermute | solution.py:499
  54.1 12.7 %copy-start = (bf16[3,1024,512]{2,1,0:T(8,128)(2,1)S(1)}, bf16[3,1024,512]{2,1,0:T(8,128)(2,1)}, u32[]{:S(2)}) copy-start(bf16[3,1024,512]{2,1,0:T(8,128)(2,1)} %refs_8_.1) | copy-start | bytes 9437188
  54.3 7.3 %collective-permute-start.10 = (bf16[384,128]{1,0:T(8,128)(2,1)S(1)}, bf16[384,128]{1,0:T(8,128)(2,1)S(1)}, u32[]{:S(2)}, u32[]{:S(2)}) collective-permute-start(bf16[384,128]{1,0:T(8,128)(2,1)S(1)} %get-tuple-element.78), channel_id=1, source_target_pairs={{0,2},{2,0},{4,6},{6,4},{8,10},{10,8},{12,14},{14,12},{16,18},{18,... | collective-permute-start | bytes 294920 | tf_op jit(solution)/shard_map/ppermute | solution.py:487
  54.3 7.5 %collective-permute-start.11 = (bf16[384,128]{1,0:T(8,128)(2,1)S(1)}, bf16[384,128]{1,0:T(8,128)(2,1)S(1)}, u32[]{:S(2)}, u32[]{:S(2)}) collective-permute-start(bf16[384,128]{1,0:T(8,128)(2,1)S(1)} %get-tuple-element.79), channel_id=1, source_target_pairs={{0,4},{2,6},{4,0},{6,2},{8,12},{10,14},{12,8},{14,10},{16,20},{18,... | collective-permute-start | bytes 294920 | tf_op jit(solution)/shard_map/ppermute | solution.py:487
  55.9 5.9 %collective-permute-start.12 = (bf16[384,128]{1,0:T(8,128)(2,1)S(1)}, bf16[384,128]{1,0:T(8,128)(2,1)S(1)}, u32[]{:S(2)}, u32[]{:S(2)}) collective-permute-start(bf16[384,128]{1,0:T(8,128)(2,1)S(1)} %get-tuple-element.80), channel_id=1, source_target_pairs={{0,6},{2,4},{4,2},{6,0},{8,14},{10,12},{12,10},{14,8},{16,22},{18,... | collective-permute-start | bytes 294920 | tf_op jit(solution)/shard_map/ppermute | solution.py:487
  59.8 2.0 %collective-permute-start.15 = (bf16[192,256]{1,0:T(8,128)(2,1)S(1)}, bf16[192,256]{1,0:T(8,128)(2,1)S(1)}, u32[]{:S(2)}, u32[]{:S(2)}) collective-permute-start(bf16[192,256]{1,0:T(8,128)(2,1)S(1)} %get-tuple-element.85), channel_id=1, source_target_pairs={{0,2},{2,0},{4,6},{6,4},{8,10},{10,8},{12,14},{14,12},{16,18},{18,... | collective-permute-start | bytes 294920 | tf_op jit(solution)/shard_map/ppermute | solution.py:487
  59.9 5.7 %collective-permute-start.16 = (bf16[192,256]{1,0:T(8,128)(2,1)S(1)}, bf16[192,256]{1,0:T(8,128)(2,1)S(1)}, u32[]{:S(2)}, u32[]{:S(2)}) collective-permute-start(bf16[192,256]{1,0:T(8,128)(2,1)S(1)} %get-tuple-element.86), channel_id=1, source_target_pairs={{0,4},{2,6},{4,0},{6,2},{8,12},{10,14},{12,8},{14,10},{16,20},{18,... | collective-permute-start | bytes 294920 | tf_op jit(solution)/shard_map/ppermute | solution.py:487
  61.5 5.3 %collective-permute-start.17 = (bf16[192,256]{1,0:T(8,128)(2,1)S(1)}, bf16[192,256]{1,0:T(8,128)(2,1)S(1)}, u32[]{:S(2)}, u32[]{:S(2)}) collective-permute-start(bf16[192,256]{1,0:T(8,128)(2,1)S(1)} %get-tuple-element.87), channel_id=1, source_target_pairs={{0,6},{2,4},{4,2},{6,0},{8,14},{10,12},{12,10},{14,8},{16,22},{18,... | collective-permute-start | bytes 294920 | tf_op jit(solution)/shard_map/ppermute | solution.py:487
  68.0 11.4 %collective-permute-start.21 = (bf16[192,1024]{1,0:T(8,128)(2,1)S(1)}, bf16[192,1024]{1,0:T(8,128)(2,1)S(1)}, u32[]{:S(2)}, u32[]{:S(2)}) collective-permute-start(bf16[192,1024]{1,0:T(8,128)(2,1)S(1)} %shard_map.110), channel_id=1, source_target_pairs={{0,1},{1,0},{2,3},{3,2},{4,5},{5,4},{6,7},{7,6},{8,9},{9,8},{10,11... | collective-permute-start | bytes 1179656 | tf_op jit(solution)/shard_map/ppermute | solution.py:653
  69.7 1.9 %collective-permute-start.18 = (bf16[192,256]{1,0:T(8,128)(2,1)S(1)}, bf16[192,256]{1,0:T(8,128)(2,1)S(1)}, u32[]{:S(2)}, u32[]{:S(2)}) collective-permute-start(bf16[192,256]{1,0:T(8,128)(2,1)S(1)} %get-tuple-element.89), channel_id=1, source_target_pairs={{0,2},{2,0},{4,6},{6,4},{8,10},{10,8},{12,14},{14,12},{16,18},{18,... | collective-permute-start | bytes 294920 | tf_op jit(solution)/shard_map/ppermute | solution.py:487
  69.7 5.6 %collective-permute-start.19 = (bf16[192,256]{1,0:T(8,128)(2,1)S(1)}, bf16[192,256]{1,0:T(8,128)(2,1)S(1)}, u32[]{:S(2)}, u32[]{:S(2)}) collective-permute-start(bf16[192,256]{1,0:T(8,128)(2,1)S(1)} %get-tuple-element.90), channel_id=1, source_target_pairs={{0,4},{2,6},{4,0},{6,2},{8,12},{10,14},{12,8},{14,10},{16,20},{18,... | collective-permute-start | bytes 294920 | tf_op jit(solution)/shard_map/ppermute | solution.py:487
  71.2 5.4 %collective-permute-start.20 = (bf16[192,256]{1,0:T(8,128)(2,1)S(1)}, bf16[192,256]{1,0:T(8,128)(2,1)S(1)}, u32[]{:S(2)}, u32[]{:S(2)}) collective-permute-start(bf16[192,256]{1,0:T(8,128)(2,1)S(1)} %get-tuple-element.91), channel_id=1, source_target_pairs={{0,6},{2,4},{4,2},{6,0},{8,14},{10,12},{12,10},{14,8},{16,22},{18,... | collective-permute-start | bytes 294920 | tf_op jit(solution)/shard_map/ppermute | solution.py:487

commit v12 on v8

--- a/solution.py
+++ b/solution.py
@@ -222,7 +222,7 @@
                 shifts[at, 0, :, high] = jnp.broadcast_to(-lse[:, high], (8, LANES))
                 shifts[at, 1, :, low] = jnp.where(usable, -lse[:, high], -1e30)
 
-        @pl.loop(0, window)
+        @pl.loop(0, window, unroll=4)
         def _(block):
             k_turn[block] = kv_win[block, :, low].T
 

time: 78.3 us -> 77 us (0.983)
  Pallas kernels: 22 us -> 20.7 us
    pallas_call x1, Pallas kernels: 9.78 us -> 8.42 us  [body(): pl.pallas_call(functools.partial(attend_kernel, False, blocks_here, head_...]
where the time goes in v12:
time: 77 us; the launch traced here: 76.7 us
  waiting for transfers between devices  29.1 us (38%)
  starting transfers between devices  21.6 us (28%)
  Pallas kernels  20.7 us (27%)
  local copies, waits for them, and re-layouts  3.71 us (5%)
  other arithmetic  0.84 us (1%)
    ppermute x15, waiting for transfers between devices, trade(): return lax.ppermute(x, 'var', [(n, n ^ distance) for n in range(devices)])  25.2 us
    ppermute x15, starting transfers between devices, trade(): return lax.ppermute(x, 'var', [(n, n ^ distance) for n in range(devices)])  10.8 us
    ppermute x6, starting transfers between devices, trade_level(): return lax.ppermute(x, ('var', 'head'), pairs)  9.12 us
    pallas_call x1, Pallas kernels, body(): pl.pallas_call(functools.partial(attend_kernel, False, blocks_here, head_...  8.42 us
    pallas_call x1, Pallas kernels, body(): pl.pallas_call(functools.partial(attend_kernel, True, blocks_here, head_d...  4.54 us
    unnamed x13, local copies, waits for them, and re-layouts  3.71 us
    ppermute x6, waiting for transfers between devices, trade_level(): return lax.ppermute(x, ('var', 'head'), pairs)  3.2 us
    pallas_call x1, Pallas kernels, body(): pl.pallas_call(pack_kv_kernel, out_shape=(shaped((rows, wide)),) * GROUP,...  2.48 us
  transfers between devices with their start and end apart: 22, of which 10 were waited for; matrix products, arithmetic and copies ran while one was open for 0% of the time, Pallas kernels for 10%

profile of v12, /device:TPU:0, one launch (start us, length us, event | category | flops | bytes accessed | tf_op | source)
XLA Modules:
  0.0 76.7 jit_solution(1389936290162279584)
XLA Ops:
  0.6 0.0 copy-start.5
  0.6 2.5 %shard_map.102 = (bf16[384,256]{1,0:T(8,128)(2,1)}, bf16[384,256]{1,0:T(8,128)(2,1)}, bf16[384,256]{1,0:T(8,128)(2,1)}, bf16[384,256]{1,0:T(8,128)(2,1)}) custom-call(bf16[384,512]{1,0:T(8,128)(2,1)} %k_hbm.1, bf16[384,512]{1,0:T(8,128)(2,1)} %v_hbm.1), custom_call_target="tpu_custom_call" | custom-call | flops 100663296 | bytes 1966080 | tf_op jit(solution)/shard_map/pallas_call | solution.py:524
  3.1 0.5 collective-permute-start
  3.6 2.6 %collective-permute-start.1 = (bf16[384,256]{1,0:T(8,128)(2,1)}, bf16[384,256]{1,0:T(8,128)(2,1)S(1)}, u32[]{:S(2)}, u32[]{:S(2)}) collective-permute-start(bf16[384,256]{1,0:T(8,128)(2,1)} %get-tuple-element.53), channel_id=1, source_target_pairs={{0,4},{2,6},{4,0},{6,2},{8,12},{10,14},{12,8},{14,10},{16,20},{18,... | collective-permute-start | bytes 589832 | tf_op jit(solution)/shard_map/ppermute | solution.py:487
  6.2 0.1 collective-permute-start.2
  6.3 0.0 collective-permute-done.after_ref.refs_1_
  6.3 1.0 %copy-done.1 = bf16[384,512]{1,0:T(8,128)(2,1)S(1)} copy-done((bf16[384,512]{1,0:T(8,128)(2,1)S(1)}, bf16[384,512]{1,0:T(8,128)(2,1)}, u32[]{:S(2)}) %copy-start.1) | copy-done | bytes 393240
  7.3 0.0 copy-start.2
  7.3 1.0 %copy-done.2 = bf16[384,512]{1,0:T(8,128)(2,1)S(1)} copy-done((bf16[384,512]{1,0:T(8,128)(2,1)S(1)}, bf16[384,512]{1,0:T(8,128)(2,1)}, u32[]{:S(2)}) %copy-start.2) | copy-done | bytes 393240
  8.3 0.0 copy-start.3
  8.3 0.9 %copy-done.3 = bf16[384,256]{1,0:T(8,128)(2,1)S(1)} copy-done((bf16[384,256]{1,0:T(8,128)(2,1)S(1)}, bf16[384,256]{1,0:T(8,128)(2,1)}, u32[]{:S(2)}) %copy-start.3) | copy-done | bytes 196632
  9.2 0.7 copy-done.4
  9.9 0.5 shard_map.103
  10.4 1.8 %collective-permute-done.1.refs_2_ = bf16[384,256]{1,0:T(8,128)(2,1)S(1)} collective-permute-done((bf16[384,256]{1,0:T(8,128)(2,1)}, bf16[384,256]{1,0:T(8,128)(2,1)S(1)}, u32[]{:S(2)}, u32[]{:S(2)}) %collective-permute-start.1) | collective-permute-done | bytes 196640 | tf_op jit(solution)/shard_map/ppermute | solution.py:487
  12.2 3.7 %collective-permute-done.2.refs_3_ = bf16[384,256]{1,0:T(8,128)(2,1)S(1)} collective-permute-done((bf16[384,256]{1,0:T(8,128)(2,1)}, bf16[384,256]{1,0:T(8,128)(2,1)S(1)}, u32[]{:S(2)}, u32[]{:S(2)}) %collective-permute-start.2) | collective-permute-done | bytes 196640 | tf_op jit(solution)/shard_map/ppermute | solution.py:487
  15.9 0.9 %shard_map.104 = (bf16[1936,256]{1,0:T(8,128)(2,1)S(1)}, bf16[1024,256]{1,0:T(8,128)(2,1)}, bf16[1024,256]{1,0:T(8,128)(2,1)S(1)}, bf16[400,256]{1,0:T(8,128)(2,...) custom-call(bf16[384,256]{1,0:T(8,128)(2,1)S(1)} %get-tuple-element., ...), custom_call_target="tpu_custom_call", output_to_operand_aliasing={{3}: (5, {}), {4}: (6, {}), {5}: (7, {})} | custom-call | bytes 1966080 | tf_op jit(solution)/shard_map/pallas_call | solution.py:545
  16.8 1.6 %collective-permute-start.3 = (bf16[1024,256]{1,0:T(8,128)(2,1)}, bf16[1024,256]{1,0:T(8,128)(2,1)S(1)}, u32[]{:S(2)}, u32[]{:S(2)}) collective-permute-start(bf16[1024,256]{1,0:T(8,128)(2,1)} %get-tuple-element.60), channel_id=1, source_target_pairs={{0,8},{1,9},{2,3},{3,2},{4,12},{5,13},{6,7},{7,6},{8,0},{9,1},{10,... | collective-permute-start | bytes 1572872 | tf_op jit(solution)/shard_map/ppermute | solution.py:499
  18.4 1.5 %collective-permute-start.4 = (bf16[1024,256]{1,0:T(8,128)(2,1)S(1)}, bf16[1024,256]{1,0:T(8,128)(2,1)S(1)}, u32[]{:S(2)}, u32[]{:S(2)}) collective-permute-start(bf16[1024,256]{1,0:T(8,128)(2,1)S(1)} %get-tuple-element.61), channel_id=1, source_target_pairs={{0,1},{1,0},{2,10},{3,11},{4,5},{5,4},{6,14},{7,15},{8,16},{9,17},... | collective-permute-start | bytes 1572872 | tf_op jit(solution)/shard_map/ppermute | solution.py:499
  19.9 0.0 collective-permute-start.5
  19.9 1.5 %collective-permute-start.6 = (bf16[400,256]{1,0:T(8,128)(2,1)S(1)}, bf16[400,256]{1,0:T(8,128)(2,1)}, u32[]{:S(2)}, u32[]{:S(2)}) collective-permute-start(bf16[400,256]{1,0:T(8,128)(2,1)S(1)} %get-tuple-element.63), channel_id=1, source_target_pairs={{0,4},{2,6},{4,0},{6,2},{8,12},{10,14},{12,8},{14,10},{16,20},{18,... | collective-permute-start | bytes 614408 | tf_op jit(solution)/shard_map/ppermute | solution.py:487
  21.5 0.3 collective-permute-start.7
  21.8 0.0 copy-done.5
  21.8 0.1 copy.18.kb_ref
  21.9 0.0 collective-permute-done.5.refs_3_
  21.9 6.0 %collective-permute-done.6.refs_4_ = bf16[400,256]{1,0:T(8,128)(2,1)} collective-permute-done((bf16[400,256]{1,0:T(8,128)(2,1)S(1)}, bf16[400,256]{1,0:T(8,128)(2,1)}, u32[]{:S(2)}, u32[]{:S(2)}) %collective-permute-start.6) | collective-permute-done | bytes 204832 | tf_op jit(solution)/shard_map/ppermute | solution.py:487
  27.9 3.6 %collective-permute-done.7.refs_5_ = bf16[400,256]{1,0:T(8,128)(2,1)} collective-permute-done((bf16[400,256]{1,0:T(8,128)(2,1)S(1)}, bf16[400,256]{1,0:T(8,128)(2,1)}, u32[]{:S(2)}, u32[]{:S(2)}) %collective-permute-start.7) | collective-permute-done | bytes 204832 | tf_op jit(solution)/shard_map/ppermute | solution.py:487
  31.5 0.0 collective-permute-done.3.refs_1_
  31.6 0.0 collective-permute-done.4.refs_2_
  31.6 8.4 %shard_map.105 = (bf16[4,128,256]{2,1,0:T(8,128)(2,1)S(1)}, bf16[4,128,256]{2,1,0:T(8,128)(2,1)S(1)}, bf16[28,128,256]{2,1,0:T(8,128)(2,1)S(1)}, bf16[28,128,128...) custom-call(s32[48,8]{1,0:T(8,128)S(1)} %copy.18.kb_ref, ...), custom_call_target="tpu_custom_call" | custom-call | flops 5395552768 | bytes 2000000 | tf_op jit(solution)/shard_map/pallas_call | solution.py:588
  40.0 1.7 %collective-permute-start.8 = (bf16[4,128,256]{2,1,0:T(8,128)(2,1)S(1)}, bf16[4,128,256]{2,1,0:T(8,128)(2,1)S(1)}, u32[]{:S(2)}, u32[]{:S(2)}) collective-permute-start(bf16[4,128,256]{2,1,0:T(8,128)(2,1)S(1)} %get-tuple-element.73), channel_id=1, source_target_pairs={{0,8},{1,9},{2,3},{3,2},{4,12},{5,13},{6,7},{7,6},{8,0},{9,1},{10,... | collective-permute-start | bytes 786440 | tf_op jit(solution)/shard_map/ppermute | solution.py:499
  41.7 1.5 %collective-permute-start.9 = (bf16[4,128,256]{2,1,0:T(8,128)(2,1)S(1)}, bf16[4,128,256]{2,1,0:T(8,128)(2,1)S(1)}, u32[]{:S(2)}, u32[]{:S(2)}) collective-permute-start(bf16[4,128,256]{2,1,0:T(8,128)(2,1)S(1)} %get-tuple-element.74), channel_id=1, source_target_pairs={{0,1},{1,0},{2,10},{3,11},{4,5},{5,4},{6,14},{7,15},{8,16},{9,17},... | collective-permute-start | bytes 786440 | tf_op jit(solution)/shard_map/ppermute | solution.py:499
  43.2 4.5 %shard_map.106 = (f32[12,128,256]{2,1,0:T(8,128)S(1)}, bf16[4,128,256]{2,1,0:T(8,128)(2,1)S(1)}, bf16[4,128,256]{2,1,0:T(8,128)(2,1)S(1)}, bf16[384,128]{1,0:T(8...) custom-call(s32[48,8]{1,0:T(8,128)S(1)} %copy.18.kb_ref, ...), custom_call_target="tpu_custom_call" | custom-call | flops 2657510912 | bytes 2000000 | tf_op jit(solution)/shard_map/pallas_call | solution.py:598
  47.7 1.7 %collective-permute-start.13 = (bf16[4,128,256]{2,1,0:T(8,128)(2,1)S(1)}, bf16[4,128,256]{2,1,0:T(8,128)(2,1)S(1)}, u32[]{:S(2)}, u32[]{:S(2)}) collective-permute-start(bf16[4,128,256]{2,1,0:T(8,128)(2,1)S(1)} %get-tuple-element.82), channel_id=1, source_target_pairs={{0,8},{1,9},{2,3},{3,2},{4,12},{5,13},{6,7},{7,6},{8,0},{9,1},{10,... | collective-permute-start | bytes 786440 | tf_op jit(solution)/shard_map/ppermute | solution.py:499
  49.4 1.1 %collective-permute-start.14 = (bf16[4,128,256]{2,1,0:T(8,128)(2,1)S(1)}, bf16[4,128,256]{2,1,0:T(8,128)(2,1)S(1)}, u32[]{:S(2)}, u32[]{:S(2)}) collective-permute-start(bf16[4,128,256]{2,1,0:T(8,128)(2,1)S(1)} %get-tuple-element.83), channel_id=1, source_target_pairs={{0,1},{1,0},{2,10},{3,11},{4,5},{5,4},{6,14},{7,15},{8,16},{9,17},... | collective-permute-start | bytes 786440 | tf_op jit(solution)/shard_map/ppermute | solution.py:499
  50.6 0.0 collective-permute-done.8.first_ref
  50.6 0.0 collective-permute-done.9.second_ref
  50.6 0.2 shard_map.107
  50.7 0.1 collective-permute-start.10
  50.8 1.6 %collective-permute-start.11 = (bf16[384,128]{1,0:T(8,128)(2,1)S(1)}, bf16[384,128]{1,0:T(8,128)(2,1)S(1)}, u32[]{:S(2)}, u32[]{:S(2)}) collective-permute-start(bf16[384,128]{1,0:T(8,128)(2,1)S(1)} %get-tuple-element.79), channel_id=1, source_target_pairs={{0,4},{2,6},{4,0},{6,2},{8,12},{10,14},{12,8},{14,10},{16,20},{18,... | collective-permute-start | bytes 294920 | tf_op jit(solution)/shard_map/ppermute | solution.py:487
  52.4 0.3 collective-permute-start.12
  52.7 3.2 %collective-permute-done.13.first_ref = bf16[4,128,256]{2,1,0:T(8,128)(2,1)S(1)} collective-permute-done((bf16[4,128,256]{2,1,0:T(8,128)(2,1)S(1)}, bf16[4,128,256]{2,1,0:T(8,128)(2,1)S(1)}, u32[]{:S(2)}, u32[]{:S(2)}) %collective-permute-start.13) | collective-permute-done | bytes 262176 | tf_op jit(solution)/shard_map/ppermute | solution.py:499
  55.8 0.0 collective-permute-done.14.second_ref
  55.8 0.5 shard_map.108
  56.3 0.1 collective-permute-start.15
  56.4 1.6 %collective-permute-start.16 = (bf16[192,256]{1,0:T(8,128)(2,1)S(1)}, bf16[192,256]{1,0:T(8,128)(2,1)S(1)}, u32[]{:S(2)}, u32[]{:S(2)}) collective-permute-start(bf16[192,256]{1,0:T(8,128)(2,1)S(1)} %get-tuple-element.86), channel_id=1, source_target_pairs={{0,4},{2,6},{4,0},{6,2},{8,12},{10,14},{12,8},{14,10},{16,20},{18,... | collective-permute-start | bytes 294920 | tf_op jit(solution)/shard_map/ppermute | solution.py:487
  58.0 0.0 collective-permute-done.10.refs_1_
  58.0 0.3 collective-permute-start.17
  58.3 0.0 collective-permute-done.11.refs_2_
  58.3 0.0 collective-permute-done.12.refs_3_
  58.3 0.0 collective-permute-done.15.refs_5_
  58.3 3.8 %collective-permute-done.16.refs_6_ = bf16[192,256]{1,0:T(8,128)(2,1)S(1)} collective-permute-done((bf16[192,256]{1,0:T(8,128)(2,1)S(1)}, bf16[192,256]{1,0:T(8,128)(2,1)S(1)}, u32[]{:S(2)}, u32[]{:S(2)}) %collective-permute-start.16) | collective-permute-done | bytes 98336 | tf_op jit(solution)/shard_map/ppermute | solution.py:487
  62.1 1.2 %collective-permute-done.17.refs_7_ = bf16[192,256]{1,0:T(8,128)(2,1)S(1)} collective-permute-done((bf16[192,256]{1,0:T(8,128)(2,1)S(1)}, bf16[192,256]{1,0:T(8,128)(2,1)S(1)}, u32[]{:S(2)}, u32[]{:S(2)}) %collective-permute-start.17) | collective-permute-done | bytes 98336 | tf_op jit(solution)/shard_map/ppermute | solution.py:487
  63.3 0.0 copy-done
  63.3 1.2 %shard_map.110 = bf16[192,1024]{1,0:T(8,128)(2,1)S(1)} custom-call(bf16[384,128]{1,0:T(8,128)(2,1)S(1)} %get-tuple-element.71.refs_0_, bf16[384,128]{1,0:T(8,128)(2,1)S(1)} %collective-permute-done.10.refs_1_, bf16[384,128]{1,0:T(8,128)(2,1)S(1)} %collective-permute-done.11.refs_2_, bf16[384,128]{1,0:T(8,128)(2,1)S(1)} %collective-permute-done.12.refs_3_, ...), custom_call_target="tpu_custom_call" | custom-call | flops 603979776 | bytes 4000000 | tf_op jit(solution)/shard_map/pallas_call | solution.py:634
  64.5 1.7 %collective-permute-start.21 = (bf16[192,1024]{1,0:T(8,128)(2,1)S(1)}, bf16[192,1024]{1,0:T(8,128)(2,1)S(1)}, u32[]{:S(2)}, u32[]{:S(2)}) collective-permute-start(bf16[192,1024]{1,0:T(8,128)(2,1)S(1)} %shard_map.110), channel_id=1, source_target_pairs={{0,1},{1,0},{2,3},{3,2},{4,5},{5,4},{6,7},{7,6},{8,9},{9,8},{10,11... | collective-permute-start | bytes 1179656 | tf_op jit(solution)/shard_map/ppermute | solution.py:653
  66.2 0.0 collective-permute-start.18
  66.2 1.5 %collective-permute-start.19 = (bf16[192,256]{1,0:T(8,128)(2,1)S(1)}, bf16[192,256]{1,0:T(8,128)(2,1)S(1)}, u32[]{:S(2)}, u32[]{:S(2)}) collective-permute-start(bf16[192,256]{1,0:T(8,128)(2,1)S(1)} %get-tuple-element.90), channel_id=1, source_target_pairs={{0,4},{2,6},{4,0},{6,2},{8,12},{10,14},{12,8},{14,10},{16,20},{18,... | collective-permute-start | bytes 294920 | tf_op jit(solution)/shard_map/ppermute | solution.py:487
  67.7 0.3 collective-permute-start.20
  68.1 0.0 collective-permute-done.18.refs_9_
  68.1 3.7 %collective-permute-done.19.refs_10_ = bf16[192,256]{1,0:T(8,128)(2,1)S(1)} collective-permute-done((bf16[192,256]{1,0:T(8,128)(2,1)S(1)}, bf16[192,256]{1,0:T(8,128)(2,1)S(1)}, u32[]{:S(2)}, u32[]{:S(2)}) %collective-permute-start.19) | collective-permute-done | bytes 98336 | tf_op jit(solution)/shard_map/ppermute | solution.py:487
  71.8 1.3 %collective-permute-done.20.refs_11_ = bf16[192,256]{1,0:T(8,128)(2,1)S(1)} collective-permute-done((bf16[192,256]{1,0:T(8,128)(2,1)S(1)}, bf16[192,256]{1,0:T(8,128)(2,1)S(1)}, u32[]{:S(2)}, u32[]{:S(2)}) %collective-permute-start.20) | collective-permute-done | bytes 98336 | tf_op jit(solution)/shard_map/ppermute | solution.py:487
  73.1 2.0 %shard_map.109 = (bf16[384,512]{1,0:T(8,128)(2,1)}, bf16[384,512]{1,0:T(8,128)(2,1)}, bf16[384,512]{1,0:T(8,128)(2,1)}, f32[192,1024]{1,0:T(8,128)S(1)}) custom-call(bf16[384,128]{1,0:T(8,128)(2,1)S(1)} %get-tuple-element.71.refs_0_, bf16[384,128]{1,0:T(8,128)(2,1)S(1)} %collective-permute-done.10.refs_1_, ...), custom_call_target="tpu_custom_call" | custom-call | flops 603979776 | bytes 6000000 | tf_op jit(solution)/shard_map/pallas_call | solution.py:643
  75.1 0.7 collective-permute-done.21
  75.8 0.8 %add_convert_fusion = bf16[192,1024]{1,0:T(8,128)(2,1)} fusion(f32[192,1024]{1,0:T(8,128)S(1)} %get-tuple-element.95, bf16[192,1024]{1,0:T(8,128)(2,1)S(1)} %collective-permute-done.21), kind=kLoop, calls=%fused_computation | loop fusion | flops 589824 | bytes 1572864 | tf_op jit(solution)/shard_map/convert_element_type | solution.py:655
  (3 shorter events, 0.0 us)
Async XLA Ops:
  0.6 21.2 %copy-start.5 = (s32[48,8]{0,1:T(8,128)S(1)}, s32[48,8]{0,1:T(8,128)}, u32[]{:S(2)}) copy-start(s32[48,8]{0,1:T(8,128)} %param.12) | copy-start | bytes 4612
  3.1 3.2 %collective-permute-start = (bf16[384,256]{1,0:T(8,128)(2,1)}, bf16[384,256]{1,0:T(8,128)(2,1)S(1)}, u32[]{:S(2)}, u32[]{:S(2)}) collective-permute-start(bf16[384,256]{1,0:T(8,128)(2,1)} %get-tuple-element.51), channel_id=1, source_target_pairs={{0,2},{2,0},{4,6},{6,4},{8,10},{10,8},{12,14},{14,12},{16,18},{18,... | collective-permute-start | bytes 589832 | tf_op jit(solution)/shard_map/ppermute | solution.py:487
  3.6 8.6 %collective-permute-start.1 = (bf16[384,256]{1,0:T(8,128)(2,1)}, bf16[384,256]{1,0:T(8,128)(2,1)S(1)}, u32[]{:S(2)}, u32[]{:S(2)}) collective-permute-start(bf16[384,256]{1,0:T(8,128)(2,1)} %get-tuple-element.53), channel_id=1, source_target_pairs={{0,4},{2,6},{4,0},{6,2},{8,12},{10,14},{12,8},{14,10},{16,20},{18,... | collective-permute-start | bytes 589832 | tf_op jit(solution)/shard_map/ppermute | solution.py:487
  6.2 9.7 %collective-permute-start.2 = (bf16[384,256]{1,0:T(8,128)(2,1)}, bf16[384,256]{1,0:T(8,128)(2,1)S(1)}, u32[]{:S(2)}, u32[]{:S(2)}) collective-permute-start(bf16[384,256]{1,0:T(8,128)(2,1)} %get-tuple-element.54), channel_id=1, source_target_pairs={{0,6},{2,4},{4,2},{6,0},{8,14},{10,12},{12,10},{14,8},{16,22},{18,... | collective-permute-start | bytes 589832 | tf_op jit(solution)/shard_map/ppermute | solution.py:487
  6.3 1.0 %copy-start.1 = (bf16[384,512]{1,0:T(8,128)(2,1)S(1)}, bf16[384,512]{1,0:T(8,128)(2,1)}, u32[]{:S(2)}) copy-start(bf16[384,512]{1,0:T(8,128)(2,1)} %q_ref.1) | copy-start | bytes 1179652
  7.3 1.0 %copy-start.2 = (bf16[384,512]{1,0:T(8,128)(2,1)S(1)}, bf16[384,512]{1,0:T(8,128)(2,1)}, u32[]{:S(2)}) copy-start(bf16[384,512]{1,0:T(8,128)(2,1)} %g_ref.1) | copy-start | bytes 1179652
  8.3 0.9 %copy-start.3 = (bf16[384,256]{1,0:T(8,128)(2,1)S(1)}, bf16[384,256]{1,0:T(8,128)(2,1)}, u32[]{:S(2)}) copy-start(bf16[384,256]{1,0:T(8,128)(2,1)} %get-tuple-element.50.mine_ref) | copy-start | bytes 589828
  9.2 0.7 copy-start.4
  16.8 14.8 %collective-permute-start.3 = (bf16[1024,256]{1,0:T(8,128)(2,1)}, bf16[1024,256]{1,0:T(8,128)(2,1)S(1)}, u32[]{:S(2)}, u32[]{:S(2)}) collective-permute-start(bf16[1024,256]{1,0:T(8,128)(2,1)} %get-tuple-element.60), channel_id=1, source_target_pairs={{0,8},{1,9},{2,3},{3,2},{4,12},{5,13},{6,7},{7,6},{8,0},{9,1},{10,... | collective-permute-start | bytes 1572872 | tf_op jit(solution)/shard_map/ppermute | solution.py:499
  18.4 13.1 %collective-permute-start.4 = (bf16[1024,256]{1,0:T(8,128)(2,1)S(1)}, bf16[1024,256]{1,0:T(8,128)(2,1)S(1)}, u32[]{:S(2)}, u32[]{:S(2)}) collective-permute-start(bf16[1024,256]{1,0:T(8,128)(2,1)S(1)} %get-tuple-element.61), channel_id=1, source_target_pairs={{0,1},{1,0},{2,10},{3,11},{4,5},{5,4},{6,14},{7,15},{8,16},{9,17},... | collective-permute-start | bytes 1572872 | tf_op jit(solution)/shard_map/ppermute | solution.py:499
  19.9 1.9 %collective-permute-start.5 = (bf16[400,256]{1,0:T(8,128)(2,1)S(1)}, bf16[400,256]{1,0:T(8,128)(2,1)S(1)}, u32[]{:S(2)}, u32[]{:S(2)}) collective-permute-start(bf16[400,256]{1,0:T(8,128)(2,1)S(1)} %get-tuple-element.62), channel_id=1, source_target_pairs={{0,2},{2,0},{4,6},{6,4},{8,10},{10,8},{12,14},{14,12},{16,18},{18,... | collective-permute-start | bytes 614408 | tf_op jit(solution)/shard_map/ppermute | solution.py:487
  19.9 8.0 %collective-permute-start.6 = (bf16[400,256]{1,0:T(8,128)(2,1)S(1)}, bf16[400,256]{1,0:T(8,128)(2,1)}, u32[]{:S(2)}, u32[]{:S(2)}) collective-permute-start(bf16[400,256]{1,0:T(8,128)(2,1)S(1)} %get-tuple-element.63), channel_id=1, source_target_pairs={{0,4},{2,6},{4,0},{6,2},{8,12},{10,14},{12,8},{14,10},{16,20},{18,... | collective-permute-start | bytes 614408 | tf_op jit(solution)/shard_map/ppermute | solution.py:487
  21.5 10.1 %collective-permute-start.7 = (bf16[400,256]{1,0:T(8,128)(2,1)S(1)}, bf16[400,256]{1,0:T(8,128)(2,1)}, u32[]{:S(2)}, u32[]{:S(2)}) collective-permute-start(bf16[400,256]{1,0:T(8,128)(2,1)S(1)} %get-tuple-element.64), channel_id=1, source_target_pairs={{0,6},{2,4},{4,2},{6,0},{8,14},{10,12},{12,10},{14,8},{16,22},{18,... | collective-permute-start | bytes 614408 | tf_op jit(solution)/shard_map/ppermute | solution.py:487
  40.0 10.6 %collective-permute-start.8 = (bf16[4,128,256]{2,1,0:T(8,128)(2,1)S(1)}, bf16[4,128,256]{2,1,0:T(8,128)(2,1)S(1)}, u32[]{:S(2)}, u32[]{:S(2)}) collective-permute-start(bf16[4,128,256]{2,1,0:T(8,128)(2,1)S(1)} %get-tuple-element.73), channel_id=1, source_target_pairs={{0,8},{1,9},{2,3},{3,2},{4,12},{5,13},{6,7},{7,6},{8,0},{9,1},{10,... | collective-permute-start | bytes 786440 | tf_op jit(solution)/shard_map/ppermute | solution.py:499
  41.7 8.9 %collective-permute-start.9 = (bf16[4,128,256]{2,1,0:T(8,128)(2,1)S(1)}, bf16[4,128,256]{2,1,0:T(8,128)(2,1)S(1)}, u32[]{:S(2)}, u32[]{:S(2)}) collective-permute-start(bf16[4,128,256]{2,1,0:T(8,128)(2,1)S(1)} %get-tuple-element.74), channel_id=1, source_target_pairs={{0,1},{1,0},{2,10},{3,11},{4,5},{5,4},{6,14},{7,15},{8,16},{9,17},... | collective-permute-start | bytes 786440 | tf_op jit(solution)/shard_map/ppermute | solution.py:499
  47.7 8.1 %collective-permute-start.13 = (bf16[4,128,256]{2,1,0:T(8,128)(2,1)S(1)}, bf16[4,128,256]{2,1,0:T(8,128)(2,1)S(1)}, u32[]{:S(2)}, u32[]{:S(2)}) collective-permute-start(bf16[4,128,256]{2,1,0:T(8,128)(2,1)S(1)} %get-tuple-element.82), channel_id=1, source_target_pairs={{0,8},{1,9},{2,3},{3,2},{4,12},{5,13},{6,7},{7,6},{8,0},{9,1},{10,... | collective-permute-start | bytes 786440 | tf_op jit(solution)/shard_map/ppermute | solution.py:499
  49.4 6.4 %collective-permute-start.14 = (bf16[4,128,256]{2,1,0:T(8,128)(2,1)S(1)}, bf16[4,128,256]{2,1,0:T(8,128)(2,1)S(1)}, u32[]{:S(2)}, u32[]{:S(2)}) collective-permute-start(bf16[4,128,256]{2,1,0:T(8,128)(2,1)S(1)} %get-tuple-element.83), channel_id=1, source_target_pairs={{0,1},{1,0},{2,10},{3,11},{4,5},{5,4},{6,14},{7,15},{8,16},{9,17},... | collective-permute-start | bytes 786440 | tf_op jit(solution)/shard_map/ppermute | solution.py:499
  50.6 12.7 %copy-start = (bf16[3,1024,512]{2,1,0:T(8,128)(2,1)S(1)}, bf16[3,1024,512]{2,1,0:T(8,128)(2,1)}, u32[]{:S(2)}) copy-start(bf16[3,1024,512]{2,1,0:T(8,128)(2,1)} %refs_8_.1) | copy-start | bytes 9437188
  50.7 7.2 %collective-permute-start.10 = (bf16[384,128]{1,0:T(8,128)(2,1)S(1)}, bf16[384,128]{1,0:T(8,128)(2,1)S(1)}, u32[]{:S(2)}, u32[]{:S(2)}) collective-permute-start(bf16[384,128]{1,0:T(8,128)(2,1)S(1)} %get-tuple-element.78), channel_id=1, source_target_pairs={{0,2},{2,0},{4,6},{6,4},{8,10},{10,8},{12,14},{14,12},{16,18},{18,... | collective-permute-start | bytes 294920 | tf_op jit(solution)/shard_map/ppermute | solution.py:487
  50.8 7.5 %collective-permute-start.11 = (bf16[384,128]{1,0:T(8,128)(2,1)S(1)}, bf16[384,128]{1,0:T(8,128)(2,1)S(1)}, u32[]{:S(2)}, u32[]{:S(2)}) collective-permute-start(bf16[384,128]{1,0:T(8,128)(2,1)S(1)} %get-tuple-element.79), channel_id=1, source_target_pairs={{0,4},{2,6},{4,0},{6,2},{8,12},{10,14},{12,8},{14,10},{16,20},{18,... | collective-permute-start | bytes 294920 | tf_op jit(solution)/shard_map/ppermute | solution.py:487
  52.4 5.9 %collective-permute-start.12 = (bf16[384,128]{1,0:T(8,128)(2,1)S(1)}, bf16[384,128]{1,0:T(8,128)(2,1)S(1)}, u32[]{:S(2)}, u32[]{:S(2)}) collective-permute-start(bf16[384,128]{1,0:T(8,128)(2,1)S(1)} %get-tuple-element.80), channel_id=1, source_target_pairs={{0,6},{2,4},{4,2},{6,0},{8,14},{10,12},{12,10},{14,8},{16,22},{18,... | collective-permute-start | bytes 294920 | tf_op jit(solution)/shard_map/ppermute | solution.py:487
  56.3 2.0 %collective-permute-start.15 = (bf16[192,256]{1,0:T(8,128)(2,1)S(1)}, bf16[192,256]{1,0:T(8,128)(2,1)S(1)}, u32[]{:S(2)}, u32[]{:S(2)}) collective-permute-start(bf16[192,256]{1,0:T(8,128)(2,1)S(1)} %get-tuple-element.85), channel_id=1, source_target_pairs={{0,2},{2,0},{4,6},{6,4},{8,10},{10,8},{12,14},{14,12},{16,18},{18,... | collective-permute-start | bytes 294920 | tf_op jit(solution)/shard_map/ppermute | solution.py:487
  56.4 5.7 %collective-permute-start.16 = (bf16[192,256]{1,0:T(8,128)(2,1)S(1)}, bf16[192,256]{1,0:T(8,128)(2,1)S(1)}, u32[]{:S(2)}, u32[]{:S(2)}) collective-permute-start(bf16[192,256]{1,0:T(8,128)(2,1)S(1)} %get-tuple-element.86), channel_id=1, source_target_pairs={{0,4},{2,6},{4,0},{6,2},{8,12},{10,14},{12,8},{14,10},{16,20},{18,... | collective-permute-start | bytes 294920 | tf_op jit(solution)/shard_map/ppermute | solution.py:487
  58.0 5.3 %collective-permute-start.17 = (bf16[192,256]{1,0:T(8,128)(2,1)S(1)}, bf16[192,256]{1,0:T(8,128)(2,1)S(1)}, u32[]{:S(2)}, u32[]{:S(2)}) collective-permute-start(bf16[192,256]{1,0:T(8,128)(2,1)S(1)} %get-tuple-element.87), channel_id=1, source_target_pairs={{0,6},{2,4},{4,2},{6,0},{8,14},{10,12},{12,10},{14,8},{16,22},{18,... | collective-permute-start | bytes 294920 | tf_op jit(solution)/shard_map/ppermute | solution.py:487
  64.5 11.4 %collective-permute-start.21 = (bf16[192,1024]{1,0:T(8,128)(2,1)S(1)}, bf16[192,1024]{1,0:T(8,128)(2,1)S(1)}, u32[]{:S(2)}, u32[]{:S(2)}) collective-permute-start(bf16[192,1024]{1,0:T(8,128)(2,1)S(1)} %shard_map.110), channel_id=1, source_target_pairs={{0,1},{1,0},{2,3},{3,2},{4,5},{5,4},{6,7},{7,6},{8,9},{9,8},{10,11... | collective-permute-start | bytes 1179656 | tf_op jit(solution)/shard_map/ppermute | solution.py:653
  66.2 1.9 %collective-permute-start.18 = (bf16[192,256]{1,0:T(8,128)(2,1)S(1)}, bf16[192,256]{1,0:T(8,128)(2,1)S(1)}, u32[]{:S(2)}, u32[]{:S(2)}) collective-permute-start(bf16[192,256]{1,0:T(8,128)(2,1)S(1)} %get-tuple-element.89), channel_id=1, source_target_pairs={{0,2},{2,0},{4,6},{6,4},{8,10},{10,8},{12,14},{14,12},{16,18},{18,... | collective-permute-start | bytes 294920 | tf_op jit(solution)/shard_map/ppermute | solution.py:487
  66.2 5.6 %collective-permute-start.19 = (bf16[192,256]{1,0:T(8,128)(2,1)S(1)}, bf16[192,256]{1,0:T(8,128)(2,1)S(1)}, u32[]{:S(2)}, u32[]{:S(2)}) collective-permute-start(bf16[192,256]{1,0:T(8,128)(2,1)S(1)} %get-tuple-element.90), channel_id=1, source_target_pairs={{0,4},{2,6},{4,0},{6,2},{8,12},{10,14},{12,8},{14,10},{16,20},{18,... | collective-permute-start | bytes 294920 | tf_op jit(solution)/shard_map/ppermute | solution.py:487
  67.7 5.4 %collective-permute-start.20 = (bf16[192,256]{1,0:T(8,128)(2,1)S(1)}, bf16[192,256]{1,0:T(8,128)(2,1)S(1)}, u32[]{:S(2)}, u32[]{:S(2)}) collective-permute-start(bf16[192,256]{1,0:T(8,128)(2,1)S(1)} %get-tuple-element.91), channel_id=1, source_target_pairs={{0,6},{2,4},{4,2},{6,0},{8,14},{10,12},{12,10},{14,8},{16,22},{18,... | collective-permute-start | bytes 294920 | tf_op jit(solution)/shard_map/ppermute | solution.py:487
